TPU v7x, 512 devices: a whole 4x8x8 slice. The times are simulated.
512 devices in a mesh: dp: 16 (over y, core), expert: 32 (over z, x).
Axes of the slice: x: 4, y: 8, z: 8, core: 2. Of those that a mesh axis runs over, the one named last changes fastest.
Arguments:
- tokens: bfloat16 [1024, 4096], P('expert', 'dp'), may hold values from -6 to 6
- out_grad: bfloat16 [1024, 4096], P('expert', 'dp'), may hold values from -6 to 6
- routes: int32 [1024, 8], P('expert'), may hold values from 0 to 31, all different within a row; in each aligned block of 32 rows (0 to 31, 32 to 63, ...) at most 12 rows name the same one
- route_weights: float32 [1024, 8], P('expert'), may hold values from 0.1 to 0.5
- gate_weight: bfloat16 [32, 4096, 768], P('expert', 'dp'), may hold values from -0.09375 to 0.09375
- up_weight: bfloat16 [32, 4096, 768], P('expert', 'dp'), may hold values from -0.09375 to 0.09375
- down_weight: bfloat16 [32, 768, 4096], P('expert', None, 'dp'), may hold values from -0.21875 to 0.21875
- sign_bits: int32 [32, 128], replicated, may hold values from 0 to 1
- partner: int32 [32], replicated, may hold values from 0 to 31, as said below
Outputs:
- gate_grad: bfloat16 [32, 4096, 768], P('expert', 'dp')
- up_grad: bfloat16 [32, 4096, 768], P('expert', 'dp')
- down_grad: bfloat16 [32, 768, 4096], P('expert', None, 'dp')
- input_grad: bfloat16 [1024, 4096], P('expert', 'dp')
Inputs may be any that keep to these rules, and one draw needn't show every extreme that they name: `routes`: each row names 8 different experts; among the 32 rows of one expert-axis index no expert is named by more than 12 rows, a bound that some block reaches. partner[partner[e]] = e; partner[e] is e or differs from e in exactly one bit; every bit position of the expert number is used by some pair.
All inputs are finite; a program needn't handle non-finite values.
Results may differ from a plain program's by a relative error of at most 0.04.
Values may be sent and summed in bfloat16 or wider, within the bound.
No kernel may reach another device: no remote copies, remote signals or barrier semaphores. Data moves between devices by JAX's collectives and lax.ppermute only.
A program may use at most 64 MiB of HBM per device.

v0:
```python
import math

import jax
import jax.numpy as jnp
from jax import lax
from jax.sharding import PartitionSpec as P

HBLOCK = 128


EPS = 1e-06
QSTEP = 2.0
TWO_PI = 2.0 * math.pi


def partner_2(x, axis, apart):
    return lax.ppermute(x, axis, [(i, i ^ 1 << apart) for i in range(lax.axis_size(axis))])


def sylvester(block_len):
    positions = jnp.arange(block_len, dtype=jnp.int32)
    common_bits = positions[:, None] & positions[None, :]
    parity = jnp.zeros((block_len, block_len), jnp.int32)
    for bit_pos in range(block_len.bit_length() - 1):
        parity = parity ^ common_bits >> bit_pos & 1
    return (1 - 2 * parity).astype(jnp.bfloat16)


def slot_tables(routes, weights, expert_count, capacity):
    experts_iota = jnp.arange(expert_count, dtype=jnp.int32)
    hit_table = (routes[:, :, None] == experts_iota[None, None, :]).astype(jnp.int32)
    member = jnp.sum(hit_table, axis=1)
    weight_sum = jnp.sum(hit_table.astype(jnp.float32) * weights[:, :, None], axis=1)
    rank_table = jnp.cumsum(member, axis=0) - member
    cap_iota = jnp.arange(capacity, dtype=jnp.int32)
    placed = (
        (rank_table[:, :, None] == cap_iota[None, None, :]) & (member[:, :, None] == 1)
    ).astype(jnp.float32)
    placed = jnp.transpose(placed, (1, 2, 0))
    slot_weight = jnp.einsum("ect,te->ec", placed, weight_sum, precision=lax.Precision.HIGHEST)
    return (placed, slot_weight)


def activation_grads(gate_sum, up_sum, hid_grad):
    sigmoid_val = jax.nn.sigmoid(gate_sum)
    silu_val = gate_sum * sigmoid_val
    hidden = (silu_val * up_sum).astype(jnp.bfloat16)
    gate_rows = (hid_grad * up_sum * sigmoid_val * (1.0 + gate_sum * (1.0 - sigmoid_val))).astype(
        jnp.bfloat16
    )
    up_rows = (hid_grad * silu_val).astype(jnp.bfloat16)
    return (hidden, gate_rows, up_rows)


def rotate_quant(operand, flip_signs, hadamard):
    row_count, col_count = operand.shape
    block_len = hadamard.shape[0]
    blocks = operand.reshape(row_count // block_len, block_len, col_count)
    signed = blocks * flip_signs[None, :, None]
    rotated = jnp.einsum("ij,bjc->bic", hadamard, signed, preferred_element_type=jnp.float32)
    meansq = jnp.mean(rotated * rotated, axis=1, keepdims=True)
    scale_val = jnp.sqrt(meansq + EPS)
    steps_t = QSTEP * rotated / scale_val
    softened = (steps_t - jnp.sin(TWO_PI * steps_t) / TWO_PI) * scale_val / QSTEP
    return softened.astype(jnp.bfloat16).reshape(row_count, col_count)


def contract_rows(left, right):
    return lax.dot_general(
        left, right, (((0,), (0,)), ((), ())), preferred_element_type=jnp.float32
    )


def contract_cols(left, right):
    return lax.dot_general(
        left, right, (((1,), (1,)), ((), ())), preferred_element_type=jnp.float32
    )


def shards(
    tokens, out_grad, routes, route_weights, gate_weight, up_weight, down_weight, sign_bits, partner
):
    expert_count = lax.axis_size("expert")
    tok_count = tokens.shape[0]
    capacity = min(tok_count, tok_count * routes.shape[1] * 3 // (2 * expert_count))
    row_total = expert_count * capacity
    my_index = lax.axis_index("expert")
    mate_index = partner[my_index]
    placed, slot_weight = slot_tables(routes, route_weights, expert_count, capacity)
    gate_local = gate_weight[0]
    up_local = up_weight[0]
    down_local = down_weight[0]
    picker = placed.astype(jnp.bfloat16)
    send_tok = jnp.einsum("ect,td->ecd", picker, tokens, preferred_element_type=jnp.float32).astype(
        jnp.bfloat16
    )
    send_grad = (
        jnp.einsum("ect,td->ecd", picker, out_grad, preferred_element_type=jnp.float32)
        * slot_weight[:, :, None]
    )
    send_grad = send_grad.astype(jnp.bfloat16)
    recv_tok, recv_grad = (
        lax.all_to_all(send_tok, "expert", split_axis=0, concat_axis=0, tiled=True),
        lax.all_to_all(send_grad, "expert", split_axis=0, concat_axis=0, tiled=True),
    )
    rows_in = recv_tok.reshape(row_total, recv_tok.shape[2])
    rows_grad = recv_grad.reshape(row_total, recv_grad.shape[2])
    gate_part = jnp.dot(rows_in, gate_local, preferred_element_type=jnp.float32)
    up_part = jnp.dot(rows_in, up_local, preferred_element_type=jnp.float32)
    hidden_part = contract_cols(rows_grad, down_local)
    gate_sum, up_sum, hid_grad = (
        lax.psum(gate_part.astype(jnp.bfloat16), "dp").astype(jnp.float32),
        lax.psum(up_part.astype(jnp.bfloat16), "dp").astype(jnp.float32),
        lax.psum(hidden_part.astype(jnp.bfloat16), "dp").astype(jnp.float32),
    )
    hidden, gate_rows, up_rows = activation_grads(gate_sum, up_sum, hid_grad)
    slot_back = (contract_cols(gate_rows, gate_local) + contract_cols(up_rows, up_local)).astype(
        jnp.bfloat16
    )
    returned_rows = lax.all_to_all(
        slot_back.reshape(expert_count, capacity, slot_back.shape[1]),
        "expert",
        split_axis=0,
        concat_axis=0,
        tiled=True,
    )
    input_grad = jnp.einsum(
        "ect,ecd->td", picker, returned_rows, preferred_element_type=jnp.float32
    ).astype(jnp.bfloat16)
    hadamard = sylvester(HBLOCK)
    flip_row = lax.dynamic_slice_in_dim(sign_bits, my_index, 1, 0)[0]
    flip_signs = (1 - 2 * flip_row).astype(jnp.bfloat16)
    quant_in = rotate_quant(rows_in, flip_signs, hadamard)
    gate_new = (
        contract_rows(quant_in, rotate_quant(gate_rows, flip_signs, hadamard)) * (1.0 / HBLOCK)
    ).astype(jnp.bfloat16)
    up_new = (
        contract_rows(quant_in, rotate_quant(up_rows, flip_signs, hadamard)) * (1.0 / HBLOCK)
    ).astype(jnp.bfloat16)
    down_new = (
        contract_rows(
            rotate_quant(hidden, flip_signs, hadamard),
            rotate_quant(rows_grad, flip_signs, hadamard),
        )
        * (1.0 / HBLOCK)
    ).astype(jnp.bfloat16)
    for bit_pos in range(expert_count.bit_length() - 1):
        arrived = partner_2((gate_new, up_new, down_new), "expert", bit_pos)
        take_it = mate_index == my_index ^ 1 << bit_pos
        gate_new = jnp.where(take_it, arrived[0], gate_new)
        up_new = jnp.where(take_it, arrived[1], up_new)
        down_new = jnp.where(take_it, arrived[2], down_new)
    return (gate_new[None], up_new[None], down_new[None], input_grad)


def solution(mesh):
    return jax.shard_map(
        shards,
        mesh=mesh,
        in_specs=(
            P("expert", "dp"),
            P("expert", "dp"),
            P("expert", None),
            P("expert", None),
            P("expert", "dp", None),
            P("expert", "dp", None),
            P("expert", None, "dp"),
            P(),
            P(),
        ),
        out_specs=(
            P("expert", "dp", None),
            P("expert", "dp", None),
            P("expert", None, "dp"),
            P("expert", "dp"),
        ),
        check_vma=False,
    )
```

profile of v0, /device:TPU:2, one launch (start us, length us, event | category | flops | bytes accessed | tf_op | source)
XLA Modules:
  0.0 374.8 jit_solution(9212636119916966859)
XLA Ops:
  10.0 13.5 %all-to-all-start = ((bf16[32,12,256]{2,1,0:T(8,128)(2,1)}), bf16[32,12,256]{2,1,0:T(8,128)(2,1)S(1)}, u32[]{:S(2)}, u32[]{:S(2)}) async-start(bf16[32,12,256]{2,1,0:T(8,128)(2,1)} %copy.45), calls=%async_computation | async-start | bytes 524288 | tf_op jit(solution)/shard_map/all_to_all | solution.py:103
  29.4 5.3 %all-to-all-done = bf16[32,12,256]{2,1,0:T(8,128)(2,1)S(1)} async-done(((bf16[32,12,256]{2,1,0:T(8,128)(2,1)}), bf16[32,12,256]{2,1,0:T(8,128)(2,1)S(1)}, u32[]{:S(2)}, u32[]{:S(2)}) %all-to-all-start) | async-done | bytes 196640 | tf_op jit(solution)/shard_map/all_to_all | solution.py:103
  34.7 5.6 %all-to-all-start.1 = ((bf16[32,12,256]{2,1,0:T(8,128)(2,1)}), bf16[32,12,256]{2,1,0:T(8,128)(2,1)S(1)}, u32[]{:S(2)}, u32[]{:S(2)}) async-start(bf16[32,12,256]{2,1,0:T(8,128)(2,1)} %copy.48), calls=%async_computation.1 | async-start | bytes 524288 | tf_op jit(solution)/shard_map/all_to_all | solution.py:104
  42.7 8.0 %all-to-all-done.1 = bf16[32,12,256]{2,1,0:T(8,128)(2,1)S(1)} async-done(((bf16[32,12,256]{2,1,0:T(8,128)(2,1)}), bf16[32,12,256]{2,1,0:T(8,128)(2,1)S(1)}, u32[]{:S(2)}, u32[]{:S(2)}) %all-to-all-start.1) | async-done | bytes 196640 | tf_op jit(solution)/shard_map/all_to_all | solution.py:104
  52.6 115.1 %all-reduce.3.cloned.1.call-done = (bf16[384,768]{1,0:T(8,128)(2,1)}, bf16[384,768]{1,0:T(8,128)(2,1)}, bf16[384,768]{1,0:T(8,128)(2,1)}) async-done(((bf16[384,768]{1,0:T(8,128)(2,1)}, bf16[384,768]{1,0:T(8,128)(2,1)}, bf16[384,768]{1,0:T(8,128)(2,1)}), (bf16[384,768]{1,0:T(8,128)(2,1)}, bf16[384,768]{1,0:T(8,128)(2,1)}, bf16[384,768]{1,0:T(8,128)(2,1)})) %all-reduce.3.cloned.1.call-update) | async-done | bytes 1769488 | tf_op jit(solution)/shard_map/psum | solution.py:113
  170.3 5.6 %fusion.5 = bf16[768,256]{1,0:T(8,128)(2,1)S(1)} fusion(f32[3,768,128]{1,2,0:T(8,128)S(1)} %get-tuple-element.17, f32[3,768]{1,0:T(4,128)S(1)} %add_sqrt_fusion, f32[3,256,128]{1,2,0:T(8,128)S(1)} %get-tuple-element.19, f32[3,256]{1,0:T(4,128)S(1)} %add_sqrt_fusion.3), kind=kOutput, calls=%fused_computation.17 | convolution fusion | flops 154533888 | bytes 1978368 | tf_op jit(solution)/shard_map/dot_general | solution.py:69
  175.9 3.6 collective-permute-start.10
  179.9 5.6 %fusion.4 = bf16[256,768]{1,0:T(8,128)(2,1)S(1)} fusion(f32[3,768,128]{1,2,0:T(8,128)S(1)} %get-tuple-element.15, f32[3,768]{1,0:T(4,128)S(1)} %add_sqrt_fusion.1, f32[3,256,128]{1,2,0:T(8,128)S(1)} %get-tuple-element.13, f32[3,256]{1,0:T(4,128)S(1)} %add_sqrt_fusion.4), kind=kOutput, calls=%fused_computation.16 | convolution fusion | flops 154533888 | bytes 1978368 | tf_op jit(solution)/shard_map/dot_general | solution.py:69
  185.5 2.4 collective-permute-start.5
  189.9 10.5 %all-to-all-start.2 = ((bf16[32,12,256]{2,1,0:T(8,128)(2,1)}), bf16[32,12,256]{2,1,0:T(8,128)(2,1)S(1)}, u32[]{:S(2)}, u32[]{:S(2)}) async-start(bf16[32,12,256]{2,1,0:T(8,128)(2,1)} %reshape.104), calls=%async_computation.2 | async-start | bytes 524288 | tf_op jit(solution)/shard_map/all_to_all | solution.py:120
  200.4 5.6 %fusion.3 = bf16[256,768]{1,0:T(8,128)(2,1)S(1)} fusion(f32[3,768,128]{1,2,0:T(8,128)S(1)} %get-tuple-element.11, f32[3,768]{1,0:T(4,128)S(1)} %add_sqrt_fusion.2, f32[3,256,128]{1,2,0:T(8,128)S(1)} %get-tuple-element.13, f32[3,256]{1,0:T(4,128)S(1)} %add_sqrt_fusion.4), kind=kOutput, calls=%fused_computation.15 | convolution fusion | flops 154533888 | bytes 1978368 | tf_op jit(solution)/shard_map/dot_general | solution.py:69
  206.0 2.4 collective-permute-start
  208.4 2.8 all-to-all-done.2
  212.1 4.0 %collective-permute-start.11 = (bf16[768,256]{1,0:T(8,128)(2,1)S(1)}, bf16[768,256]{1,0:T(8,128)(2,1)S(1)}, u32[]{:S(2)}, u32[]{:S(2)}) collective-permute-start(bf16[768,256]{1,0:T(8,128)(2,1)S(1)} %broadcast_select_fusion), channel_id=1, source_target_pairs={{0,2},{1,3},{2,0},{3,1},{4,6},{5,7},{6,4},{7,5},{8,10},{9,11},{10,... | collective-permute-start | bytes 1179656 | tf_op jit(solution)/shard_map/ppermute | solution.py:17
  216.2 3.3 collective-permute-start.6
  219.8 4.2 %collective-permute-start.1 = (bf16[256,768]{1,0:T(8,128)(2,1)S(1)}, bf16[256,768]{1,0:T(8,128)(2,1)S(1)}, u32[]{:S(2)}, u32[]{:S(2)}) collective-permute-start(bf16[256,768]{1,0:T(8,128)(2,1)S(1)} %broadcast_select_fusion.5), channel_id=1, source_target_pairs={{0,2},{1,3},{2,0},{3,1},{4,6},{5,7},{6,4},{7,5},{8,10},{9,11},{10,... | collective-permute-start | bytes 1179656 | tf_op jit(solution)/shard_map/ppermute | solution.py:17
  224.0 5.3 %collective-permute-done.11 = bf16[768,256]{1,0:T(8,128)(2,1)S(1)} collective-permute-done((bf16[768,256]{1,0:T(8,128)(2,1)S(1)}, bf16[768,256]{1,0:T(8,128)(2,1)S(1)}, u32[]{:S(2)}, u32[]{:S(2)}) %collective-permute-start.11) | collective-permute-done | bytes 393248 | tf_op jit(solution)/shard_map/ppermute | solution.py:17
  229.3 3.4 collective-permute-start.12
  232.7 5.0 %collective-permute-done.6 = bf16[256,768]{1,0:T(8,128)(2,1)S(1)} collective-permute-done((bf16[256,768]{1,0:T(8,128)(2,1)S(1)}, bf16[256,768]{1,0:T(8,128)(2,1)S(1)}, u32[]{:S(2)}, u32[]{:S(2)}) %collective-permute-start.6) | collective-permute-done | bytes 393248 | tf_op jit(solution)/shard_map/ppermute | solution.py:17
  237.8 3.4 collective-permute-start.7
  241.2 3.0 collective-permute-done.1
  244.3 3.4 collective-permute-start.2
  247.7 4.1 %collective-permute-start.13 = (bf16[768,256]{1,0:T(8,128)(2,1)S(1)}, bf16[768,256]{1,0:T(8,128)(2,1)S(1)}, u32[]{:S(2)}, u32[]{:S(2)}) collective-permute-start(bf16[768,256]{1,0:T(8,128)(2,1)S(1)} %broadcast_select_fusion.2), channel_id=1, source_target_pairs={{0,8},{1,9},{2,10},{3,11},{4,12},{5,13},{6,14},{7,15},{8,0},{9,1},... | collective-permute-start | bytes 1179656 | tf_op jit(solution)/shard_map/ppermute | solution.py:17
  251.9 2.6 collective-permute-start.8
  254.5 8.2 %collective-permute-done.2 = bf16[256,768]{1,0:T(8,128)(2,1)S(1)} collective-permute-done((bf16[256,768]{1,0:T(8,128)(2,1)S(1)}, bf16[256,768]{1,0:T(8,128)(2,1)S(1)}, u32[]{:S(2)}, u32[]{:S(2)}) %collective-permute-start.2) | collective-permute-done | bytes 393248 | tf_op jit(solution)/shard_map/ppermute | solution.py:17
  262.8 2.5 collective-permute-start.3
  265.3 30.9 %collective-permute-done.13 = bf16[768,256]{1,0:T(8,128)(2,1)S(1)} collective-permute-done((bf16[768,256]{1,0:T(8,128)(2,1)S(1)}, bf16[768,256]{1,0:T(8,128)(2,1)S(1)}, u32[]{:S(2)}, u32[]{:S(2)}) %collective-permute-start.13) | collective-permute-done | bytes 393248 | tf_op jit(solution)/shard_map/ppermute | solution.py:17
  296.3 6.3 %collective-permute-start.14 = (bf16[768,256]{1,0:T(8,128)(2,1)S(1)}, bf16[768,256]{1,0:T(8,128)(2,1)S(1)}, u32[]{:S(2)}, u32[]{:S(2)}) collective-permute-start(bf16[768,256]{1,0:T(8,128)(2,1)S(1)} %broadcast_select_fusion.3), channel_id=1, source_target_pairs={{0,16},{1,17},{2,18},{3,19},{4,20},{5,21},{6,22},{7,23},{8,24},{9,... | collective-permute-start | bytes 1179656 | tf_op jit(solution)/shard_map/ppermute | solution.py:17
  302.5 2.2 collective-permute-done.8
  304.8 14.9 %collective-permute-start.9 = (bf16[256,768]{1,0:T(8,128)(2,1)S(1)}, bf16[256,768]{1,0:T(8,128)(2,1)S(1)}, u32[]{:S(2)}, u32[]{:S(2)}) collective-permute-start(bf16[256,768]{1,0:T(8,128)(2,1)S(1)} %broadcast_select_fusion.10), channel_id=1, source_target_pairs={{0,16},{1,17},{2,18},{3,19},{4,20},{5,21},{6,22},{7,23},{8,24},{9,... | collective-permute-start | bytes 1179656 | tf_op jit(solution)/shard_map/ppermute | solution.py:17
  319.7 38.7 %collective-permute-start.4 = (bf16[256,768]{1,0:T(8,128)(2,1)S(1)}, bf16[256,768]{1,0:T(8,128)(2,1)S(1)}, u32[]{:S(2)}, u32[]{:S(2)}) collective-permute-start(bf16[256,768]{1,0:T(8,128)(2,1)S(1)} %broadcast_select_fusion.11), channel_id=1, source_target_pairs={{0,16},{1,17},{2,18},{3,19},{4,20},{5,21},{6,22},{7,23},{8,24},{9,... | collective-permute-start | bytes 1179656 | tf_op jit(solution)/shard_map/ppermute | solution.py:17
  360.1 7.1 %collective-permute-done.4 = bf16[256,768]{1,0:T(8,128)(2,1)S(1)} collective-permute-done((bf16[256,768]{1,0:T(8,128)(2,1)S(1)}, bf16[256,768]{1,0:T(8,128)(2,1)S(1)}, u32[]{:S(2)}, u32[]{:S(2)}) %collective-permute-start.4) | collective-permute-done | bytes 393248 | tf_op jit(solution)/shard_map/ppermute | solution.py:17
  (73 shorter events, 18.6 us)
Async XLA Ops:
  7.2 33.2 %copy-start = (bf16[1,256,768]{2,1,0:T(8,128)(2,1)S(1)}, bf16[1,256,768]{2,1,0:T(8,128)(2,1)}, u32[]{:S(2)}) copy-start(bf16[1,256,768]{2,1,0:T(8,128)(2,1)} %param.13) | copy-start | bytes 1179652
  7.2 16.3 %copy-start.4 = (f32[32,8]{0,1:T(8,128)S(1)}, f32[32,8]{0,1:T(8,128)}, u32[]{:S(2)}) copy-start(f32[32,8]{0,1:T(8,128)} %param.12) | copy-start | bytes 3076
  7.2 16.6 %copy-start.3 = (bf16[32,256]{1,0:T(8,128)(2,1)S(1)}, bf16[32,256]{1,0:T(8,128)(2,1)}, u32[]{:S(2)}) copy-start(bf16[32,256]{1,0:T(8,128)(2,1)} %param.10) | copy-start | bytes 49156
  7.2 17.7 %copy-start.5 = (s32[32]{0:T(128)S(1)}, s32[32]{0:T(128)}, u32[]{:S(2)}) copy-start(s32[32]{0:T(128)} %param.17) | copy-start | bytes 388
  10.0 24.7 %all-to-all-start = ((bf16[32,12,256]{2,1,0:T(8,128)(2,1)}), bf16[32,12,256]{2,1,0:T(8,128)(2,1)S(1)}, u32[]{:S(2)}, u32[]{:S(2)}) async-start(bf16[32,12,256]{2,1,0:T(8,128)(2,1)} %copy.45), calls=%async_computation | async-start | bytes 524288 | tf_op jit(solution)/shard_map/all_to_all | solution.py:103
  24.8 16.7 %copy-start.1 = (bf16[1,256,768]{2,1,0:T(8,128)(2,1)S(1)}, bf16[1,256,768]{2,1,0:T(8,128)(2,1)}, u32[]{:S(2)}) copy-start(bf16[1,256,768]{2,1,0:T(8,128)(2,1)} %param.14) | copy-start | bytes 1179652
  34.7 16.0 %all-to-all-start.1 = ((bf16[32,12,256]{2,1,0:T(8,128)(2,1)}), bf16[32,12,256]{2,1,0:T(8,128)(2,1)S(1)}, u32[]{:S(2)}, u32[]{:S(2)}) async-start(bf16[32,12,256]{2,1,0:T(8,128)(2,1)} %copy.48), calls=%async_computation.1 | async-start | bytes 524288 | tf_op jit(solution)/shard_map/all_to_all | solution.py:104
  40.3 127.5 %all-reduce.3.cloned.1.call-start = ((), (), s32[]{:S(2)}) async-start(), calls=%async_computation.3 | async-start | bytes 3538944 | tf_op jit(solution)/shard_map/psum | solution.py:113
  40.4 10.3 %copy-start.2 = (bf16[1,768,256]{2,1,0:T(8,128)(2,1)S(1)}, bf16[1,768,256]{2,1,0:T(8,128)(2,1)}, u32[]{:S(2)}) copy-start(bf16[1,768,256]{2,1,0:T(8,128)(2,1)} %param.15) | copy-start | bytes 1179652
  175.9 36.2 %collective-permute-start.10 = (bf16[768,256]{1,0:T(8,128)(2,1)S(1)}, bf16[768,256]{1,0:T(8,128)(2,1)}, u32[]{:S(2)}, u32[]{:S(2)}) collective-permute-start(bf16[768,256]{1,0:T(8,128)(2,1)S(1)} %fusion.5), channel_id=1, source_target_pairs={{0,1},{1,0},{2,3},{3,2},{4,5},{5,4},{6,7},{7,6},{8,9},{9,8},{10,11... | collective-permute-start | bytes 1179656 | tf_op jit(solution)/shard_map/ppermute | solution.py:17
  185.5 30.6 %collective-permute-start.5 = (bf16[256,768]{1,0:T(8,128)(2,1)S(1)}, bf16[256,768]{1,0:T(8,128)(2,1)}, u32[]{:S(2)}, u32[]{:S(2)}) collective-permute-start(bf16[256,768]{1,0:T(8,128)(2,1)S(1)} %fusion.4), channel_id=1, source_target_pairs={{0,1},{1,0},{2,3},{3,2},{4,5},{5,4},{6,7},{7,6},{8,9},{9,8},{10,11... | collective-permute-start | bytes 1179656 | tf_op jit(solution)/shard_map/ppermute | solution.py:17
  189.9 21.4 %all-to-all-start.2 = ((bf16[32,12,256]{2,1,0:T(8,128)(2,1)}), bf16[32,12,256]{2,1,0:T(8,128)(2,1)S(1)}, u32[]{:S(2)}, u32[]{:S(2)}) async-start(bf16[32,12,256]{2,1,0:T(8,128)(2,1)} %reshape.104), calls=%async_computation.2 | async-start | bytes 524288 | tf_op jit(solution)/shard_map/all_to_all | solution.py:120
  206.0 13.7 %collective-permute-start = (bf16[256,768]{1,0:T(8,128)(2,1)S(1)}, bf16[256,768]{1,0:T(8,128)(2,1)S(1)}, u32[]{:S(2)}, u32[]{:S(2)}) collective-permute-start(bf16[256,768]{1,0:T(8,128)(2,1)S(1)} %fusion.3), channel_id=1, source_target_pairs={{0,1},{1,0},{2,3},{3,2},{4,5},{5,4},{6,7},{7,6},{8,9},{9,8},{10,11... | collective-permute-start | bytes 1179656 | tf_op jit(solution)/shard_map/ppermute | solution.py:17
  212.1 17.2 %collective-permute-start.11 = (bf16[768,256]{1,0:T(8,128)(2,1)S(1)}, bf16[768,256]{1,0:T(8,128)(2,1)S(1)}, u32[]{:S(2)}, u32[]{:S(2)}) collective-permute-start(bf16[768,256]{1,0:T(8,128)(2,1)S(1)} %broadcast_select_fusion), channel_id=1, source_target_pairs={{0,2},{1,3},{2,0},{3,1},{4,6},{5,7},{6,4},{7,5},{8,10},{9,11},{10,... | collective-permute-start | bytes 1179656 | tf_op jit(solution)/shard_map/ppermute | solution.py:17
  216.2 21.5 %collective-permute-start.6 = (bf16[256,768]{1,0:T(8,128)(2,1)S(1)}, bf16[256,768]{1,0:T(8,128)(2,1)S(1)}, u32[]{:S(2)}, u32[]{:S(2)}) collective-permute-start(bf16[256,768]{1,0:T(8,128)(2,1)S(1)} %broadcast_select_fusion.4), channel_id=1, source_target_pairs={{0,2},{1,3},{2,0},{3,1},{4,6},{5,7},{6,4},{7,5},{8,10},{9,11},{10,... | collective-permute-start | bytes 1179656 | tf_op jit(solution)/shard_map/ppermute | solution.py:17
  219.8 24.4 %collective-permute-start.1 = (bf16[256,768]{1,0:T(8,128)(2,1)S(1)}, bf16[256,768]{1,0:T(8,128)(2,1)S(1)}, u32[]{:S(2)}, u32[]{:S(2)}) collective-permute-start(bf16[256,768]{1,0:T(8,128)(2,1)S(1)} %broadcast_select_fusion.5), channel_id=1, source_target_pairs={{0,2},{1,3},{2,0},{3,1},{4,6},{5,7},{6,4},{7,5},{8,10},{9,11},{10,... | collective-permute-start | bytes 1179656 | tf_op jit(solution)/shard_map/ppermute | solution.py:17
  229.3 18.3 %collective-permute-start.12 = (bf16[768,256]{1,0:T(8,128)(2,1)S(1)}, bf16[768,256]{1,0:T(8,128)(2,1)S(1)}, u32[]{:S(2)}, u32[]{:S(2)}) collective-permute-start(bf16[768,256]{1,0:T(8,128)(2,1)S(1)} %broadcast_select_fusion.1), channel_id=1, source_target_pairs={{0,4},{1,5},{2,6},{3,7},{4,0},{5,1},{6,2},{7,3},{8,12},{9,13},{10,... | collective-permute-start | bytes 1179656 | tf_op jit(solution)/shard_map/ppermute | solution.py:17
  237.8 14.0 %collective-permute-start.7 = (bf16[256,768]{1,0:T(8,128)(2,1)S(1)}, bf16[256,768]{1,0:T(8,128)(2,1)S(1)}, u32[]{:S(2)}, u32[]{:S(2)}) collective-permute-start(bf16[256,768]{1,0:T(8,128)(2,1)S(1)} %broadcast_select_fusion.6), channel_id=1, source_target_pairs={{0,4},{1,5},{2,6},{3,7},{4,0},{5,1},{6,2},{7,3},{8,12},{9,13},{10,... | collective-permute-start | bytes 1179656 | tf_op jit(solution)/shard_map/ppermute | solution.py:17
  244.3 18.5 %collective-permute-start.2 = (bf16[256,768]{1,0:T(8,128)(2,1)S(1)}, bf16[256,768]{1,0:T(8,128)(2,1)S(1)}, u32[]{:S(2)}, u32[]{:S(2)}) collective-permute-start(bf16[256,768]{1,0:T(8,128)(2,1)S(1)} %broadcast_select_fusion.7), channel_id=1, source_target_pairs={{0,4},{1,5},{2,6},{3,7},{4,0},{5,1},{6,2},{7,3},{8,12},{9,13},{10,... | collective-permute-start | bytes 1179656 | tf_op jit(solution)/shard_map/ppermute | solution.py:17
  247.7 48.6 %collective-permute-start.13 = (bf16[768,256]{1,0:T(8,128)(2,1)S(1)}, bf16[768,256]{1,0:T(8,128)(2,1)S(1)}, u32[]{:S(2)}, u32[]{:S(2)}) collective-permute-start(bf16[768,256]{1,0:T(8,128)(2,1)S(1)} %broadcast_select_fusion.2), channel_id=1, source_target_pairs={{0,8},{1,9},{2,10},{3,11},{4,12},{5,13},{6,14},{7,15},{8,0},{9,1},... | collective-permute-start | bytes 1179656 | tf_op jit(solution)/shard_map/ppermute | solution.py:17
  251.9 52.9 %collective-permute-start.8 = (bf16[256,768]{1,0:T(8,128)(2,1)S(1)}, bf16[256,768]{1,0:T(8,128)(2,1)S(1)}, u32[]{:S(2)}, u32[]{:S(2)}) collective-permute-start(bf16[256,768]{1,0:T(8,128)(2,1)S(1)} %broadcast_select_fusion.8), channel_id=1, source_target_pairs={{0,8},{1,9},{2,10},{3,11},{4,12},{5,13},{6,14},{7,15},{8,0},{9,1},... | collective-permute-start | bytes 1179656 | tf_op jit(solution)/shard_map/ppermute | solution.py:17
  262.8 56.9 %collective-permute-start.3 = (bf16[256,768]{1,0:T(8,128)(2,1)S(1)}, bf16[256,768]{1,0:T(8,128)(2,1)S(1)}, u32[]{:S(2)}, u32[]{:S(2)}) collective-permute-start(bf16[256,768]{1,0:T(8,128)(2,1)S(1)} %broadcast_select_fusion.9), channel_id=1, source_target_pairs={{0,8},{1,9},{2,10},{3,11},{4,12},{5,13},{6,14},{7,15},{8,0},{9,1},... | collective-permute-start | bytes 1179656 | tf_op jit(solution)/shard_map/ppermute | solution.py:17
  296.3 62.2 %collective-permute-start.14 = (bf16[768,256]{1,0:T(8,128)(2,1)S(1)}, bf16[768,256]{1,0:T(8,128)(2,1)S(1)}, u32[]{:S(2)}, u32[]{:S(2)}) collective-permute-start(bf16[768,256]{1,0:T(8,128)(2,1)S(1)} %broadcast_select_fusion.3), channel_id=1, source_target_pairs={{0,16},{1,17},{2,18},{3,19},{4,20},{5,21},{6,22},{7,23},{8,24},{9,... | collective-permute-start | bytes 1179656 | tf_op jit(solution)/shard_map/ppermute | solution.py:17
  304.8 54.5 %collective-permute-start.9 = (bf16[256,768]{1,0:T(8,128)(2,1)S(1)}, bf16[256,768]{1,0:T(8,128)(2,1)S(1)}, u32[]{:S(2)}, u32[]{:S(2)}) collective-permute-start(bf16[256,768]{1,0:T(8,128)(2,1)S(1)} %broadcast_select_fusion.10), channel_id=1, source_target_pairs={{0,16},{1,17},{2,18},{3,19},{4,20},{5,21},{6,22},{7,23},{8,24},{9,... | collective-permute-start | bytes 1179656 | tf_op jit(solution)/shard_map/ppermute | solution.py:17
  319.7 47.4 %collective-permute-start.4 = (bf16[256,768]{1,0:T(8,128)(2,1)S(1)}, bf16[256,768]{1,0:T(8,128)(2,1)S(1)}, u32[]{:S(2)}, u32[]{:S(2)}) collective-permute-start(bf16[256,768]{1,0:T(8,128)(2,1)S(1)} %broadcast_select_fusion.11), channel_id=1, source_target_pairs={{0,16},{1,17},{2,18},{3,19},{4,20},{5,21},{6,22},{7,23},{8,24},{9,... | collective-permute-start | bytes 1179656 | tf_op jit(solution)/shard_map/ppermute | solution.py:17
Sparse Core Ops, SparseCore 0:
  52.0 115.6 all-reduce.2
where the time goes:
time: 376 us; the launch traced here: 375 us
  waiting for transfers between devices  193 us (51%)
  starting transfers between devices  129 us (34%)
  matrix products  24.8 us (7%)
  between operations  17.8 us (5%)
  other arithmetic  6.2 us (2%)
  local copies, waits for them, and re-layouts  4.07 us (1%)
    psum x1, waiting for transfers between devices, shards(): lax.psum(up_part.astype(jnp.bfloat16), 'dp').astype(jnp.float32)  115 us
    ppermute x15, starting transfers between devices, partner_2(): lax.ppermute(x, axis, [(i, i ^ 1 << apart) for i in range(lax.axis_size(a...  99.1 us
    ppermute x15, waiting for transfers between devices, partner_2(): lax.ppermute(x, axis, [(i, i ^ 1 << apart) for i in range(lax.axis_size(a...  62 us
    dot_general x3, matrix products, contract_rows(): lax.dot_general(left, right, (((0,), (0,)), ((), ())), preferred_element_...  16.8 us
    all_to_all x1, starting transfers between devices, shards(): lax.all_to_all(send_tok, 'expert', split_axis=0, concat_axis=0, tiled=True)  13.5 us
    all_to_all x1, starting transfers between devices, shards(): lax.all_to_all(slot_back.reshape(expert_count, capacity, slot_back.shape[...  10.5 us
    all_to_all x1, waiting for transfers between devices, shards(): lax.all_to_all(send_grad, 'expert', split_axis=0, concat_axis=0, tiled=True)  7.96 us
  transfers between devices with their start and end apart: 19, of which 12 were waited for; matrix products, arithmetic and copies ran while one was open for 6% of the time, Pallas kernels for 0%

commit v1 on v0

v1 whole, which is shorter than its diff:
```python
import math

import jax
import jax.numpy as jnp
from jax import lax
from jax.sharding import Mesh
from jax.sharding import PartitionSpec as P

HBLOCK = 128
EPS = 1e-06
QSTEP = 2.0
TWO_PI = 2.0 * math.pi
BF16 = jnp.bfloat16
F32 = jnp.float32


def dot(left, right, left_dim, right_dim):
    return lax.dot_general(
        left, right, (((left_dim,), (right_dim,)), ((), ())), preferred_element_type=F32
    )


def sylvester(block_len):
    positions = jnp.arange(block_len, dtype=jnp.int32)
    common_bits = positions[:, None] & positions[None, :]
    parity = jnp.zeros((block_len, block_len), jnp.int32)
    for bit_pos in range(block_len.bit_length() - 1):
        parity = parity ^ common_bits >> bit_pos & 1
    return (1 - 2 * parity).astype(BF16)


def slot_tables(routes, weights, expert_count, capacity):
    experts_iota = jnp.arange(expert_count, dtype=jnp.int32)
    hit_table = (routes[:, :, None] == experts_iota[None, None, :]).astype(jnp.int32)
    member = jnp.sum(hit_table, axis=1)
    weight_sum = jnp.sum(hit_table.astype(F32) * weights[:, :, None], axis=1)
    rank_table = jnp.cumsum(member, axis=0) - member
    cap_iota = jnp.arange(capacity, dtype=jnp.int32)
    placed = (rank_table[:, :, None] == cap_iota[None, None, :]) & (member[:, :, None] == 1)
    placed = jnp.transpose(placed.astype(F32), (1, 2, 0))
    slot_weight = jnp.einsum("ect,te->ec", placed, weight_sum, precision=lax.Precision.HIGHEST)
    return placed, slot_weight


def rotate_quant_t(operand, rotation):
    cols, rows = operand.shape
    rotated = lax.dot_general(
        operand.reshape(cols, rows // HBLOCK, HBLOCK),
        rotation,
        (((2,), (0,)), ((), ())),
        preferred_element_type=F32,
    )
    scale = jnp.sqrt(jnp.mean(rotated * rotated, axis=2, keepdims=True) + EPS)
    steps = QSTEP * rotated / scale
    soft = (steps - jnp.sin(TWO_PI * steps) / TWO_PI) * scale / QSTEP
    return soft.astype(BF16).reshape(cols, rows)


def exchange(x, axis, apart):
    return lax.ppermute(x, axis, [(i, i ^ apart) for i in range(lax.axis_size(axis))])


def partner_swap(x, partner):
    count = lax.axis_size("expert")
    me = lax.axis_index("expert")
    apart = me ^ partner[me]
    bits = [1 << k for k in range(count.bit_length() - 1)]
    which = sum((apart == bit).astype(jnp.int32) * (k + 1) for k, bit in enumerate(bits))
    branches = [lambda v: v] + [lambda v, bit=bit: exchange(v, "expert", bit) for bit in bits]
    return lax.switch(which, branches, x)


def gather_y(x):
    count = lax.axis_size("y")
    copies = jnp.broadcast_to(x[None], (count,) + x.shape)
    return lax.all_to_all(copies, "y", 0, 0, tiled=True)


def shards(
    tokens, out_grad, routes, route_weights, gate_weight, up_weight, down_weight, sign_bits, partner
):
    experts = lax.axis_size("expert")
    n_y = lax.axis_size("y")
    core = lax.axis_index("core")
    tok_count, width = tokens.shape
    capacity = min(tok_count, tok_count * routes.shape[1] * 3 // (2 * experts))
    rows = experts * capacity
    gate_w, up_w, down_w = gate_weight[0], up_weight[0], down_weight[0]
    ff = gate_w.shape[1]
    half = ff // 2
    part = half // n_y

    placed, slot_weight = slot_tables(routes, route_weights, experts, capacity)
    picker = placed.astype(BF16)
    nothing = jnp.zeros_like(picker)
    pick_both = jnp.concatenate(
        [jnp.concatenate([picker, nothing], 2), jnp.concatenate([nothing, picker], 2)], 1
    )
    factor = jnp.concatenate([jnp.ones_like(slot_weight), slot_weight], 1)
    both = jnp.concatenate([tokens, out_grad], 0)
    send = jnp.einsum("ect,td->ecd", pick_both, both, preferred_element_type=F32)
    send = (send * factor[:, :, None]).astype(BF16)
    recv = lax.all_to_all(send, "expert", 0, 0, tiled=True)
    rows_in = recv[:, :capacity].reshape(rows, width)
    rows_grad = recv[:, capacity:].reshape(rows, width)

    def partials(which):
        start = which * half
        gate_part = dot(lax.dynamic_slice_in_dim(gate_w, start, half, 1), rows_in, 0, 1)
        up_part = dot(lax.dynamic_slice_in_dim(up_w, start, half, 1), rows_in, 0, 1)
        hid_part = dot(lax.dynamic_slice_in_dim(down_w, start, half, 0), rows_grad, 1, 1)
        return jnp.concatenate(
            [v.reshape(n_y, part, rows) for v in (gate_part, up_part, hid_part)], 1
        )

    away = partials(1 - core).astype(BF16)
    arrived = exchange(away, "core", 1)
    chip_sum = (partials(core) + arrived.astype(F32)).astype(BF16)
    blocks = lax.all_to_all(chip_sum, "y", 0, 0, tiled=True)
    sums = jnp.sum(blocks.astype(F32), axis=0)
    gate_sum, up_sum, hid_grad = sums[:part], sums[part : 2 * part], sums[2 * part :]

    me = lax.axis_index("expert")
    flip_signs = (1 - 2 * lax.dynamic_index_in_dim(sign_bits, me, 0, keepdims=False)).astype(BF16)
    rotation = sylvester(HBLOCK) * flip_signs[:, None]
    quant_rows = rotate_quant_t(jnp.concatenate([rows_in.T, rows_grad.T], 0), rotation)
    mate_rows = partner_swap(quant_rows, partner)
    mate_in, mate_grad = mate_rows[:width], mate_rows[width:]

    sig = jax.nn.sigmoid(gate_sum)
    silu = gate_sum * sig
    hidden = (silu * up_sum).astype(BF16)
    gate_rows = (hid_grad * up_sum * sig * (1.0 + gate_sum * (1.0 - sig))).astype(BF16)
    up_rows = (hid_grad * silu).astype(BF16)

    own = jnp.concatenate([gate_rows, up_rows], 0)
    own_half = gather_y(own)
    quant = rotate_quant_t(jnp.concatenate([gate_rows, up_rows, hidden], 0), rotation)
    mate_half = gather_y(partner_swap(quant, partner))

    def back(half_rows, which):
        start = which * half
        gate_t = half_rows[:, :part].reshape(half, rows)
        up_t = half_rows[:, part:].reshape(half, rows)
        return dot(gate_t, lax.dynamic_slice_in_dim(gate_w, start, half, 1), 0, 1) + dot(
            up_t, lax.dynamic_slice_in_dim(up_w, start, half, 1), 0, 1
        )

    own_other = exchange(own_half, "core", 1)
    slot_back = (back(own_half, core) + back(own_other, 1 - core)).astype(BF16)
    returned = lax.all_to_all(
        slot_back.reshape(experts, capacity, width), "expert", 0, 0, tiled=True
    )
    input_grad = jnp.einsum("ect,ecd->td", picker, returned, preferred_element_type=F32)

    mate_other = exchange(mate_half, "core", 1)
    low = jnp.where(core == 0, mate_half, mate_other)
    high = jnp.where(core == 0, mate_other, mate_half)

    def whole(k):
        cut = slice(k * part, (k + 1) * part)
        return jnp.concatenate([low[:, cut].reshape(half, rows), high[:, cut].reshape(half, rows)], 0)

    scale = 1.0 / HBLOCK
    gate_new = (dot(mate_in, whole(0), 1, 1) * scale).astype(BF16)
    up_new = (dot(mate_in, whole(1), 1, 1) * scale).astype(BF16)
    down_new = (dot(whole(2), mate_grad, 1, 1) * scale).astype(BF16)
    return gate_new[None], up_new[None], down_new[None], input_grad.astype(BF16)


def solution(mesh):
    n_dp, n_expert = mesh.shape["dp"], mesh.shape["expert"]
    split = Mesh(mesh.devices.reshape(n_dp // 2, 2, n_expert), ("y", "core", "expert"))
    dp = ("y", "core")
    return jax.shard_map(
        shards,
        mesh=split,
        in_specs=(
            P("expert", dp),
            P("expert", dp),
            P("expert", None),
            P("expert", None),
            P("expert", dp, None),
            P("expert", dp, None),
            P("expert", None, dp),
            P(),
            P(),
        ),
        out_specs=(
            P("expert", dp, None),
            P("expert", dp, None),
            P("expert", None, dp),
            P("expert", dp),
        ),
        check_vma=False,
    )
```

time: 376 us -> 164 us (0.44)
  the two profiles are of different devices: /device:TPU:2 before, /device:TPU:68 now
where the time goes in v1:
time: 164 us; the launch traced here: 163 us
  waiting for transfers between devices  62.6 us (38%)
  starting transfers between devices  38.5 us (23%)
  blocking collectives  32.4 us (20%)
  matrix products  10.2 us (6%)
  local copies, waits for them, and re-layouts  8.88 us (5%)
  other arithmetic  8.76 us (5%)
  between operations  1.76 us (1%)
    all_to_all x1, blocking collectives, shards(): blocks = lax.all_to_all(chip_sum, 'y', 0, 0, tiled=True)  32.4 us
    all_to_all x2, waiting for transfers between devices, gather_y(): return lax.all_to_all(copies, 'y', 0, 0, tiled=True)  27.4 us
    ppermute x5, waiting for transfers between devices, exchange(): lax.ppermute(x, axis, [(i, i ^ apart) for i in range(lax.axis_size(axis))])  23.9 us
    all_to_all x1, starting transfers between devices, shards(): recv = lax.all_to_all(send, 'expert', 0, 0, tiled=True)  12.5 us
    ppermute x5, starting transfers between devices, exchange(): lax.ppermute(x, axis, [(i, i ^ apart) for i in range(lax.axis_size(axis))])  12.4 us
    all_to_all x1, waiting for transfers between devices, shards(): recv = lax.all_to_all(send, 'expert', 0, 0, tiled=True)  11.3 us
    all_to_all x2, starting transfers between devices, gather_y(): return lax.all_to_all(copies, 'y', 0, 0, tiled=True)  7.09 us
    all_to_all x1, starting transfers between devices, shards(): lax.all_to_all(slot_back.reshape(experts, capacity, width), 'expert', 0,...  6.44 us
  transfers between devices with their start and end apart: 9, of which 6 were waited for; matrix products, arithmetic and copies ran while one was open for 8% of the time, Pallas kernels for 0%

profile of v1, /device:TPU:68, one launch (start us, length us, event | category | flops | bytes accessed | tf_op | source)
XLA Modules:
  0.0 163.2 jit_solution(3489953151860436738)
XLA Ops:
  3.2 1.9 %fusion.1 = bf16[32,24,256]{2,1,0:T(8,128)(2,1)} fusion(f32[32,24]{1,0:T(8,128)S(1)} %concatenate.44, bf16[32,12,32]{2,1,0:T(8,128)(2,1)S(1)} %convert_convert_fusion, bf16[32,256]{1,0:T(8,128)(2,1)} %param.22, bf16[32,256]{1,0:T(8,128)(2,1)} %param.21), kind=kOutput, calls=%fused_computation.7 | convolution fusion | flops 26017792 | bytes 453632 | tf_op jit(solution)/shard_map/ect,td->ecd/dot_general | solution.py:101
  5.1 12.5 %all-to-all-start = ((bf16[32,24,256]{2,1,0:T(8,128)(2,1)}), bf16[32,24,256]{2,1,0:T(8,128)(2,1)S(1)}, u32[]{:S(2)}, u32[]{:S(2)}) async-start(bf16[32,24,256]{2,1,0:T(8,128)(2,1)} %fusion.1), calls=%async_computation | async-start | bytes 786432 | tf_op jit(solution)/shard_map/all_to_all | solution.py:103
  17.7 0.8 dynamic-slice_bitcast_fusion
  19.5 11.3 %all-to-all-done = bf16[32,24,256]{2,1,0:T(8,128)(2,1)S(1)} async-done(((bf16[32,24,256]{2,1,0:T(8,128)(2,1)}), bf16[32,24,256]{2,1,0:T(8,128)(2,1)S(1)}, u32[]{:S(2)}, u32[]{:S(2)}) %all-to-all-start) | async-done | bytes 393248 | tf_op jit(solution)/shard_map/all_to_all | solution.py:103
  31.9 1.0 pad_maximum_fusion
  32.9 1.9 %collective-permute-start.10 = (bf16[8,144,384]{2,1,0:T(8,128)(2,1)}, bf16[8,144,384]{2,1,0:T(8,128)(2,1)}, u32[]{:S(2)}, u32[]{:S(2)}) collective-permute-start(bf16[8,144,384]{2,1,0:T(8,128)(2,1)} %pad_maximum_fusion), channel_id=1, source_target_pairs={{0,32},{32,0},{1,33},{33,1},{2,34},{34,2},{3,35},{35,3},{4,36},{36... | collective-permute-start | bytes 2654216 | tf_op jit(solution)/shard_map/ppermute | solution.py:60
  36.0 1.6 collective-permute-done.10
  37.6 1.4 fusion
  39.0 32.4 %all_to_all.25 = bf16[8,144,384]{2,1,0:T(8,128)(2,1)S(1)} all-to-all(bf16[8,144,384]{2,1,0:T(8,128)(2,1)S(1)} %fusion), channel_id=1, replica_groups=mesh['y'=8,'core'=2,'expert'=32] {'y'}, dimensions={0} | all-to-all | bytes 1769472 | tf_op jit(solution)/shard_map/all_to_all | solution.py:119
  71.6 0.9 broadcast_in_dim.14
  72.5 3.5 %all-to-all-start.3 = ((bf16[8,96,384]{2,1,0:T(8,128)(2,1)}), bf16[8,96,384]{2,1,0:T(8,128)(2,1)S(1)}, u32[]{:S(2)}, u32[]{:S(2)}) async-start(bf16[8,96,384]{2,1,0:T(8,128)(2,1)} %broadcast_in_dim.14), calls=%async_computation.3 | async-start | bytes 1179648 | tf_op jit(solution)/shard_map/all_to_all | solution.py:76
  78.5 0.9 copy_bitcast_fusion
  79.3 7.6 %conditional.3 = (bf16[144,384]{1,0:T(8,128)(2,1)S(1)}) conditional(s32[]{:T(128)} %clamp.4, bf16[144,384]{1,0:T(8,128)(2,1)S(1)} %copy_bitcast_fusion, bf16[144,384]{1,0:T(8,128)(2,1)S(1)} %copy_bitcast_fusion, bf16[144,384]{1,0:T(8,128)(2,1)S(1)} %copy_bitcast_fusion, ...), branch_computations={%region_12.13_spmd, %region_13.14_spmd, %region_14.15_spmd, %regio... | conditional | bytes 663600 | solution.py:70
  79.4 2.2 %collective-permute-start.3 = (bf16[144,384]{1,0:T(8,128)(2,1)S(1)}, bf16[144,384]{1,0:T(8,128)(2,1)S(1)}, u32[]{:S(2)}, u32[]{:S(2)}) collective-permute-start(bf16[144,384]{1,0:T(8,128)(2,1)S(1)} %param.10), channel_id=1, source_target_pairs={{0,8},{1,9},{2,10},{3,11},{4,12},{5,13},{6,14},{7,15},{8,0},{9,1},... | collective-permute-start | bytes 331784 | tf_op jit(solution)/shard_map/cond/branch_4_fun/ppermute | solution.py:60
  81.6 5.3 %collective-permute-done.3 = bf16[144,384]{1,0:T(8,128)(2,1)S(1)} collective-permute-done((bf16[144,384]{1,0:T(8,128)(2,1)S(1)}, bf16[144,384]{1,0:T(8,128)(2,1)S(1)}, u32[]{:S(2)}, u32[]{:S(2)}) %collective-permute-start.3) | collective-permute-done | bytes 110624 | tf_op jit(solution)/shard_map/cond/branch_4_fun/ppermute | solution.py:60
  87.0 7.0 %all-to-all-done.3 = bf16[8,96,384]{2,1,0:T(8,128)(2,1)S(1)} async-done(((bf16[8,96,384]{2,1,0:T(8,128)(2,1)}), bf16[8,96,384]{2,1,0:T(8,128)(2,1)S(1)}, u32[]{:S(2)}, u32[]{:S(2)}) %all-to-all-start.3) | async-done | bytes 589856 | tf_op jit(solution)/shard_map/all_to_all | solution.py:76
  94.0 1.0 broadcast_in_dim.10
  95.0 3.5 %all-to-all-start.2 = ((bf16[8,144,384]{2,1,0:T(8,128)(2,1)}), bf16[8,144,384]{2,1,0:T(8,128)(2,1)S(1)}, u32[]{:S(2)}, u32[]{:S(2)}) async-start(bf16[8,144,384]{2,1,0:T(8,128)(2,1)} %broadcast_in_dim.10), calls=%async_computation.2 | async-start | bytes 1769472 | tf_op jit(solution)/shard_map/all_to_all | solution.py:76
  99.1 1.9 %collective-permute-start.12 = (bf16[8,96,384]{2,1,0:T(8,128)(2,1)S(1)}, bf16[8,96,384]{2,1,0:T(8,128)(2,1)}, u32[]{:S(2)}, u32[]{:S(2)}) collective-permute-start(bf16[8,96,384]{2,1,0:T(8,128)(2,1)S(1)} %all-to-all-done.3), channel_id=1, source_target_pairs={{0,32},{32,0},{1,33},{33,1},{2,34},{34,2},{3,35},{35,3},{4,36},{36... | collective-permute-start | bytes 1769480 | tf_op jit(solution)/shard_map/ppermute | solution.py:60
  101.7 20.4 %all-to-all-done.2 = bf16[8,144,384]{2,1,0:T(8,128)(2,1)S(1)} async-done(((bf16[8,144,384]{2,1,0:T(8,128)(2,1)}), bf16[8,144,384]{2,1,0:T(8,128)(2,1)S(1)}, u32[]{:S(2)}, u32[]{:S(2)}) %all-to-all-start.2) | async-done | bytes 884768 | tf_op jit(solution)/shard_map/all_to_all | solution.py:76
  122.1 1.9 %collective-permute-start.11 = (bf16[8,144,384]{2,1,0:T(8,128)(2,1)S(1)}, bf16[8,144,384]{2,1,0:T(8,128)(2,1)}, u32[]{:S(2)}, u32[]{:S(2)}) collective-permute-start(bf16[8,144,384]{2,1,0:T(8,128)(2,1)S(1)} %all-to-all-done.2), channel_id=1, source_target_pairs={{0,32},{32,0},{1,33},{33,1},{2,34},{34,2},{3,35},{35,3},{4,36},{36... | collective-permute-start | bytes 2654216 | tf_op jit(solution)/shard_map/ppermute | solution.py:60
  124.1 1.1 fusion.100
  126.6 6.4 %all-to-all-start.4 = ((bf16[32,12,256]{2,1,0:T(8,128)(2,1)}), bf16[32,12,256]{2,1,0:T(8,128)(2,1)S(1)}, u32[]{:S(2)}, u32[]{:S(2)}) async-start(bf16[32,12,256]{2,1,0:T(8,128)(2,1)} %reshape.188), calls=%async_computation.4 | async-start | bytes 524288 | tf_op jit(solution)/shard_map/all_to_all | solution.py:151
  133.1 2.8 %multiply_convert_fusion = bf16[512,3,128]{0,2,1:T(8,128)(2,1)S(1)} fusion(f32[512,3,128]{0,2,1:T(8,128)S(1)} %get-tuple-element.73, f32[512,3]{0,1:T(4,128)S(1)} %add_sqrt_fusion), kind=kLoop, calls=%fused_computation.26 | loop fusion | flops 1572864 | bytes 1185792 | tf_op jit(solution)/shard_map/convert_element_type | solution.py:56
  135.9 21.6 %conditional.2 = (bf16[512,384]{0,1:T(8,128)(2,1)S(1)}, bf16[256,384]{0,1:T(8,128)(2,1)S(1)}, bf16[256,384]{0,1:T(8,128)(2,1)S(1)}) conditional(s32[]{:T(128)} %clamp.4, bf16[512,3,128]{0,2,1:T(8,128)(2,1)S(1)} %multiply_convert_fusion, bf16[512,3,128]{0,2,1:T(8,128)(2,1)S(1)} %multiply_convert_fusion, ...), branch_computations={%region_4.5_spmd, %region_5.6_spmd, %region_6.7_spmd, %region_7.8_... | conditional | bytes 3145792 | solution.py:70
  135.9 4.4 %collective-permute-start.8 = (bf16[512,384]{0,1:T(8,128)(2,1)S(1)}, bf16[512,384]{0,1:T(8,128)(2,1)S(1)}, u32[]{:S(2)}, u32[]{:S(2)}) collective-permute-start(bf16[512,384]{0,1:T(8,128)(2,1)S(1)} %bitcast.122), channel_id=1, source_target_pairs={{0,8},{1,9},{2,10},{3,11},{4,12},{5,13},{6,14},{7,15},{8,0},{9,1},... | collective-permute-start | bytes 1179656 | tf_op jit(solution)/shard_map/cond/branch_4_fun/ppermute | solution.py:60
  140.3 17.0 %collective-permute-done.8 = bf16[512,384]{0,1:T(8,128)(2,1)S(1)} collective-permute-done((bf16[512,384]{0,1:T(8,128)(2,1)S(1)}, bf16[512,384]{0,1:T(8,128)(2,1)S(1)}, u32[]{:S(2)}, u32[]{:S(2)}) %collective-permute-start.8) | collective-permute-done | bytes 393248 | tf_op jit(solution)/shard_map/cond/branch_4_fun/ppermute | solution.py:60
  157.5 0.8 fusion.10
  158.3 1.3 broadcast_select_fusion.1
  159.8 1.2 fusion.6
  161.0 1.1 fusion.7
  162.1 1.1 fusion.5
  (69 shorter events, 10.5 us)
Async XLA Ops:
  2.8 2.3 %copy-start.4 = (bf16[32,12,32]{2,1,0:T(8,128)(2,1)}, bf16[32,12,32]{2,1,0:T(8,128)(2,1)S(1)}, u32[]{:S(2)}) copy-start(bf16[32,12,32]{2,1,0:T(8,128)(2,1)S(1)} %convert_convert_fusion) | copy-start | bytes 73732
  3.2 14.4 %copy-start = (bf16[1,256,768]{2,1,0:T(8,128)(2,1)S(1)}, bf16[1,256,768]{2,1,0:T(8,128)(2,1)}, u32[]{:S(2)}) copy-start(bf16[1,256,768]{2,1,0:T(8,128)(2,1)} %param.26) | copy-start | bytes 1179652
  3.2 14.4 %copy-start.1 = (bf16[1,256,768]{2,1,0:T(8,128)(2,1)S(1)}, bf16[1,256,768]{2,1,0:T(8,128)(2,1)}, u32[]{:S(2)}) copy-start(bf16[1,256,768]{2,1,0:T(8,128)(2,1)} %param.25) | copy-start | bytes 1179652
  5.1 25.7 %all-to-all-start = ((bf16[32,24,256]{2,1,0:T(8,128)(2,1)}), bf16[32,24,256]{2,1,0:T(8,128)(2,1)S(1)}, u32[]{:S(2)}, u32[]{:S(2)}) async-start(bf16[32,24,256]{2,1,0:T(8,128)(2,1)} %fusion.1), calls=%async_computation | async-start | bytes 786432 | tf_op jit(solution)/shard_map/all_to_all | solution.py:103
  17.7 1.1 copy-start.6
  31.9 3.0 %copy-start.2 = (bf16[384,256]{0,1:T(8,128)(2,1)S(1)}, bf16[384,256]{0,1:T(8,128)(2,1)}, u32[]{:S(2)}) copy-start(bf16[384,256]{0,1:T(8,128)(2,1)} %get-tuple-element.64) | copy-start | bytes 589828
  31.9 3.3 %copy-start.3 = (bf16[1,384,256]{2,1,0:T(8,128)(2,1)S(1)}, bf16[1,384,256]{2,1,0:T(8,128)(2,1)}, u32[]{:S(2)}) copy-start(bf16[1,384,256]{2,1,0:T(8,128)(2,1)} %get-tuple-element.66) | copy-start | bytes 589828
  32.9 4.7 %collective-permute-start.10 = (bf16[8,144,384]{2,1,0:T(8,128)(2,1)}, bf16[8,144,384]{2,1,0:T(8,128)(2,1)}, u32[]{:S(2)}, u32[]{:S(2)}) collective-permute-start(bf16[8,144,384]{2,1,0:T(8,128)(2,1)} %pad_maximum_fusion), channel_id=1, source_target_pairs={{0,32},{32,0},{1,33},{33,1},{2,34},{34,2},{3,35},{35,3},{4,36},{36... | collective-permute-start | bytes 2654216 | tf_op jit(solution)/shard_map/ppermute | solution.py:60
  71.6 4.4 %copy-start.7 = (s32[32]{0:T(128)S(1)}, s32[32]{0:T(128)}, u32[]{:S(2)}) copy-start(s32[32]{0:T(128)} %param.29) | copy-start | bytes 388
  72.5 21.5 %all-to-all-start.3 = ((bf16[8,96,384]{2,1,0:T(8,128)(2,1)}), bf16[8,96,384]{2,1,0:T(8,128)(2,1)S(1)}, u32[]{:S(2)}, u32[]{:S(2)}) async-start(bf16[8,96,384]{2,1,0:T(8,128)(2,1)} %broadcast_in_dim.14), calls=%async_computation.3 | async-start | bytes 1179648 | tf_op jit(solution)/shard_map/all_to_all | solution.py:76
  79.4 7.5 %collective-permute-start.3 = (bf16[144,384]{1,0:T(8,128)(2,1)S(1)}, bf16[144,384]{1,0:T(8,128)(2,1)S(1)}, u32[]{:S(2)}, u32[]{:S(2)}) collective-permute-start(bf16[144,384]{1,0:T(8,128)(2,1)S(1)} %param.10), channel_id=1, source_target_pairs={{0,8},{1,9},{2,10},{3,11},{4,12},{5,13},{6,14},{7,15},{8,0},{9,1},... | collective-permute-start | bytes 331784 | tf_op jit(solution)/shard_map/cond/branch_4_fun/ppermute | solution.py:60
  95.0 27.1 %all-to-all-start.2 = ((bf16[8,144,384]{2,1,0:T(8,128)(2,1)}), bf16[8,144,384]{2,1,0:T(8,128)(2,1)S(1)}, u32[]{:S(2)}, u32[]{:S(2)}) async-start(bf16[8,144,384]{2,1,0:T(8,128)(2,1)} %broadcast_in_dim.10), calls=%async_computation.2 | async-start | bytes 1769472 | tf_op jit(solution)/shard_map/all_to_all | solution.py:76
  99.1 25.0 %collective-permute-start.12 = (bf16[8,96,384]{2,1,0:T(8,128)(2,1)S(1)}, bf16[8,96,384]{2,1,0:T(8,128)(2,1)}, u32[]{:S(2)}, u32[]{:S(2)}) collective-permute-start(bf16[8,96,384]{2,1,0:T(8,128)(2,1)S(1)} %all-to-all-done.3), channel_id=1, source_target_pairs={{0,32},{32,0},{1,33},{33,1},{2,34},{34,2},{3,35},{35,3},{4,36},{36... | collective-permute-start | bytes 1769480 | tf_op jit(solution)/shard_map/ppermute | solution.py:60
  122.1 36.2 %collective-permute-start.11 = (bf16[8,144,384]{2,1,0:T(8,128)(2,1)S(1)}, bf16[8,144,384]{2,1,0:T(8,128)(2,1)}, u32[]{:S(2)}, u32[]{:S(2)}) collective-permute-start(bf16[8,144,384]{2,1,0:T(8,128)(2,1)S(1)} %all-to-all-done.2), channel_id=1, source_target_pairs={{0,32},{32,0},{1,33},{33,1},{2,34},{34,2},{3,35},{35,3},{4,36},{36... | collective-permute-start | bytes 2654216 | tf_op jit(solution)/shard_map/ppermute | solution.py:60
  126.6 30.9 %all-to-all-start.4 = ((bf16[32,12,256]{2,1,0:T(8,128)(2,1)}), bf16[32,12,256]{2,1,0:T(8,128)(2,1)S(1)}, u32[]{:S(2)}, u32[]{:S(2)}) async-start(bf16[32,12,256]{2,1,0:T(8,128)(2,1)} %reshape.188), calls=%async_computation.4 | async-start | bytes 524288 | tf_op jit(solution)/shard_map/all_to_all | solution.py:151
  135.9 21.6 %copy-start.5 = (bf16[32,12,32]{2,1,0:T(8,128)(2,1)S(1)}, bf16[32,12,32]{2,1,0:T(8,128)(2,1)}, u32[]{:S(2)}) copy-start(bf16[32,12,32]{2,1,0:T(8,128)(2,1)} %copy-done.4) | copy-start | bytes 73732
  135.9 21.5 %collective-permute-start.8 = (bf16[512,384]{0,1:T(8,128)(2,1)S(1)}, bf16[512,384]{0,1:T(8,128)(2,1)S(1)}, u32[]{:S(2)}, u32[]{:S(2)}) collective-permute-start(bf16[512,384]{0,1:T(8,128)(2,1)S(1)} %bitcast.122), channel_id=1, source_target_pairs={{0,8},{1,9},{2,10},{3,11},{4,12},{5,13},{6,14},{7,15},{8,0},{9,1},... | collective-permute-start | bytes 1179656 | tf_op jit(solution)/shard_map/cond/branch_4_fun/ppermute | solution.py:60

commit v2 on v1

--- a/solution.py
+++ b/solution.py
@@ -74,6 +74,17 @@
     count = lax.axis_size("y")
     copies = jnp.broadcast_to(x[None], (count,) + x.shape)
     return lax.all_to_all(copies, "y", 0, 0, tiled=True)
+
+
+def gather_y_shifts(x):
+    count = lax.axis_size("y")
+    me = lax.axis_index("y")
+    out = jnp.zeros((count,) + x.shape, x.dtype)
+    out = lax.dynamic_update_index_in_dim(out, x, me, 0)
+    for apart in sorted(range(1, count), key=lambda k: -min(k, count - k)):
+        piece = lax.ppermute(x, "y", [(i, (i + apart) % count) for i in range(count)])
+        out = lax.dynamic_update_index_in_dim(out, piece, (me - apart) % count, 0)
+    return out
 
 
 def shards(
@@ -117,15 +128,17 @@
     arrived = exchange(away, "core", 1)
     chip_sum = (partials(core) + arrived.astype(F32)).astype(BF16)
     blocks = lax.all_to_all(chip_sum, "y", 0, 0, tiled=True)
-    sums = jnp.sum(blocks.astype(F32), axis=0)
-    gate_sum, up_sum, hid_grad = sums[:part], sums[part : 2 * part], sums[2 * part :]
 
     me = lax.axis_index("expert")
     flip_signs = (1 - 2 * lax.dynamic_index_in_dim(sign_bits, me, 0, keepdims=False)).astype(BF16)
     rotation = sylvester(HBLOCK) * flip_signs[:, None]
     quant_rows = rotate_quant_t(jnp.concatenate([rows_in.T, rows_grad.T], 0), rotation)
     mate_rows = partner_swap(quant_rows, partner)
+
+    blocks, mate_rows = lax.optimization_barrier((blocks, mate_rows))
     mate_in, mate_grad = mate_rows[:width], mate_rows[width:]
+    sums = jnp.sum(blocks.astype(F32), axis=0)
+    gate_sum, up_sum, hid_grad = sums[:part], sums[part : 2 * part], sums[2 * part :]
 
     sig = jax.nn.sigmoid(gate_sum)
     silu = gate_sum * sig
@@ -136,7 +149,7 @@
     own = jnp.concatenate([gate_rows, up_rows], 0)
     own_half = gather_y(own)
     quant = rotate_quant_t(jnp.concatenate([gate_rows, up_rows, hidden], 0), rotation)
-    mate_half = gather_y(partner_swap(quant, partner))
+    mate_half = gather_y_shifts(partner_swap(quant, partner))
 
     def back(half_rows, which):
         start = which * half

time: 164 us -> 176 us (1.073)
  the two profiles are of different devices: /device:TPU:68 before, /device:TPU:1 now
where the time goes in v2:
time: 176 us; the launch traced here: 175 us
  starting transfers between devices  80.5 us (46%)
  waiting for transfers between devices  58.6 us (33%)
  matrix products  14.1 us (8%)
  local copies, waits for them, and re-layouts  13 us (7%)
  other arithmetic  6.41 us (4%)
  between operations  1.98 us (1%)
    ppermute x7, starting transfers between devices, gather_y_shifts(): lax.ppermute(x, 'y', [(i, (i + apart) % count) for i in range(count)])  24.1 us
    all_to_all x1, waiting for transfers between devices, shards(): blocks = lax.all_to_all(chip_sum, 'y', 0, 0, tiled=True)  19.3 us
    all_to_all x1, waiting for transfers between devices, gather_y(): return lax.all_to_all(copies, 'y', 0, 0, tiled=True)  18.2 us
    all_to_all x1, starting transfers between devices, shards(): lax.all_to_all(slot_back.reshape(experts, capacity, width), 'expert', 0,...  17.8 us
    all_to_all x1, starting transfers between devices, shards(): recv = lax.all_to_all(send, 'expert', 0, 0, tiled=True)  13.7 us
    all_to_all x1, waiting for transfers between devices, shards(): recv = lax.all_to_all(send, 'expert', 0, 0, tiled=True)  11.9 us
    ppermute x3, starting transfers between devices, exchange(): lax.ppermute(x, axis, [(i, i ^ apart) for i in range(lax.axis_size(axis))])  11.3 us
    dot_general x13, matrix products, dot(): lax.dot_general(left, right, (((left_dim,), (right_dim,)), ((), ())), pre...  10.2 us
  transfers between devices with their start and end apart: 14, of which 7 were waited for; matrix products, arithmetic and copies ran while one was open for 13% of the time, Pallas kernels for 0%

profile of v2, /device:TPU:1, one launch (start us, length us, event | category | flops | bytes accessed | tf_op | source)
XLA Modules:
  0.0 174.7 jit_solution(3768281080032420652)
XLA Ops:
  3.5 1.9 %fusion.1 = bf16[32,24,256]{2,1,0:T(8,128)(2,1)} fusion(f32[32,24]{1,0:T(8,128)S(1)} %concatenate.44, bf16[32,12,32]{2,1,0:T(8,128)(2,1)S(1)} %convert_convert_fusion, bf16[32,256]{1,0:T(8,128)(2,1)} %param.22, bf16[32,256]{1,0:T(8,128)(2,1)} %param.21), kind=kOutput, calls=%fused_computation.13 | convolution fusion | flops 26017792 | bytes 453632 | tf_op jit(solution)/shard_map/ect,td->ecd/dot_general | solution.py:112
  5.3 13.7 %all-to-all-start = ((bf16[32,24,256]{2,1,0:T(8,128)(2,1)}), bf16[32,24,256]{2,1,0:T(8,128)(2,1)S(1)}, u32[]{:S(2)}, u32[]{:S(2)}) async-start(bf16[32,24,256]{2,1,0:T(8,128)(2,1)} %fusion.1), calls=%async_computation | async-start | bytes 786432 | tf_op jit(solution)/shard_map/all_to_all | solution.py:114
  21.0 11.9 %all-to-all-done = bf16[32,24,256]{2,1,0:T(8,128)(2,1)S(1)} async-done(((bf16[32,24,256]{2,1,0:T(8,128)(2,1)}), bf16[32,24,256]{2,1,0:T(8,128)(2,1)S(1)}, u32[]{:S(2)}, u32[]{:S(2)}) %all-to-all-start) | async-done | bytes 393248 | tf_op jit(solution)/shard_map/all_to_all | solution.py:114
  34.0 4.4 %collective-permute-start.10 = (bf16[8,144,384]{2,1,0:T(8,128)(2,1)S(1)}, bf16[8,144,384]{2,1,0:T(8,128)(2,1)S(1)}, u32[]{:S(2)}, u32[]{:S(2)}) collective-permute-start(bf16[8,144,384]{2,1,0:T(8,128)(2,1)S(1)} %pad_maximum_fusion), channel_id=1, source_target_pairs={{0,32},{32,0},{1,33},{33,1},{2,34},{34,2},{3,35},{35,3},{4,36},{36... | collective-permute-start | bytes 2654216 | tf_op jit(solution)/shard_map/ppermute | solution.py:60
  38.5 1.7 copy.112
  40.2 1.7 copy.107
  41.9 1.3 fusion.100
  43.8 1.2 fusion
  45.0 6.9 %all-to-all-start.1 = ((bf16[8,144,384]{2,1,0:T(8,128)(2,1)}), bf16[8,144,384]{2,1,0:T(8,128)(2,1)S(1)}, u32[]{:S(2)}, u32[]{:S(2)}) async-start(bf16[8,144,384]{2,1,0:T(8,128)(2,1)} %fusion), calls=%async_computation.1 | async-start | bytes 1769472 | tf_op jit(solution)/shard_map/all_to_all | solution.py:130
  54.6 2.8 %multiply_convert_fusion = bf16[512,3,128]{0,2,1:T(8,128)(2,1)S(1)} fusion(f32[512,3,128]{0,2,1:T(8,128)S(1)} %get-tuple-element.64, f32[512,3]{0,1:T(4,128)S(1)} %add_sqrt_fusion), kind=kLoop, calls=%fused_computation.32 | loop fusion | flops 1572864 | bytes 1185792 | tf_op jit(solution)/shard_map/convert_element_type | solution.py:56
  57.4 1.0 conditional.2
  57.4 0.9 copy.117
  58.4 19.3 %all-to-all-done.1 = bf16[8,144,384]{2,1,0:T(8,128)(2,1)S(1)} async-done(((bf16[8,144,384]{2,1,0:T(8,128)(2,1)}), bf16[8,144,384]{2,1,0:T(8,128)(2,1)S(1)}, u32[]{:S(2)}, u32[]{:S(2)}) %all-to-all-start.1) | async-done | bytes 884768 | tf_op jit(solution)/shard_map/all_to_all | solution.py:130
  80.0 1.9 %collective-permute-start.11 = (bf16[144,384]{1,0:T(8,128)(2,1)}, bf16[144,384]{1,0:T(8,128)(2,1)S(1)}, u32[]{:S(2)}, u32[]{:S(2)}) collective-permute-start(bf16[144,384]{1,0:T(8,128)(2,1)} %get-tuple-element.39), channel_id=1, source_target_pairs={{0,256},{64,320},{128,384},{192,448},{256,0},{320,64},{384,128},{4... | collective-permute-start | bytes 331784 | tf_op jit(solution)/shard_map/ppermute | solution.py:85
  81.9 2.0 %collective-permute-start.12 = (bf16[144,384]{1,0:T(8,128)(2,1)}, bf16[144,384]{1,0:T(8,128)(2,1)S(1)}, u32[]{:S(2)}, u32[]{:S(2)}) collective-permute-start(bf16[144,384]{1,0:T(8,128)(2,1)} %get-tuple-element.39), channel_id=1, source_target_pairs={{0,192},{64,256},{128,320},{192,384},{256,448},{320,0},{384,64},{4... | collective-permute-start | bytes 331784 | tf_op jit(solution)/shard_map/ppermute | solution.py:85
  83.9 6.3 %collective-permute-start.13 = (bf16[144,384]{1,0:T(8,128)(2,1)}, bf16[144,384]{1,0:T(8,128)(2,1)S(1)}, u32[]{:S(2)}, u32[]{:S(2)}) collective-permute-start(bf16[144,384]{1,0:T(8,128)(2,1)} %get-tuple-element.39), channel_id=1, source_target_pairs={{0,320},{64,384},{128,448},{192,0},{256,64},{320,128},{384,192},{4... | collective-permute-start | bytes 331784 | tf_op jit(solution)/shard_map/ppermute | solution.py:85
  90.2 4.0 %collective-permute-start.14 = (bf16[144,384]{1,0:T(8,128)(2,1)}, bf16[144,384]{1,0:T(8,128)(2,1)S(1)}, u32[]{:S(2)}, u32[]{:S(2)}) collective-permute-start(bf16[144,384]{1,0:T(8,128)(2,1)} %get-tuple-element.39), channel_id=1, source_target_pairs={{0,128},{64,192},{128,256},{192,320},{256,384},{320,448},{384,0},{... | collective-permute-start | bytes 331784 | tf_op jit(solution)/shard_map/ppermute | solution.py:85
  94.2 3.4 %collective-permute-start.15 = (bf16[144,384]{1,0:T(8,128)(2,1)}, bf16[144,384]{1,0:T(8,128)(2,1)S(1)}, u32[]{:S(2)}, u32[]{:S(2)}) collective-permute-start(bf16[144,384]{1,0:T(8,128)(2,1)} %get-tuple-element.39), channel_id=1, source_target_pairs={{0,384},{64,448},{128,0},{192,64},{256,128},{320,192},{384,256},{4... | collective-permute-start | bytes 331784 | tf_op jit(solution)/shard_map/ppermute | solution.py:85
  97.7 3.1 %collective-permute-start.16 = (bf16[144,384]{1,0:T(8,128)(2,1)}, bf16[144,384]{1,0:T(8,128)(2,1)S(1)}, u32[]{:S(2)}, u32[]{:S(2)}) collective-permute-start(bf16[144,384]{1,0:T(8,128)(2,1)} %get-tuple-element.39), channel_id=1, source_target_pairs={{0,64},{64,128},{128,192},{192,256},{256,320},{320,384},{384,448},... | collective-permute-start | bytes 331784 | tf_op jit(solution)/shard_map/ppermute | solution.py:85
  100.9 3.4 %collective-permute-start.17 = (bf16[144,384]{1,0:T(8,128)(2,1)}, bf16[144,384]{1,0:T(8,128)(2,1)S(1)}, u32[]{:S(2)}, u32[]{:S(2)}) collective-permute-start(bf16[144,384]{1,0:T(8,128)(2,1)} %get-tuple-element.39), channel_id=1, source_target_pairs={{0,448},{64,0},{128,64},{192,128},{256,192},{320,256},{384,320},{4... | collective-permute-start | bytes 331784 | tf_op jit(solution)/shard_map/ppermute | solution.py:85
  104.4 2.3 %collective-permute-done.15 = bf16[144,384]{1,0:T(8,128)(2,1)S(1)} collective-permute-done((bf16[144,384]{1,0:T(8,128)(2,1)}, bf16[144,384]{1,0:T(8,128)(2,1)S(1)}, u32[]{:S(2)}, u32[]{:S(2)}) %collective-permute-start.15) | collective-permute-done | bytes 110624 | tf_op jit(solution)/shard_map/ppermute | solution.py:85
  106.7 0.9 collective-permute-done.17
  107.7 4.4 %collective-permute-start.18 = (bf16[8,144,384]{2,1,0:T(8,128)(2,1)S(1)}, bf16[8,144,384]{2,1,0:T(8,128)(2,1)S(1)}, u32[]{:S(2)}, u32[]{:S(2)}) collective-permute-start(bf16[8,144,384]{2,1,0:T(8,128)(2,1)S(1)} %bitcast_dynamic-update-slice_fusion), channel_id=1, source_target_pairs={{0,32},{32,0},{1,33},{33,1},{2,34},{34,2},{3,35},{35,3},{4,36},{36... | collective-permute-start | bytes 2654216 | tf_op jit(solution)/shard_map/ppermute | solution.py:60
  112.9 6.7 %all-to-all-start.2 = ((bf16[8,96,384]{2,1,0:T(8,128)(2,1)}), bf16[8,96,384]{2,1,0:T(8,128)(2,1)S(1)}, u32[]{:S(2)}, u32[]{:S(2)}) async-start(bf16[8,96,384]{2,1,0:T(8,128)(2,1)} %broadcast_in_dim.84), calls=%async_computation.2 | async-start | bytes 1179648 | tf_op jit(solution)/shard_map/all_to_all | solution.py:76
  119.9 0.9 fusion.95
  120.8 18.2 %all-to-all-done.2 = bf16[8,96,384]{2,1,0:T(8,128)(2,1)S(1)} async-done(((bf16[8,96,384]{2,1,0:T(8,128)(2,1)}), bf16[8,96,384]{2,1,0:T(8,128)(2,1)S(1)}, u32[]{:S(2)}, u32[]{:S(2)}) %all-to-all-start.2) | async-done | bytes 589856 | tf_op jit(solution)/shard_map/all_to_all | solution.py:76
  139.1 2.5 %collective-permute-start.19 = (bf16[8,96,384]{2,1,0:T(8,128)(2,1)S(1)}, bf16[8,96,384]{2,1,0:T(8,128)(2,1)S(1)}, u32[]{:S(2)}, u32[]{:S(2)}) collective-permute-start(bf16[8,96,384]{2,1,0:T(8,128)(2,1)S(1)} %all-to-all-done.2), channel_id=1, source_target_pairs={{0,32},{32,0},{1,33},{33,1},{2,34},{34,2},{3,35},{35,3},{4,36},{36... | collective-permute-start | bytes 1769480 | tf_op jit(solution)/shard_map/ppermute | solution.py:60
  144.5 17.8 %all-to-all-start.3 = ((bf16[32,12,256]{2,1,0:T(8,128)(2,1)}), bf16[32,12,256]{2,1,0:T(8,128)(2,1)S(1)}, u32[]{:S(2)}, u32[]{:S(2)}) async-start(bf16[32,12,256]{2,1,0:T(8,128)(2,1)} %reshape.186), calls=%async_computation.3 | async-start | bytes 524288 | tf_op jit(solution)/shard_map/all_to_all | solution.py:164
  162.3 2.1 %fusion.6 = bf16[1,256,768]{2,1,0:T(8,128)(2,1)} fusion(bf16[384,384]{1,0:T(8,128)(2,1)S(1)} %bitcast.176, bf16[384,384]{1,0:T(8,128)(2,1)S(1)} %bitcast.174, bf16[512,384]{1,0:T(8,128)(2,1)} %get-tuple-element.81), kind=kOutput, calls=%fused_computation.21 | convolution fusion | flops 152567808 | bytes 1179648 | tf_op jit(solution)/shard_map/dot_general | solution.py:18
  164.4 2.1 %fusion.7 = bf16[1,256,768]{2,1,0:T(8,128)(2,1)} fusion(bf16[384,384]{1,0:T(8,128)(2,1)S(1)} %bitcast.175, bf16[384,384]{1,0:T(8,128)(2,1)S(1)} %bitcast.172, bf16[512,384]{1,0:T(8,128)(2,1)} %get-tuple-element.81), kind=kOutput, calls=%fused_computation.22 | convolution fusion | flops 152567808 | bytes 1179648 | tf_op jit(solution)/shard_map/dot_general | solution.py:18
  166.5 2.1 %fusion.5 = bf16[1,768,256]{2,1,0:T(8,128)(2,1)} fusion(bf16[384,384]{1,0:T(8,128)(2,1)S(1)} %bitcast.173, bf16[384,384]{1,0:T(8,128)(2,1)S(1)} %bitcast.171, bf16[512,384]{1,0:T(8,128)(2,1)} %get-tuple-element.81), kind=kOutput, calls=%fused_computation.20 | convolution fusion | flops 152567808 | bytes 1179648 | tf_op jit(solution)/shard_map/dot_general | solution.py:18
  168.6 5.3 %all-to-all-done.3 = bf16[32,12,256]{2,1,0:T(8,128)(2,1)S(1)} async-done(((bf16[32,12,256]{2,1,0:T(8,128)(2,1)}), bf16[32,12,256]{2,1,0:T(8,128)(2,1)S(1)}, u32[]{:S(2)}, u32[]{:S(2)}) %all-to-all-start.3) | async-done | bytes 196640 | tf_op jit(solution)/shard_map/all_to_all | solution.py:164
  (91 shorter events, 16.3 us)
Async XLA Ops:
  2.8 0.6 copy-start.4
  3.5 15.6 %copy-start = (bf16[1,256,768]{2,1,0:T(8,128)(2,1)S(1)}, bf16[1,256,768]{2,1,0:T(8,128)(2,1)}, u32[]{:S(2)}) copy-start(bf16[1,256,768]{2,1,0:T(8,128)(2,1)} %param.26) | copy-start | bytes 1179652
  3.5 15.6 %copy-start.1 = (bf16[1,256,768]{2,1,0:T(8,128)(2,1)S(1)}, bf16[1,256,768]{2,1,0:T(8,128)(2,1)}, u32[]{:S(2)}) copy-start(bf16[1,256,768]{2,1,0:T(8,128)(2,1)} %param.25) | copy-start | bytes 1179652
  5.3 27.5 %all-to-all-start = ((bf16[32,24,256]{2,1,0:T(8,128)(2,1)}), bf16[32,24,256]{2,1,0:T(8,128)(2,1)S(1)}, u32[]{:S(2)}, u32[]{:S(2)}) async-start(bf16[32,24,256]{2,1,0:T(8,128)(2,1)} %fusion.1), calls=%async_computation | async-start | bytes 786432 | tf_op jit(solution)/shard_map/all_to_all | solution.py:114
  19.1 1.1 copy-start.6
  34.0 9.8 %collective-permute-start.10 = (bf16[8,144,384]{2,1,0:T(8,128)(2,1)S(1)}, bf16[8,144,384]{2,1,0:T(8,128)(2,1)S(1)}, u32[]{:S(2)}, u32[]{:S(2)}) collective-permute-start(bf16[8,144,384]{2,1,0:T(8,128)(2,1)S(1)} %pad_maximum_fusion), channel_id=1, source_target_pairs={{0,32},{32,0},{1,33},{33,1},{2,34},{34,2},{3,35},{35,3},{4,36},{36... | collective-permute-start | bytes 2654216 | tf_op jit(solution)/shard_map/ppermute | solution.py:60
  41.9 1.3 copy-start.2
  41.9 1.6 copy-start.3
  45.0 6.9 %copy-start.9 = (s32[32]{0:T(128)S(1)}, s32[32]{0:T(128)}, u32[]{:S(2)}) copy-start(s32[32]{0:T(128)} %param.29) | copy-start | bytes 388
  45.0 32.6 %all-to-all-start.1 = ((bf16[8,144,384]{2,1,0:T(8,128)(2,1)}), bf16[8,144,384]{2,1,0:T(8,128)(2,1)S(1)}, u32[]{:S(2)}, u32[]{:S(2)}) async-start(bf16[8,144,384]{2,1,0:T(8,128)(2,1)} %fusion), calls=%async_computation.1 | async-start | bytes 1769472 | tf_op jit(solution)/shard_map/all_to_all | solution.py:130
  80.0 17.7 %collective-permute-start.11 = (bf16[144,384]{1,0:T(8,128)(2,1)}, bf16[144,384]{1,0:T(8,128)(2,1)S(1)}, u32[]{:S(2)}, u32[]{:S(2)}) collective-permute-start(bf16[144,384]{1,0:T(8,128)(2,1)} %get-tuple-element.39), channel_id=1, source_target_pairs={{0,256},{64,320},{128,384},{192,448},{256,0},{320,64},{384,128},{4... | collective-permute-start | bytes 331784 | tf_op jit(solution)/shard_map/ppermute | solution.py:85
  81.9 19.0 %collective-permute-start.12 = (bf16[144,384]{1,0:T(8,128)(2,1)}, bf16[144,384]{1,0:T(8,128)(2,1)S(1)}, u32[]{:S(2)}, u32[]{:S(2)}) collective-permute-start(bf16[144,384]{1,0:T(8,128)(2,1)} %get-tuple-element.39), channel_id=1, source_target_pairs={{0,192},{64,256},{128,320},{192,384},{256,448},{320,0},{384,64},{4... | collective-permute-start | bytes 331784 | tf_op jit(solution)/shard_map/ppermute | solution.py:85
  83.9 20.4 %collective-permute-start.13 = (bf16[144,384]{1,0:T(8,128)(2,1)}, bf16[144,384]{1,0:T(8,128)(2,1)S(1)}, u32[]{:S(2)}, u32[]{:S(2)}) collective-permute-start(bf16[144,384]{1,0:T(8,128)(2,1)} %get-tuple-element.39), channel_id=1, source_target_pairs={{0,320},{64,384},{128,448},{192,0},{256,64},{320,128},{384,192},{4... | collective-permute-start | bytes 331784 | tf_op jit(solution)/shard_map/ppermute | solution.py:85
  90.2 14.2 %collective-permute-start.14 = (bf16[144,384]{1,0:T(8,128)(2,1)}, bf16[144,384]{1,0:T(8,128)(2,1)S(1)}, u32[]{:S(2)}, u32[]{:S(2)}) collective-permute-start(bf16[144,384]{1,0:T(8,128)(2,1)} %get-tuple-element.39), channel_id=1, source_target_pairs={{0,128},{64,192},{128,256},{192,320},{256,384},{320,448},{384,0},{... | collective-permute-start | bytes 331784 | tf_op jit(solution)/shard_map/ppermute | solution.py:85
  94.2 12.5 %collective-permute-start.15 = (bf16[144,384]{1,0:T(8,128)(2,1)}, bf16[144,384]{1,0:T(8,128)(2,1)S(1)}, u32[]{:S(2)}, u32[]{:S(2)}) collective-permute-start(bf16[144,384]{1,0:T(8,128)(2,1)} %get-tuple-element.39), channel_id=1, source_target_pairs={{0,384},{64,448},{128,0},{192,64},{256,128},{320,192},{384,256},{4... | collective-permute-start | bytes 331784 | tf_op jit(solution)/shard_map/ppermute | solution.py:85
  97.7 9.0 %collective-permute-start.16 = (bf16[144,384]{1,0:T(8,128)(2,1)}, bf16[144,384]{1,0:T(8,128)(2,1)S(1)}, u32[]{:S(2)}, u32[]{:S(2)}) collective-permute-start(bf16[144,384]{1,0:T(8,128)(2,1)} %get-tuple-element.39), channel_id=1, source_target_pairs={{0,64},{64,128},{128,192},{192,256},{256,320},{320,384},{384,448},... | collective-permute-start | bytes 331784 | tf_op jit(solution)/shard_map/ppermute | solution.py:85
  100.9 6.8 %collective-permute-start.17 = (bf16[144,384]{1,0:T(8,128)(2,1)}, bf16[144,384]{1,0:T(8,128)(2,1)S(1)}, u32[]{:S(2)}, u32[]{:S(2)}) collective-permute-start(bf16[144,384]{1,0:T(8,128)(2,1)} %get-tuple-element.39), channel_id=1, source_target_pairs={{0,448},{64,0},{128,64},{192,128},{256,192},{320,256},{384,320},{4... | collective-permute-start | bytes 331784 | tf_op jit(solution)/shard_map/ppermute | solution.py:85
  107.7 11.9 %collective-permute-start.18 = (bf16[8,144,384]{2,1,0:T(8,128)(2,1)S(1)}, bf16[8,144,384]{2,1,0:T(8,128)(2,1)S(1)}, u32[]{:S(2)}, u32[]{:S(2)}) collective-permute-start(bf16[8,144,384]{2,1,0:T(8,128)(2,1)S(1)} %bitcast_dynamic-update-slice_fusion), channel_id=1, source_target_pairs={{0,32},{32,0},{1,33},{33,1},{2,34},{34,2},{3,35},{35,3},{4,36},{36... | collective-permute-start | bytes 2654216 | tf_op jit(solution)/shard_map/ppermute | solution.py:60
  112.9 26.1 %all-to-all-start.2 = ((bf16[8,96,384]{2,1,0:T(8,128)(2,1)}), bf16[8,96,384]{2,1,0:T(8,128)(2,1)S(1)}, u32[]{:S(2)}, u32[]{:S(2)}) async-start(bf16[8,96,384]{2,1,0:T(8,128)(2,1)} %broadcast_in_dim.84), calls=%async_computation.2 | async-start | bytes 1179648 | tf_op jit(solution)/shard_map/all_to_all | solution.py:76
  139.1 4.0 %collective-permute-start.19 = (bf16[8,96,384]{2,1,0:T(8,128)(2,1)S(1)}, bf16[8,96,384]{2,1,0:T(8,128)(2,1)S(1)}, u32[]{:S(2)}, u32[]{:S(2)}) collective-permute-start(bf16[8,96,384]{2,1,0:T(8,128)(2,1)S(1)} %all-to-all-done.2), channel_id=1, source_target_pairs={{0,32},{32,0},{1,33},{33,1},{2,34},{34,2},{3,35},{35,3},{4,36},{36... | collective-permute-start | bytes 1769480 | tf_op jit(solution)/shard_map/ppermute | solution.py:60
  143.4 18.9 %copy-start.8 = (bf16[8,48,384]{2,1,0:T(8,128)(2,1)S(1)}, bf16[8,48,384]{2,1,0:T(8,128)(2,1)}, u32[]{:S(2)}) copy-start(bf16[8,48,384]{2,1,0:T(8,128)(2,1)} %get-tuple-element.46) | copy-start | bytes 884740
  144.5 29.4 %all-to-all-start.3 = ((bf16[32,12,256]{2,1,0:T(8,128)(2,1)}), bf16[32,12,256]{2,1,0:T(8,128)(2,1)S(1)}, u32[]{:S(2)}, u32[]{:S(2)}) async-start(bf16[32,12,256]{2,1,0:T(8,128)(2,1)} %reshape.186), calls=%async_computation.3 | async-start | bytes 524288 | tf_op jit(solution)/shard_map/all_to_all | solution.py:164
  162.3 2.1 %copy-start.7 = (bf16[8,48,384]{2,1,0:T(8,128)(2,1)S(1)}, bf16[8,48,384]{2,1,0:T(8,128)(2,1)}, u32[]{:S(2)}) copy-start(bf16[8,48,384]{2,1,0:T(8,128)(2,1)} %get-tuple-element.47) | copy-start | bytes 884740
  166.5 7.4 %copy-start.5 = (bf16[32,12,32]{2,1,0:T(8,128)(2,1)S(1)}, bf16[32,12,32]{2,1,0:T(8,128)(2,1)}, u32[]{:S(2)}) copy-start(bf16[32,12,32]{2,1,0:T(8,128)(2,1)} %copy-done.4) | copy-start | bytes 73732

commit v3 on v1

--- a/solution.py
+++ b/solution.py
@@ -117,15 +117,17 @@
     arrived = exchange(away, "core", 1)
     chip_sum = (partials(core) + arrived.astype(F32)).astype(BF16)
     blocks = lax.all_to_all(chip_sum, "y", 0, 0, tiled=True)
-    sums = jnp.sum(blocks.astype(F32), axis=0)
-    gate_sum, up_sum, hid_grad = sums[:part], sums[part : 2 * part], sums[2 * part :]
 
     me = lax.axis_index("expert")
     flip_signs = (1 - 2 * lax.dynamic_index_in_dim(sign_bits, me, 0, keepdims=False)).astype(BF16)
     rotation = sylvester(HBLOCK) * flip_signs[:, None]
     quant_rows = rotate_quant_t(jnp.concatenate([rows_in.T, rows_grad.T], 0), rotation)
     mate_rows = partner_swap(quant_rows, partner)
+
+    blocks, mate_rows = lax.optimization_barrier((blocks, mate_rows))
     mate_in, mate_grad = mate_rows[:width], mate_rows[width:]
+    sums = jnp.sum(blocks.astype(F32), axis=0)
+    gate_sum, up_sum, hid_grad = sums[:part], sums[part : 2 * part], sums[2 * part :]
 
     sig = jax.nn.sigmoid(gate_sum)
     silu = gate_sum * sig
@@ -136,7 +138,7 @@
     own = jnp.concatenate([gate_rows, up_rows], 0)
     own_half = gather_y(own)
     quant = rotate_quant_t(jnp.concatenate([gate_rows, up_rows, hidden], 0), rotation)
-    mate_half = gather_y(partner_swap(quant, partner))
+    mate_all = lax.all_gather(partner_swap(quant, partner), ("y", "core"))
 
     def back(half_rows, which):
         start = which * half
@@ -153,13 +155,10 @@
     )
     input_grad = jnp.einsum("ect,ecd->td", picker, returned, preferred_element_type=F32)
 
-    mate_other = exchange(mate_half, "core", 1)
-    low = jnp.where(core == 0, mate_half, mate_other)
-    high = jnp.where(core == 0, mate_other, mate_half)
+    mate_all = mate_all.reshape(n_y, 2, 3, part, rows)
 
     def whole(k):
-        cut = slice(k * part, (k + 1) * part)
-        return jnp.concatenate([low[:, cut].reshape(half, rows), high[:, cut].reshape(half, rows)], 0)
+        return jnp.swapaxes(mate_all[:, :, k], 0, 1).reshape(ff, rows)
 
     scale = 1.0 / HBLOCK
     gate_new = (dot(mate_in, whole(0), 1, 1) * scale).astype(BF16)

time: 164 us -> 162 us (0.988)
  the two profiles are of different devices: /device:TPU:68 before, /device:TPU:1 now
where the time goes in v3:
time: 162 us
  blocking collectives  42.3 us (26%)
  starting transfers between devices  38.5 us (24%)
  waiting for transfers between devices  33.2 us (20%)
  between operations  15.1 us (9%)
  matrix products  14.8 us (9%)
  local copies, waits for them, and re-layouts  11.2 us (7%)
  other arithmetic  6.25 us (4%)
    all_to_all x1, blocking collectives, shards(): lax.all_to_all(slot_back.reshape(experts, capacity, width), 'expert', 0,...  22.2 us
    all_to_all x1, blocking collectives, gather_y(): return lax.all_to_all(copies, 'y', 0, 0, tiled=True)  20.1 us
    ppermute x4, starting transfers between devices, exchange(): lax.ppermute(x, axis, [(i, i ^ apart) for i in range(lax.axis_size(axis))])  17.7 us
    ppermute x4, waiting for transfers between devices, exchange(): lax.ppermute(x, axis, [(i, i ^ apart) for i in range(lax.axis_size(axis))])  15.2 us
    all_to_all x1, starting transfers between devices, shards(): recv = lax.all_to_all(send, 'expert', 0, 0, tiled=True)  13.9 us
    all_to_all x1, waiting for transfers between devices, shards(): recv = lax.all_to_all(send, 'expert', 0, 0, tiled=True)  11.9 us
    dot_general x13, matrix products, dot(): lax.dot_general(left, right, (((left_dim,), (right_dim,)), ((), ())), pre...  11.1 us
    all_to_all x1, starting transfers between devices, shards(): blocks = lax.all_to_all(chip_sum, 'y', 0, 0, tiled=True)  6.94 us
  transfers between devices with their start and end apart: 7, of which 5 were waited for; matrix products, arithmetic and copies ran while one was open for 9% of the time, Pallas kernels for 0%

profile of v3, /device:TPU:1, one launch (start us, length us, event | category | flops | bytes accessed | tf_op | source)
XLA Modules:
  0.0 161.6 jit_solution(8642818823206911252)
XLA Ops:
  7.2 0.8 copy.93
  8.4 0.8 copy.96
  10.1 1.8 %fusion.1 = bf16[32,24,256]{2,1,0:T(8,128)(2,1)} fusion(f32[32,24]{1,0:T(8,128)S(1)} %concatenate.35, bf16[32,12,32]{2,1,0:T(8,128)(2,1)S(1)} %convert_convert_fusion, bf16[32,256]{1,0:T(8,128)(2,1)} %param.22, bf16[32,256]{1,0:T(8,128)(2,1)} %param.21), kind=kOutput, calls=%fused_computation.7 | convolution fusion | flops 26017792 | bytes 453632 | tf_op jit(solution)/shard_map/ect,td->ecd/dot_general | solution.py:101
  11.9 13.9 %all-to-all-start = ((bf16[32,24,256]{2,1,0:T(8,128)(2,1)}), bf16[32,24,256]{2,1,0:T(8,128)(2,1)S(1)}, u32[]{:S(2)}, u32[]{:S(2)}) async-start(bf16[32,24,256]{2,1,0:T(8,128)(2,1)} %fusion.1), calls=%async_computation | async-start | bytes 786432 | tf_op jit(solution)/shard_map/all_to_all | solution.py:103
  25.8 0.8 dynamic-slice_bitcast_fusion
  26.9 0.7 constant_dynamic-slice_fusion.1
  27.7 11.9 %all-to-all-done = bf16[32,24,256]{2,1,0:T(8,128)(2,1)S(1)} async-done(((bf16[32,24,256]{2,1,0:T(8,128)(2,1)}), bf16[32,24,256]{2,1,0:T(8,128)(2,1)S(1)}, u32[]{:S(2)}, u32[]{:S(2)}) %all-to-all-start) | async-done | bytes 393248 | tf_op jit(solution)/shard_map/all_to_all | solution.py:103
  40.7 4.4 %collective-permute-start.10 = (bf16[8,144,384]{2,1,0:T(8,128)(2,1)S(1)}, bf16[8,144,384]{2,1,0:T(8,128)(2,1)S(1)}, u32[]{:S(2)}, u32[]{:S(2)}) collective-permute-start(bf16[8,144,384]{2,1,0:T(8,128)(2,1)S(1)} %pad_maximum_fusion), channel_id=1, source_target_pairs={{0,32},{32,0},{1,33},{33,1},{2,34},{34,2},{3,35},{35,3},{4,36},{36... | collective-permute-start | bytes 2654216 | tf_op jit(solution)/shard_map/ppermute | solution.py:60
  45.2 1.7 %copy.92 = bf16[384,256]{1,0:T(8,128)(2,1)} copy(bf16[384,256]{0,1:T(8,128)(2,1)} %get-tuple-element.56) | data formatting | bytes 393216 | tf_op jit(solution)/shard_map/dot_general | solution.py:18
  46.9 1.7 %copy.97 = bf16[384,256]{1,0:T(8,128)(2,1)} copy(bf16[384,256]{0,1:T(8,128)(2,1)} %get-tuple-element.44) | data formatting | bytes 393216 | tf_op jit(solution)/shard_map/dot_general | solution.py:18
  48.7 1.2 fusion.86
  49.9 1.2 fusion.87
  51.4 1.2 fusion
  52.6 6.9 %all-to-all-start.1 = ((bf16[8,144,384]{2,1,0:T(8,128)(2,1)}), bf16[8,144,384]{2,1,0:T(8,128)(2,1)S(1)}, u32[]{:S(2)}, u32[]{:S(2)}) async-start(bf16[8,144,384]{2,1,0:T(8,128)(2,1)} %fusion), calls=%async_computation.1 | async-start | bytes 1769472 | tf_op jit(solution)/shard_map/all_to_all | solution.py:119
  62.1 2.8 %multiply_convert_fusion = bf16[512,3,128]{0,2,1:T(8,128)(2,1)S(1)} fusion(f32[512,3,128]{0,2,1:T(8,128)S(1)} %get-tuple-element.53, f32[512,3]{0,1:T(4,128)S(1)} %add_sqrt_fusion), kind=kLoop, calls=%fused_computation.24 | loop fusion | flops 1572864 | bytes 1185792 | tf_op jit(solution)/shard_map/convert_element_type | solution.py:56
  64.9 14.2 %conditional.2 = (bf16[512,384]{1,0:T(8,128)(2,1)}) conditional(s32[]{:T(128)} %clamp.4, bf16[512,384]{0,1:T(8,128)(2,1)S(1)} %bitcast.121, bf16[512,384]{0,1:T(8,128)(2,1)S(1)} %bitcast.122, bf16[512,384]{0,1:T(8,128)(2,1)S(1)} %bitcast.123, bf16[512,384]{0,1:T(8,128)(2,1)S(1)} %bitcast.124, ...), branch_computations={%region_4.5_spmd, %region_5.6_spmd, %region_6.7_spmd, %region_7.8_... | conditional | bytes 2359344 | solution.py:70
  65.2 3.6 %collective-permute-start.1 = (bf16[512,384]{1,0:T(8,128)(2,1)S(1)}, bf16[512,384]{1,0:T(8,128)(2,1)}, u32[]{:S(2)}, u32[]{:S(2)}) collective-permute-start(bf16[512,384]{1,0:T(8,128)(2,1)S(1)} %copy.104), channel_id=1, source_target_pairs={{0,2},{1,3},{2,0},{3,1},{4,6},{5,7},{6,4},{7,5},{8,10},{9,11},{10,... | collective-permute-start | bytes 1179656 | tf_op jit(solution)/shard_map/cond/branch_2_fun/ppermute | solution.py:60
  68.8 10.3 %collective-permute-done.1 = bf16[512,384]{1,0:T(8,128)(2,1)} collective-permute-done((bf16[512,384]{1,0:T(8,128)(2,1)S(1)}, bf16[512,384]{1,0:T(8,128)(2,1)}, u32[]{:S(2)}, u32[]{:S(2)}) %collective-permute-start.1) | collective-permute-done | bytes 393248 | tf_op jit(solution)/shard_map/cond/branch_2_fun/ppermute | solution.py:60
  79.1 6.1 %all-to-all-done.1 = bf16[8,144,384]{2,1,0:T(8,128)(2,1)S(1)} async-done(((bf16[8,144,384]{2,1,0:T(8,128)(2,1)}), bf16[8,144,384]{2,1,0:T(8,128)(2,1)S(1)}, u32[]{:S(2)}, u32[]{:S(2)}) %all-to-all-start.1) | async-done | bytes 884768 | tf_op jit(solution)/shard_map/all_to_all | solution.py:119
  85.9 0.9 copy_bitcast_fusion
  86.7 7.6 %conditional.3 = (bf16[144,384]{1,0:T(8,128)(2,1)S(1)}) conditional(s32[]{:T(128)} %clamp.4, bf16[144,384]{1,0:T(8,128)(2,1)S(1)} %copy_bitcast_fusion, bf16[144,384]{1,0:T(8,128)(2,1)S(1)} %copy_bitcast_fusion, bf16[144,384]{1,0:T(8,128)(2,1)S(1)} %copy_bitcast_fusion, ...), branch_computations={%region_12.13_spmd, %region_13.14_spmd, %region_14.15_spmd, %regio... | conditional | bytes 663600 | solution.py:70
  86.8 3.6 %collective-permute-start.6 = (bf16[144,384]{1,0:T(8,128)(2,1)S(1)}, bf16[144,384]{1,0:T(8,128)(2,1)S(1)}, u32[]{:S(2)}, u32[]{:S(2)}) collective-permute-start(bf16[144,384]{1,0:T(8,128)(2,1)S(1)} %param.8), channel_id=1, source_target_pairs={{0,2},{1,3},{2,0},{3,1},{4,6},{5,7},{6,4},{7,5},{8,10},{9,11},{10,... | collective-permute-start | bytes 331784 | tf_op jit(solution)/shard_map/cond/branch_2_fun/ppermute | solution.py:60
  90.4 3.9 %collective-permute-done.6 = bf16[144,384]{1,0:T(8,128)(2,1)S(1)} collective-permute-done((bf16[144,384]{1,0:T(8,128)(2,1)S(1)}, bf16[144,384]{1,0:T(8,128)(2,1)S(1)}, u32[]{:S(2)}, u32[]{:S(2)}) %collective-permute-start.6) | collective-permute-done | bytes 110624 | tf_op jit(solution)/shard_map/cond/branch_2_fun/ppermute | solution.py:60
  95.1 20.1 %all_to_all.20 = bf16[8,96,384]{2,1,0:T(8,128)(2,1)S(1)} all-to-all(bf16[8,96,384]{2,1,0:T(8,128)(2,1)S(1)} %broadcast_in_dim.11), channel_id=1, replica_groups=mesh['y'=8,'core'=2,'expert'=32] {'y'}, dimensions={0} | all-to-all | bytes 1179648 | tf_op jit(solution)/shard_map/all_to_all | solution.py:76
  115.2 6.1 %collective-permute-start.11 = (bf16[8,96,384]{2,1,0:T(8,128)(2,1)S(1)}, bf16[8,96,384]{2,1,0:T(8,128)(2,1)S(1)}, u32[]{:S(2)}, u32[]{:S(2)}) collective-permute-start(bf16[8,96,384]{2,1,0:T(8,128)(2,1)S(1)} %all_to_all.20), channel_id=1, source_target_pairs={{0,32},{32,0},{1,33},{33,1},{2,34},{34,2},{3,35},{35,3},{4,36},{36... | collective-permute-start | bytes 1769480 | tf_op jit(solution)/shard_map/ppermute | solution.py:60
  122.0 0.9 collective-permute-done.11
  123.7 22.2 %all_to_all.21 = bf16[32,12,256]{2,1,0:T(8,128)(2,1)S(1)} all-to-all(bf16[32,12,256]{2,1,0:T(8,128)(2,1)S(1)} %reshape.168), channel_id=1, replica_groups=mesh['y'=8,'core'=2,'expert'=32] {'expert'}, dimensions={0} | all-to-all | bytes 393216 | tf_op jit(solution)/shard_map/all_to_all | solution.py:153
  145.9 0.8 fusion.10
  146.7 1.6 slice_bitcast_fusion
  148.5 2.1 %fusion.5 = bf16[1,768,256]{2,1,0:T(8,128)(2,1)} fusion(bf16[768,384]{1,0:T(8,128)(2,1)S(1)} %bitcast.127, bf16[512,384]{1,0:T(8,128)(2,1)} %get-tuple-element.58), kind=kOutput, calls=%fused_computation.14 | convolution fusion | flops 151388160 | bytes 1179648 | tf_op jit(solution)/shard_map/dot_general | solution.py:18
  150.5 2.1 %fusion.6 = bf16[1,256,768]{2,1,0:T(8,128)(2,1)} fusion(bf16[768,384]{1,0:T(8,128)(2,1)S(1)} %bitcast.128, bf16[512,384]{1,0:T(8,128)(2,1)} %get-tuple-element.58), kind=kOutput, calls=%fused_computation.15 | convolution fusion | flops 151388160 | bytes 1179648 | tf_op jit(solution)/shard_map/dot_general | solution.py:18
  152.7 2.1 %fusion.7 = bf16[1,256,768]{2,1,0:T(8,128)(2,1)} fusion(bf16[768,384]{1,0:T(8,128)(2,1)S(1)} %bitcast.129, bf16[512,384]{1,0:T(8,128)(2,1)} %get-tuple-element.58), kind=kOutput, calls=%fused_computation.16 | convolution fusion | flops 151388160 | bytes 1179648 | tf_op jit(solution)/shard_map/dot_general | solution.py:18
  (66 shorter events, 8.0 us)
Async XLA Ops:
  7.2 18.6 %copy-start.1 = (bf16[1,256,768]{2,1,0:T(8,128)(2,1)S(1)}, bf16[1,256,768]{2,1,0:T(8,128)(2,1)}, u32[]{:S(2)}) copy-start(bf16[1,256,768]{2,1,0:T(8,128)(2,1)} %param.25) | copy-start | bytes 1179652
  7.2 18.6 %copy-start = (bf16[1,256,768]{2,1,0:T(8,128)(2,1)S(1)}, bf16[1,256,768]{2,1,0:T(8,128)(2,1)}, u32[]{:S(2)}) copy-start(bf16[1,256,768]{2,1,0:T(8,128)(2,1)} %param.26) | copy-start | bytes 1179652
  9.4 0.7 copy-start.4
  11.9 15.0 %copy-start.6 = (bf16[1,768,256]{2,1,0:T(8,128)(2,1)S(1)}, bf16[1,768,256]{2,1,0:T(8,128)(2,1)}, u32[]{:S(2)}) copy-start(bf16[1,768,256]{2,1,0:T(8,128)(2,1)} %param.27) | copy-start | bytes 1179652
  11.9 27.7 %all-to-all-start = ((bf16[32,24,256]{2,1,0:T(8,128)(2,1)}), bf16[32,24,256]{2,1,0:T(8,128)(2,1)S(1)}, u32[]{:S(2)}, u32[]{:S(2)}) async-start(bf16[32,24,256]{2,1,0:T(8,128)(2,1)} %fusion.1), calls=%async_computation | async-start | bytes 786432 | tf_op jit(solution)/shard_map/all_to_all | solution.py:103
  40.7 10.7 %collective-permute-start.10 = (bf16[8,144,384]{2,1,0:T(8,128)(2,1)S(1)}, bf16[8,144,384]{2,1,0:T(8,128)(2,1)S(1)}, u32[]{:S(2)}, u32[]{:S(2)}) collective-permute-start(bf16[8,144,384]{2,1,0:T(8,128)(2,1)S(1)} %pad_maximum_fusion), channel_id=1, source_target_pairs={{0,32},{32,0},{1,33},{33,1},{2,34},{34,2},{3,35},{35,3},{4,36},{36... | collective-permute-start | bytes 2654216 | tf_op jit(solution)/shard_map/ppermute | solution.py:60
  48.6 2.5 %copy-start.2 = (bf16[1,384,256]{2,1,0:T(8,128)(2,1)S(1)}, bf16[1,384,256]{2,1,0:T(8,128)(2,1)}, u32[]{:S(2)}) copy-start(bf16[1,384,256]{2,1,0:T(8,128)(2,1)} %get-tuple-element.46) | copy-start | bytes 589828
  52.6 7.0 %copy-start.7 = (s32[32]{0:T(128)S(1)}, s32[32]{0:T(128)}, u32[]{:S(2)}) copy-start(s32[32]{0:T(128)} %param.29) | copy-start | bytes 388
  52.6 32.6 %all-to-all-start.1 = ((bf16[8,144,384]{2,1,0:T(8,128)(2,1)}), bf16[8,144,384]{2,1,0:T(8,128)(2,1)S(1)}, u32[]{:S(2)}, u32[]{:S(2)}) async-start(bf16[8,144,384]{2,1,0:T(8,128)(2,1)} %fusion), calls=%async_computation.1 | async-start | bytes 1769472 | tf_op jit(solution)/shard_map/all_to_all | solution.py:119
  59.5 87.2 %all-gather.3.cloned.1.call-start = ((), (), s32[]{:S(2)}) async-start(), calls=%async_computation.4 | async-start | bytes 1880064 | tf_op jit(solution)/shard_map/all_gather | solution.py:141
  65.2 13.9 %collective-permute-start.1 = (bf16[512,384]{1,0:T(8,128)(2,1)S(1)}, bf16[512,384]{1,0:T(8,128)(2,1)}, u32[]{:S(2)}, u32[]{:S(2)}) collective-permute-start(bf16[512,384]{1,0:T(8,128)(2,1)S(1)} %copy.104), channel_id=1, source_target_pairs={{0,2},{1,3},{2,0},{3,1},{4,6},{5,7},{6,4},{7,5},{8,10},{9,11},{10,... | collective-permute-start | bytes 1179656 | tf_op jit(solution)/shard_map/cond/branch_2_fun/ppermute | solution.py:60
  86.8 7.5 %collective-permute-start.6 = (bf16[144,384]{1,0:T(8,128)(2,1)S(1)}, bf16[144,384]{1,0:T(8,128)(2,1)S(1)}, u32[]{:S(2)}, u32[]{:S(2)}) collective-permute-start(bf16[144,384]{1,0:T(8,128)(2,1)S(1)} %param.8), channel_id=1, source_target_pairs={{0,2},{1,3},{2,0},{3,1},{4,6},{5,7},{6,4},{7,5},{8,10},{9,11},{10,... | collective-permute-start | bytes 331784 | tf_op jit(solution)/shard_map/cond/branch_2_fun/ppermute | solution.py:60
  94.4 0.6 copy-start.3
  115.2 7.7 %collective-permute-start.11 = (bf16[8,96,384]{2,1,0:T(8,128)(2,1)S(1)}, bf16[8,96,384]{2,1,0:T(8,128)(2,1)S(1)}, u32[]{:S(2)}, u32[]{:S(2)}) collective-permute-start(bf16[8,96,384]{2,1,0:T(8,128)(2,1)S(1)} %all_to_all.20), channel_id=1, source_target_pairs={{0,32},{32,0},{1,33},{33,1},{2,34},{34,2},{3,35},{35,3},{4,36},{36... | collective-permute-start | bytes 1769480 | tf_op jit(solution)/shard_map/ppermute | solution.py:60
  123.0 22.9 %copy-start.5 = (bf16[32,12,32]{2,1,0:T(8,128)(2,1)S(1)}, bf16[32,12,32]{2,1,0:T(8,128)(2,1)}, u32[]{:S(2)}) copy-start(bf16[32,12,32]{2,1,0:T(8,128)(2,1)} %copy-done.4) | copy-start | bytes 73732
Sparse Core Ops, SparseCore 0:
  95.1 41.7 all-gather.2

commit v4 on v3

--- a/solution.py
+++ b/solution.py
@@ -1,5 +1,3 @@
-import math
-
 import jax
 import jax.numpy as jnp
 from jax import lax
@@ -9,7 +7,14 @@
 HBLOCK = 128
 EPS = 1e-06
 QSTEP = 2.0
-TWO_PI = 2.0 * math.pi
+SINE = (
+    0.9999995827674866,
+    -6.579691410064697,
+    12.986429214477539,
+    -12.18803596496582,
+    6.557779312133789,
+    -1.952649712562561,
+)
 BF16 = jnp.bfloat16
 F32 = jnp.float32
 
@@ -42,6 +47,17 @@
     return placed, slot_weight
 
 
+def soft_steps(rotated, meansq):
+    scale = jnp.sqrt(meansq + EPS)
+    steps = QSTEP * rotated / scale
+    near = steps - jnp.round(steps)
+    square = near * near
+    series = jnp.full_like(near, SINE[-1])
+    for term in SINE[-2::-1]:
+        series = series * square + term
+    return ((steps - near * series) * (scale / QSTEP)).astype(BF16)
+
+
 def rotate_quant_t(operand, rotation):
     cols, rows = operand.shape
     rotated = lax.dot_general(
@@ -50,10 +66,8 @@
         (((2,), (0,)), ((), ())),
         preferred_element_type=F32,
     )
-    scale = jnp.sqrt(jnp.mean(rotated * rotated, axis=2, keepdims=True) + EPS)
-    steps = QSTEP * rotated / scale
-    soft = (steps - jnp.sin(TWO_PI * steps) / TWO_PI) * scale / QSTEP
-    return soft.astype(BF16).reshape(cols, rows)
+    meansq = jnp.mean(rotated * rotated, axis=2, keepdims=True)
+    return soft_steps(rotated, meansq).reshape(cols, rows)
 
 
 def exchange(x, axis, apart):
@@ -117,53 +131,47 @@
     arrived = exchange(away, "core", 1)
     chip_sum = (partials(core) + arrived.astype(F32)).astype(BF16)
     blocks = lax.all_to_all(chip_sum, "y", 0, 0, tiled=True)
-
-    me = lax.axis_index("expert")
-    flip_signs = (1 - 2 * lax.dynamic_index_in_dim(sign_bits, me, 0, keepdims=False)).astype(BF16)
-    rotation = sylvester(HBLOCK) * flip_signs[:, None]
-    quant_rows = rotate_quant_t(jnp.concatenate([rows_in.T, rows_grad.T], 0), rotation)
-    mate_rows = partner_swap(quant_rows, partner)
-
-    blocks, mate_rows = lax.optimization_barrier((blocks, mate_rows))
-    mate_in, mate_grad = mate_rows[:width], mate_rows[width:]
+    mate_w = partner_swap(jnp.concatenate([gate_w, up_w], 0), partner)
+    blocks, mate_w = lax.optimization_barrier((blocks, mate_w))
     sums = jnp.sum(blocks.astype(F32), axis=0)
     gate_sum, up_sum, hid_grad = sums[:part], sums[part : 2 * part], sums[2 * part :]
 
     sig = jax.nn.sigmoid(gate_sum)
     silu = gate_sum * sig
-    hidden = (silu * up_sum).astype(BF16)
-    gate_rows = (hid_grad * up_sum * sig * (1.0 + gate_sum * (1.0 - sig))).astype(BF16)
-    up_rows = (hid_grad * silu).astype(BF16)
-
-    own = jnp.concatenate([gate_rows, up_rows], 0)
-    own_half = gather_y(own)
-    quant = rotate_quant_t(jnp.concatenate([gate_rows, up_rows, hidden], 0), rotation)
-    mate_all = lax.all_gather(partner_swap(quant, partner), ("y", "core"))
-
-    def back(half_rows, which):
-        start = which * half
-        gate_t = half_rows[:, :part].reshape(half, rows)
-        up_t = half_rows[:, part:].reshape(half, rows)
-        return dot(gate_t, lax.dynamic_slice_in_dim(gate_w, start, half, 1), 0, 1) + dot(
-            up_t, lax.dynamic_slice_in_dim(up_w, start, half, 1), 0, 1
-        )
-
-    own_other = exchange(own_half, "core", 1)
-    slot_back = (back(own_half, core) + back(own_other, 1 - core)).astype(BF16)
+    hidden = silu * up_sum
+    gate_rows = hid_grad * up_sum * sig * (1.0 + gate_sum * (1.0 - sig))
+    up_rows = hid_grad * silu
+    acts = jnp.concatenate([gate_rows, up_rows, hidden], 0).astype(BF16)
+    mine = gather_y(partner_swap(acts, partner))
+    mate_recv = partner_swap(recv, partner)
+    mine, mate_recv = lax.optimization_barrier((mine, mate_recv))
+
+    theirs = exchange(mine, "core", 1)
+    low = jnp.where(core == 0, mine, theirs)
+    high = jnp.where(core == 0, theirs, mine)
+
+    def whole(k):
+        cut = slice(k * part, (k + 1) * part)
+        return jnp.concatenate([low[:, cut].reshape(half, rows), high[:, cut].reshape(half, rows)], 0)
+
+    gate_t, up_t, hidden_t = whole(0), whole(1), whole(2)
+    slot_back = (dot(gate_t, mate_w[:width], 0, 1) + dot(up_t, mate_w[width:], 0, 1)).astype(BF16)
     returned = lax.all_to_all(
         slot_back.reshape(experts, capacity, width), "expert", 0, 0, tiled=True
     )
-    input_grad = jnp.einsum("ect,ecd->td", picker, returned, preferred_element_type=F32)
-
-    mate_all = mate_all.reshape(n_y, 2, 3, part, rows)
-
-    def whole(k):
-        return jnp.swapaxes(mate_all[:, :, k], 0, 1).reshape(ff, rows)
-
+    input_grad = jnp.einsum(
+        "ect,ecd->td", jnp.take(picker, partner, axis=0), returned, preferred_element_type=F32
+    )
+
+    mate = partner[lax.axis_index("expert")]
+    flip_signs = (1 - 2 * lax.dynamic_index_in_dim(sign_bits, mate, 0, keepdims=False)).astype(BF16)
+    rotation = sylvester(HBLOCK) * flip_signs[:, None]
+    mate_in = rotate_quant_t(mate_recv[:, :capacity].reshape(rows, width).T, rotation)
+    mate_grad = rotate_quant_t(mate_recv[:, capacity:].reshape(rows, width).T, rotation)
     scale = 1.0 / HBLOCK
-    gate_new = (dot(mate_in, whole(0), 1, 1) * scale).astype(BF16)
-    up_new = (dot(mate_in, whole(1), 1, 1) * scale).astype(BF16)
-    down_new = (dot(whole(2), mate_grad, 1, 1) * scale).astype(BF16)
+    gate_new = (dot(mate_in, rotate_quant_t(gate_t, rotation), 1, 1) * scale).astype(BF16)
+    up_new = (dot(mate_in, rotate_quant_t(up_t, rotation), 1, 1) * scale).astype(BF16)
+    down_new = (dot(rotate_quant_t(hidden_t, rotation), mate_grad, 1, 1) * scale).astype(BF16)
     return gate_new[None], up_new[None], down_new[None], input_grad.astype(BF16)
 
 

time: 162 us -> 163 us (level)
  blocking collectives: 42.3 us -> 0 us
  starting transfers between devices: 38.5 us -> 67.7 us
  waiting for transfers between devices: 33.2 us -> 59.7 us
  between operations: 15.1 us -> 3.77 us
  other arithmetic: 6.25 us -> 4.49 us
    all_to_all x2 -> x0, blocking collectives: 42.3 us -> none  [the longest x1 22.2 us: shards(): lax.all_to_all(slot_back.reshape(experts, capacity, width), 'expert', 0,...]
    all_to_all x0 -> x2, starting transfers between devices: none -> 38.1 us  [the longest x1 34.5 us: shards(): lax.all_to_all(slot_back.reshape(experts, capacity, width), 'expert', 0,...]
    all_to_all x0 -> x2, waiting for transfers between devices: none -> 22.5 us  [the longest x1 18.6 us: gather_y(): return lax.all_to_all(copies, 'y', 0, 0, tiled=True)]
    all_to_all x1, waiting for transfers between devices: 6.13 us -> 24.3 us  [shards(): blocks = lax.all_to_all(chip_sum, 'y', 0, 0, tiled=True)]
    ppermute x4 -> x2, waiting for transfers between devices: 15.2 us -> 0.88 us  [exchange(): lax.ppermute(x, axis, [(i, i ^ apart) for i in range(lax.axis_size(axis))])]
    ppermute x4 -> x2, starting transfers between devices: 17.7 us -> 8.93 us  [exchange(): lax.ppermute(x, axis, [(i, i ^ apart) for i in range(lax.axis_size(axis))])]
    dot_general x5, local copies, waits for them, and re-layouts: 4.6 us -> 0.68 us  [dot(): lax.dot_general(left, right, (((left_dim,), (right_dim,)), ((), ())), pre...]
    convert_element_type x3 -> x1, other arithmetic: 3.56 us -> 0.7 us  [shards(): (1 - 2 * lax.dynamic_index_in_dim(sign_bits, mate, 0, keepdims=False)).as...]
  transfers between devices with their start and end apart: 7 -> 6, of which waited for: 5 -> 5; matrix products, arithmetic and copies ran while one was open for 9% -> 10% of each run, Pallas kernels for 0% -> 0%
where the time goes in v4:
time: 163 us; the launch traced here: 162 us
  starting transfers between devices  67.7 us (42%)
  waiting for transfers between devices  59.7 us (37%)
  matrix products  15.2 us (9%)
  local copies, waits for them, and re-layouts  10.8 us (7%)
  other arithmetic  4.49 us (3%)
  between operations  3.77 us (2%)
    all_to_all x1, starting transfers between devices, shards(): lax.all_to_all(slot_back.reshape(experts, capacity, width), 'expert', 0,...  34.5 us
    all_to_all x1, waiting for transfers between devices, shards(): blocks = lax.all_to_all(chip_sum, 'y', 0, 0, tiled=True)  24.3 us
    all_to_all x1, waiting for transfers between devices, gather_y(): return lax.all_to_all(copies, 'y', 0, 0, tiled=True)  18.6 us
    all_to_all x1, starting transfers between devices, shards(): recv = lax.all_to_all(send, 'expert', 0, 0, tiled=True)  13.7 us
    all_to_all x1, waiting for transfers between devices, shards(): recv = lax.all_to_all(send, 'expert', 0, 0, tiled=True)  12.1 us
    dot_general x11, matrix products, dot(): lax.dot_general(left, right, (((left_dim,), (right_dim,)), ((), ())), pre...  9.31 us
    ppermute x2, starting transfers between devices, exchange(): lax.ppermute(x, axis, [(i, i ^ apart) for i in range(lax.axis_size(axis))])  8.93 us
    all_to_all x1, starting transfers between devices, shards(): blocks = lax.all_to_all(chip_sum, 'y', 0, 0, tiled=True)  6.95 us
  transfers between devices with their start and end apart: 6, of which 5 were waited for; matrix products, arithmetic and copies ran while one was open for 10% of the time, Pallas kernels for 0%

profile of v4, /device:TPU:1, one launch (start us, length us, event | category | flops | bytes accessed | tf_op | source)
XLA Modules:
  0.0 161.8 jit_solution(4633872728602302445)
XLA Ops:
  0.6 0.8 copy.74
  1.8 0.8 copy.77
  3.5 1.8 %fusion.4 = bf16[32,24,256]{2,1,0:T(8,128)(2,1)} fusion(f32[32,24]{1,0:T(8,128)S(1)} %concatenate.85, bf16[32,12,32]{2,1,0:T(8,128)(2,1)S(1)} %convert_convert_fusion, bf16[32,256]{1,0:T(8,128)(2,1)} %param.28, bf16[32,256]{1,0:T(8,128)(2,1)} %param.27), kind=kOutput, calls=%fused_computation.14 | convolution fusion | flops 26017792 | bytes 453632 | tf_op jit(solution)/shard_map/ect,td->ecd/dot_general | solution.py:115
  5.3 13.7 %all-to-all-start = ((bf16[32,24,256]{2,1,0:T(8,128)(2,1)}), bf16[32,24,256]{2,1,0:T(8,128)(2,1)S(1)}, u32[]{:S(2)}, u32[]{:S(2)}) async-start(bf16[32,24,256]{2,1,0:T(8,128)(2,1)} %fusion.4), calls=%async_computation | async-start | bytes 786432 | tf_op jit(solution)/shard_map/all_to_all | solution.py:117
  20.0 0.7 constant_dynamic-slice_fusion.1
  20.7 12.1 %all-to-all-done = bf16[32,24,256]{2,1,0:T(8,128)(2,1)S(1)} async-done(((bf16[32,24,256]{2,1,0:T(8,128)(2,1)}), bf16[32,24,256]{2,1,0:T(8,128)(2,1)S(1)}, u32[]{:S(2)}, u32[]{:S(2)}) %all-to-all-start) | async-done | bytes 393248 | tf_op jit(solution)/shard_map/all_to_all | solution.py:117
  33.9 1.0 pad_maximum_fusion
  34.9 4.4 %collective-permute-start.15 = (bf16[8,144,384]{2,1,0:T(8,128)(2,1)}, bf16[8,144,384]{2,1,0:T(8,128)(2,1)S(1)}, u32[]{:S(2)}, u32[]{:S(2)}) collective-permute-start(bf16[8,144,384]{2,1,0:T(8,128)(2,1)} %pad_maximum_fusion), channel_id=1, source_target_pairs={{0,32},{32,0},{1,33},{33,1},{2,34},{34,2},{3,35},{35,3},{4,36},{36... | collective-permute-start | bytes 2654216 | tf_op jit(solution)/shard_map/ppermute | solution.py:74
  40.6 0.9 collective-permute-done.15
  41.5 1.2 fusion
  42.7 6.9 %all-to-all-start.1 = ((bf16[8,144,384]{2,1,0:T(8,128)(2,1)}), bf16[8,144,384]{2,1,0:T(8,128)(2,1)S(1)}, u32[]{:S(2)}, u32[]{:S(2)}) async-start(bf16[8,144,384]{2,1,0:T(8,128)(2,1)} %fusion), calls=%async_computation.1 | async-start | bytes 1769472 | tf_op jit(solution)/shard_map/all_to_all | solution.py:133
  51.0 24.3 %all-to-all-done.1 = bf16[8,144,384]{2,1,0:T(8,128)(2,1)S(1)} async-done(((bf16[8,144,384]{2,1,0:T(8,128)(2,1)}), bf16[8,144,384]{2,1,0:T(8,128)(2,1)S(1)}, u32[]{:S(2)}, u32[]{:S(2)}) %all-to-all-start.1) | async-done | bytes 884768 | tf_op jit(solution)/shard_map/all_to_all | solution.py:133
  75.6 1.0 broadcast_in_dim.20
  76.6 3.5 %all-to-all-start.2 = ((bf16[8,144,384]{2,1,0:T(8,128)(2,1)}), bf16[8,144,384]{2,1,0:T(8,128)(2,1)S(1)}, u32[]{:S(2)}, u32[]{:S(2)}) async-start(bf16[8,144,384]{2,1,0:T(8,128)(2,1)} %broadcast_in_dim.20), calls=%async_computation.2 | async-start | bytes 1769472 | tf_op jit(solution)/shard_map/all_to_all | solution.py:90
  81.5 0.6 gather_fusion
  82.7 0.7 convert_bitcast_fusion
  83.4 0.7 broadcast_select_fusion.2
  84.2 0.7 conditional.5
  84.2 0.7 copy.123
  84.9 18.6 %all-to-all-done.2 = bf16[8,144,384]{2,1,0:T(8,128)(2,1)S(1)} async-done(((bf16[8,144,384]{2,1,0:T(8,128)(2,1)}), bf16[8,144,384]{2,1,0:T(8,128)(2,1)S(1)}, u32[]{:S(2)}, u32[]{:S(2)}) %all-to-all-start.2) | async-done | bytes 884768 | tf_op jit(solution)/shard_map/all_to_all | solution.py:90
  103.5 4.6 %collective-permute-start.16 = (bf16[8,144,384]{2,1,0:T(8,128)(2,1)S(1)}, bf16[8,144,384]{2,1,0:T(8,128)(2,1)S(1)}, u32[]{:S(2)}, u32[]{:S(2)}) collective-permute-start(bf16[8,144,384]{2,1,0:T(8,128)(2,1)S(1)} %all-to-all-done.2), channel_id=1, source_target_pairs={{0,32},{32,0},{1,33},{33,1},{2,34},{34,2},{3,35},{35,3},{4,36},{36... | collective-permute-start | bytes 2654216 | tf_op jit(solution)/shard_map/ppermute | solution.py:74
  108.1 1.1 fusion.171
  109.3 1.0 multiply_reduce_fusion.3
  110.3 1.0 multiply_reduce_fusion.4
  112.1 1.4 fusion.34
  113.9 0.7 reshape.187
  114.6 34.5 %all-to-all-start.3 = ((bf16[32,12,256]{2,1,0:T(8,128)(2,1)}), bf16[32,12,256]{2,1,0:T(8,128)(2,1)S(1)}, u32[]{:S(2)}, u32[]{:S(2)}) async-start(bf16[32,12,256]{2,1,0:T(8,128)(2,1)} %reshape.187), calls=%async_computation.3 | async-start | bytes 524288 | tf_op jit(solution)/shard_map/all_to_all | solution.py:159
  151.3 1.9 %fusion.8 = bf16[1,768,256]{2,1,0:T(8,128)(2,1)} fusion(f32[768,3,128]{0,2,1:T(8,128)S(1)} %get-tuple-element.89, f32[768,3]{0,1:T(4,128)S(1)} %get-tuple-element.73, f32[768,3]{0,1:T(4,128)S(1)} %get-tuple-element.72, f32[256,3,128]{0,2,1:T(8,128)S(1)} %copy-done.11, f32[256,3]{0,1:T(4,128)S(1)} %get-tuple-element.79, f32[256,3]{0,1:T(4,128)S(1)} %get-tuple-element.78), kind=kOutput, calls=%fused_computation.21 | convolution fusion | flops 158859264 | bytes 1990656 | tf_op jit(solution)/shard_map/dot_general | solution.py:23
  153.3 1.9 %fusion.9 = bf16[1,256,768]{2,1,0:T(8,128)(2,1)} fusion(f32[768,3,128]{0,2,1:T(8,128)S(1)} %get-tuple-element.87, f32[768,3]{0,1:T(4,128)S(1)} %get-tuple-element.75, f32[768,3]{0,1:T(4,128)S(1)} %get-tuple-element.74, f32[256,3,128]{0,2,1:T(8,128)S(1)} %copy-done.10, f32[256,3]{0,1:T(4,128)S(1)} %get-tuple-element.81, f32[256,3]{0,1:T(4,128)S(1)} %get-tuple-element.80), kind=kOutput, calls=%fused_computation.22 | convolution fusion | flops 158859264 | bytes 1990656 | tf_op jit(solution)/shard_map/dot_general | solution.py:23
  155.2 1.9 %fusion.10 = bf16[1,256,768]{2,1,0:T(8,128)(2,1)} fusion(f32[768,3,128]{0,2,1:T(8,128)S(1)} %get-tuple-element.83, f32[768,3]{0,1:T(4,128)S(1)} %get-tuple-element.77, f32[768,3]{0,1:T(4,128)S(1)} %get-tuple-element.76, f32[256,3,128]{0,2,1:T(8,128)S(1)} %copy-done.10, f32[256,3]{0,1:T(4,128)S(1)} %get-tuple-element.81, f32[256,3]{0,1:T(4,128)S(1)} %get-tuple-element.80), kind=kOutput, calls=%fused_computation.23 | convolution fusion | flops 158859264 | bytes 1990656 | tf_op jit(solution)/shard_map/dot_general | solution.py:23
  157.1 3.8 %all-to-all-done.3 = bf16[32,12,256]{2,1,0:T(8,128)(2,1)S(1)} async-done(((bf16[32,12,256]{2,1,0:T(8,128)(2,1)}), bf16[32,12,256]{2,1,0:T(8,128)(2,1)S(1)}, u32[]{:S(2)}, u32[]{:S(2)}) %all-to-all-start.3) | async-done | bytes 196640 | tf_op jit(solution)/shard_map/all_to_all | solution.py:159
  161.0 0.8 fusion.21
  (86 shorter events, 8.8 us)
Async XLA Ops:
  2.8 0.7 copy-start.5
  2.8 16.2 %copy-start = (bf16[1,256,768]{2,1,0:T(8,128)(2,1)S(1)}, bf16[1,256,768]{2,1,0:T(8,128)(2,1)}, u32[]{:S(2)}) copy-start(bf16[1,256,768]{2,1,0:T(8,128)(2,1)} %param.32) | copy-start | bytes 1179652
  2.8 16.2 %copy-start.1 = (bf16[1,256,768]{2,1,0:T(8,128)(2,1)S(1)}, bf16[1,256,768]{2,1,0:T(8,128)(2,1)}, u32[]{:S(2)}) copy-start(bf16[1,256,768]{2,1,0:T(8,128)(2,1)} %param.31) | copy-start | bytes 1179652
  5.3 27.6 %all-to-all-start = ((bf16[32,24,256]{2,1,0:T(8,128)(2,1)}), bf16[32,24,256]{2,1,0:T(8,128)(2,1)S(1)}, u32[]{:S(2)}, u32[]{:S(2)}) async-start(bf16[32,24,256]{2,1,0:T(8,128)(2,1)} %fusion.4), calls=%async_computation | async-start | bytes 786432 | tf_op jit(solution)/shard_map/all_to_all | solution.py:117
  19.0 1.0 copy-start.8
  34.9 6.6 %collective-permute-start.15 = (bf16[8,144,384]{2,1,0:T(8,128)(2,1)}, bf16[8,144,384]{2,1,0:T(8,128)(2,1)S(1)}, u32[]{:S(2)}, u32[]{:S(2)}) collective-permute-start(bf16[8,144,384]{2,1,0:T(8,128)(2,1)} %pad_maximum_fusion), channel_id=1, source_target_pairs={{0,32},{32,0},{1,33},{33,1},{2,34},{34,2},{3,35},{35,3},{4,36},{36... | collective-permute-start | bytes 2654216 | tf_op jit(solution)/shard_map/ppermute | solution.py:74
  39.4 0.9 copy-start.4
  42.7 7.0 %copy-start.9 = (s32[32]{0:T(128)S(1)}, s32[32]{0:T(128)}, u32[]{:S(2)}) copy-start(s32[32]{0:T(128)} %param.35) | copy-start | bytes 388
  42.7 32.6 %all-to-all-start.1 = ((bf16[8,144,384]{2,1,0:T(8,128)(2,1)}), bf16[8,144,384]{2,1,0:T(8,128)(2,1)S(1)}, u32[]{:S(2)}, u32[]{:S(2)}) async-start(bf16[8,144,384]{2,1,0:T(8,128)(2,1)} %fusion), calls=%async_computation.1 | async-start | bytes 1769472 | tf_op jit(solution)/shard_map/all_to_all | solution.py:133
  51.0 33.9 %copy-start.2 = (bf16[512,768]{1,0:T(8,128)(2,1)}, bf16[512,768]{1,0:T(8,128)(2,1)S(1)}, u32[]{:S(2)}) copy-start(bf16[512,768]{1,0:T(8,128)(2,1)S(1)} %get-tuple-element.94) | copy-start | bytes 2359300
  75.6 5.9 %copy-start.6 = (bf16[32,12,32]{2,1,0:T(8,128)(2,1)S(1)}, bf16[32,12,32]{2,1,0:T(8,128)(2,1)}, u32[]{:S(2)}) copy-start(bf16[32,12,32]{2,1,0:T(8,128)(2,1)} %copy-done.5) | copy-start | bytes 73732
  76.6 27.0 %all-to-all-start.2 = ((bf16[8,144,384]{2,1,0:T(8,128)(2,1)}), bf16[8,144,384]{2,1,0:T(8,128)(2,1)S(1)}, u32[]{:S(2)}, u32[]{:S(2)}) async-start(bf16[8,144,384]{2,1,0:T(8,128)(2,1)} %broadcast_in_dim.20), calls=%async_computation.2 | async-start | bytes 1769472 | tf_op jit(solution)/shard_map/all_to_all | solution.py:90
  103.5 7.8 %collective-permute-start.16 = (bf16[8,144,384]{2,1,0:T(8,128)(2,1)S(1)}, bf16[8,144,384]{2,1,0:T(8,128)(2,1)S(1)}, u32[]{:S(2)}, u32[]{:S(2)}) collective-permute-start(bf16[8,144,384]{2,1,0:T(8,128)(2,1)S(1)} %all-to-all-done.2), channel_id=1, source_target_pairs={{0,32},{32,0},{1,33},{33,1},{2,34},{34,2},{3,35},{35,3},{4,36},{36... | collective-permute-start | bytes 2654216 | tf_op jit(solution)/shard_map/ppermute | solution.py:74
  112.0 1.5 copy-start.3
  114.6 46.3 %all-to-all-start.3 = ((bf16[32,12,256]{2,1,0:T(8,128)(2,1)}), bf16[32,12,256]{2,1,0:T(8,128)(2,1)S(1)}, u32[]{:S(2)}, u32[]{:S(2)}) async-start(bf16[32,12,256]{2,1,0:T(8,128)(2,1)} %reshape.187), calls=%async_computation.3 | async-start | bytes 524288 | tf_op jit(solution)/shard_map/all_to_all | solution.py:159
  150.3 1.0 copy-start.11
  151.3 1.9 %copy-start.10 = (f32[256,3,128]{0,2,1:T(8,128)S(1)}, f32[256,3,128]{0,2,1:T(8,128)}, u32[]{:S(2)}) copy-start(f32[256,3,128]{0,2,1:T(8,128)} %get-tuple-element.85) | copy-start | bytes 1179652
  155.2 5.8 %copy-start.7 = (bf16[32,12,32]{2,1,0:T(8,128)(2,1)S(1)}, bf16[32,12,32]{2,1,0:T(8,128)(2,1)}, u32[]{:S(2)}) copy-start(bf16[32,12,32]{2,1,0:T(8,128)(2,1)} %broadcast_select_fusion.2) | copy-start | bytes 73732

commit v5 on v4

v5 whole, which is shorter than its diff:
```python
import functools

import jax
import jax.numpy as jnp
from jax import lax
from jax.experimental import pallas as pl
from jax.experimental.pallas import tpu as pltpu
from jax.sharding import Mesh
from jax.sharding import PartitionSpec as P

HBLOCK = 128
EPS = 1e-06
QSTEP = 2.0
SINE = (
    0.9999995827674866,
    -6.579691410064697,
    12.986429214477539,
    -12.18803596496582,
    6.557779312133789,
    -1.952649712562561,
)
BF16 = jnp.bfloat16
F32 = jnp.float32
BITS = ("b4", "b3", "b2", "b1", "b0")
VMEM_BYTES = 16 * 2**20


def dot(left, right, left_dim, right_dim):
    return lax.dot_general(
        left, right, (((left_dim,), (right_dim,)), ((), ())), preferred_element_type=F32
    )


def sylvester(block_len):
    positions = jnp.arange(block_len, dtype=jnp.int32)
    common_bits = positions[:, None] & positions[None, :]
    parity = jnp.zeros((block_len, block_len), jnp.int32)
    for bit_pos in range(block_len.bit_length() - 1):
        parity = parity ^ common_bits >> bit_pos & 1
    return (1 - 2 * parity).astype(BF16)


def pick_kernel(capacity, routes_ref, weights_ref, tok_ref, grad_ref, out_ref):
    choices, tok_count = routes_ref.shape
    block = 2 * capacity
    out_rows = out_ref.shape[0]
    experts = out_rows // block
    expert_ids = lax.broadcasted_iota(jnp.int32, (experts, tok_count), 0)
    member = jnp.zeros((experts, tok_count), F32)
    weight = jnp.zeros((experts, tok_count), F32)
    for k in range(choices):
        hit = routes_ref[k : k + 1, :] == expert_ids
        member = member + jnp.where(hit, 1.0, 0.0)
        weight = weight + jnp.where(hit, weights_ref[k : k + 1, :], 0.0)
    square = (tok_count, tok_count)
    earlier = lax.broadcasted_iota(jnp.int32, square, 0) < lax.broadcasted_iota(jnp.int32, square, 1)
    rank = dot(member.astype(BF16), jnp.where(earlier, 1.0, 0.0).astype(BF16), 1, 0)
    rank = jnp.where(member > 0.0, rank, -1.0).astype(BF16)
    weight_hi = weight.astype(BF16)
    weight_lo = (weight - weight_hi.astype(F32)).astype(BF16)

    row = lax.broadcasted_iota(jnp.int32, (out_rows, experts), 0)
    start = lax.broadcasted_iota(jnp.int32, (out_rows, experts), 1) * block
    owns = (row >= start) & (row < start + block)
    spread = jnp.where(owns, 1.0, 0.0).astype(BF16)
    place = jnp.sum(jnp.where(owns, row - start, 0).astype(F32), axis=1, keepdims=True)
    rank_of = dot(spread, rank, 1, 0)
    is_tok = place < capacity
    tok_pick = jnp.where(is_tok & (rank_of == place), 1.0, 0.0)
    grad_pick = jnp.where(jnp.logical_not(is_tok) & (rank_of == place - capacity), 1.0, 0.0)
    hi = (grad_pick * dot(spread, weight_hi, 1, 0)).astype(BF16)
    lo = (grad_pick * dot(spread, weight_lo, 1, 0)).astype(BF16)
    out = dot(tok_pick.astype(BF16), tok_ref[...], 1, 0)
    out = out + dot(hi, grad_ref[...], 1, 0) + dot(lo, grad_ref[...], 1, 0)
    out_ref[...] = out.astype(BF16)


def pick_rows(routes, weights, tokens, out_grad, experts, capacity):
    out_rows = 2 * capacity * experts
    out = pl.pallas_call(
        functools.partial(pick_kernel, capacity),
        out_shape=jax.ShapeDtypeStruct((out_rows, tokens.shape[1]), BF16),
        compiler_params=pltpu.CompilerParams(vmem_limit_bytes=VMEM_BYTES),
        name="pick_rows",
    )(routes.T, weights.T, tokens, out_grad)
    return out.reshape(experts, 2 * capacity, tokens.shape[1])


def partial_kernel(gate_up_ref, down_ref, in_ref, grad_ref, out_ref):
    cut = gate_up_ref.shape[0]
    out_ref[:cut, :] = dot(gate_up_ref[...], in_ref[...], 1, 1).astype(BF16)
    out_ref[cut:, :] = dot(down_ref[...], grad_ref[...], 1, 1).astype(BF16)


def partials_out(gate_up, down, rows_in, rows_grad):
    total = gate_up.shape[0] + down.shape[0]
    return pl.pallas_call(
        partial_kernel,
        out_shape=jax.ShapeDtypeStruct((total, rows_in.shape[0]), BF16),
        compiler_params=pltpu.CompilerParams(vmem_limit_bytes=VMEM_BYTES),
        name="partials_out",
    )(gate_up, down, rows_in, rows_grad)


def slot_picker(routes, expert_count, capacity):
    experts_iota = jnp.arange(expert_count, dtype=jnp.int32)
    member = jnp.sum((routes[:, :, None] == experts_iota[None, None, :]).astype(jnp.int32), axis=1)
    rank_table = jnp.cumsum(member, axis=0) - member
    cap_iota = jnp.arange(capacity, dtype=jnp.int32)
    placed = (rank_table[:, :, None] == cap_iota[None, None, :]) & (member[:, :, None] == 1)
    return jnp.transpose(placed.astype(BF16), (1, 2, 0))


def soft_steps(rotated, meansq):
    scale = jnp.sqrt(meansq + EPS)
    steps = QSTEP * rotated / scale
    near = steps - jnp.round(steps)
    square = near * near
    series = jnp.full_like(near, SINE[-1])
    for term in SINE[-2::-1]:
        series = series * square + term
    return ((steps - near * series) * (scale / QSTEP)).astype(BF16)


def rotate_quant_t(operand, rotation):
    cols, rows = operand.shape
    rotated = lax.dot_general(
        operand.reshape(cols, rows // HBLOCK, HBLOCK),
        rotation,
        (((2,), (0,)), ((), ())),
        preferred_element_type=F32,
    )
    meansq = jnp.mean(rotated * rotated, axis=2, keepdims=True)
    return soft_steps(rotated, meansq).reshape(cols, rows)


def pair_permute(x, axis):
    return lax.ppermute(x, axis, [(0, 1), (1, 0)])


def by_pair(which, alone, paired, *operands):
    branches = [alone] + [functools.partial(paired, axis) for axis in BITS[::-1]]
    return lax.switch(which, branches, *operands)


def swap(which, x):
    return by_pair(which, lambda v: v, lambda axis, v: pair_permute(v, axis), x)


def shards(
    tokens, out_grad, routes, route_weights, gate_weight, up_weight, down_weight, sign_bits, partner
):
    experts = lax.axis_size(BITS)
    n_y = lax.axis_size("y")
    core = lax.axis_index("core")
    me = lax.axis_index(BITS)
    mate = partner[me]
    apart = me ^ mate
    which = sum((apart == 1 << k).astype(jnp.int32) * (k + 1) for k in range(len(BITS)))
    tok_count, width = tokens.shape
    capacity = min(tok_count, tok_count * routes.shape[1] * 3 // (2 * experts))
    rows = experts * capacity
    ff = gate_weight.shape[2]
    half = ff // 2
    pieces = 2 * n_y
    unit = half // pieces

    send = pick_rows(routes, route_weights, tokens, out_grad, experts, capacity)
    recv = lax.all_to_all(send, BITS, 0, 0, tiled=True)

    gate_t = gate_weight[0].T.reshape(2, pieces, unit, width)
    up_t = up_weight[0].T.reshape(2, pieces, unit, width)
    gate_up = jnp.concatenate([gate_t, up_t], 2).reshape(2, ff, width)
    down = down_weight[0].reshape(2, half, width)
    gu_keep = lax.dynamic_index_in_dim(gate_up, core, 0, keepdims=False)
    gu_away = lax.dynamic_index_in_dim(gate_up, 1 - core, 0, keepdims=False)
    down_keep = lax.dynamic_index_in_dim(down, core, 0, keepdims=False)
    down_away = lax.dynamic_index_in_dim(down, 1 - core, 0, keepdims=False)
    mate_keep = swap(which, gu_keep)
    recv, mate_keep = lax.optimization_barrier((recv, mate_keep))
    rows_in = recv[:, :capacity].reshape(rows, width)
    rows_grad = recv[:, capacity:].reshape(rows, width)

    arrived = pair_permute(partials_out(gu_away, down_away, rows_in, rows_grad), "core")
    sum_gu = dot(gu_keep, rows_in, 1, 1) + arrived[:ff].astype(F32)
    sum_down = dot(down_keep, rows_grad, 1, 1) + arrived[ff:].astype(F32)
    chip_sum = jnp.concatenate(
        [sum_gu.reshape(pieces, 2 * unit, rows), sum_down.reshape(pieces, unit, rows)], 1
    ).astype(BF16)

    def spread_alone(x, w):
        merged = x.reshape(n_y, 2 * x.shape[1], rows)
        return lax.all_to_all(merged, "y", 0, 0, tiled=True).reshape(x.shape), w

    def spread_paired(axis, x, w):
        return lax.all_to_all(x, ("y", axis), 0, 0, tiled=True), pair_permute(w, axis)

    blocks, mate_away = by_pair(which, spread_alone, spread_paired, chip_sum, gu_away)
    sums = jnp.sum(blocks.reshape(n_y, 2, 3 * unit, rows).astype(F32), axis=0)
    gate_sum, up_sum, hid_grad = sums[:, :unit], sums[:, unit : 2 * unit], sums[:, 2 * unit :]
    sig = jax.nn.sigmoid(gate_sum)
    silu = gate_sum * sig
    hidden = silu * up_sum
    gate_rows = hid_grad * up_sum * sig * (1.0 + gate_sum * (1.0 - sig))
    up_rows = hid_grad * silu
    acts = jnp.concatenate([gate_rows, up_rows, hidden], 1).astype(BF16)

    def copies(x):
        return jnp.broadcast_to(x[None], (n_y,) + x.shape)

    def gather_alone(x, r):
        merged = copies(x).reshape(n_y, 2 * x.shape[1], rows)
        out = lax.all_to_all(merged, "y", 0, 0, tiled=True)
        return out.reshape(pieces, x.shape[1], rows), r

    def gather_paired(axis, x, r):
        out = copies(x[::-1]).reshape(pieces, x.shape[1], rows)
        return lax.all_to_all(out, ("y", axis), 0, 0, tiled=True), pair_permute(r, axis)

    mine, mate_recv = by_pair(which, gather_alone, gather_paired, acts, recv)

    theirs = pair_permute(mine, "core")

    def gate_up_rows(x):
        return x[:, : 2 * unit].reshape(ff, rows)

    slot_back = dot(gate_up_rows(mine), mate_keep, 0, 0) + dot(gate_up_rows(theirs), mate_away, 0, 0)
    returned = lax.all_to_all(
        slot_back.astype(BF16).reshape(experts, capacity, width), BITS, 0, 0, tiled=True
    )
    picker = jnp.take(slot_picker(routes, experts, capacity), partner, axis=0)
    input_grad = jnp.einsum("ect,ecd->td", picker, returned, preferred_element_type=F32)

    low = jnp.where(core == 0, mine, theirs)
    high = jnp.where(core == 0, theirs, mine)

    def whole(k):
        cut = slice(k * unit, (k + 1) * unit)
        return jnp.concatenate([low[:, cut].reshape(half, rows), high[:, cut].reshape(half, rows)], 0)

    flip_signs = (1 - 2 * lax.dynamic_index_in_dim(sign_bits, mate, 0, keepdims=False)).astype(BF16)
    rotation = sylvester(HBLOCK) * flip_signs[:, None]
    mate_in = rotate_quant_t(mate_recv[:, :capacity].reshape(rows, width).T, rotation)
    mate_grad = rotate_quant_t(mate_recv[:, capacity:].reshape(rows, width).T, rotation)
    scale = 1.0 / HBLOCK
    gate_new = (dot(mate_in, rotate_quant_t(whole(0), rotation), 1, 1) * scale).astype(BF16)
    up_new = (dot(mate_in, rotate_quant_t(whole(1), rotation), 1, 1) * scale).astype(BF16)
    down_new = (dot(rotate_quant_t(whole(2), rotation), mate_grad, 1, 1) * scale).astype(BF16)
    return gate_new[None], up_new[None], down_new[None], input_grad.astype(BF16)


def solution(mesh):
    n_dp = mesh.shape["dp"]
    split = Mesh(mesh.devices.reshape((n_dp // 2, 2) + (2,) * len(BITS)), ("y", "core") + BITS)
    dp = ("y", "core")
    return jax.shard_map(
        shards,
        mesh=split,
        in_specs=(
            P(BITS, dp),
            P(BITS, dp),
            P(BITS, None),
            P(BITS, None),
            P(BITS, dp, None),
            P(BITS, dp, None),
            P(BITS, None, dp),
            P(),
            P(),
        ),
        out_specs=(
            P(BITS, dp, None),
            P(BITS, dp, None),
            P(BITS, None, dp),
            P(BITS, dp),
        ),
        check_vma=False,
    )
```

time: 163 us -> 174 us (1.067)
  blocking collectives: 0 us -> 57 us
  waiting for transfers between devices: 59.7 us -> 9.48 us
  Pallas kernels: 0 us -> 2.08 us
    all_to_all x0 -> x2, blocking collectives: none -> 57 us  [the longest x1 31.2 us: spread_alone(): return (lax.all_to_all(merged, 'y', 0, 0, tiled=True).reshape(x.shape), w)]
    all_to_all x4 -> x2, waiting for transfers between devices: 58.9 us -> 9.46 us  [the longest x1 9.46 us: shards(): recv = lax.all_to_all(send, BITS, 0, 0, tiled=True)]
    all_to_all x4 -> x2, starting transfers between devices: 58.7 us -> 56 us  [the longest x1 42.3 us: shards(): lax.all_to_all(slot_back.astype(BF16).reshape(experts, capacity, width),...]
    slice x2 -> x4, local copies, waits for them, and re-layouts: 0.18 us -> 2.79 us  [the longest x1 1.52 us: shards(): sums[:, :unit]]
    dot_general x3 -> x1, matrix products: 2.95 us -> 0.81 us  [shards(): jnp.einsum('ect,ecd->td', picker, returned, preferred_element_type=F32)]
    pallas_call x0 -> x2, Pallas kernels: none -> 2.08 us  [the longest x1 1.61 us: pick_rows(): pl.pallas_call(functools.partial(pick_kernel, capacity), out_shape=jax.Sh...]
    dot_general x5, matrix products: 2.98 us -> 5 us  [rotate_quant_t(): lax.dot_general(operand.reshape(cols, rows // HBLOCK, HBLOCK), rotation,...]
    ppermute x2, starting transfers between devices: 8.93 us -> 10.9 us  [pair_permute(): return lax.ppermute(x, axis, [(0, 1), (1, 0)])]
  transfers between devices with their start and end apart: 6 -> 4, of which waited for: 5 -> 1; matrix products, arithmetic and copies ran while one was open for 10% -> 11% of each run, Pallas kernels for 0% -> 0%
where the time goes in v5:
time: 174 us; the launch traced here: 173 us
  starting transfers between devices  67 us (39%)
  blocking collectives  57 us (33%)
  matrix products  16 us (9%)
  local copies, waits for them, and re-layouts  12.2 us (7%)
  waiting for transfers between devices  9.48 us (5%)
  other arithmetic  5.33 us (3%)
  between operations  3.72 us (2%)
  Pallas kernels  2.08 us (1%)
    all_to_all x1, starting transfers between devices, shards(): lax.all_to_all(slot_back.astype(BF16).reshape(experts, capacity, width),...  42.3 us
    all_to_all x1, blocking collectives, spread_alone(): return (lax.all_to_all(merged, 'y', 0, 0, tiled=True).reshape(x.shape), w)  31.2 us
    all_to_all x1, blocking collectives, gather_alone(): out = lax.all_to_all(merged, 'y', 0, 0, tiled=True)  25.8 us
    all_to_all x1, starting transfers between devices, shards(): recv = lax.all_to_all(send, BITS, 0, 0, tiled=True)  13.7 us
    ppermute x2, starting transfers between devices, pair_permute(): return lax.ppermute(x, axis, [(0, 1), (1, 0)])  10.9 us
    dot_general x7, matrix products, dot(): lax.dot_general(left, right, (((left_dim,), (right_dim,)), ((), ())), pre...  10.2 us
    all_to_all x1, waiting for transfers between devices, shards(): recv = lax.all_to_all(send, BITS, 0, 0, tiled=True)  9.46 us
    dot_general x5, matrix products, rotate_quant_t(): lax.dot_general(operand.reshape(cols, rows // HBLOCK, HBLOCK), rotation,...  5 us
  transfers between devices with their start and end apart: 4, of which 1 were waited for; matrix products, arithmetic and copies ran while one was open for 11% of the time, Pallas kernels for 0%

profile of v5, /device:TPU:1, one launch (start us, length us, event | category | flops | bytes accessed | tf_op | source)
XLA Modules:
  0.0 172.9 jit_solution(61072235031063687)
XLA Ops:
  0.7 0.7 copy-done.1
  3.5 1.6 pick_rows.1
  5.1 13.7 %all-to-all-start.12 = ((bf16[32,24,256]{2,1,0:T(8,128)(2,1)}), bf16[32,24,256]{2,1,0:T(8,128)(2,1)S(1)}, u32[]{:S(2)}, u32[]{:S(2)}) async-start(bf16[32,24,256]{2,1,0:T(8,128)(2,1)} %bitcast.31), calls=%async_computation.12 | async-start | bytes 786432 | tf_op jit(solution)/shard_map/all_to_all | solution.py:169
  22.4 0.8 conditional.3
  22.4 0.7 copy.99
  23.2 9.5 %all-to-all-done.12 = bf16[32,24,256]{2,1,0:T(8,128)(2,1)S(1)} async-done(((bf16[32,24,256]{2,1,0:T(8,128)(2,1)}), bf16[32,24,256]{2,1,0:T(8,128)(2,1)S(1)}, u32[]{:S(2)}, u32[]{:S(2)}) %all-to-all-start.12) | async-done | bytes 393248 | tf_op jit(solution)/shard_map/all_to_all | solution.py:169
  33.3 5.6 %collective-permute-start.15 = (bf16[1152,384]{1,0:T(8,128)(2,1)S(1)}, bf16[1152,384]{1,0:T(8,128)(2,1)}, u32[]{:S(2)}, u32[]{:S(2)}) collective-permute-start(bf16[1152,384]{1,0:T(8,128)(2,1)S(1)} %partials_out.1), channel_id=1, source_target_pairs={{0,32},{32,0},{1,33},{33,1},{2,34},{34,2},{3,35},{35,3},{4,36},{36... | collective-permute-start | bytes 2654216 | tf_op jit(solution)/shard_map/ppermute | solution.py:138
  41.1 1.5 add_convert_fusion
  42.5 1.3 add_convert_fusion.1
  43.8 1.0 pad_maximum_fusion
  44.8 34.4 %conditional.4 = (bf16[768,256]{1,0:T(8,128)(2,1)S(1)}, f32[2,72,384]{2,1,0:T(8,128)}, f32[2,24,384]{2,1,0:T(8,128)}, f32[2,24,384]{2,1,0:T(8,128)S(1)}) conditional(s32[]{:T(128)} %clamp.2, (bf16[16,72,384]{2,1,0:T(8,128)(2,1)}, bf16[768,256]{1,0:T(8,128)(2,1)S(1)}) %tuple.134, (bf16[768,256]{1,0:T(8,128)(2,1)S(1)}, ...), branch_computations={%region_6.8_spmd, %region_8.10_spmd, %region_10.12_spmd, %region_1... | conditional | flops 829440 | bytes 6414440 | solution.py:143
  44.8 31.2 %all_to_all.58 = bf16[8,144,384]{2,1,0:T(8,128)(2,1)S(1)} all-to-all(bf16[8,144,384]{2,1,0:T(8,128)(2,1)} %bitcast), channel_id=1, replica_groups=mesh['y'=8,'core'=2,'b4'=2,'b3'=2,'b2'=2,'b1'=2,'b0'=2] {'y'}, dimensions={0} | all-to-all | bytes 1769472 | tf_op jit(solution)/shard_map/cond/branch_0_fun/all_to_all | solution.py:193
  76.0 0.8 convert_reduce_fusion
  76.8 1.5 slice.147
  78.3 0.9 copy.153
  79.2 1.0 multiply_convert_fusion.11
  80.2 27.1 %conditional.5 = (bf16[16,72,384]{2,1,0:T(8,128)(2,1)}, bf16[32,24,256]{2,1,0:T(8,128)(2,1)S(1)}, bf16[768,384]{1,0:T(8,128)(2,1)S(1)}) conditional(s32[]{:T(128)} %clamp.2, (bf16[2,72,384]{2,1,0:T(8,128)(2,1)S(1)}, bf16[32,24,256]{2,1,0:T(8,128)(2,1)S(1)}) %tuple.136, (bf16[2,72,384]{2,1,0:T(8,128)(2,1)S(1)}, ...), branch_computations={%region_18.19_spmd, %region_19.20_spmd, %region_20.21_spmd, %regio... | conditional | bytes 7409760 | solution.py:143
  80.3 25.8 %all_to_all.59 = bf16[8,144,384]{2,1,0:T(8,128)(2,1)} all-to-all(bf16[8,144,384]{2,1,0:T(8,128)(2,1)S(1)} %broadcast_in_dim.33), channel_id=1, replica_groups=mesh['y'=8,'core'=2,'b4'=2,'b3'=2,'b2'=2,'b1'=2,'b0'=2] {'y'}, dimensions={0} | all-to-all | bytes 1769472 | tf_op jit(solution)/shard_map/cond/branch_0_fun/all_to_all | solution.py:213
  106.1 1.1 slice.153
  107.3 5.4 %collective-permute-start.16 = (bf16[16,72,384]{2,1,0:T(8,128)(2,1)}, bf16[16,72,384]{2,1,0:T(8,128)(2,1)S(1)}, u32[]{:S(2)}, u32[]{:S(2)}) collective-permute-start(bf16[16,72,384]{2,1,0:T(8,128)(2,1)} %get-tuple-element.122), channel_id=1, source_target_pairs={{0,32},{32,0},{1,33},{33,1},{2,34},{34,2},{3,35},{35,3},{4,36},{36... | collective-permute-start | bytes 2654216 | tf_op jit(solution)/shard_map/ppermute | solution.py:138
  112.9 1.0 multiply_reduce_fusion.3
  113.8 1.0 multiply_reduce_fusion.4
  114.8 1.4 fusion.148
  116.6 0.8 reshape.250
  117.4 42.3 %all-to-all-start.13 = ((bf16[32,12,256]{2,1,0:T(8,128)(2,1)}), bf16[32,12,256]{2,1,0:T(8,128)(2,1)S(1)}, u32[]{:S(2)}, u32[]{:S(2)}) async-start(bf16[32,12,256]{2,1,0:T(8,128)(2,1)} %reshape.250), calls=%async_computation.13 | async-start | bytes 524288 | tf_op jit(solution)/shard_map/all_to_all | solution.py:228
  159.7 1.3 broadcast_select_fusion.1
  161.6 1.3 multiply_reduce_fusion
  163.2 1.4 multiply_reduce_fusion.1
  166.3 1.9 %fusion.6 = bf16[1,768,256]{2,1,0:T(8,128)(2,1)} fusion(f32[768,3,128]{0,2,1:T(8,128)S(1)} %copy-done.11, f32[768,3]{0,1:T(4,128)S(1)} %get-tuple-element.151, f32[768,3]{0,1:T(4,128)S(1)} %get-tuple-element.150, f32[256,3,128]{0,2,1:T(8,128)S(1)} %copy-done.10, f32[256,3]{0,1:T(4,128)S(1)} %get-tuple-element.157, f32[256,3]{0,1:T(4,128)S(1)} %get-tuple-element.156), kind=kOutput, calls=%fused_computation.19 | convolution fusion | flops 158859264 | bytes 1990656 | tf_op jit(solution)/shard_map/dot_general | solution.py:29
  168.2 2.0 %fusion.7 = bf16[1,256,768]{2,1,0:T(8,128)(2,1)} fusion(f32[768,3,128]{0,2,1:T(8,128)S(1)} %copy-done.12, f32[768,3]{0,1:T(4,128)S(1)} %get-tuple-element.153, f32[768,3]{0,1:T(4,128)S(1)} %get-tuple-element.152, f32[256,3,128]{0,2,1:T(8,128)S(1)} %copy-done.9, f32[256,3]{0,1:T(4,128)S(1)} %get-tuple-element.159, f32[256,3]{0,1:T(4,128)S(1)} %get-tuple-element.158), kind=kOutput, calls=%fused_computation.20 | convolution fusion | flops 158859264 | bytes 1990656 | tf_op jit(solution)/shard_map/dot_general | solution.py:29
  170.1 1.9 %fusion.8 = bf16[1,256,768]{2,1,0:T(8,128)(2,1)} fusion(f32[768,3,128]{0,2,1:T(8,128)S(1)} %get-tuple-element.161, f32[768,3]{0,1:T(4,128)S(1)} %get-tuple-element.155, f32[768,3]{0,1:T(4,128)S(1)} %get-tuple-element.154, f32[256,3,128]{0,2,1:T(8,128)S(1)} %copy-done.9, f32[256,3]{0,1:T(4,128)S(1)} %get-tuple-element.159, f32[256,3]{0,1:T(4,128)S(1)} %get-tuple-element.158), kind=kOutput, calls=%fused_computation.21 | convolution fusion | flops 158859264 | bytes 1990656 | tf_op jit(solution)/shard_map/dot_general | solution.py:29
  172.1 0.8 fusion.19
  (78 shorter events, 8.9 us)
Async XLA Ops:
  0.6 22.5 %copy-start = (bf16[1,768,256]{2,1,0:T(8,128)(2,1)S(1)}, bf16[1,768,256]{2,1,0:T(8,128)(2,1)}, u32[]{:S(2)}) copy-start(bf16[1,768,256]{2,1,0:T(8,128)(2,1)} %param.33) | copy-start | bytes 1179652
  0.6 18.2 %copy-start.8 = (s32[32]{0:T(128)S(1)}, s32[32]{0:T(128)}, u32[]{:S(2)}) copy-start(s32[32]{0:T(128)} %param.35) | copy-start | bytes 388
  0.7 0.7 copy-start.1
  1.4 0.7 copy-start.3
  2.1 0.7 copy-start.4
  2.8 0.7 copy-start.5
  3.5 16.6 %copy-start.2 = (s32[32,8]{0,1:T(8,128)S(1)}, s32[32,8]{0,1:T(8,128)}, u32[]{:S(2)}) copy-start(s32[32,8]{0,1:T(8,128)} %param.29) | copy-start | bytes 3076
  3.5 18.0 %copy-start.6 = (bf16[1,256,768]{2,1,0:T(8,128)(2,1)S(1)}, bf16[1,256,768]{2,1,0:T(8,128)(2,1)}, u32[]{:S(2)}) copy-start(bf16[1,256,768]{2,1,0:T(8,128)(2,1)} %param.31) | copy-start | bytes 1179652
  3.5 18.2 %copy-start.7 = (bf16[1,256,768]{2,1,0:T(8,128)(2,1)S(1)}, bf16[1,256,768]{2,1,0:T(8,128)(2,1)}, u32[]{:S(2)}) copy-start(bf16[1,256,768]{2,1,0:T(8,128)(2,1)} %param.32) | copy-start | bytes 1179652
  5.1 27.5 %all-to-all-start.12 = ((bf16[32,24,256]{2,1,0:T(8,128)(2,1)}), bf16[32,24,256]{2,1,0:T(8,128)(2,1)S(1)}, u32[]{:S(2)}, u32[]{:S(2)}) async-start(bf16[32,24,256]{2,1,0:T(8,128)(2,1)} %bitcast.31), calls=%async_computation.12 | async-start | bytes 786432 | tf_op jit(solution)/shard_map/all_to_all | solution.py:169
  33.3 7.7 %collective-permute-start.15 = (bf16[1152,384]{1,0:T(8,128)(2,1)S(1)}, bf16[1152,384]{1,0:T(8,128)(2,1)}, u32[]{:S(2)}, u32[]{:S(2)}) collective-permute-start(bf16[1152,384]{1,0:T(8,128)(2,1)S(1)} %partials_out.1), channel_id=1, source_target_pairs={{0,32},{32,0},{1,33},{33,1},{2,34},{34,2},{3,35},{35,3},{4,36},{36... | collective-permute-start | bytes 2654216 | tf_op jit(solution)/shard_map/ppermute | solution.py:138
  107.3 8.9 %collective-permute-start.16 = (bf16[16,72,384]{2,1,0:T(8,128)(2,1)}, bf16[16,72,384]{2,1,0:T(8,128)(2,1)S(1)}, u32[]{:S(2)}, u32[]{:S(2)}) collective-permute-start(bf16[16,72,384]{2,1,0:T(8,128)(2,1)} %get-tuple-element.122), channel_id=1, source_target_pairs={{0,32},{32,0},{1,33},{33,1},{2,34},{34,2},{3,35},{35,3},{4,36},{36... | collective-permute-start | bytes 2654216 | tf_op jit(solution)/shard_map/ppermute | solution.py:138
  117.4 54.7 %all-to-all-start.13 = ((bf16[32,12,256]{2,1,0:T(8,128)(2,1)}), bf16[32,12,256]{2,1,0:T(8,128)(2,1)S(1)}, u32[]{:S(2)}, u32[]{:S(2)}) async-start(bf16[32,12,256]{2,1,0:T(8,128)(2,1)} %reshape.250), calls=%async_computation.13 | async-start | bytes 524288 | tf_op jit(solution)/shard_map/all_to_all | solution.py:228
  164.9 1.0 copy-start.10
  164.9 1.4 copy-start.11
  166.3 1.9 %copy-start.9 = (f32[256,3,128]{0,2,1:T(8,128)S(1)}, f32[256,3,128]{0,2,1:T(8,128)}, u32[]{:S(2)}) copy-start(f32[256,3,128]{0,2,1:T(8,128)} %get-tuple-element.163) | copy-start | bytes 1179652
  166.3 1.9 %copy-start.12 = (f32[768,3,128]{0,2,1:T(8,128)S(1)}, f32[768,3,128]{0,2,1:T(8,128)}, u32[]{:S(2)}) copy-start(f32[768,3,128]{0,2,1:T(8,128)} %get-tuple-element.165) | copy-start | bytes 3538948

commit v6 on v5

v6 whole, which is shorter than its diff:
```python
import functools

import jax
import jax.numpy as jnp
from jax import lax
from jax.experimental import pallas as pl
from jax.experimental.pallas import tpu as pltpu
from jax.sharding import Mesh
from jax.sharding import PartitionSpec as P

HBLOCK = 128
EPS = 1e-06
QSTEP = 2.0
SINE = (
    0.9999995827674866,
    -6.579691410064697,
    12.986429214477539,
    -12.18803596496582,
    6.557779312133789,
    -1.952649712562561,
)
BF16 = jnp.bfloat16
F32 = jnp.float32
BITS = ("b4", "b3", "b2", "b1", "b0")
VMEM_BYTES = 16 * 2**20


def dot(left, right, left_dim, right_dim):
    return lax.dot_general(
        left, right, (((left_dim,), (right_dim,)), ((), ())), preferred_element_type=F32
    )


def sylvester(block_len):
    positions = jnp.arange(block_len, dtype=jnp.int32)
    common_bits = positions[:, None] & positions[None, :]
    parity = jnp.zeros((block_len, block_len), jnp.int32)
    for bit_pos in range(block_len.bit_length() - 1):
        parity = parity ^ common_bits >> bit_pos & 1
    return (1 - 2 * parity).astype(BF16)


def pick_kernel(
    capacity, routes_in, weights_in, tok_in, grad_in, out_ref, routes_ref, weights_ref, tok_ref, grad_ref, sems
):
    loads = [
        pltpu.make_async_copy(src, dst, sems.at[k])
        for k, (src, dst) in enumerate(
            ((routes_in, routes_ref), (weights_in, weights_ref), (tok_in, tok_ref), (grad_in, grad_ref))
        )
    ]
    for load in loads:
        load.start()
    choices, tok_count = routes_ref.shape
    block = 2 * capacity
    out_rows = out_ref.shape[0]
    experts = out_rows // block

    row = lax.broadcasted_iota(jnp.int32, (out_rows, experts), 0)
    start = lax.broadcasted_iota(jnp.int32, (out_rows, experts), 1) * block
    owns = (row >= start) & (row < start + block)
    spread = jnp.where(owns, 1.0, 0.0).astype(BF16)
    place = jnp.sum(jnp.where(owns, row - start, 0).astype(F32), axis=1, keepdims=True)
    is_tok = place < capacity
    tok_place = jnp.where(is_tok, place, -2.0)
    grad_place = jnp.where(is_tok, -2.0, place - capacity)
    square = (tok_count, tok_count)
    earlier = lax.broadcasted_iota(jnp.int32, square, 0) < lax.broadcasted_iota(jnp.int32, square, 1)
    earlier = jnp.where(earlier, 1.0, 0.0).astype(BF16)
    expert_ids = lax.broadcasted_iota(jnp.int32, (experts, tok_count), 0)

    for load in loads:
        load.wait()
    member = jnp.zeros((experts, tok_count), F32)
    weight = jnp.zeros((experts, tok_count), F32)
    for k in range(choices):
        hit = routes_ref[k : k + 1, :] == expert_ids
        member = member + jnp.where(hit, 1.0, 0.0)
        weight = weight + jnp.where(hit, weights_ref[k : k + 1, :], 0.0)
    rank = dot(member.astype(BF16), earlier, 1, 0)
    rank = jnp.where(member > 0.0, rank, -1.0).astype(BF16)
    weight_hi = weight.astype(BF16)
    weight_lo = (weight - weight_hi.astype(F32)).astype(BF16)
    rank_of = dot(spread, rank, 1, 0)
    tok_pick = jnp.where(rank_of == tok_place, 1.0, 0.0).astype(BF16)
    grad_here = rank_of == grad_place
    hi = jnp.where(grad_here, dot(spread, weight_hi, 1, 0), 0.0).astype(BF16)
    lo = jnp.where(grad_here, dot(spread, weight_lo, 1, 0), 0.0).astype(BF16)
    out = dot(tok_pick, tok_ref[...], 1, 0)
    out = out + dot(hi, grad_ref[...], 1, 0) + dot(lo, grad_ref[...], 1, 0)
    out_ref[...] = out.astype(BF16)


def call(kernel, name, out_shapes, operands, scalars=0, in_hbm=False, scratch=()):
    smem = pl.BlockSpec(memory_space=pltpu.SMEM)
    rest = pl.BlockSpec(memory_space=pltpu.HBM) if in_hbm else pl.BlockSpec(memory_space=pltpu.VMEM)
    outs = [jax.ShapeDtypeStruct(shape, BF16) for shape in out_shapes]
    flops = 2 * 384 * 768 * 768
    moved = sum(v.size * 2 for v in list(operands) + outs)
    return pl.pallas_call(
        kernel,
        out_shape=outs,
        in_specs=[smem] * scalars + [rest] * (len(operands) - scalars),
        out_specs=[pl.BlockSpec(memory_space=pltpu.VMEM)] * len(outs),
        scratch_shapes=list(scratch),
        compiler_params=pltpu.CompilerParams(vmem_limit_bytes=VMEM_BYTES),
        cost_estimate=pl.CostEstimate(flops=flops, bytes_accessed=moved, transcendentals=0),
        name=name,
    )(*operands)


def pick_rows(routes, weights, tokens, out_grad, experts, capacity):
    operands = (routes.T, weights.T, tokens, out_grad)
    out = call(
        functools.partial(pick_kernel, capacity),
        "pick_rows",
        [(2 * capacity * experts, tokens.shape[1])],
        operands,
        in_hbm=True,
        scratch=[pltpu.VMEM(v.shape, v.dtype) for v in operands] + [pltpu.SemaphoreType.DMA((4,))],
    )[0]
    return out.reshape(experts, 2 * capacity, tokens.shape[1])


def side(which, size):
    return pl.ds(pl.multiple_of(which * size, size), size)


def away_kernel(core_ref, gate_ref, up_ref, down_ref, in_ref, grad_ref, out_ref):
    units, rows = out_ref.shape[0], in_ref.shape[0]
    cut = side(1 - core_ref[0], units)
    out_ref[:, :rows] = dot(gate_ref[cut, :], in_ref[...], 1, 1).astype(BF16)
    out_ref[:, rows : 2 * rows] = dot(up_ref[cut, :], in_ref[...], 1, 1).astype(BF16)
    out_ref[:, 2 * rows :] = dot(down_ref[cut, :], grad_ref[...], 1, 1).astype(BF16)


def keep_kernel(core_ref, gate_ref, up_ref, down_ref, in_ref, grad_ref, add_ref, out_ref):
    units, rows = out_ref.shape[0], in_ref.shape[0]
    cut = side(core_ref[0], units)

    def put(k, part):
        lanes = slice(k * rows, (k + 1) * rows)
        out_ref[:, lanes] = (part + add_ref[:, lanes].astype(F32)).astype(BF16)

    put(0, dot(gate_ref[cut, :], in_ref[...], 1, 1))
    put(1, dot(up_ref[cut, :], in_ref[...], 1, 1))
    put(2, dot(down_ref[cut, :], grad_ref[...], 1, 1))


def act_kernel(n_y, cross_ref, blocks_ref, out_ref):
    both = blocks_ref.shape[0] // n_y
    rows = blocks_ref.shape[1] // 3
    total = blocks_ref[:both, :].astype(F32)
    for k in range(1, n_y):
        total = total + blocks_ref[k * both : (k + 1) * both, :].astype(F32)
    gate_sum, up_sum, hid_grad = total[:, :rows], total[:, rows : 2 * rows], total[:, 2 * rows :]
    sig = 1.0 / (1.0 + jnp.exp(-gate_sum))
    silu = gate_sum * sig
    gate_rows = hid_grad * up_sum * sig * (1.0 + gate_sum * (1.0 - sig))
    acts = jnp.concatenate([gate_rows, hid_grad * silu, silu * up_sum], 1)
    turned = jnp.concatenate([acts[both // 2 :], acts[: both // 2]], 0)
    acts = jnp.where(cross_ref[0] > 0, turned, acts).astype(BF16)
    for k in range(n_y):
        out_ref[k * both : (k + 1) * both, :] = acts


def back_kernel(capacity, core_ref, mine_ref, theirs_ref, gate_ref, up_ref, out_ref):
    units, rows = mine_ref.shape[0], mine_ref.shape[1] // 3
    core = core_ref[0]
    total = jnp.zeros((gate_ref.shape[0], rows), F32)
    for ref, which in ((mine_ref, core), (theirs_ref, 1 - core)):
        cut = side(which, units)
        total = total + dot(gate_ref[:, cut], ref[:, :rows], 1, 0)
        total = total + dot(up_ref[:, cut], ref[:, rows : 2 * rows], 1, 0)
    padded = out_ref.shape[0] * capacity // rows
    shape = (out_ref.shape[0], rows)
    groups = rows // capacity
    row = lax.broadcasted_iota(jnp.int32, (out_ref.shape[0], groups), 0)
    start = lax.broadcasted_iota(jnp.int32, (out_ref.shape[0], groups), 1) * padded
    inside = (row >= start) & (row < start + capacity)
    shift = lax.broadcasted_iota(jnp.int32, (out_ref.shape[0], groups), 1) * (padded - capacity)
    source = jnp.sum(jnp.where(inside, row - shift + 1, 0).astype(F32), axis=1, keepdims=True) - 1.0
    column = lax.broadcasted_iota(jnp.int32, shape, 1).astype(F32)
    place = jnp.where(column == source, 1.0, 0.0).astype(BF16)
    out_ref[...] = dot(place, total.astype(BF16), 1, 1).astype(BF16)


def soft_rotate(block, rotation):
    rotated = dot(block, rotation, 1, 0)
    meansq = jnp.sum(rotated * rotated, axis=1, keepdims=True) * (1.0 / HBLOCK) + EPS
    steps = rotated * (QSTEP * lax.rsqrt(meansq))
    near = steps - jnp.round(steps)
    square = near * near
    series = square * SINE[-1] + SINE[-2]
    for term in SINE[-3::-1]:
        series = series * square + term
    return ((steps - near * series) * (jnp.sqrt(meansq) / QSTEP)).astype(BF16)


def grads_kernel(
    core_ref, mine_ref, theirs_ref, rows_ref, rotation_ref, gate_ref, up_ref, down_ref, in_q, grad_q, gate_q, up_q, hid_q
):
    units, rows = mine_ref.shape[0], mine_ref.shape[1] // 3
    width = in_q.shape[0]
    rotation = rotation_ref[...]
    core = core_ref[0]
    scale = 1.0 / HBLOCK
    for b in range(rows // HBLOCK):
        cut = slice(b * HBLOCK, (b + 1) * HBLOCK)
        in_q[:, cut] = soft_rotate(rows_ref[:width, cut], rotation)
        grad_q[:, cut] = soft_rotate(rows_ref[width:, cut], rotation)
    for ref, which in ((mine_ref, core), (theirs_ref, 1 - core)):
        place = side(which, units)
        for k, dst in enumerate((gate_q, up_q, hid_q)):
            for b in range(rows // HBLOCK):
                cut = slice(b * HBLOCK, (b + 1) * HBLOCK)
                lanes = slice(k * rows + b * HBLOCK, k * rows + (b + 1) * HBLOCK)
                dst[:, cut] = soft_rotate(ref[:, lanes], rotation)
        gate_ref[:, place] = (dot(in_q[...], gate_q[...], 1, 1) * scale).astype(BF16)
        up_ref[:, place] = (dot(in_q[...], up_q[...], 1, 1) * scale).astype(BF16)
        down_ref[place, :] = (dot(hid_q[...], grad_q[...], 1, 1) * scale).astype(BF16)


def slot_picker(routes, expert_count, capacity):
    experts_iota = jnp.arange(expert_count, dtype=jnp.int32)
    member = jnp.sum((routes[:, :, None] == experts_iota[None, None, :]).astype(jnp.int32), axis=1)
    rank_table = jnp.cumsum(member, axis=0) - member
    cap_iota = jnp.arange(capacity, dtype=jnp.int32)
    placed = (rank_table[:, :, None] == cap_iota[None, None, :]) & (member[:, :, None] == 1)
    return jnp.transpose(placed.astype(BF16), (1, 2, 0))


def pair_permute(x, axis):
    return lax.ppermute(x, axis, [(0, 1), (1, 0)])


def by_pair(which, alone, paired, *operands):
    branches = [alone] + [functools.partial(paired, axis) for axis in BITS[::-1]]
    return lax.switch(which, branches, *operands)


def swap(which, x):
    return by_pair(which, lambda v: v, lambda axis, v: pair_permute(v, axis), x)


def shards(
    tokens, out_grad, routes, route_weights, gate_weight, up_weight, down_weight, sign_bits, partner
):
    experts = lax.axis_size(BITS)
    n_y = lax.axis_size("y")
    core = lax.axis_index("core")
    me = lax.axis_index(BITS)
    mate = partner[me]
    apart = me ^ mate
    which = sum((apart == 1 << k).astype(jnp.int32) * (k + 1) for k in range(len(BITS)))
    tok_count, width = tokens.shape
    capacity = min(tok_count, tok_count * routes.shape[1] * 3 // (2 * experts))
    rows = experts * capacity
    ff = gate_weight.shape[2]
    half = ff // 2
    core_arg = core.astype(jnp.int32)[None]
    cross_arg = (which > 0).astype(jnp.int32)[None]

    gate_w, up_w, down_w = gate_weight[0], up_weight[0], down_weight[0]
    send = pick_rows(routes, route_weights, tokens, out_grad, experts, capacity)
    recv = lax.all_to_all(send, BITS, 0, 0, tiled=True)
    mate_gate = swap(which, gate_w)
    recv, mate_gate = lax.optimization_barrier((recv, mate_gate))
    rows_in = recv[:, :capacity].reshape(rows, width)
    rows_grad = recv[:, capacity:].reshape(rows, width)

    feeds = (core_arg, gate_w.T, up_w.T, down_w, rows_in, rows_grad)
    wide = (half, 3 * rows)
    away = call(away_kernel, "away_partials", [wide], feeds, 1)[0]
    arrived = pair_permute(away, "core")
    chip_sum = call(keep_kernel, "keep_partials", [wide], feeds + (arrived,), 1)[0]

    def over_y(x):
        return lax.all_to_all(x.reshape(n_y, half // n_y, 3 * rows), "y", 0, 0, tiled=True).reshape(wide)

    def over_pair(axis, x):
        cut = x.reshape(2 * n_y, half // (2 * n_y), 3 * rows)
        return lax.all_to_all(cut, ("y", axis), 0, 0, tiled=True).reshape(wide)

    def with_swap(x, v):
        return by_pair(
            which,
            lambda x, v: (over_y(x), v),
            lambda axis, x, v: (over_pair(axis, x), pair_permute(v, axis)),
            x,
            v,
        )

    blocks, mate_up = with_swap(chip_sum, up_w)

    acts = call(functools.partial(act_kernel, n_y), "activation", [wide], (cross_arg, blocks), 1)[0]
    mine, mate_recv = with_swap(acts, recv)
    theirs = pair_permute(mine, "core")

    padded = -(-capacity // 16) * 16
    slot_back = call(
        functools.partial(back_kernel, capacity),
        "slot_back",
        [(experts * padded, width)],
        (core_arg, mine, theirs, mate_gate, mate_up),
        1,
    )[0]
    returned = lax.all_to_all(slot_back.reshape(experts, padded, width), BITS, 0, 0, tiled=True)
    picker = jnp.take(slot_picker(routes, experts, capacity), partner, axis=0)
    picker = jnp.pad(picker, ((0, 0), (0, padded - capacity), (0, 0))).reshape(experts * padded, tok_count)
    input_grad = dot(picker, returned.reshape(experts * padded, width), 0, 0).astype(BF16)

    flip_signs = (1 - 2 * lax.dynamic_index_in_dim(sign_bits, mate, 0, keepdims=False)).astype(BF16)
    rotation = sylvester(HBLOCK) * flip_signs[:, None]
    mate_rows = jnp.concatenate(
        [mate_recv[:, :capacity].reshape(rows, width).T, mate_recv[:, capacity:].reshape(rows, width).T], 0
    )
    gate_new, up_new, down_new = call(
        grads_kernel,
        "weight_grads",
        [(width, ff), (width, ff), (ff, width)],
        (core_arg, mine, theirs, mate_rows, rotation),
        1,
        scratch=[pltpu.VMEM((n, rows), BF16) for n in (width, width, half, half, half)],
    )
    return gate_new[None], up_new[None], down_new[None], input_grad


def solution(mesh):
    n_dp = mesh.shape["dp"]
    split = Mesh(mesh.devices.reshape((n_dp // 2, 2) + (2,) * len(BITS)), ("y", "core") + BITS)
    dp = ("y", "core")
    return jax.shard_map(
        shards,
        mesh=split,
        in_specs=(
            P(BITS, dp),
            P(BITS, dp),
            P(BITS, None),
            P(BITS, None),
            P(BITS, dp, None),
            P(BITS, dp, None),
            P(BITS, None, dp),
            P(),
            P(),
        ),
        out_specs=(
            P(BITS, dp, None),
            P(BITS, dp, None),
            P(BITS, None, dp),
            P(BITS, dp),
        ),
        check_vma=False,
    )
```

time: 174 us -> 177 us (1.017)
  blocking collectives: 57 us -> 0 us
  waiting for transfers between devices: 9.48 us -> 53.7 us
  starting transfers between devices: 67 us -> 91.2 us
  matrix products: 16 us -> 0.83 us
  Pallas kernels: 2.08 us -> 16.1 us
  other arithmetic: 5.33 us -> 1.09 us
  local copies, waits for them, and re-layouts: 12.2 us -> 8.62 us
    all_to_all x2 -> x0, blocking collectives: 57 us -> none  [the longest x1 31.2 us: spread_alone(): return (lax.all_to_all(merged, 'y', 0, 0, tiled=True).reshape(x.shape), w)]
    ppermute x2 -> x5, waiting for transfers between devices: 0.02 us -> 32.8 us  [pair_permute(): return lax.ppermute(x, axis, [(0, 1), (1, 0)])]
    all_to_all x1 -> x3, waiting for transfers between devices: 0.01 us -> 20.9 us  [the longest x2 17.8 us: over_pair(): return lax.all_to_all(cut, ('y', axis), 0, 0, tiled=True).reshape(wide)]
    all_to_all x1 -> x3, starting transfers between devices: 42.3 us -> 58.4 us  [the longest x1 45.4 us: shards(): lax.all_to_all(slot_back.reshape(experts, padded, width), BITS, 0, 0, til...]
    pallas_call x2 -> x6, Pallas kernels: 2.08 us -> 16.1 us  [call(): pl.pallas_call(kernel, out_shape=outs, in_specs=[smem] * scalars + [rest]...]
    all_to_all x1, waiting for transfers between devices: 9.46 us -> 0.01 us  [shards(): recv = lax.all_to_all(send, BITS, 0, 0, tiled=True)]
    dot_general x7 -> x1, matrix products: 10.2 us -> 0.83 us  [dot(): lax.dot_general(left, right, (((left_dim,), (right_dim,)), ((), ())), pre...]
    ppermute x2 -> x5, starting transfers between devices: 10.9 us -> 18.9 us  [pair_permute(): return lax.ppermute(x, axis, [(0, 1), (1, 0)])]
  transfers between devices with their start and end apart: 4 -> 9, of which waited for: 1 -> 7; matrix products, arithmetic and copies ran while one was open for 11% -> 2% of each run, Pallas kernels for 0% -> 4%
where the time goes in v6:
time: 177 us; the launch traced here: 175 us
  starting transfers between devices  91.2 us (52%)
  waiting for transfers between devices  53.7 us (30%)
  Pallas kernels  16.1 us (9%)
  local copies, waits for them, and re-layouts  8.62 us (5%)
  between operations  3.51 us (2%)
    all_to_all x1, starting transfers between devices, shards(): lax.all_to_all(slot_back.reshape(experts, padded, width), BITS, 0, 0, til...  45.4 us
    ppermute x5, waiting for transfers between devices, pair_permute(): return lax.ppermute(x, axis, [(0, 1), (1, 0)])  32.8 us
    ppermute x5, starting transfers between devices, pair_permute(): return lax.ppermute(x, axis, [(0, 1), (1, 0)])  18.9 us
    all_to_all x2, waiting for transfers between devices, over_pair(): return lax.all_to_all(cut, ('y', axis), 0, 0, tiled=True).reshape(wide)  17.8 us
    pallas_call x6, Pallas kernels, call(): pl.pallas_call(kernel, out_shape=outs, in_specs=[smem] * scalars + [rest]...  16.1 us
    all_to_all x1, starting transfers between devices, shards(): recv = lax.all_to_all(send, BITS, 0, 0, tiled=True)  13.9 us
    all_to_all x2, starting transfers between devices, over_pair(): return lax.all_to_all(cut, ('y', axis), 0, 0, tiled=True).reshape(wide)  13.1 us
    unnamed x25, local copies, waits for them, and re-layouts  6.24 us
  transfers between devices with their start and end apart: 9, of which 7 were waited for; matrix products, arithmetic and copies ran while one was open for 2% of the time, Pallas kernels for 4%

profile of v6, /device:TPU:1, one launch (start us, length us, event | category | flops | bytes accessed | tf_op | source)
XLA Modules:
  0.0 175.2 jit_solution(15891770156254908002)
XLA Ops:
  0.6 0.7 copy-done.1
  1.3 0.7 copy-done.3
  2.0 0.7 copy-done.4
  2.8 0.7 copy-done.5
  3.4 1.8 %pick_rows.1 = bf16[768,256]{1,0:T(8,128)(2,1)} custom-call(s32[8,32]{1,0:T(8,128)S(1)} %bitcast.63, f32[8,32]{1,0:T(8,128)S(1)} %bitcast.64, bf16[32,256]{1,0:T(8,128)(2,1)S(1)} %copy-done.3, bf16[32,256]{1,0:T(8,128)(2,1)S(1)} %copy-done.4), custom_call_target="tpu_custom_call" | custom-call | flops 452984832 | bytes 427008 | tf_op jit(solution)/shard_map/pick_rows/pallas_call | solution.py:100
  5.3 13.9 %all-to-all-start.12 = ((bf16[32,24,256]{2,1,0:T(8,128)(2,1)}), bf16[32,24,256]{2,1,0:T(8,128)(2,1)S(1)}, u32[]{:S(2)}, u32[]{:S(2)}) async-start(bf16[32,24,256]{2,1,0:T(8,128)(2,1)} %bitcast.34), calls=%async_computation.12 | async-start | bytes 786432 | tf_op jit(solution)/shard_map/all_to_all | solution.py:266
  21.3 0.8 copy-done.8
  22.3 14.2 %conditional.3 = (bf16[256,768]{1,0:T(8,128)(2,1)}) conditional(s32[]{:T(128)} %clamp.2, bf16[256,768]{1,0:T(8,128)(2,1)S(1)} %bitcast.73, bf16[256,768]{1,0:T(8,128)(2,1)S(1)} %bitcast.74, bf16[256,768]{1,0:T(8,128)(2,1)S(1)} %bitcast.75, bf16[256,768]{1,0:T(8,128)(2,1)S(1)} %bitcast.76, ...), branch_computations={%region_0.0_spmd, %region_1.0_spmd, %region_2.0_spmd, %region_3.0_... | conditional | bytes 1572912 | solution.py:239
  22.3 3.1 %collective-permute-start = (bf16[256,768]{1,0:T(8,128)(2,1)S(1)}, bf16[256,768]{1,0:T(8,128)(2,1)}, u32[]{:S(2)}, u32[]{:S(2)}) collective-permute-start(bf16[256,768]{1,0:T(8,128)(2,1)S(1)} %param.1), channel_id=1, source_target_pairs={{0,1},{1,0},{2,3},{3,2},{4,5},{5,4},{6,7},{7,6},{8,9},{9,8},{10,11... | collective-permute-start | bytes 1179656 | tf_op jit(solution)/shard_map/cond/branch_1_fun/ppermute | solution.py:234
  25.4 11.1 %collective-permute-done = bf16[256,768]{1,0:T(8,128)(2,1)} collective-permute-done((bf16[256,768]{1,0:T(8,128)(2,1)S(1)}, bf16[256,768]{1,0:T(8,128)(2,1)}, u32[]{:S(2)}, u32[]{:S(2)}) %collective-permute-start) | collective-permute-done | bytes 393248 | tf_op jit(solution)/shard_map/cond/branch_1_fun/ppermute | solution.py:234
  37.4 0.9 copy-done
  38.7 3.2 %collective-permute-start.15 = (bf16[384,1152]{1,0:T(8,128)(2,1)S(1)}, bf16[384,1152]{1,0:T(8,128)(2,1)S(1)}, u32[]{:S(2)}, u32[]{:S(2)}) collective-permute-start(bf16[384,1152]{1,0:T(8,128)(2,1)S(1)} %away_partials.1), channel_id=1, source_target_pairs={{0,32},{32,0},{1,33},{33,1},{2,34},{34,2},{3,35},{35,3},{4,36},{36... | collective-permute-start | bytes 2654216 | tf_op jit(solution)/shard_map/ppermute | solution.py:234
  44.4 0.7 convert_bitcast_fusion
  45.1 1.4 keep_partials.1
  46.5 30.9 %conditional.4 = (bf16[384,1152]{1,0:T(8,128)(2,1)}, bf16[256,768]{1,0:T(8,128)(2,1)}) conditional(s32[]{:T(128)} %clamp.2, (bf16[384,1152]{1,0:T(8,128)(2,1)}, bf16[256,768]{0,1:T(8,128)(2,1)S(1)}) %tuple.123, (bf16[384,1152]{1,0:T(8,128)(2,1)}, bf16[256,768]{0,1:T(8,128)(2,1)S(1)}) %tuple.124, ...), branch_computations={%region_6.0_spmd, %region_7.0_spmd, %region_8.0_spmd, %region_9.0_... | conditional | bytes 5013592 | solution.py:239
  46.5 7.8 %all-to-all-start.1 = ((bf16[16,24,1152]{2,1,0:T(8,128)(2,1)}), bf16[16,24,1152]{2,1,0:T(8,128)(2,1)}, u32[]{:S(2)}, u32[]{:S(2)}) async-start(bf16[16,24,1152]{2,1,0:T(8,128)(2,1)} %bitcast.2), calls=%async_computation.1 | async-start | bytes 1769472 | tf_op jit(solution)/shard_map/cond/branch_1_fun/all_to_all | solution.py:283
  54.5 3.2 %collective-permute-start.5 = (bf16[256,768]{1,0:T(8,128)(2,1)S(1)}, bf16[256,768]{1,0:T(8,128)(2,1)}, u32[]{:S(2)}, u32[]{:S(2)}) collective-permute-start(bf16[256,768]{1,0:T(8,128)(2,1)S(1)} %copy.84), channel_id=1, source_target_pairs={{0,1},{1,0},{2,3},{3,2},{4,5},{5,4},{6,7},{7,6},{8,9},{9,8},{10,11... | collective-permute-start | bytes 1179656 | tf_op jit(solution)/shard_map/cond/branch_1_fun/ppermute | solution.py:234
  57.7 10.0 %collective-permute-done.5 = bf16[256,768]{1,0:T(8,128)(2,1)} collective-permute-done((bf16[256,768]{1,0:T(8,128)(2,1)S(1)}, bf16[256,768]{1,0:T(8,128)(2,1)}, u32[]{:S(2)}, u32[]{:S(2)}) %collective-permute-start.5) | collective-permute-done | bytes 393248 | tf_op jit(solution)/shard_map/cond/branch_1_fun/ppermute | solution.py:234
  67.8 9.6 %all-to-all-done.1 = bf16[16,24,1152]{2,1,0:T(8,128)(2,1)} async-done(((bf16[16,24,1152]{2,1,0:T(8,128)(2,1)}), bf16[16,24,1152]{2,1,0:T(8,128)(2,1)}, u32[]{:S(2)}, u32[]{:S(2)}) %all-to-all-start.1) | async-done | bytes 884768 | tf_op jit(solution)/shard_map/cond/branch_1_fun/all_to_all | solution.py:283
  77.4 2.3 %activation.1 = bf16[384,1152]{1,0:T(8,128)(2,1)} custom-call(s32[1]{0:T(128)} %bitcast.26.cross_ref, bf16[384,1152]{1,0:T(8,128)(2,1)} %get-tuple-element.99.blocks_ref), custom_call_target="tpu_custom_call" | custom-call | flops 452984832 | bytes 1769474 | tf_op jit(solution)/shard_map/activation/pallas_call | solution.py:100
  79.7 26.4 %conditional.5 = (bf16[384,1152]{1,0:T(8,128)(2,1)}, bf16[32,24,256]{2,1,0:T(8,128)(2,1)S(1)}) conditional(s32[]{:T(128)} %clamp.2, (bf16[384,1152]{1,0:T(8,128)(2,1)}, bf16[32,24,256]{2,1,0:T(8,128)(2,1)S(1)}) %tuple.129, (bf16[384,1152]{1,0:T(8,128)(2,1)}, bf16[32,24,256]{2,1,0:T(8,128)(2,1)S(1)}) %tuple.130, ...), branch_computations={%region_12.0_spmd, %region_13.0_spmd, %region_14.0_spmd, %region_1... | conditional | bytes 5013592 | solution.py:239
  79.7 5.3 %all-to-all-start.7 = ((bf16[16,24,1152]{2,1,0:T(8,128)(2,1)}), bf16[16,24,1152]{2,1,0:T(8,128)(2,1)}, u32[]{:S(2)}, u32[]{:S(2)}) async-start(bf16[16,24,1152]{2,1,0:T(8,128)(2,1)} %bitcast.14), calls=%async_computation.7 | async-start | bytes 1769472 | tf_op jit(solution)/shard_map/cond/branch_1_fun/all_to_all | solution.py:283
  85.0 3.2 %collective-permute-start.10 = (bf16[32,24,256]{2,1,0:T(8,128)(2,1)S(1)}, bf16[32,24,256]{2,1,0:T(8,128)(2,1)S(1)}, u32[]{:S(2)}, u32[]{:S(2)}) collective-permute-start(bf16[32,24,256]{2,1,0:T(8,128)(2,1)S(1)} %get-tuple-element.76), channel_id=1, source_target_pairs={{0,1},{1,0},{2,3},{3,2},{4,5},{5,4},{6,7},{7,6},{8,9},{9,8},{10,11... | collective-permute-start | bytes 1179656 | tf_op jit(solution)/shard_map/cond/branch_1_fun/ppermute | solution.py:234
  88.2 9.6 %collective-permute-done.10 = bf16[32,24,256]{2,1,0:T(8,128)(2,1)S(1)} collective-permute-done((bf16[32,24,256]{2,1,0:T(8,128)(2,1)S(1)}, bf16[32,24,256]{2,1,0:T(8,128)(2,1)S(1)}, u32[]{:S(2)}, u32[]{:S(2)}) %collective-permute-start.10) | collective-permute-done | bytes 393248 | tf_op jit(solution)/shard_map/cond/branch_1_fun/ppermute | solution.py:234
  97.8 8.3 %all-to-all-done.7 = bf16[16,24,1152]{2,1,0:T(8,128)(2,1)} async-done(((bf16[16,24,1152]{2,1,0:T(8,128)(2,1)}), bf16[16,24,1152]{2,1,0:T(8,128)(2,1)}, u32[]{:S(2)}, u32[]{:S(2)}) %all-to-all-start.7) | async-done | bytes 884768 | tf_op jit(solution)/shard_map/cond/branch_1_fun/all_to_all | solution.py:283
  106.1 6.1 %collective-permute-start.16 = (bf16[384,1152]{1,0:T(8,128)(2,1)}, bf16[384,1152]{1,0:T(8,128)(2,1)S(1)}, u32[]{:S(2)}, u32[]{:S(2)}) collective-permute-start(bf16[384,1152]{1,0:T(8,128)(2,1)} %get-tuple-element.100.mine_ref), channel_id=1, source_target_pairs={{0,32},{32,0},{1,33},{33,1},{2,34},{34,2},{3,35},{35,3},{4,36},{36... | collective-permute-start | bytes 2654216 | tf_op jit(solution)/shard_map/ppermute | solution.py:234
  112.4 2.1 %collective-permute-done.16.theirs_ref = bf16[384,1152]{1,0:T(8,128)(2,1)S(1)} collective-permute-done((bf16[384,1152]{1,0:T(8,128)(2,1)}, bf16[384,1152]{1,0:T(8,128)(2,1)S(1)}, u32[]{:S(2)}, u32[]{:S(2)}) %collective-permute-start.16) | collective-permute-done | bytes 884768 | tf_op jit(solution)/shard_map/ppermute | solution.py:234
  114.5 3.1 %slot_back.1 = bf16[512,256]{1,0:T(8,128)(2,1)} custom-call(s32[1]{0:T(128)} %bitcast.24.core_ref, bf16[384,1152]{1,0:T(8,128)(2,1)} %get-tuple-element.100.mine_ref, bf16[384,1152]{1,0:T(8,128)(2,1)S(1)} %collective-permute-done.16.theirs_ref, bf16[256,768]{1,0:T(8,128)(2,1)} %get-tuple-element.183.gate_ref, bf16[256,768]{1,0:T(8,128)(2,1)} %get-tuple-element.106.up_ref), custom_call_target="tpu_custom_call" | custom-call | flops 452984832 | bytes 2818050 | tf_op jit(solution)/shard_map/slot_back/pallas_call | solution.py:100
  117.6 45.4 %all-to-all-start.13 = ((bf16[32,16,256]{2,1,0:T(8,128)(2,1)}), bf16[32,16,256]{2,1,0:T(8,128)(2,1)S(1)}, u32[]{:S(2)}, u32[]{:S(2)}) async-start(bf16[32,16,256]{2,1,0:T(8,128)(2,1)} %bitcast.51), calls=%async_computation.13 | async-start | bytes 524288 | tf_op jit(solution)/shard_map/all_to_all | solution.py:308
  164.3 6.9 %weight_grads.1 = (bf16[256,768]{1,0:T(8,128)(2,1)}, bf16[256,768]{1,0:T(8,128)(2,1)}, bf16[768,256]{1,0:T(8,128)(2,1)}) custom-call(s32[1]{0:T(128)} %bitcast.24.core_ref, bf16[384,1152]{1,0:T(8,128)(2,1)} %get-tuple-element.100.mine_ref, bf16[384,1152]{1,0:T(8,128)(2,1)S(1)} %collective-permute-done.16.theirs_ref, ...), custom_call_target="tpu_custom_call" | custom-call | flops 452984832 | bytes 3375106 | tf_op jit(solution)/shard_map/weight_grads/pallas_call | solution.py:100
  171.3 3.1 %all-to-all-done.13 = bf16[32,16,256]{2,1,0:T(8,128)(2,1)S(1)} async-done(((bf16[32,16,256]{2,1,0:T(8,128)(2,1)}), bf16[32,16,256]{2,1,0:T(8,128)(2,1)S(1)}, u32[]{:S(2)}, u32[]{:S(2)}) %all-to-all-start.13) | async-done | bytes 262176 | tf_op jit(solution)/shard_map/all_to_all | solution.py:308
  174.4 0.8 fusion
  (47 shorter events, 5.0 us)
Async XLA Ops:
  0.6 0.7 copy-start.1
  1.3 0.7 copy-start.3
  2.0 0.7 copy-start.4
  2.8 0.7 copy-start.5
  5.3 15.8 %copy-start.9 = (bf16[1,256,768]{2,1,0:T(8,128)(2,1)S(1)}, bf16[1,256,768]{2,1,0:T(8,128)(2,1)}, u32[]{:S(2)}) copy-start(bf16[1,256,768]{2,1,0:T(8,128)(2,1)} %param.32) | copy-start | bytes 1179652
  5.3 31.2 %all-to-all-start.12 = ((bf16[32,24,256]{2,1,0:T(8,128)(2,1)}), bf16[32,24,256]{2,1,0:T(8,128)(2,1)S(1)}, u32[]{:S(2)}, u32[]{:S(2)}) async-start(bf16[32,24,256]{2,1,0:T(8,128)(2,1)} %bitcast.34), calls=%async_computation.12 | async-start | bytes 786432 | tf_op jit(solution)/shard_map/all_to_all | solution.py:266
  19.2 0.7 copy-start.10
  21.1 1.0 copy-start.8
  22.3 14.2 %collective-permute-start = (bf16[256,768]{1,0:T(8,128)(2,1)S(1)}, bf16[256,768]{1,0:T(8,128)(2,1)}, u32[]{:S(2)}, u32[]{:S(2)}) collective-permute-start(bf16[256,768]{1,0:T(8,128)(2,1)S(1)} %param.1), channel_id=1, source_target_pairs={{0,1},{1,0},{2,3},{3,2},{4,5},{5,4},{6,7},{7,6},{8,9},{9,8},{10,11... | collective-permute-start | bytes 1179656 | tf_op jit(solution)/shard_map/cond/branch_1_fun/ppermute | solution.py:234
  36.5 0.7 copy-start.6
  37.3 1.0 copy-start
  38.3 3.7 %copy-start.2 = (s32[32,8]{0,1:T(8,128)S(1)}, s32[32,8]{0,1:T(8,128)}, u32[]{:S(2)}) copy-start(s32[32,8]{0,1:T(8,128)} %param.29) | copy-start | bytes 3076
  38.7 6.3 %collective-permute-start.15 = (bf16[384,1152]{1,0:T(8,128)(2,1)S(1)}, bf16[384,1152]{1,0:T(8,128)(2,1)S(1)}, u32[]{:S(2)}, u32[]{:S(2)}) collective-permute-start(bf16[384,1152]{1,0:T(8,128)(2,1)S(1)} %away_partials.1), channel_id=1, source_target_pairs={{0,32},{32,0},{1,33},{33,1},{2,34},{34,2},{3,35},{35,3},{4,36},{36... | collective-permute-start | bytes 2654216 | tf_op jit(solution)/shard_map/ppermute | solution.py:234
  46.5 30.9 %all-to-all-start.1 = ((bf16[16,24,1152]{2,1,0:T(8,128)(2,1)}), bf16[16,24,1152]{2,1,0:T(8,128)(2,1)}, u32[]{:S(2)}, u32[]{:S(2)}) async-start(bf16[16,24,1152]{2,1,0:T(8,128)(2,1)} %bitcast.2), calls=%async_computation.1 | async-start | bytes 1769472 | tf_op jit(solution)/shard_map/cond/branch_1_fun/all_to_all | solution.py:283
  54.5 13.3 %collective-permute-start.5 = (bf16[256,768]{1,0:T(8,128)(2,1)S(1)}, bf16[256,768]{1,0:T(8,128)(2,1)}, u32[]{:S(2)}, u32[]{:S(2)}) collective-permute-start(bf16[256,768]{1,0:T(8,128)(2,1)S(1)} %copy.84), channel_id=1, source_target_pairs={{0,1},{1,0},{2,3},{3,2},{4,5},{5,4},{6,7},{7,6},{8,9},{9,8},{10,11... | collective-permute-start | bytes 1179656 | tf_op jit(solution)/shard_map/cond/branch_1_fun/ppermute | solution.py:234
  77.4 2.4 %copy-start.7 = (bf16[32,24,256]{2,1,0:T(8,128)(2,1)S(1)}, bf16[32,24,256]{2,1,0:T(8,128)(2,1)}, u32[]{:S(2)}) copy-start(bf16[32,24,256]{2,1,0:T(8,128)(2,1)} %copy-done.6) | copy-start | bytes 1179652
  79.7 26.4 %all-to-all-start.7 = ((bf16[16,24,1152]{2,1,0:T(8,128)(2,1)}), bf16[16,24,1152]{2,1,0:T(8,128)(2,1)}, u32[]{:S(2)}, u32[]{:S(2)}) async-start(bf16[16,24,1152]{2,1,0:T(8,128)(2,1)} %bitcast.14), calls=%async_computation.7 | async-start | bytes 1769472 | tf_op jit(solution)/shard_map/cond/branch_1_fun/all_to_all | solution.py:283
  85.0 12.8 %collective-permute-start.10 = (bf16[32,24,256]{2,1,0:T(8,128)(2,1)S(1)}, bf16[32,24,256]{2,1,0:T(8,128)(2,1)S(1)}, u32[]{:S(2)}, u32[]{:S(2)}) collective-permute-start(bf16[32,24,256]{2,1,0:T(8,128)(2,1)S(1)} %get-tuple-element.76), channel_id=1, source_target_pairs={{0,1},{1,0},{2,3},{3,2},{4,5},{5,4},{6,7},{7,6},{8,9},{9,8},{10,11... | collective-permute-start | bytes 1179656 | tf_op jit(solution)/shard_map/cond/branch_1_fun/ppermute | solution.py:234
  106.1 8.4 %collective-permute-start.16 = (bf16[384,1152]{1,0:T(8,128)(2,1)}, bf16[384,1152]{1,0:T(8,128)(2,1)S(1)}, u32[]{:S(2)}, u32[]{:S(2)}) collective-permute-start(bf16[384,1152]{1,0:T(8,128)(2,1)} %get-tuple-element.100.mine_ref), channel_id=1, source_target_pairs={{0,32},{32,0},{1,33},{33,1},{2,34},{34,2},{3,35},{35,3},{4,36},{36... | collective-permute-start | bytes 2654216 | tf_op jit(solution)/shard_map/ppermute | solution.py:234
  117.6 56.8 %all-to-all-start.13 = ((bf16[32,16,256]{2,1,0:T(8,128)(2,1)}), bf16[32,16,256]{2,1,0:T(8,128)(2,1)S(1)}, u32[]{:S(2)}, u32[]{:S(2)}) async-start(bf16[32,16,256]{2,1,0:T(8,128)(2,1)} %bitcast.51), calls=%async_computation.13 | async-start | bytes 524288 | tf_op jit(solution)/shard_map/all_to_all | solution.py:308

commit v7 on v6

--- a/solution.py
+++ b/solution.py
@@ -23,6 +23,7 @@
 F32 = jnp.float32
 BITS = ("b4", "b3", "b2", "b1", "b0")
 VMEM_BYTES = 16 * 2**20
+ALL_VMEM = 60 * 2**20
 
 
 def dot(left, right, left_dim, right_dim):
@@ -91,10 +92,10 @@
     out_ref[...] = out.astype(BF16)
 
 
-def call(kernel, name, out_shapes, operands, scalars=0, in_hbm=False, scratch=()):
+def call(kernel, name, out_shapes, operands, scalars=0, in_hbm=False, scratch=(), dtype=BF16):
     smem = pl.BlockSpec(memory_space=pltpu.SMEM)
     rest = pl.BlockSpec(memory_space=pltpu.HBM) if in_hbm else pl.BlockSpec(memory_space=pltpu.VMEM)
-    outs = [jax.ShapeDtypeStruct(shape, BF16) for shape in out_shapes]
+    outs = [jax.ShapeDtypeStruct(shape, dtype) for shape in out_shapes]
     flops = 2 * 384 * 768 * 768
     moved = sum(v.size * 2 for v in list(operands) + outs)
     return pl.pallas_call(
@@ -103,7 +104,7 @@
         in_specs=[smem] * scalars + [rest] * (len(operands) - scalars),
         out_specs=[pl.BlockSpec(memory_space=pltpu.VMEM)] * len(outs),
         scratch_shapes=list(scratch),
-        compiler_params=pltpu.CompilerParams(vmem_limit_bytes=VMEM_BYTES),
+        compiler_params=pltpu.CompilerParams(vmem_limit_bytes=ALL_VMEM if in_hbm else VMEM_BYTES),
         cost_estimate=pl.CostEstimate(flops=flops, bytes_accessed=moved, transcendentals=0),
         name=name,
     )(*operands)
@@ -134,53 +135,39 @@
     out_ref[:, 2 * rows :] = dot(down_ref[cut, :], grad_ref[...], 1, 1).astype(BF16)
 
 
-def keep_kernel(core_ref, gate_ref, up_ref, down_ref, in_ref, grad_ref, add_ref, out_ref):
+def keep_kernel(core_ref, gate_ref, up_ref, down_ref, in_ref, grad_ref, out_ref):
     units, rows = out_ref.shape[0], in_ref.shape[0]
     cut = side(core_ref[0], units)
-
-    def put(k, part):
-        lanes = slice(k * rows, (k + 1) * rows)
-        out_ref[:, lanes] = (part + add_ref[:, lanes].astype(F32)).astype(BF16)
-
-    put(0, dot(gate_ref[cut, :], in_ref[...], 1, 1))
-    put(1, dot(up_ref[cut, :], in_ref[...], 1, 1))
-    put(2, dot(down_ref[cut, :], grad_ref[...], 1, 1))
-
-
-def act_kernel(n_y, cross_ref, blocks_ref, out_ref):
-    both = blocks_ref.shape[0] // n_y
-    rows = blocks_ref.shape[1] // 3
-    total = blocks_ref[:both, :].astype(F32)
-    for k in range(1, n_y):
-        total = total + blocks_ref[k * both : (k + 1) * both, :].astype(F32)
-    gate_sum, up_sum, hid_grad = total[:, :rows], total[:, rows : 2 * rows], total[:, 2 * rows :]
-    sig = 1.0 / (1.0 + jnp.exp(-gate_sum))
-    silu = gate_sum * sig
-    gate_rows = hid_grad * up_sum * sig * (1.0 + gate_sum * (1.0 - sig))
-    acts = jnp.concatenate([gate_rows, hid_grad * silu, silu * up_sum], 1)
-    turned = jnp.concatenate([acts[both // 2 :], acts[: both // 2]], 0)
-    acts = jnp.where(cross_ref[0] > 0, turned, acts).astype(BF16)
-    for k in range(n_y):
-        out_ref[k * both : (k + 1) * both, :] = acts
-
-
-def back_kernel(capacity, core_ref, mine_ref, theirs_ref, gate_ref, up_ref, out_ref):
-    units, rows = mine_ref.shape[0], mine_ref.shape[1] // 3
-    core = core_ref[0]
-    total = jnp.zeros((gate_ref.shape[0], rows), F32)
-    for ref, which in ((mine_ref, core), (theirs_ref, 1 - core)):
-        cut = side(which, units)
-        total = total + dot(gate_ref[:, cut], ref[:, :rows], 1, 0)
-        total = total + dot(up_ref[:, cut], ref[:, rows : 2 * rows], 1, 0)
-    padded = out_ref.shape[0] * capacity // rows
-    shape = (out_ref.shape[0], rows)
+    out_ref[:, :rows] = dot(gate_ref[cut, :], in_ref[...], 1, 1)
+    out_ref[:, rows : 2 * rows] = dot(up_ref[cut, :], in_ref[...], 1, 1)
+    out_ref[:, 2 * rows :] = dot(down_ref[cut, :], grad_ref[...], 1, 1)
+
+
+def half_back(units_ref, first_ref, rest_ref, cut, rows):
+    split = first_ref.shape[0]
+    gate, up = units_ref[:, :rows], units_ref[:, rows : 2 * rows]
+    upper = dot(first_ref[:, cut], gate, 1, 0)
+    lower = dot(rest_ref[: rest_ref.shape[0] - 2 * split, cut], gate, 1, 0)
+    return jnp.concatenate([upper, lower], 0) + dot(rest_ref[split:, cut], up, 1, 0)
+
+
+def mine_back_kernel(core_ref, mine_ref, first_ref, rest_ref, out_ref):
+    units, rows = mine_ref.shape[0], out_ref.shape[1]
+    out_ref[...] = half_back(mine_ref, first_ref, rest_ref, side(core_ref[0], units), rows)
+
+
+def back_kernel(capacity, core_ref, theirs_ref, first_ref, rest_ref, total_ref, out_ref):
+    units, rows = theirs_ref.shape[0], total_ref.shape[1]
+    out_rows = out_ref.shape[0]
+    total = total_ref[...] + half_back(theirs_ref, first_ref, rest_ref, side(1 - core_ref[0], units), rows)
     groups = rows // capacity
-    row = lax.broadcasted_iota(jnp.int32, (out_ref.shape[0], groups), 0)
-    start = lax.broadcasted_iota(jnp.int32, (out_ref.shape[0], groups), 1) * padded
-    inside = (row >= start) & (row < start + capacity)
-    shift = lax.broadcasted_iota(jnp.int32, (out_ref.shape[0], groups), 1) * (padded - capacity)
-    source = jnp.sum(jnp.where(inside, row - shift + 1, 0).astype(F32), axis=1, keepdims=True) - 1.0
-    column = lax.broadcasted_iota(jnp.int32, shape, 1).astype(F32)
+    padded = out_rows // groups
+    row = lax.broadcasted_iota(jnp.int32, (out_rows, groups), 0)
+    group = lax.broadcasted_iota(jnp.int32, (out_rows, groups), 1)
+    inside = (row >= group * padded) & (row < group * padded + capacity)
+    source = jnp.where(inside, row - group * (padded - capacity) + 1, 0).astype(F32)
+    source = jnp.sum(source, axis=1, keepdims=True) - 1.0
+    column = lax.broadcasted_iota(jnp.int32, (out_rows, rows), 1).astype(F32)
     place = jnp.where(column == source, 1.0, 0.0).astype(BF16)
     out_ref[...] = dot(place, total.astype(BF16), 1, 1).astype(BF16)
 
@@ -240,7 +227,10 @@
 
 
 def swap(which, x):
-    return by_pair(which, lambda v: v, lambda axis, v: pair_permute(v, axis), x)
+    def paired(axis, v):
+        return jax.tree.map(lambda leaf: pair_permute(leaf, axis), v)
+
+    return by_pair(which, lambda v: v, paired, x)
 
 
 def shards(
@@ -259,50 +249,57 @@
     ff = gate_weight.shape[2]
     half = ff // 2
     core_arg = core.astype(jnp.int32)[None]
-    cross_arg = (which > 0).astype(jnp.int32)[None]
 
     gate_w, up_w, down_w = gate_weight[0], up_weight[0], down_weight[0]
     send = pick_rows(routes, route_weights, tokens, out_grad, experts, capacity)
     recv = lax.all_to_all(send, BITS, 0, 0, tiled=True)
-    mate_gate = swap(which, gate_w)
-    recv, mate_gate = lax.optimization_barrier((recv, mate_gate))
+    gate_first = gate_w[: width // 2]
+    weight_rest = jnp.concatenate([gate_w[width // 2 :], up_w], 0)
+    gate_t, up_t = gate_w.T, up_w.T
+    recv, weight_rest, gate_t, up_t = lax.optimization_barrier((recv, weight_rest, gate_t, up_t))
     rows_in = recv[:, :capacity].reshape(rows, width)
     rows_grad = recv[:, capacity:].reshape(rows, width)
 
-    feeds = (core_arg, gate_w.T, up_w.T, down_w, rows_in, rows_grad)
+    feeds = (core_arg, gate_t, up_t, down_w, rows_in, rows_grad)
     wide = (half, 3 * rows)
     away = call(away_kernel, "away_partials", [wide], feeds, 1)[0]
     arrived = pair_permute(away, "core")
-    chip_sum = call(keep_kernel, "keep_partials", [wide], feeds + (arrived,), 1)[0]
-
-    def over_y(x):
-        return lax.all_to_all(x.reshape(n_y, half // n_y, 3 * rows), "y", 0, 0, tiled=True).reshape(wide)
-
-    def over_pair(axis, x):
-        cut = x.reshape(2 * n_y, half // (2 * n_y), 3 * rows)
-        return lax.all_to_all(cut, ("y", axis), 0, 0, tiled=True).reshape(wide)
-
-    def with_swap(x, v):
-        return by_pair(
-            which,
-            lambda x, v: (over_y(x), v),
-            lambda axis, x, v: (over_pair(axis, x), pair_permute(v, axis)),
-            x,
-            v,
-        )
-
-    blocks, mate_up = with_swap(chip_sum, up_w)
-
-    acts = call(functools.partial(act_kernel, n_y), "activation", [wide], (cross_arg, blocks), 1)[0]
-    mine, mate_recv = with_swap(acts, recv)
+    kept = call(keep_kernel, "keep_partials", [wide], feeds, 1, dtype=F32)[0]
+    chip_sum = (kept + arrived.astype(F32)).astype(BF16)
+
+    chip_sum, recv, gate_first = lax.optimization_barrier((chip_sum, recv, gate_first))
+
+    piece = (half // n_y, 3 * rows)
+    blocks = lax.all_to_all(chip_sum.reshape((n_y,) + piece), "y", 0, 0, tiled=True)
+    mate_recv, gate_first = swap(which, (recv, gate_first))
+    blocks, mate_recv, gate_first = lax.optimization_barrier((blocks, mate_recv, gate_first))
+    sums = jnp.sum(blocks.astype(F32), axis=0)
+    gate_sum, up_sum, hid_grad = sums[:, :rows], sums[:, rows : 2 * rows], sums[:, 2 * rows :]
+    sig = jax.nn.sigmoid(gate_sum)
+    silu = gate_sum * sig
+    gate_rows = hid_grad * up_sum * sig * (1.0 + gate_sum * (1.0 - sig))
+    acts = jnp.concatenate([gate_rows, hid_grad * silu, silu * up_sum], 1).astype(BF16)
+
+    acts, weight_rest = lax.optimization_barrier((swap(which, acts), weight_rest))
+    acts = jnp.broadcast_to(acts[None], (n_y,) + piece)
+    mine = lax.all_to_all(acts, "y", 0, 0, tiled=True).reshape(wide)
+    weight_rest = swap(which, weight_rest)
+    mate_rows = jnp.concatenate(
+        [mate_recv[:, :capacity].reshape(rows, width).T, mate_recv[:, capacity:].reshape(rows, width).T], 0
+    )
+    mine, weight_rest, mate_rows = lax.optimization_barrier((mine, weight_rest, mate_rows))
     theirs = pair_permute(mine, "core")
 
     padded = -(-capacity // 16) * 16
+    weights = (gate_first, weight_rest)
+    mine_back = call(
+        mine_back_kernel, "mine_back", [(width, rows)], (core_arg, mine) + weights, 1, dtype=F32
+    )[0]
     slot_back = call(
         functools.partial(back_kernel, capacity),
         "slot_back",
         [(experts * padded, width)],
-        (core_arg, mine, theirs, mate_gate, mate_up),
+        (core_arg, theirs) + weights + (mine_back,),
         1,
     )[0]
     returned = lax.all_to_all(slot_back.reshape(experts, padded, width), BITS, 0, 0, tiled=True)
@@ -312,9 +309,6 @@
 
     flip_signs = (1 - 2 * lax.dynamic_index_in_dim(sign_bits, mate, 0, keepdims=False)).astype(BF16)
     rotation = sylvester(HBLOCK) * flip_signs[:, None]
-    mate_rows = jnp.concatenate(
-        [mate_recv[:, :capacity].reshape(rows, width).T, mate_recv[:, capacity:].reshape(rows, width).T], 0
-    )
     gate_new, up_new, down_new = call(
         grads_kernel,
         "weight_grads",

time: 177 us -> 137 us (0.77)
  starting transfers between devices: 91.2 us -> 49.4 us
  waiting for transfers between devices: 53.7 us -> 63.2 us
  local copies, waits for them, and re-layouts: 8.62 us -> 3.95 us
  Pallas kernels: 16.1 us -> 13 us
    all_to_all x1, starting transfers between devices: 45.4 us -> 7.53 us  [shards(): lax.all_to_all(slot_back.reshape(experts, padded, width), BITS, 0, 0, til...]
    all_to_all x1, waiting for transfers between devices: 0.01 us -> 13.3 us  [shards(): recv = lax.all_to_all(send, BITS, 0, 0, tiled=True)]
    unnamed x25 -> x13, local copies, waits for them, and re-layouts: 6.24 us -> 0.44 us
    ppermute x5 -> x6, waiting for transfers between devices: 32.8 us -> 28.3 us  [pair_permute(): return lax.ppermute(x, axis, [(0, 1), (1, 0)])]
    pallas_call x6, Pallas kernels: 16.1 us -> 13 us  [call(): pl.pallas_call(kernel, out_shape=outs, in_specs=[smem] * scalars + [rest]...]
    all_to_all x2, starting transfers between devices: 13.1 us -> 10.5 us  [the longest x1 6.95 us: shards(): lax.all_to_all(chip_sum.reshape((n_y,) + piece), 'y', 0, 0, tiled=True)]
    ppermute x5 -> x6, starting transfers between devices: 18.9 us -> 17.6 us  [pair_permute(): return lax.ppermute(x, axis, [(0, 1), (1, 0)])]
  transfers between devices with their start and end apart: 9 -> 10, of which waited for: 7 -> 8; matrix products, arithmetic and copies ran while one was open for 2% -> 3% of each run, Pallas kernels for 4% -> 6%
where the time goes in v7:
time: 137 us
  waiting for transfers between devices  63.2 us (46%)
  starting transfers between devices  49.4 us (36%)
  Pallas kernels  13 us (9%)
  local copies, waits for them, and re-layouts  3.95 us (3%)
  between operations  3.59 us (3%)
  other arithmetic  2.44 us (2%)
    ppermute x6, waiting for transfers between devices, pair_permute(): return lax.ppermute(x, axis, [(0, 1), (1, 0)])  28.3 us
    ppermute x6, starting transfers between devices, pair_permute(): return lax.ppermute(x, axis, [(0, 1), (1, 0)])  17.6 us
    all_to_all x1, starting transfers between devices, shards(): recv = lax.all_to_all(send, BITS, 0, 0, tiled=True)  13.7 us
    all_to_all x1, waiting for transfers between devices, shards(): recv = lax.all_to_all(send, BITS, 0, 0, tiled=True)  13.3 us
    pallas_call x6, Pallas kernels, call(): pl.pallas_call(kernel, out_shape=outs, in_specs=[smem] * scalars + [rest]...  13 us
    all_to_all x1, waiting for transfers between devices, shards(): mine = lax.all_to_all(acts, 'y', 0, 0, tiled=True).reshape(wide)  8.98 us
    all_to_all x1, waiting for transfers between devices, shards(): lax.all_to_all(chip_sum.reshape((n_y,) + piece), 'y', 0, 0, tiled=True)  8.2 us
    all_to_all x1, starting transfers between devices, shards(): lax.all_to_all(slot_back.reshape(experts, padded, width), BITS, 0, 0, til...  7.53 us
  transfers between devices with their start and end apart: 10, of which 8 were waited for; matrix products, arithmetic and copies ran while one was open for 3% of the time, Pallas kernels for 6%

profile of v7, /device:TPU:1, one launch (start us, length us, event | category | flops | bytes accessed | tf_op | source)
XLA Modules:
  0.0 136.6 jit_solution(17650375884166657418)
XLA Ops:
  0.7 2.4 %pick_rows.1 = bf16[768,256]{1,0:T(8,128)(2,1)} custom-call(s32[8,32]{1,0:T(8,128)} %bitcast.47, f32[8,32]{1,0:T(8,128)} %bitcast.51, bf16[32,256]{1,0:T(8,128)(2,1)} %tok_in.1, bf16[32,256]{1,0:T(8,128)(2,1)} %grad_in.1), custom_call_target="tpu_custom_call" | custom-call | flops 452984832 | bytes 427008 | tf_op jit(solution)/shard_map/pick_rows/pallas_call | solution.py:101
  3.1 13.7 %all-to-all-start = ((bf16[32,24,256]{2,1,0:T(8,128)(2,1)}), bf16[32,24,256]{2,1,0:T(8,128)(2,1)S(1)}, u32[]{:S(2)}, u32[]{:S(2)}) async-start(bf16[32,24,256]{2,1,0:T(8,128)(2,1)} %bitcast.46), calls=%async_computation | async-start | bytes 786432 | tf_op jit(solution)/shard_map/all_to_all | solution.py:255
  17.3 13.3 %all-to-all-done = bf16[32,24,256]{2,1,0:T(8,128)(2,1)S(1)} async-done(((bf16[32,24,256]{2,1,0:T(8,128)(2,1)}), bf16[32,24,256]{2,1,0:T(8,128)(2,1)S(1)}, u32[]{:S(2)}, u32[]{:S(2)}) %all-to-all-start) | async-done | bytes 393248 | tf_op jit(solution)/shard_map/all_to_all | solution.py:255
  30.8 0.5 away_partials.1
  31.3 4.4 %collective-permute-start.20 = (bf16[384,1152]{1,0:T(8,128)(2,1)S(1)}, bf16[384,1152]{1,0:T(8,128)(2,1)S(1)}, u32[]{:S(2)}, u32[]{:S(2)}) collective-permute-start(bf16[384,1152]{1,0:T(8,128)(2,1)S(1)} %away_partials.1), channel_id=1, source_target_pairs={{0,32},{32,0},{1,33},{33,1},{2,34},{34,2},{3,35},{35,3},{4,36},{36... | collective-permute-start | bytes 2654216 | tf_op jit(solution)/shard_map/ppermute | solution.py:221
  36.2 1.5 %collective-permute-done.20 = bf16[384,1152]{1,0:T(8,128)(2,1)S(1)} collective-permute-done((bf16[384,1152]{1,0:T(8,128)(2,1)S(1)}, bf16[384,1152]{1,0:T(8,128)(2,1)S(1)}, u32[]{:S(2)}, u32[]{:S(2)}) %collective-permute-start.20) | collective-permute-done | bytes 884768 | tf_op jit(solution)/shard_map/ppermute | solution.py:221
  37.7 1.1 add_convert_fusion
  38.9 7.0 %all-to-all-start.1 = ((bf16[8,48,1152]{2,1,0:T(8,128)(2,1)}), bf16[8,48,1152]{2,1,0:T(8,128)(2,1)S(1)}, u32[]{:S(2)}, u32[]{:S(2)}) async-start(bf16[8,48,1152]{2,1,0:T(8,128)(2,1)} %bitcast.12), calls=%async_computation.1 | async-start | bytes 1769472 | tf_op jit(solution)/shard_map/all_to_all | solution.py:273
  45.8 0.6 dynamic_slice.7
  47.1 16.2 %conditional.3 = ((bf16[32,24,256]{2,1,0:T(8,128)(2,1)S(1)}, bf16[128,768]{1,0:T(8,128)(2,1)S(1)})) conditional(s32[]{:T(128)} %clamp.2, (bf16[32,24,256]{2,1,0:T(8,128)(2,1)S(1)}, bf16[128,768]{1,0:T(8,128)(2,1)S(1)}) %tuple.74, (bf16[32,24,256]{2,1,0:T(8,128)(2,1)S(1)}, bf16[128,768]{1,0:T(8,128)(2,1)S(1)}) %tuple.74, ...), branch_computations={%region_0.0_spmd, %region_1.0_spmd, %region_2.0_spmd, %region_3.0_... | conditional | bytes 3539048 | solution.py:226
  47.1 2.8 %collective-permute-start.4 = (bf16[32,24,256]{2,1,0:T(8,128)(2,1)S(1)}, bf16[32,24,256]{2,1,0:T(8,128)(2,1)S(1)}, u32[]{:S(2)}, u32[]{:S(2)}) collective-permute-start(bf16[32,24,256]{2,1,0:T(8,128)(2,1)S(1)} %get-tuple-element.54), channel_id=1, source_target_pairs={{0,4},{4,0},{1,5},{5,1},{2,6},{6,2},{3,7},{7,3},{8,12},{12,8},{9,1... | collective-permute-start | bytes 1179656 | tf_op jit(solution)/shard_map/cond/branch_3_fun/ppermute | solution.py:221
  49.9 2.5 %collective-permute-start.5 = (bf16[128,768]{1,0:T(8,128)(2,1)S(1)}, bf16[128,768]{1,0:T(8,128)(2,1)S(1)}, u32[]{:S(2)}, u32[]{:S(2)}) collective-permute-start(bf16[128,768]{1,0:T(8,128)(2,1)S(1)} %get-tuple-element.55), channel_id=1, source_target_pairs={{0,4},{4,0},{1,5},{5,1},{2,6},{6,2},{3,7},{7,3},{8,12},{12,8},{9,1... | collective-permute-start | bytes 589832 | tf_op jit(solution)/shard_map/cond/branch_3_fun/ppermute | solution.py:221
  52.4 10.8 %collective-permute-done.5 = bf16[128,768]{1,0:T(8,128)(2,1)S(1)} collective-permute-done((bf16[128,768]{1,0:T(8,128)(2,1)S(1)}, bf16[128,768]{1,0:T(8,128)(2,1)S(1)}, u32[]{:S(2)}, u32[]{:S(2)}) %collective-permute-start.5) | collective-permute-done | bytes 196640 | tf_op jit(solution)/shard_map/cond/branch_3_fun/ppermute | solution.py:221
  63.3 8.2 %all-to-all-done.1 = bf16[8,48,1152]{2,1,0:T(8,128)(2,1)S(1)} async-done(((bf16[8,48,1152]{2,1,0:T(8,128)(2,1)}), bf16[8,48,1152]{2,1,0:T(8,128)(2,1)S(1)}, u32[]{:S(2)}, u32[]{:S(2)}) %all-to-all-start.1) | async-done | bytes 884768 | tf_op jit(solution)/shard_map/all_to_all | solution.py:273
  71.7 6.1 %conditional.4 = (bf16[48,1152]{1,0:T(8,128)(2,1)S(1)}) conditional(s32[]{:T(128)} %clamp.2, bf16[48,1152]{1,0:T(8,128)(2,1)S(1)} %pad_maximum_fusion.2, bf16[48,1152]{1,0:T(8,128)(2,1)S(1)} %pad_maximum_fusion.2, bf16[48,1152]{1,0:T(8,128)(2,1)S(1)} %pad_maximum_fusion.2, ...), branch_computations={%region_7.0_spmd, %region_8.0_spmd, %region_9.0_spmd, %region_10.0... | conditional | bytes 663600 | solution.py:226
  71.7 2.8 %collective-permute-start.12 = (bf16[48,1152]{1,0:T(8,128)(2,1)S(1)}, bf16[48,1152]{1,0:T(8,128)(2,1)S(1)}, u32[]{:S(2)}, u32[]{:S(2)}) collective-permute-start(bf16[48,1152]{1,0:T(8,128)(2,1)S(1)} %param.9), channel_id=1, source_target_pairs={{0,4},{4,0},{1,5},{5,1},{2,6},{6,2},{3,7},{7,3},{8,12},{12,8},{9,1... | collective-permute-start | bytes 331784 | tf_op jit(solution)/shard_map/cond/branch_3_fun/ppermute | solution.py:221
  74.5 3.2 %collective-permute-done.12 = bf16[48,1152]{1,0:T(8,128)(2,1)S(1)} collective-permute-done((bf16[48,1152]{1,0:T(8,128)(2,1)S(1)}, bf16[48,1152]{1,0:T(8,128)(2,1)S(1)}, u32[]{:S(2)}, u32[]{:S(2)}) %collective-permute-start.12) | collective-permute-done | bytes 110624 | tf_op jit(solution)/shard_map/cond/branch_3_fun/ppermute | solution.py:221
  77.8 1.0 broadcast_in_dim.39
  78.8 3.5 %all-to-all-start.2 = ((bf16[8,48,1152]{2,1,0:T(8,128)(2,1)}), bf16[8,48,1152]{2,1,0:T(8,128)(2,1)S(1)}, u32[]{:S(2)}, u32[]{:S(2)}) async-start(bf16[8,48,1152]{2,1,0:T(8,128)(2,1)} %broadcast_in_dim.39), calls=%async_computation.2 | async-start | bytes 1769472 | tf_op jit(solution)/shard_map/all_to_all | solution.py:285
  83.1 15.8 %conditional.5 = (bf16[384,768]{1,0:T(8,128)(2,1)}) conditional(s32[]{:T(128)} %clamp.2, bf16[384,768]{0,1:T(8,128)(2,1)S(1)} %pad_maximum_fusion, bf16[384,768]{0,1:T(8,128)(2,1)S(1)} %pad_maximum_fusion, bf16[384,768]{0,1:T(8,128)(2,1)S(1)} %pad_maximum_fusion, bf16[384,768]{0,1:T(8,128)(2,1)S(1)} %pad_maximum_fusion, ...), branch_computations={%region_13.0_spmd, %region_14.0_spmd, %region_15.0_spmd, %region_1... | conditional | bytes 3538992 | solution.py:226
  83.4 2.8 %collective-permute-start.17 = (bf16[384,768]{1,0:T(8,128)(2,1)S(1)}, bf16[384,768]{1,0:T(8,128)(2,1)}, u32[]{:S(2)}, u32[]{:S(2)}) collective-permute-start(bf16[384,768]{1,0:T(8,128)(2,1)S(1)} %copy.66), channel_id=1, source_target_pairs={{0,4},{4,0},{1,5},{5,1},{2,6},{6,2},{3,7},{7,3},{8,12},{12,8},{9,1... | collective-permute-start | bytes 1769480 | tf_op jit(solution)/shard_map/cond/branch_3_fun/ppermute | solution.py:221
  86.2 12.7 %collective-permute-done.17 = bf16[384,768]{1,0:T(8,128)(2,1)} collective-permute-done((bf16[384,768]{1,0:T(8,128)(2,1)S(1)}, bf16[384,768]{1,0:T(8,128)(2,1)}, u32[]{:S(2)}, u32[]{:S(2)}) %collective-permute-start.17) | collective-permute-done | bytes 589856 | tf_op jit(solution)/shard_map/cond/branch_3_fun/ppermute | solution.py:221
  98.9 9.0 %all-to-all-done.2 = bf16[8,48,1152]{2,1,0:T(8,128)(2,1)S(1)} async-done(((bf16[8,48,1152]{2,1,0:T(8,128)(2,1)}), bf16[8,48,1152]{2,1,0:T(8,128)(2,1)S(1)}, u32[]{:S(2)}, u32[]{:S(2)}) %all-to-all-start.2) | async-done | bytes 884768 | tf_op jit(solution)/shard_map/all_to_all | solution.py:285
  107.9 2.4 %collective-permute-start.21 = (bf16[384,1152]{1,0:T(8,128)(2,1)S(1)}, bf16[384,1152]{1,0:T(8,128)(2,1)S(1)}, u32[]{:S(2)}, u32[]{:S(2)}) collective-permute-start(bf16[384,1152]{1,0:T(8,128)(2,1)S(1)} %bitcast.34), channel_id=1, source_target_pairs={{0,32},{32,0},{1,33},{33,1},{2,34},{34,2},{3,35},{35,3},{4,36},{36... | collective-permute-start | bytes 2654216 | tf_op jit(solution)/shard_map/ppermute | solution.py:221
  112.5 1.5 %mine_back.1.total_ref = f32[256,384]{1,0:T(8,128)S(1)} custom-call(s32[1]{0:T(128)} %bitcast.core_ref, bf16[384,1152]{1,0:T(8,128)(2,1)S(1)} %bitcast.35, bf16[128,768]{1,0:T(8,128)(2,1)S(1)} %get-tuple-element.102.first_ref, bf16[384,768]{1,0:T(8,128)(2,1)} %get-tuple-element.125.rest_ref), custom_call_target="tpu_custom_call" | custom-call | flops 452984832 | bytes 1867778 | tf_op jit(solution)/shard_map/mine_back/pallas_call | solution.py:101
  114.0 2.4 %slot_back.1 = bf16[512,256]{1,0:T(8,128)(2,1)} custom-call(s32[1]{0:T(128)} %bitcast.core_ref, bf16[384,1152]{1,0:T(8,128)(2,1)S(1)} %collective-permute-done.21.theirs_ref, bf16[128,768]{1,0:T(8,128)(2,1)S(1)} %get-tuple-element.102.first_ref, bf16[384,768]{1,0:T(8,128)(2,1)} %get-tuple-element.125.rest_ref, f32[256,384]{1,0:T(8,128)S(1)} %mine_back.1.total_ref), custom_call_target="tpu_custom_call" | custom-call | flops 452984832 | bytes 2129922 | tf_op jit(solution)/shard_map/slot_back/pallas_call | solution.py:101
  116.5 7.5 %all-to-all-start.3 = ((bf16[32,16,256]{2,1,0:T(8,128)(2,1)}), bf16[32,16,256]{2,1,0:T(8,128)(2,1)S(1)}, u32[]{:S(2)}, u32[]{:S(2)}) async-start(bf16[32,16,256]{2,1,0:T(8,128)(2,1)} %bitcast.22), calls=%async_computation.3 | async-start | bytes 524288 | tf_op jit(solution)/shard_map/all_to_all | solution.py:305
  124.0 0.7 convert_bitcast_fusion
  124.7 0.6 gather_fusion
  125.6 5.8 %weight_grads.1 = (bf16[256,768]{1,0:T(8,128)(2,1)}, bf16[256,768]{1,0:T(8,128)(2,1)}, bf16[768,256]{1,0:T(8,128)(2,1)}) custom-call(s32[1]{0:T(128)} %bitcast.core_ref, bf16[384,1152]{1,0:T(8,128)(2,1)S(1)} %bitcast.36, bf16[384,1152]{1,0:T(8,128)(2,1)S(1)} %collective-permute-done.21.theirs_ref, bf16[512,384]{1,0:T(8,128)(2,1)S(1)} %pad_maximum_fusion.1.rows_ref, ...), custom_call_target="tpu_custom_call" | custom-call | flops 452984832 | bytes 3375106 | tf_op jit(solution)/shard_map/weight_grads/pallas_call | solution.py:101
  131.3 4.5 %all-to-all-done.3 = bf16[32,16,256]{2,1,0:T(8,128)(2,1)S(1)} async-done(((bf16[32,16,256]{2,1,0:T(8,128)(2,1)}), bf16[32,16,256]{2,1,0:T(8,128)(2,1)S(1)}, u32[]{:S(2)}, u32[]{:S(2)}) %all-to-all-start.3) | async-done | bytes 262176 | tf_op jit(solution)/shard_map/all_to_all | solution.py:305
  135.8 0.8 fusion
  (47 shorter events, 2.9 us)
Async XLA Ops:
  0.6 16.2 %copy-start.1 = (bf16[1,256,768]{2,1,0:T(8,128)(2,1)S(1)}, bf16[1,256,768]{2,1,0:T(8,128)(2,1)}, u32[]{:S(2)}) copy-start(bf16[1,256,768]{2,1,0:T(8,128)(2,1)} %param.31) | copy-start | bytes 1179652
  0.6 16.4 %copy-start.2 = (bf16[1,256,768]{2,1,0:T(8,128)(2,1)S(1)}, bf16[1,256,768]{2,1,0:T(8,128)(2,1)}, u32[]{:S(2)}) copy-start(bf16[1,256,768]{2,1,0:T(8,128)(2,1)} %param.32) | copy-start | bytes 1179652
  3.1 27.5 %all-to-all-start = ((bf16[32,24,256]{2,1,0:T(8,128)(2,1)}), bf16[32,24,256]{2,1,0:T(8,128)(2,1)S(1)}, u32[]{:S(2)}, u32[]{:S(2)}) async-start(bf16[32,24,256]{2,1,0:T(8,128)(2,1)} %bitcast.46), calls=%async_computation | async-start | bytes 786432 | tf_op jit(solution)/shard_map/all_to_all | solution.py:255
  17.2 13.6 %copy-start = (bf16[1,768,256]{2,1,0:T(8,128)(2,1)S(1)}, bf16[1,768,256]{2,1,0:T(8,128)(2,1)}, u32[]{:S(2)}) copy-start(bf16[1,768,256]{2,1,0:T(8,128)(2,1)} %param.33) | copy-start | bytes 1179652
  31.3 6.4 %collective-permute-start.20 = (bf16[384,1152]{1,0:T(8,128)(2,1)S(1)}, bf16[384,1152]{1,0:T(8,128)(2,1)S(1)}, u32[]{:S(2)}, u32[]{:S(2)}) collective-permute-start(bf16[384,1152]{1,0:T(8,128)(2,1)S(1)} %away_partials.1), channel_id=1, source_target_pairs={{0,32},{32,0},{1,33},{33,1},{2,34},{34,2},{3,35},{35,3},{4,36},{36... | collective-permute-start | bytes 2654216 | tf_op jit(solution)/shard_map/ppermute | solution.py:221
  38.9 7.0 %copy-start.4 = (s32[32]{0:T(128)S(1)}, s32[32]{0:T(128)}, u32[]{:S(2)}) copy-start(s32[32]{0:T(128)} %param.35) | copy-start | bytes 388
  38.9 32.6 %all-to-all-start.1 = ((bf16[8,48,1152]{2,1,0:T(8,128)(2,1)}), bf16[8,48,1152]{2,1,0:T(8,128)(2,1)S(1)}, u32[]{:S(2)}, u32[]{:S(2)}) async-start(bf16[8,48,1152]{2,1,0:T(8,128)(2,1)} %bitcast.12), calls=%async_computation.1 | async-start | bytes 1769472 | tf_op jit(solution)/shard_map/all_to_all | solution.py:273
  47.1 16.1 %collective-permute-start.4 = (bf16[32,24,256]{2,1,0:T(8,128)(2,1)S(1)}, bf16[32,24,256]{2,1,0:T(8,128)(2,1)S(1)}, u32[]{:S(2)}, u32[]{:S(2)}) collective-permute-start(bf16[32,24,256]{2,1,0:T(8,128)(2,1)S(1)} %get-tuple-element.54), channel_id=1, source_target_pairs={{0,4},{4,0},{1,5},{5,1},{2,6},{6,2},{3,7},{7,3},{8,12},{12,8},{9,1... | collective-permute-start | bytes 1179656 | tf_op jit(solution)/shard_map/cond/branch_3_fun/ppermute | solution.py:221
  49.9 13.3 %collective-permute-start.5 = (bf16[128,768]{1,0:T(8,128)(2,1)S(1)}, bf16[128,768]{1,0:T(8,128)(2,1)S(1)}, u32[]{:S(2)}, u32[]{:S(2)}) collective-permute-start(bf16[128,768]{1,0:T(8,128)(2,1)S(1)} %get-tuple-element.55), channel_id=1, source_target_pairs={{0,4},{4,0},{1,5},{5,1},{2,6},{6,2},{3,7},{7,3},{8,12},{12,8},{9,1... | collective-permute-start | bytes 589832 | tf_op jit(solution)/shard_map/cond/branch_3_fun/ppermute | solution.py:221
  71.7 10.6 %copy-start.3 = (s32[32,8]{0,1:T(8,128)S(1)}, s32[32,8]{0,1:T(8,128)}, u32[]{:S(2)}) copy-start(s32[32,8]{0,1:T(8,128)} %param.29) | copy-start | bytes 3076
  71.7 6.0 %collective-permute-start.12 = (bf16[48,1152]{1,0:T(8,128)(2,1)S(1)}, bf16[48,1152]{1,0:T(8,128)(2,1)S(1)}, u32[]{:S(2)}, u32[]{:S(2)}) collective-permute-start(bf16[48,1152]{1,0:T(8,128)(2,1)S(1)} %param.9), channel_id=1, source_target_pairs={{0,4},{4,0},{1,5},{5,1},{2,6},{6,2},{3,7},{7,3},{8,12},{12,8},{9,1... | collective-permute-start | bytes 331784 | tf_op jit(solution)/shard_map/cond/branch_3_fun/ppermute | solution.py:221
  78.8 29.1 %all-to-all-start.2 = ((bf16[8,48,1152]{2,1,0:T(8,128)(2,1)}), bf16[8,48,1152]{2,1,0:T(8,128)(2,1)S(1)}, u32[]{:S(2)}, u32[]{:S(2)}) async-start(bf16[8,48,1152]{2,1,0:T(8,128)(2,1)} %broadcast_in_dim.39), calls=%async_computation.2 | async-start | bytes 1769472 | tf_op jit(solution)/shard_map/all_to_all | solution.py:285
  83.4 15.5 %collective-permute-start.17 = (bf16[384,768]{1,0:T(8,128)(2,1)S(1)}, bf16[384,768]{1,0:T(8,128)(2,1)}, u32[]{:S(2)}, u32[]{:S(2)}) collective-permute-start(bf16[384,768]{1,0:T(8,128)(2,1)S(1)} %copy.66), channel_id=1, source_target_pairs={{0,4},{4,0},{1,5},{5,1},{2,6},{6,2},{3,7},{7,3},{8,12},{12,8},{9,1... | collective-permute-start | bytes 1769480 | tf_op jit(solution)/shard_map/cond/branch_3_fun/ppermute | solution.py:221
  107.9 6.1 %collective-permute-start.21 = (bf16[384,1152]{1,0:T(8,128)(2,1)S(1)}, bf16[384,1152]{1,0:T(8,128)(2,1)S(1)}, u32[]{:S(2)}, u32[]{:S(2)}) collective-permute-start(bf16[384,1152]{1,0:T(8,128)(2,1)S(1)} %bitcast.34), channel_id=1, source_target_pairs={{0,32},{32,0},{1,33},{33,1},{2,34},{34,2},{3,35},{35,3},{4,36},{36... | collective-permute-start | bytes 2654216 | tf_op jit(solution)/shard_map/ppermute | solution.py:221
  116.5 19.4 %all-to-all-start.3 = ((bf16[32,16,256]{2,1,0:T(8,128)(2,1)}), bf16[32,16,256]{2,1,0:T(8,128)(2,1)S(1)}, u32[]{:S(2)}, u32[]{:S(2)}) async-start(bf16[32,16,256]{2,1,0:T(8,128)(2,1)} %bitcast.22), calls=%async_computation.3 | async-start | bytes 524288 | tf_op jit(solution)/shard_map/all_to_all | solution.py:305

commit v8 on v7

--- a/solution.py
+++ b/solution.py
@@ -143,23 +143,20 @@
     out_ref[:, 2 * rows :] = dot(down_ref[cut, :], grad_ref[...], 1, 1)
 
 
-def half_back(units_ref, first_ref, rest_ref, cut, rows):
-    split = first_ref.shape[0]
-    gate, up = units_ref[:, :rows], units_ref[:, rows : 2 * rows]
-    upper = dot(first_ref[:, cut], gate, 1, 0)
-    lower = dot(rest_ref[: rest_ref.shape[0] - 2 * split, cut], gate, 1, 0)
-    return jnp.concatenate([upper, lower], 0) + dot(rest_ref[split:, cut], up, 1, 0)
-
-
-def mine_back_kernel(core_ref, mine_ref, first_ref, rest_ref, out_ref):
+def half_back(units_ref, gate_ref, up_ref, cut, rows):
+    part = dot(gate_ref[:, cut], units_ref[:, :rows], 1, 0)
+    return part + dot(up_ref[:, cut], units_ref[:, rows:], 1, 0)
+
+
+def mine_back_kernel(core_ref, mine_ref, gate_ref, up_ref, out_ref):
     units, rows = mine_ref.shape[0], out_ref.shape[1]
-    out_ref[...] = half_back(mine_ref, first_ref, rest_ref, side(core_ref[0], units), rows)
-
-
-def back_kernel(capacity, core_ref, theirs_ref, first_ref, rest_ref, total_ref, out_ref):
+    out_ref[...] = half_back(mine_ref, gate_ref, up_ref, side(core_ref[0], units), rows)
+
+
+def back_kernel(capacity, core_ref, theirs_ref, gate_ref, up_ref, total_ref, out_ref):
     units, rows = theirs_ref.shape[0], total_ref.shape[1]
     out_rows = out_ref.shape[0]
-    total = total_ref[...] + half_back(theirs_ref, first_ref, rest_ref, side(1 - core_ref[0], units), rows)
+    total = total_ref[...] + half_back(theirs_ref, gate_ref, up_ref, side(1 - core_ref[0], units), rows)
     groups = rows // capacity
     padded = out_rows // groups
     row = lax.broadcasted_iota(jnp.int32, (out_rows, groups), 0)
@@ -184,28 +181,23 @@
     return ((steps - near * series) * (jnp.sqrt(meansq) / QSTEP)).astype(BF16)
 
 
-def grads_kernel(
-    core_ref, mine_ref, theirs_ref, rows_ref, rotation_ref, gate_ref, up_ref, down_ref, in_q, grad_q, gate_q, up_q, hid_q
-):
-    units, rows = mine_ref.shape[0], mine_ref.shape[1] // 3
-    width = in_q.shape[0]
+def quant_kernel(rows_ref, rotation_ref, out_ref):
     rotation = rotation_ref[...]
+    for b in range(rows_ref.shape[1] // HBLOCK):
+        cut = slice(b * HBLOCK, (b + 1) * HBLOCK)
+        out_ref[:, cut] = soft_rotate(rows_ref[:, cut], rotation)
+
+
+def grads_kernel(core_ref, mine_ref, theirs_ref, rows_ref, gate_ref, up_ref, down_ref):
+    units, rows = mine_ref.shape[0], rows_ref.shape[1]
+    width = gate_ref.shape[0]
     core = core_ref[0]
     scale = 1.0 / HBLOCK
-    for b in range(rows // HBLOCK):
-        cut = slice(b * HBLOCK, (b + 1) * HBLOCK)
-        in_q[:, cut] = soft_rotate(rows_ref[:width, cut], rotation)
-        grad_q[:, cut] = soft_rotate(rows_ref[width:, cut], rotation)
     for ref, which in ((mine_ref, core), (theirs_ref, 1 - core)):
         place = side(which, units)
-        for k, dst in enumerate((gate_q, up_q, hid_q)):
-            for b in range(rows // HBLOCK):
-                cut = slice(b * HBLOCK, (b + 1) * HBLOCK)
-                lanes = slice(k * rows + b * HBLOCK, k * rows + (b + 1) * HBLOCK)
-                dst[:, cut] = soft_rotate(ref[:, lanes], rotation)
-        gate_ref[:, place] = (dot(in_q[...], gate_q[...], 1, 1) * scale).astype(BF16)
-        up_ref[:, place] = (dot(in_q[...], up_q[...], 1, 1) * scale).astype(BF16)
-        down_ref[place, :] = (dot(hid_q[...], grad_q[...], 1, 1) * scale).astype(BF16)
+        gate_ref[:, place] = (dot(rows_ref[:width, :], ref[:, :rows], 1, 1) * scale).astype(BF16)
+        up_ref[:, place] = (dot(rows_ref[:width, :], ref[:, rows : 2 * rows], 1, 1) * scale).astype(BF16)
+        down_ref[place, :] = (dot(ref[:, 2 * rows :], rows_ref[width:, :], 1, 1) * scale).astype(BF16)
 
 
 def slot_picker(routes, expert_count, capacity):
@@ -253,10 +245,8 @@
     gate_w, up_w, down_w = gate_weight[0], up_weight[0], down_weight[0]
     send = pick_rows(routes, route_weights, tokens, out_grad, experts, capacity)
     recv = lax.all_to_all(send, BITS, 0, 0, tiled=True)
-    gate_first = gate_w[: width // 2]
-    weight_rest = jnp.concatenate([gate_w[width // 2 :], up_w], 0)
     gate_t, up_t = gate_w.T, up_w.T
-    recv, weight_rest, gate_t, up_t = lax.optimization_barrier((recv, weight_rest, gate_t, up_t))
+    recv, gate_t, up_t = lax.optimization_barrier((recv, gate_t, up_t))
     rows_in = recv[:, :capacity].reshape(rows, width)
     rows_grad = recv[:, capacity:].reshape(rows, width)
 
@@ -267,12 +257,17 @@
     kept = call(keep_kernel, "keep_partials", [wide], feeds, 1, dtype=F32)[0]
     chip_sum = (kept + arrived.astype(F32)).astype(BF16)
 
-    chip_sum, recv, gate_first = lax.optimization_barrier((chip_sum, recv, gate_first))
-
-    piece = (half // n_y, 3 * rows)
-    blocks = lax.all_to_all(chip_sum.reshape((n_y,) + piece), "y", 0, 0, tiled=True)
-    mate_recv, gate_first = swap(which, (recv, gate_first))
-    blocks, mate_recv, gate_first = lax.optimization_barrier((blocks, mate_recv, gate_first))
+    chip_sum, recv = lax.optimization_barrier((chip_sum, recv))
+
+    def copies(x):
+        return jnp.broadcast_to(x[None], (n_y,) + x.shape)
+
+    def over_y(x):
+        return lax.all_to_all(x, "y", 0, 0, tiled=True)
+
+    blocks = over_y(chip_sum.reshape(n_y, half // n_y, 3 * rows))
+    mate_recv = swap(which, recv)
+    blocks, mate_recv = lax.optimization_barrier((blocks, mate_recv))
     sums = jnp.sum(blocks.astype(F32), axis=0)
     gate_sum, up_sum, hid_grad = sums[:, :rows], sums[:, rows : 2 * rows], sums[:, 2 * rows :]
     sig = jax.nn.sigmoid(gate_sum)
@@ -280,42 +275,48 @@
     gate_rows = hid_grad * up_sum * sig * (1.0 + gate_sum * (1.0 - sig))
     acts = jnp.concatenate([gate_rows, hid_grad * silu, silu * up_sum], 1).astype(BF16)
 
-    acts, weight_rest = lax.optimization_barrier((swap(which, acts), weight_rest))
-    acts = jnp.broadcast_to(acts[None], (n_y,) + piece)
-    mine = lax.all_to_all(acts, "y", 0, 0, tiled=True).reshape(wide)
-    weight_rest = swap(which, weight_rest)
-    mate_rows = jnp.concatenate(
-        [mate_recv[:, :capacity].reshape(rows, width).T, mate_recv[:, capacity:].reshape(rows, width).T], 0
-    )
-    mine, weight_rest, mate_rows = lax.optimization_barrier((mine, weight_rest, mate_rows))
-    theirs = pair_permute(mine, "core")
-
+    own = over_y(copies(acts[:, : 2 * rows])).reshape(half, 2 * rows)
+
+    def rotation_of(expert):
+        bits = lax.dynamic_index_in_dim(sign_bits, expert, 0, keepdims=False)
+        return sylvester(HBLOCK) * (1 - 2 * bits).astype(BF16)[:, None]
+
+    def quantized(x, expert, name):
+        return call(quant_kernel, name, [x.shape], (x, rotation_of(expert)))[0]
+
+    mate_units = swap(which, quantized(acts, me, "quant_units"))
+    own, mate_units = lax.optimization_barrier((own, mate_units))
+
+    mine = over_y(copies(mate_units)).reshape(half, 3 * rows)
+    own_other = pair_permute(own, "core")
+    mine_back = call(
+        mine_back_kernel, "mine_back", [(width, rows)], (core_arg, own, gate_w, up_w), 1, dtype=F32
+    )[0]
     padded = -(-capacity // 16) * 16
-    weights = (gate_first, weight_rest)
-    mine_back = call(
-        mine_back_kernel, "mine_back", [(width, rows)], (core_arg, mine) + weights, 1, dtype=F32
-    )[0]
     slot_back = call(
         functools.partial(back_kernel, capacity),
         "slot_back",
         [(experts * padded, width)],
-        (core_arg, theirs) + weights + (mine_back,),
+        (core_arg, own_other, gate_w, up_w, mine_back),
         1,
     )[0]
+    mate_rows = jnp.concatenate(
+        [mate_recv[:, :capacity].reshape(rows, width).T, mate_recv[:, capacity:].reshape(rows, width).T], 0
+    )
+    mate_rows = quantized(mate_rows, mate, "quant_rows")
+    mine, slot_back, mate_rows = lax.optimization_barrier((mine, slot_back, mate_rows))
+
     returned = lax.all_to_all(slot_back.reshape(experts, padded, width), BITS, 0, 0, tiled=True)
-    picker = jnp.take(slot_picker(routes, experts, capacity), partner, axis=0)
-    picker = jnp.pad(picker, ((0, 0), (0, padded - capacity), (0, 0))).reshape(experts * padded, tok_count)
+    picker = jnp.pad(slot_picker(routes, experts, capacity), ((0, 0), (0, padded - capacity), (0, 0)))
+    picker = picker.reshape(experts * padded, tok_count)
     input_grad = dot(picker, returned.reshape(experts * padded, width), 0, 0).astype(BF16)
-
-    flip_signs = (1 - 2 * lax.dynamic_index_in_dim(sign_bits, mate, 0, keepdims=False)).astype(BF16)
-    rotation = sylvester(HBLOCK) * flip_signs[:, None]
+    theirs = pair_permute(mine, "core")
     gate_new, up_new, down_new = call(
         grads_kernel,
         "weight_grads",
         [(width, ff), (width, ff), (ff, width)],
-        (core_arg, mine, theirs, mate_rows, rotation),
+        (core_arg, mine, theirs, mate_rows),
         1,
-        scratch=[pltpu.VMEM((n, rows), BF16) for n in (width, width, half, half, half)],
     )
     return gate_new[None], up_new[None], down_new[None], input_grad
 

time: 137 us -> 148 us (1.080)
  waiting for transfers between devices: 63.2 us -> 79 us
  Pallas kernels: 13 us -> 8.4 us
  starting transfers between devices: 49.4 us -> 47.3 us
  local copies, waits for them, and re-layouts: 3.95 us -> 5.71 us
    all_to_all x2 -> x3, waiting for transfers between devices: 17.2 us -> 38 us  [over_y(): return lax.all_to_all(x, 'y', 0, 0, tiled=True)]
    ppermute x6 -> x5, waiting for transfers between devices: 28.3 us -> 15.3 us  [pair_permute(): return lax.ppermute(x, axis, [(0, 1), (1, 0)])]
    all_to_all x1, waiting for transfers between devices: 4.48 us -> 11.9 us  [shards(): lax.all_to_all(slot_back.reshape(experts, padded, width), BITS, 0, 0, til...]
    pallas_call x6 -> x8, Pallas kernels: 13 us -> 8.4 us  [call(): pl.pallas_call(kernel, out_shape=outs, in_specs=[smem] * scalars + [rest]...]
    all_to_all x1, starting transfers between devices: 7.53 us -> 3.98 us  [shards(): lax.all_to_all(slot_back.reshape(experts, padded, width), BITS, 0, 0, til...]
    all_to_all x2 -> x3, starting transfers between devices: 10.5 us -> 14 us  [over_y(): return lax.all_to_all(x, 'y', 0, 0, tiled=True)]
    ppermute x6 -> x5, starting transfers between devices: 17.6 us -> 15.5 us  [pair_permute(): return lax.ppermute(x, axis, [(0, 1), (1, 0)])]
  transfers between devices with their start and end apart: 10 -> 10, of which waited for: 8 -> 8; matrix products, arithmetic and copies ran while one was open for 3% -> 3% of each run, Pallas kernels for 6% -> 3%
where the time goes in v8:
time: 148 us; the launch traced here: 147 us
  waiting for transfers between devices  79 us (53%)
  starting transfers between devices  47.3 us (32%)
  Pallas kernels  8.4 us (6%)
  local copies, waits for them, and re-layouts  5.71 us (4%)
  between operations  3.53 us (2%)
  other arithmetic  2.51 us (2%)
    all_to_all x3, waiting for transfers between devices, over_y(): return lax.all_to_all(x, 'y', 0, 0, tiled=True)  38 us
    ppermute x5, starting transfers between devices, pair_permute(): return lax.ppermute(x, axis, [(0, 1), (1, 0)])  15.5 us
    ppermute x5, waiting for transfers between devices, pair_permute(): return lax.ppermute(x, axis, [(0, 1), (1, 0)])  15.3 us
    all_to_all x3, starting transfers between devices, over_y(): return lax.all_to_all(x, 'y', 0, 0, tiled=True)  14 us
    all_to_all x1, waiting for transfers between devices, shards(): recv = lax.all_to_all(send, BITS, 0, 0, tiled=True)  13.8 us
    all_to_all x1, starting transfers between devices, shards(): recv = lax.all_to_all(send, BITS, 0, 0, tiled=True)  13.7 us
    all_to_all x1, waiting for transfers between devices, shards(): lax.all_to_all(slot_back.reshape(experts, padded, width), BITS, 0, 0, til...  11.9 us
    pallas_call x8, Pallas kernels, call(): pl.pallas_call(kernel, out_shape=outs, in_specs=[smem] * scalars + [rest]...  8.4 us
  transfers between devices with their start and end apart: 10, of which 8 were waited for; matrix products, arithmetic and copies ran while one was open for 3% of the time, Pallas kernels for 3%

profile of v8, /device:TPU:1, one launch (start us, length us, event | category | flops | bytes accessed | tf_op | source)
XLA Modules:
  0.0 147.4 jit_solution(6683837213170643524)
XLA Ops:
  0.7 2.4 %pick_rows.1 = bf16[768,256]{1,0:T(8,128)(2,1)} custom-call(s32[8,32]{1,0:T(8,128)} %bitcast.48, f32[8,32]{1,0:T(8,128)} %bitcast.52, bf16[32,256]{1,0:T(8,128)(2,1)} %tok_in.1, bf16[32,256]{1,0:T(8,128)(2,1)} %grad_in.1), custom_call_target="tpu_custom_call" | custom-call | flops 452984832 | bytes 427008 | tf_op jit(solution)/shard_map/pick_rows/pallas_call | solution.py:101
  3.1 13.7 %all-to-all-start = ((bf16[32,24,256]{2,1,0:T(8,128)(2,1)}), bf16[32,24,256]{2,1,0:T(8,128)(2,1)S(1)}, u32[]{:S(2)}, u32[]{:S(2)}) async-start(bf16[32,24,256]{2,1,0:T(8,128)(2,1)} %bitcast.47), calls=%async_computation | async-start | bytes 786432 | tf_op jit(solution)/shard_map/all_to_all | solution.py:247
  16.8 13.8 %all-to-all-done = bf16[32,24,256]{2,1,0:T(8,128)(2,1)S(1)} async-done(((bf16[32,24,256]{2,1,0:T(8,128)(2,1)}), bf16[32,24,256]{2,1,0:T(8,128)(2,1)S(1)}, u32[]{:S(2)}, u32[]{:S(2)}) %all-to-all-start) | async-done | bytes 393248 | tf_op jit(solution)/shard_map/all_to_all | solution.py:247
  32.1 4.4 %collective-permute-start.10 = (bf16[384,1152]{1,0:T(8,128)(2,1)S(1)}, bf16[384,1152]{1,0:T(8,128)(2,1)S(1)}, u32[]{:S(2)}, u32[]{:S(2)}) collective-permute-start(bf16[384,1152]{1,0:T(8,128)(2,1)S(1)} %away_partials.1), channel_id=1, source_target_pairs={{0,32},{32,0},{1,33},{33,1},{2,34},{34,2},{3,35},{35,3},{4,36},{36... | collective-permute-start | bytes 2654216 | tf_op jit(solution)/shard_map/ppermute | solution.py:213
  37.0 1.6 %collective-permute-done.10 = bf16[384,1152]{1,0:T(8,128)(2,1)S(1)} collective-permute-done((bf16[384,1152]{1,0:T(8,128)(2,1)S(1)}, bf16[384,1152]{1,0:T(8,128)(2,1)S(1)}, u32[]{:S(2)}, u32[]{:S(2)}) %collective-permute-start.10) | collective-permute-done | bytes 884768 | tf_op jit(solution)/shard_map/ppermute | solution.py:213
  38.5 1.1 add_convert_fusion
  39.6 7.0 %all-to-all-start.1 = ((bf16[8,48,1152]{2,1,0:T(8,128)(2,1)}), bf16[8,48,1152]{2,1,0:T(8,128)(2,1)S(1)}, u32[]{:S(2)}, u32[]{:S(2)}) async-start(bf16[8,48,1152]{2,1,0:T(8,128)(2,1)} %bitcast.9), calls=%async_computation.1 | async-start | bytes 1769472 | tf_op jit(solution)/shard_map/all_to_all | solution.py:266
  46.6 0.6 dynamic_slice.10
  47.9 12.0 %conditional.2 = (bf16[32,24,256]{2,1,0:T(8,128)(2,1)S(1)}) conditional(s32[]{:T(128)} %clamp.4, bf16[32,24,256]{2,1,0:T(8,128)(2,1)S(1)} %all-to-all-done, bf16[32,24,256]{2,1,0:T(8,128)(2,1)S(1)} %all-to-all-done, bf16[32,24,256]{2,1,0:T(8,128)(2,1)S(1)} %all-to-all-done, ...), branch_computations={%region_0.0_spmd, %region_1.0_spmd, %region_2.0_spmd, %region_3.0_... | conditional | bytes 2359344 | solution.py:218
  47.9 2.1 %collective-permute-start = (bf16[32,24,256]{2,1,0:T(8,128)(2,1)S(1)}, bf16[32,24,256]{2,1,0:T(8,128)(2,1)S(1)}, u32[]{:S(2)}, u32[]{:S(2)}) collective-permute-start(bf16[32,24,256]{2,1,0:T(8,128)(2,1)S(1)} %param.1), channel_id=1, source_target_pairs={{0,1},{1,0},{2,3},{3,2},{4,5},{5,4},{6,7},{7,6},{8,9},{9,8},{10,11... | collective-permute-start | bytes 1179656 | tf_op jit(solution)/shard_map/cond/branch_1_fun/ppermute | solution.py:213
  50.0 9.8 %collective-permute-done = bf16[32,24,256]{2,1,0:T(8,128)(2,1)S(1)} collective-permute-done((bf16[32,24,256]{2,1,0:T(8,128)(2,1)S(1)}, bf16[32,24,256]{2,1,0:T(8,128)(2,1)S(1)}, u32[]{:S(2)}, u32[]{:S(2)}) %collective-permute-start) | collective-permute-done | bytes 393248 | tf_op jit(solution)/shard_map/cond/branch_1_fun/ppermute | solution.py:213
  59.8 12.4 %all-to-all-done.1 = bf16[8,48,1152]{2,1,0:T(8,128)(2,1)S(1)} async-done(((bf16[8,48,1152]{2,1,0:T(8,128)(2,1)}), bf16[8,48,1152]{2,1,0:T(8,128)(2,1)S(1)}, u32[]{:S(2)}, u32[]{:S(2)}) %all-to-all-start.1) | async-done | bytes 884768 | tf_op jit(solution)/shard_map/all_to_all | solution.py:266
  72.5 0.9 broadcast_in_dim.13
  73.4 3.5 %all-to-all-start.2 = ((bf16[8,48,768]{2,1,0:T(8,128)(2,1)}), bf16[8,48,768]{2,1,0:T(8,128)(2,1)S(1)}, u32[]{:S(2)}, u32[]{:S(2)}) async-start(bf16[8,48,768]{2,1,0:T(8,128)(2,1)} %broadcast_in_dim.13), calls=%async_computation.2 | async-start | bytes 1179648 | tf_op jit(solution)/shard_map/all_to_all | solution.py:266
  78.8 0.8 convert_bitcast_fusion
  80.2 6.1 %conditional.3 = (bf16[48,1152]{1,0:T(8,128)(2,1)S(1)}) conditional(s32[]{:T(128)} %clamp.4, bf16[48,1152]{1,0:T(8,128)(2,1)S(1)} %quant_units.1, bf16[48,1152]{1,0:T(8,128)(2,1)S(1)} %quant_units.1, bf16[48,1152]{1,0:T(8,128)(2,1)S(1)} %quant_units.1, bf16[48,1152]{1,0:T(8,128)(2,1)S(1)} %quant_units.1, ...), branch_computations={%region_7.8_spmd, %region_8.9_spmd, %region_9.10_spmd, %region_10.... | conditional | bytes 663600 | solution.py:218
  80.2 2.1 %collective-permute-start.5 = (bf16[48,1152]{1,0:T(8,128)(2,1)S(1)}, bf16[48,1152]{1,0:T(8,128)(2,1)S(1)}, u32[]{:S(2)}, u32[]{:S(2)}) collective-permute-start(bf16[48,1152]{1,0:T(8,128)(2,1)S(1)} %param.7), channel_id=1, source_target_pairs={{0,1},{1,0},{2,3},{3,2},{4,5},{5,4},{6,7},{7,6},{8,9},{9,8},{10,11... | collective-permute-start | bytes 331784 | tf_op jit(solution)/shard_map/cond/branch_1_fun/ppermute | solution.py:213
  82.3 3.9 %collective-permute-done.5 = bf16[48,1152]{1,0:T(8,128)(2,1)S(1)} collective-permute-done((bf16[48,1152]{1,0:T(8,128)(2,1)S(1)}, bf16[48,1152]{1,0:T(8,128)(2,1)S(1)}, u32[]{:S(2)}, u32[]{:S(2)}) %collective-permute-start.5) | collective-permute-done | bytes 110624 | tf_op jit(solution)/shard_map/cond/branch_1_fun/ppermute | solution.py:213
  86.3 9.9 %all-to-all-done.2 = bf16[8,48,768]{2,1,0:T(8,128)(2,1)S(1)} async-done(((bf16[8,48,768]{2,1,0:T(8,128)(2,1)}), bf16[8,48,768]{2,1,0:T(8,128)(2,1)S(1)}, u32[]{:S(2)}, u32[]{:S(2)}) %all-to-all-start.2) | async-done | bytes 589856 | tf_op jit(solution)/shard_map/all_to_all | solution.py:266
  96.2 1.0 broadcast_in_dim.14
  97.2 3.5 %all-to-all-start.3 = ((bf16[8,48,1152]{2,1,0:T(8,128)(2,1)}), bf16[8,48,1152]{2,1,0:T(8,128)(2,1)S(1)}, u32[]{:S(2)}, u32[]{:S(2)}) async-start(bf16[8,48,1152]{2,1,0:T(8,128)(2,1)} %broadcast_in_dim.14), calls=%async_computation.3 | async-start | bytes 1769472 | tf_op jit(solution)/shard_map/all_to_all | solution.py:266
  100.8 2.4 %collective-permute-start.11 = (bf16[384,768]{1,0:T(8,128)(2,1)S(1)}, bf16[384,768]{1,0:T(8,128)(2,1)S(1)}, u32[]{:S(2)}, u32[]{:S(2)}) collective-permute-start(bf16[384,768]{1,0:T(8,128)(2,1)S(1)} %bitcast.41), channel_id=1, source_target_pairs={{0,32},{32,0},{1,33},{33,1},{2,34},{34,2},{3,35},{35,3},{4,36},{36... | collective-permute-start | bytes 1769480 | tf_op jit(solution)/shard_map/ppermute | solution.py:213
  103.5 0.8 fusion.8
  104.3 1.0 reshape.84
  105.7 1.0 quant_rows.1.rows_ref
  107.1 1.4 slot_back.1
  108.5 15.7 %all-to-all-done.3 = bf16[8,48,1152]{2,1,0:T(8,128)(2,1)S(1)} async-done(((bf16[8,48,1152]{2,1,0:T(8,128)(2,1)}), bf16[8,48,1152]{2,1,0:T(8,128)(2,1)S(1)}, u32[]{:S(2)}, u32[]{:S(2)}) %all-to-all-start.3) | async-done | bytes 884768 | tf_op jit(solution)/shard_map/all_to_all | solution.py:266
  124.2 4.6 %collective-permute-start.12 = (bf16[384,1152]{1,0:T(8,128)(2,1)S(1)}, bf16[384,1152]{1,0:T(8,128)(2,1)S(1)}, u32[]{:S(2)}, u32[]{:S(2)}) collective-permute-start(bf16[384,1152]{1,0:T(8,128)(2,1)S(1)} %bitcast.33), channel_id=1, source_target_pairs={{0,32},{32,0},{1,33},{33,1},{2,34},{34,2},{3,35},{35,3},{4,36},{36... | collective-permute-start | bytes 2654216 | tf_op jit(solution)/shard_map/ppermute | solution.py:213
  128.8 4.0 %all-to-all-start.4 = ((bf16[32,16,256]{2,1,0:T(8,128)(2,1)}), bf16[32,16,256]{2,1,0:T(8,128)(2,1)S(1)}, u32[]{:S(2)}, u32[]{:S(2)}) async-start(bf16[32,16,256]{2,1,0:T(8,128)(2,1)} %bitcast.22), calls=%async_computation.4 | async-start | bytes 524288 | tf_op jit(solution)/shard_map/all_to_all | solution.py:309
  132.9 11.9 %all-to-all-done.4 = bf16[32,16,256]{2,1,0:T(8,128)(2,1)S(1)} async-done(((bf16[32,16,256]{2,1,0:T(8,128)(2,1)}), bf16[32,16,256]{2,1,0:T(8,128)(2,1)S(1)}, u32[]{:S(2)}, u32[]{:S(2)}) %all-to-all-start.4) | async-done | bytes 262176 | tf_op jit(solution)/shard_map/all_to_all | solution.py:309
  144.7 0.8 fusion
  145.6 1.8 %weight_grads.1 = (bf16[256,768]{1,0:T(8,128)(2,1)}, bf16[256,768]{1,0:T(8,128)(2,1)}, bf16[768,256]{1,0:T(8,128)(2,1)}) custom-call(s32[1]{0:T(128)} %bitcast.core_ref, bf16[384,1152]{1,0:T(8,128)(2,1)S(1)} %bitcast.34, bf16[384,1152]{1,0:T(8,128)(2,1)S(1)} %collective-permute-done.12.theirs_ref, bf16[512,384]{1,0:T(8,128)(2,1)S(1)} %quant_rows.1.rows_ref), custom_call_target="tpu_custom_call" | custom-call | flops 452984832 | bytes 3342338 | tf_op jit(solution)/shard_map/weight_grads/pallas_call | solution.py:101
  (39 shorter events, 3.9 us)
Async XLA Ops:
  0.6 30.0 %copy-start = (bf16[1,256,768]{2,1,0:T(8,128)(2,1)S(1)}, bf16[1,256,768]{2,1,0:T(8,128)(2,1)}, u32[]{:S(2)}) copy-start(bf16[1,256,768]{2,1,0:T(8,128)(2,1)} %param.25) | copy-start | bytes 1179652
  0.6 30.1 %copy-start.1 = (bf16[1,256,768]{2,1,0:T(8,128)(2,1)S(1)}, bf16[1,256,768]{2,1,0:T(8,128)(2,1)}, u32[]{:S(2)}) copy-start(bf16[1,256,768]{2,1,0:T(8,128)(2,1)} %param.26) | copy-start | bytes 1179652
  3.1 27.5 %all-to-all-start = ((bf16[32,24,256]{2,1,0:T(8,128)(2,1)}), bf16[32,24,256]{2,1,0:T(8,128)(2,1)S(1)}, u32[]{:S(2)}, u32[]{:S(2)}) async-start(bf16[32,24,256]{2,1,0:T(8,128)(2,1)} %bitcast.47), calls=%async_computation | async-start | bytes 786432 | tf_op jit(solution)/shard_map/all_to_all | solution.py:247
  30.6 1.0 copy-start.2
  32.1 6.4 %collective-permute-start.10 = (bf16[384,1152]{1,0:T(8,128)(2,1)S(1)}, bf16[384,1152]{1,0:T(8,128)(2,1)S(1)}, u32[]{:S(2)}, u32[]{:S(2)}) collective-permute-start(bf16[384,1152]{1,0:T(8,128)(2,1)S(1)} %away_partials.1), channel_id=1, source_target_pairs={{0,32},{32,0},{1,33},{33,1},{2,34},{34,2},{3,35},{35,3},{4,36},{36... | collective-permute-start | bytes 2654216 | tf_op jit(solution)/shard_map/ppermute | solution.py:213
  39.6 7.0 %copy-start.4 = (s32[32]{0:T(128)S(1)}, s32[32]{0:T(128)}, u32[]{:S(2)}) copy-start(s32[32]{0:T(128)} %param.29) | copy-start | bytes 388
  39.6 32.6 %all-to-all-start.1 = ((bf16[8,48,1152]{2,1,0:T(8,128)(2,1)}), bf16[8,48,1152]{2,1,0:T(8,128)(2,1)S(1)}, u32[]{:S(2)}, u32[]{:S(2)}) async-start(bf16[8,48,1152]{2,1,0:T(8,128)(2,1)} %bitcast.9), calls=%async_computation.1 | async-start | bytes 1769472 | tf_op jit(solution)/shard_map/all_to_all | solution.py:266
  47.9 11.9 %collective-permute-start = (bf16[32,24,256]{2,1,0:T(8,128)(2,1)S(1)}, bf16[32,24,256]{2,1,0:T(8,128)(2,1)S(1)}, u32[]{:S(2)}, u32[]{:S(2)}) collective-permute-start(bf16[32,24,256]{2,1,0:T(8,128)(2,1)S(1)} %param.1), channel_id=1, source_target_pairs={{0,1},{1,0},{2,3},{3,2},{4,5},{5,4},{6,7},{7,6},{8,9},{9,8},{10,11... | collective-permute-start | bytes 1179656 | tf_op jit(solution)/shard_map/cond/branch_1_fun/ppermute | solution.py:213
  73.4 22.9 %all-to-all-start.2 = ((bf16[8,48,768]{2,1,0:T(8,128)(2,1)}), bf16[8,48,768]{2,1,0:T(8,128)(2,1)S(1)}, u32[]{:S(2)}, u32[]{:S(2)}) async-start(bf16[8,48,768]{2,1,0:T(8,128)(2,1)} %broadcast_in_dim.13), calls=%async_computation.2 | async-start | bytes 1179648 | tf_op jit(solution)/shard_map/all_to_all | solution.py:266
  80.2 23.1 %copy-start.3 = (s32[32,8]{0,1:T(8,128)S(1)}, s32[32,8]{0,1:T(8,128)}, u32[]{:S(2)}) copy-start(s32[32,8]{0,1:T(8,128)} %param.23) | copy-start | bytes 3076
  80.2 6.0 %collective-permute-start.5 = (bf16[48,1152]{1,0:T(8,128)(2,1)S(1)}, bf16[48,1152]{1,0:T(8,128)(2,1)S(1)}, u32[]{:S(2)}, u32[]{:S(2)}) collective-permute-start(bf16[48,1152]{1,0:T(8,128)(2,1)S(1)} %param.7), channel_id=1, source_target_pairs={{0,1},{1,0},{2,3},{3,2},{4,5},{5,4},{6,7},{7,6},{8,9},{9,8},{10,11... | collective-permute-start | bytes 331784 | tf_op jit(solution)/shard_map/cond/branch_1_fun/ppermute | solution.py:213
  97.2 27.0 %all-to-all-start.3 = ((bf16[8,48,1152]{2,1,0:T(8,128)(2,1)}), bf16[8,48,1152]{2,1,0:T(8,128)(2,1)S(1)}, u32[]{:S(2)}, u32[]{:S(2)}) async-start(bf16[8,48,1152]{2,1,0:T(8,128)(2,1)} %broadcast_in_dim.14), calls=%async_computation.3 | async-start | bytes 1769472 | tf_op jit(solution)/shard_map/all_to_all | solution.py:266
  100.8 6.3 %collective-permute-start.11 = (bf16[384,768]{1,0:T(8,128)(2,1)S(1)}, bf16[384,768]{1,0:T(8,128)(2,1)S(1)}, u32[]{:S(2)}, u32[]{:S(2)}) collective-permute-start(bf16[384,768]{1,0:T(8,128)(2,1)S(1)} %bitcast.41), channel_id=1, source_target_pairs={{0,32},{32,0},{1,33},{33,1},{2,34},{34,2},{3,35},{35,3},{4,36},{36... | collective-permute-start | bytes 1769480 | tf_op jit(solution)/shard_map/ppermute | solution.py:213
  124.2 21.4 %collective-permute-start.12 = (bf16[384,1152]{1,0:T(8,128)(2,1)S(1)}, bf16[384,1152]{1,0:T(8,128)(2,1)S(1)}, u32[]{:S(2)}, u32[]{:S(2)}) collective-permute-start(bf16[384,1152]{1,0:T(8,128)(2,1)S(1)} %bitcast.33), channel_id=1, source_target_pairs={{0,32},{32,0},{1,33},{33,1},{2,34},{34,2},{3,35},{35,3},{4,36},{36... | collective-permute-start | bytes 2654216 | tf_op jit(solution)/shard_map/ppermute | solution.py:213
  128.8 16.0 %all-to-all-start.4 = ((bf16[32,16,256]{2,1,0:T(8,128)(2,1)}), bf16[32,16,256]{2,1,0:T(8,128)(2,1)S(1)}, u32[]{:S(2)}, u32[]{:S(2)}) async-start(bf16[32,16,256]{2,1,0:T(8,128)(2,1)} %bitcast.22), calls=%async_computation.4 | async-start | bytes 524288 | tf_op jit(solution)/shard_map/all_to_all | solution.py:309

commit v9 on v7

--- a/solution.py
+++ b/solution.py
@@ -123,6 +123,26 @@
     return out.reshape(experts, 2 * capacity, tokens.shape[1])
 
 
+def copies_kernel(in_ref, out_ref, sems):
+    stores = [pltpu.make_async_copy(in_ref, out_ref.at[k], sems.at[k]) for k in range(out_ref.shape[0])]
+    for store in stores:
+        store.start()
+    for store in stores:
+        store.wait()
+
+
+def copies(x, count):
+    return pl.pallas_call(
+        copies_kernel,
+        out_shape=jax.ShapeDtypeStruct((count,) + x.shape, x.dtype),
+        in_specs=[pl.BlockSpec(memory_space=pltpu.VMEM)],
+        out_specs=pl.BlockSpec(memory_space=pl.ANY),
+        scratch_shapes=[pltpu.SemaphoreType.DMA((count,))],
+        compiler_params=pltpu.CompilerParams(vmem_limit_bytes=VMEM_BYTES),
+        name="copies",
+    )(x)
+
+
 def side(which, size):
     return pl.ds(pl.multiple_of(which * size, size), size)
 
@@ -143,23 +163,32 @@
     out_ref[:, 2 * rows :] = dot(down_ref[cut, :], grad_ref[...], 1, 1)
 
 
-def half_back(units_ref, first_ref, rest_ref, cut, rows):
-    split = first_ref.shape[0]
+def half_back(units_ref, weight_refs, cut, rows):
     gate, up = units_ref[:, :rows], units_ref[:, rows : 2 * rows]
-    upper = dot(first_ref[:, cut], gate, 1, 0)
-    lower = dot(rest_ref[: rest_ref.shape[0] - 2 * split, cut], gate, 1, 0)
-    return jnp.concatenate([upper, lower], 0) + dot(rest_ref[split:, cut], up, 1, 0)
-
-
-def mine_back_kernel(core_ref, mine_ref, first_ref, rest_ref, out_ref):
+    width = sum(ref.shape[0] for ref in weight_refs) // 2
+    parts = []
+    done = 0
+    for ref in weight_refs:
+        for_gate = min(max(width - done, 0), ref.shape[0])
+        if for_gate > 0:
+            parts.append(dot(ref[:for_gate, cut], gate, 1, 0))
+        if for_gate < ref.shape[0]:
+            upper = dot(ref[for_gate:, cut], up, 1, 0)
+        done += ref.shape[0]
+    return jnp.concatenate(parts, 0) + upper
+
+
+def mine_back_kernel(core_ref, mine_ref, *refs):
+    weight_refs, out_ref = refs[:-1], refs[-1]
     units, rows = mine_ref.shape[0], out_ref.shape[1]
-    out_ref[...] = half_back(mine_ref, first_ref, rest_ref, side(core_ref[0], units), rows)
-
-
-def back_kernel(capacity, core_ref, theirs_ref, first_ref, rest_ref, total_ref, out_ref):
+    out_ref[...] = half_back(mine_ref, weight_refs, side(core_ref[0], units), rows)
+
+
+def back_kernel(capacity, core_ref, theirs_ref, *refs):
+    weight_refs, (total_ref, out_ref) = refs[:-2], refs[-2:]
     units, rows = theirs_ref.shape[0], total_ref.shape[1]
     out_rows = out_ref.shape[0]
-    total = total_ref[...] + half_back(theirs_ref, first_ref, rest_ref, side(1 - core_ref[0], units), rows)
+    total = total_ref[...] + half_back(theirs_ref, weight_refs, side(1 - core_ref[0], units), rows)
     groups = rows // capacity
     padded = out_rows // groups
     row = lax.broadcasted_iota(jnp.int32, (out_rows, groups), 0)
@@ -253,10 +282,16 @@
     gate_w, up_w, down_w = gate_weight[0], up_weight[0], down_weight[0]
     send = pick_rows(routes, route_weights, tokens, out_grad, experts, capacity)
     recv = lax.all_to_all(send, BITS, 0, 0, tiled=True)
-    gate_first = gate_w[: width // 2]
-    weight_rest = jnp.concatenate([gate_w[width // 2 :], up_w], 0)
     gate_t, up_t = gate_w.T, up_w.T
-    recv, weight_rest, gate_t, up_t = lax.optimization_barrier((recv, weight_rest, gate_t, up_t))
+    cut_1, cut_2 = width // 2, width * 3 // 4
+    weight_3 = jnp.concatenate([gate_w[cut_2:], up_w], 0)
+    padded = -(-capacity // 16) * 16
+    picker = jnp.take(slot_picker(routes, experts, capacity), partner, axis=0)
+    picker = jnp.pad(picker, ((0, 0), (0, padded - capacity), (0, 0))).reshape(experts * padded, tok_count)
+    weight_1 = swap(which, gate_w[:cut_1])
+    recv, weight_1, weight_3, gate_t, up_t, picker = lax.optimization_barrier(
+        (recv, weight_1, weight_3, gate_t, up_t, picker)
+    )
     rows_in = recv[:, :capacity].reshape(rows, width)
     rows_grad = recv[:, capacity:].reshape(rows, width)
 
@@ -267,12 +302,13 @@
     kept = call(keep_kernel, "keep_partials", [wide], feeds, 1, dtype=F32)[0]
     chip_sum = (kept + arrived.astype(F32)).astype(BF16)
 
-    chip_sum, recv, gate_first = lax.optimization_barrier((chip_sum, recv, gate_first))
+    weight_2 = gate_w[cut_1:cut_2]
+    chip_sum, recv, weight_2 = lax.optimization_barrier((chip_sum, recv, weight_2))
 
     piece = (half // n_y, 3 * rows)
     blocks = lax.all_to_all(chip_sum.reshape((n_y,) + piece), "y", 0, 0, tiled=True)
-    mate_recv, gate_first = swap(which, (recv, gate_first))
-    blocks, mate_recv, gate_first = lax.optimization_barrier((blocks, mate_recv, gate_first))
+    mate_recv, weight_2 = swap(which, (recv, weight_2))
+    blocks, mate_recv, weight_2 = lax.optimization_barrier((blocks, mate_recv, weight_2))
     sums = jnp.sum(blocks.astype(F32), axis=0)
     gate_sum, up_sum, hid_grad = sums[:, :rows], sums[:, rows : 2 * rows], sums[:, 2 * rows :]
     sig = jax.nn.sigmoid(gate_sum)
@@ -280,18 +316,18 @@
     gate_rows = hid_grad * up_sum * sig * (1.0 + gate_sum * (1.0 - sig))
     acts = jnp.concatenate([gate_rows, hid_grad * silu, silu * up_sum], 1).astype(BF16)
 
-    acts, weight_rest = lax.optimization_barrier((swap(which, acts), weight_rest))
-    acts = jnp.broadcast_to(acts[None], (n_y,) + piece)
-    mine = lax.all_to_all(acts, "y", 0, 0, tiled=True).reshape(wide)
-    weight_rest = swap(which, weight_rest)
+    acts, weight_3 = lax.optimization_barrier((swap(which, acts), weight_3))
+    mine = lax.all_to_all(copies(acts, n_y), "y", 0, 0, tiled=True).reshape(wide)
+    weight_3 = swap(which, weight_3)
     mate_rows = jnp.concatenate(
         [mate_recv[:, :capacity].reshape(rows, width).T, mate_recv[:, capacity:].reshape(rows, width).T], 0
     )
-    mine, weight_rest, mate_rows = lax.optimization_barrier((mine, weight_rest, mate_rows))
+    flip_signs = (1 - 2 * lax.dynamic_index_in_dim(sign_bits, mate, 0, keepdims=False)).astype(BF16)
+    rotation = sylvester(HBLOCK) * flip_signs[:, None]
+    mine, weight_3, mate_rows, rotation = lax.optimization_barrier((mine, weight_3, mate_rows, rotation))
     theirs = pair_permute(mine, "core")
 
-    padded = -(-capacity // 16) * 16
-    weights = (gate_first, weight_rest)
+    weights = (weight_1, weight_2, weight_3)
     mine_back = call(
         mine_back_kernel, "mine_back", [(width, rows)], (core_arg, mine) + weights, 1, dtype=F32
     )[0]
@@ -303,12 +339,8 @@
         1,
     )[0]
     returned = lax.all_to_all(slot_back.reshape(experts, padded, width), BITS, 0, 0, tiled=True)
-    picker = jnp.take(slot_picker(routes, experts, capacity), partner, axis=0)
-    picker = jnp.pad(picker, ((0, 0), (0, padded - capacity), (0, 0))).reshape(experts * padded, tok_count)
     input_grad = dot(picker, returned.reshape(experts * padded, width), 0, 0).astype(BF16)
 
-    flip_signs = (1 - 2 * lax.dynamic_index_in_dim(sign_bits, mate, 0, keepdims=False)).astype(BF16)
-    rotation = sylvester(HBLOCK) * flip_signs[:, None]
     gate_new, up_new, down_new = call(
         grads_kernel,
         "weight_grads",

time: 137 us -> 149 us (1.088)
  starting transfers between devices: 49.4 us -> 58.2 us
    ppermute x6 -> x2, waiting for transfers between devices: 28.3 us -> 2.09 us  [pair_permute(): return lax.ppermute(x, axis, [(0, 1), (1, 0)])]
    all_to_all x1, waiting for transfers between devices: 8.2 us -> 25.7 us  [shards(): lax.all_to_all(chip_sum.reshape((n_y,) + piece), 'y', 0, 0, tiled=True)]
    all_to_all x1, starting transfers between devices: 7.53 us -> 23.9 us  [shards(): lax.all_to_all(slot_back.reshape(experts, padded, width), BITS, 0, 0, til...]
    all_to_all x1, waiting for transfers between devices: 8.98 us -> 19.1 us  [shards(): lax.all_to_all(copies(acts, n_y), 'y', 0, 0, tiled=True).reshape(wide)]
    ppermute x6 -> x2, starting transfers between devices: 17.6 us -> 10.1 us  [pair_permute(): return lax.ppermute(x, axis, [(0, 1), (1, 0)])]
    all_to_all x1, waiting for transfers between devices: 13.3 us -> 10.4 us  [shards(): recv = lax.all_to_all(send, BITS, 0, 0, tiled=True)]
  transfers between devices with their start and end apart: 10 -> 6, of which waited for: 8 -> 6; matrix products, arithmetic and copies ran while one was open for 3% -> 3% of each run, Pallas kernels for 6% -> 5%
where the time goes in v9:
time: 149 us; the launch traced here: 148 us
  waiting for transfers between devices  62.8 us (42%)
  starting transfers between devices  58.2 us (39%)
  Pallas kernels  14.1 us (9%)
  local copies, waits for them, and re-layouts  5.31 us (4%)
  between operations  3.62 us (2%)
  other arithmetic  2.74 us (2%)
    all_to_all x1, waiting for transfers between devices, shards(): lax.all_to_all(chip_sum.reshape((n_y,) + piece), 'y', 0, 0, tiled=True)  25.7 us
    all_to_all x1, starting transfers between devices, shards(): lax.all_to_all(slot_back.reshape(experts, padded, width), BITS, 0, 0, til...  23.9 us
    all_to_all x1, waiting for transfers between devices, shards(): lax.all_to_all(copies(acts, n_y), 'y', 0, 0, tiled=True).reshape(wide)  19.1 us
    all_to_all x1, starting transfers between devices, shards(): recv = lax.all_to_all(send, BITS, 0, 0, tiled=True)  13.7 us
    pallas_call x6, Pallas kernels, call(): pl.pallas_call(kernel, out_shape=outs, in_specs=[smem] * scalars + [rest]...  13.1 us
    all_to_all x1, waiting for transfers between devices, shards(): recv = lax.all_to_all(send, BITS, 0, 0, tiled=True)  10.4 us
    ppermute x2, starting transfers between devices, pair_permute(): return lax.ppermute(x, axis, [(0, 1), (1, 0)])  10.1 us
    all_to_all x1, starting transfers between devices, shards(): lax.all_to_all(chip_sum.reshape((n_y,) + piece), 'y', 0, 0, tiled=True)  6.82 us
  transfers between devices with their start and end apart: 6, of which 6 were waited for; matrix products, arithmetic and copies ran while one was open for 3% of the time, Pallas kernels for 5%

profile of v9, /device:TPU:1, one launch (start us, length us, event | category | flops | bytes accessed | tf_op | source)
XLA Modules:
  0.0 147.6 jit_solution(12533964756988591131)
XLA Ops:
  0.7 2.4 %pick_rows.1 = bf16[768,256]{1,0:T(8,128)(2,1)} custom-call(s32[8,32]{1,0:T(8,128)} %bitcast.51, f32[8,32]{1,0:T(8,128)} %bitcast.55, bf16[32,256]{1,0:T(8,128)(2,1)} %tok_in.1, bf16[32,256]{1,0:T(8,128)(2,1)} %grad_in.1), custom_call_target="tpu_custom_call" | custom-call | flops 452984832 | bytes 427008 | tf_op jit(solution)/shard_map/pick_rows/pallas_call | solution.py:101
  3.1 13.7 %all-to-all-start = ((bf16[32,24,256]{2,1,0:T(8,128)(2,1)}), bf16[32,24,256]{2,1,0:T(8,128)(2,1)S(1)}, u32[]{:S(2)}, u32[]{:S(2)}) async-start(bf16[32,24,256]{2,1,0:T(8,128)(2,1)} %bitcast.50), calls=%async_computation | async-start | bytes 786432 | tf_op jit(solution)/shard_map/all_to_all | solution.py:284
  16.9 0.6 dynamic_slice.7
  18.4 0.2 copy.41
  18.8 0.2 copy.42
  19.1 0.6 gather_fusion
  20.0 0.3 pad_maximum_fusion
  20.3 10.4 %all-to-all-done = bf16[32,24,256]{2,1,0:T(8,128)(2,1)S(1)} async-done(((bf16[32,24,256]{2,1,0:T(8,128)(2,1)}), bf16[32,24,256]{2,1,0:T(8,128)(2,1)S(1)}, u32[]{:S(2)}, u32[]{:S(2)}) %all-to-all-start) | async-done | bytes 393248 | tf_op jit(solution)/shard_map/all_to_all | solution.py:284
  30.6 0.8 fusion.5
  31.4 1.0 reshape.74.in_ref
  32.5 0.5 away_partials.1
  33.0 5.6 %collective-permute-start.25 = (bf16[384,1152]{1,0:T(8,128)(2,1)S(1)}, bf16[384,1152]{1,0:T(8,128)(2,1)S(1)}, u32[]{:S(2)}, u32[]{:S(2)}) collective-permute-start(bf16[384,1152]{1,0:T(8,128)(2,1)S(1)} %away_partials.1), channel_id=1, source_target_pairs={{0,32},{32,0},{1,33},{33,1},{2,34},{34,2},{3,35},{35,3},{4,36},{36... | collective-permute-start | bytes 2654216 | tf_op jit(solution)/shard_map/ppermute | solution.py:250
  38.6 0.5 keep_partials.1
  39.0 1.5 %collective-permute-done.25 = bf16[384,1152]{1,0:T(8,128)(2,1)S(1)} collective-permute-done((bf16[384,1152]{1,0:T(8,128)(2,1)S(1)}, bf16[384,1152]{1,0:T(8,128)(2,1)S(1)}, u32[]{:S(2)}, u32[]{:S(2)}) %collective-permute-start.25) | collective-permute-done | bytes 884768 | tf_op jit(solution)/shard_map/ppermute | solution.py:250
  40.6 1.1 add_convert_fusion
  41.7 6.8 %all-to-all-start.1 = ((bf16[8,48,1152]{2,1,0:T(8,128)(2,1)}), bf16[8,48,1152]{2,1,0:T(8,128)(2,1)S(1)}, u32[]{:S(2)}, u32[]{:S(2)}) async-start(bf16[8,48,1152]{2,1,0:T(8,128)(2,1)} %bitcast.16), calls=%async_computation.1 | async-start | bytes 1769472 | tf_op jit(solution)/shard_map/all_to_all | solution.py:309
  48.5 25.7 %all-to-all-done.1 = bf16[8,48,1152]{2,1,0:T(8,128)(2,1)S(1)} async-done(((bf16[8,48,1152]{2,1,0:T(8,128)(2,1)}), bf16[8,48,1152]{2,1,0:T(8,128)(2,1)S(1)}, u32[]{:S(2)}, u32[]{:S(2)}) %all-to-all-start.1) | async-done | bytes 884768 | tf_op jit(solution)/shard_map/all_to_all | solution.py:309
  74.4 1.0 copies.1
  75.4 3.6 %all-to-all-start.2 = ((bf16[8,48,1152]{2,1,0:T(8,128)(2,1)}), bf16[8,48,1152]{2,1,0:T(8,128)(2,1)S(1)}, u32[]{:S(2)}, u32[]{:S(2)}) async-start(bf16[8,48,1152]{2,1,0:T(8,128)(2,1)} %copies.1), calls=%async_computation.2 | async-start | bytes 1769472 | tf_op jit(solution)/shard_map/all_to_all | solution.py:320
  80.9 0.7 convert_bitcast_fusion
  81.9 0.2 copy.53
  82.2 1.0 conditional.7
  82.3 1.0 copy.47
  83.3 19.1 %all-to-all-done.2 = bf16[8,48,1152]{2,1,0:T(8,128)(2,1)S(1)} async-done(((bf16[8,48,1152]{2,1,0:T(8,128)(2,1)}), bf16[8,48,1152]{2,1,0:T(8,128)(2,1)S(1)}, u32[]{:S(2)}, u32[]{:S(2)}) %all-to-all-start.2) | async-done | bytes 884768 | tf_op jit(solution)/shard_map/all_to_all | solution.py:320
  102.4 4.6 %collective-permute-start.26 = (bf16[384,1152]{1,0:T(8,128)(2,1)S(1)}, bf16[384,1152]{1,0:T(8,128)(2,1)S(1)}, u32[]{:S(2)}, u32[]{:S(2)}) collective-permute-start(bf16[384,1152]{1,0:T(8,128)(2,1)S(1)} %bitcast.36), channel_id=1, source_target_pairs={{0,32},{32,0},{1,33},{33,1},{2,34},{34,2},{3,35},{35,3},{4,36},{36... | collective-permute-start | bytes 2654216 | tf_op jit(solution)/shard_map/ppermute | solution.py:250
  107.0 1.5 mine_back.1.refs_3_
  108.4 0.6 collective-permute-done.26.theirs_ref
  109.0 2.5 %slot_back.1 = bf16[512,256]{1,0:T(8,128)(2,1)} custom-call(s32[1]{0:T(128)} %bitcast.core_ref, bf16[384,1152]{1,0:T(8,128)(2,1)S(1)} %collective-permute-done.26.theirs_ref, bf16[128,768]{1,0:T(8,128)(2,1)S(1)} %get-tuple-element.142.refs_0_, bf16[64,768]{1,0:T(8,128)(2,1)S(1)} %get-tuple-element.121.refs_1_, bf16[320,768]{1,0:T(8,128)(2,1)} %get-tuple-element.145.refs_2_, ...), custom_call_target="tpu_custom_call" | custom-call | flops 452984832 | bytes 2129922 | tf_op jit(solution)/shard_map/slot_back/pallas_call | solution.py:101
  111.5 23.9 %all-to-all-start.3 = ((bf16[32,16,256]{2,1,0:T(8,128)(2,1)}), bf16[32,16,256]{2,1,0:T(8,128)(2,1)S(1)}, u32[]{:S(2)}, u32[]{:S(2)}) async-start(bf16[32,16,256]{2,1,0:T(8,128)(2,1)} %bitcast.24), calls=%async_computation.3 | async-start | bytes 524288 | tf_op jit(solution)/shard_map/all_to_all | solution.py:341
  135.4 5.8 %weight_grads.1 = (bf16[256,768]{1,0:T(8,128)(2,1)}, bf16[256,768]{1,0:T(8,128)(2,1)}, bf16[768,256]{1,0:T(8,128)(2,1)}) custom-call(s32[1]{0:T(128)} %bitcast.core_ref, bf16[384,1152]{1,0:T(8,128)(2,1)S(1)} %bitcast.38, bf16[384,1152]{1,0:T(8,128)(2,1)S(1)} %collective-permute-done.26.theirs_ref, bf16[512,384]{1,0:T(8,128)(2,1)S(1)} %pad_maximum_fusion.1.rows_ref, ...), custom_call_target="tpu_custom_call" | custom-call | flops 452984832 | bytes 3375106 | tf_op jit(solution)/shard_map/weight_grads/pallas_call | solution.py:101
  141.2 5.6 %all-to-all-done.3 = bf16[32,16,256]{2,1,0:T(8,128)(2,1)S(1)} async-done(((bf16[32,16,256]{2,1,0:T(8,128)(2,1)}), bf16[32,16,256]{2,1,0:T(8,128)(2,1)S(1)}, u32[]{:S(2)}, u32[]{:S(2)}) %all-to-all-start.3) | async-done | bytes 262176 | tf_op jit(solution)/shard_map/all_to_all | solution.py:341
  146.8 0.8 convolution_convert_fusion
  (39 shorter events, 1.5 us)
Async XLA Ops:
  0.6 17.5 %copy-start.3 = (s32[32,8]{0,1:T(8,128)S(1)}, s32[32,8]{0,1:T(8,128)}, u32[]{:S(2)}) copy-start(s32[32,8]{0,1:T(8,128)} %param.35) | copy-start | bytes 3076
  0.6 16.2 %copy-start.4 = (s32[32]{0:T(128)S(1)}, s32[32]{0:T(128)}, u32[]{:S(2)}) copy-start(s32[32]{0:T(128)} %param.41) | copy-start | bytes 388
  0.7 17.7 %copy-start.1 = (bf16[1,256,768]{2,1,0:T(8,128)(2,1)S(1)}, bf16[1,256,768]{2,1,0:T(8,128)(2,1)}, u32[]{:S(2)}) copy-start(bf16[1,256,768]{2,1,0:T(8,128)(2,1)} %param.37) | copy-start | bytes 1179652
  0.7 18.1 %copy-start.2 = (bf16[1,256,768]{2,1,0:T(8,128)(2,1)S(1)}, bf16[1,256,768]{2,1,0:T(8,128)(2,1)}, u32[]{:S(2)}) copy-start(bf16[1,256,768]{2,1,0:T(8,128)(2,1)} %param.38) | copy-start | bytes 1179652
  3.1 27.5 %all-to-all-start = ((bf16[32,24,256]{2,1,0:T(8,128)(2,1)}), bf16[32,24,256]{2,1,0:T(8,128)(2,1)S(1)}, u32[]{:S(2)}, u32[]{:S(2)}) async-start(bf16[32,24,256]{2,1,0:T(8,128)(2,1)} %bitcast.50), calls=%async_computation | async-start | bytes 786432 | tf_op jit(solution)/shard_map/all_to_all | solution.py:284
  19.9 12.6 %copy-start = (bf16[1,768,256]{2,1,0:T(8,128)(2,1)S(1)}, bf16[1,768,256]{2,1,0:T(8,128)(2,1)}, u32[]{:S(2)}) copy-start(bf16[1,768,256]{2,1,0:T(8,128)(2,1)} %param.39) | copy-start | bytes 1179652
  33.0 7.6 %collective-permute-start.25 = (bf16[384,1152]{1,0:T(8,128)(2,1)S(1)}, bf16[384,1152]{1,0:T(8,128)(2,1)S(1)}, u32[]{:S(2)}, u32[]{:S(2)}) collective-permute-start(bf16[384,1152]{1,0:T(8,128)(2,1)S(1)} %away_partials.1), channel_id=1, source_target_pairs={{0,32},{32,0},{1,33},{33,1},{2,34},{34,2},{3,35},{35,3},{4,36},{36... | collective-permute-start | bytes 2654216 | tf_op jit(solution)/shard_map/ppermute | solution.py:250
  41.7 32.5 %all-to-all-start.1 = ((bf16[8,48,1152]{2,1,0:T(8,128)(2,1)}), bf16[8,48,1152]{2,1,0:T(8,128)(2,1)S(1)}, u32[]{:S(2)}, u32[]{:S(2)}) async-start(bf16[8,48,1152]{2,1,0:T(8,128)(2,1)} %bitcast.16), calls=%async_computation.1 | async-start | bytes 1769472 | tf_op jit(solution)/shard_map/all_to_all | solution.py:309
  75.4 27.0 %all-to-all-start.2 = ((bf16[8,48,1152]{2,1,0:T(8,128)(2,1)}), bf16[8,48,1152]{2,1,0:T(8,128)(2,1)S(1)}, u32[]{:S(2)}, u32[]{:S(2)}) async-start(bf16[8,48,1152]{2,1,0:T(8,128)(2,1)} %copies.1), calls=%async_computation.2 | async-start | bytes 1769472 | tf_op jit(solution)/shard_map/all_to_all | solution.py:320
  102.4 6.6 %collective-permute-start.26 = (bf16[384,1152]{1,0:T(8,128)(2,1)S(1)}, bf16[384,1152]{1,0:T(8,128)(2,1)S(1)}, u32[]{:S(2)}, u32[]{:S(2)}) collective-permute-start(bf16[384,1152]{1,0:T(8,128)(2,1)S(1)} %bitcast.36), channel_id=1, source_target_pairs={{0,32},{32,0},{1,33},{33,1},{2,34},{34,2},{3,35},{35,3},{4,36},{36... | collective-permute-start | bytes 2654216 | tf_op jit(solution)/shard_map/ppermute | solution.py:250
  111.5 35.3 %all-to-all-start.3 = ((bf16[32,16,256]{2,1,0:T(8,128)(2,1)}), bf16[32,16,256]{2,1,0:T(8,128)(2,1)S(1)}, u32[]{:S(2)}, u32[]{:S(2)}) async-start(bf16[32,16,256]{2,1,0:T(8,128)(2,1)} %bitcast.24), calls=%async_computation.3 | async-start | bytes 524288 | tf_op jit(solution)/shard_map/all_to_all | solution.py:341

commit v10 on v9

--- a/solution.py
+++ b/solution.py
@@ -22,6 +22,7 @@
 BF16 = jnp.bfloat16
 F32 = jnp.float32
 BITS = ("b4", "b3", "b2", "b1", "b0")
+GROUP = 8
 VMEM_BYTES = 16 * 2**20
 ALL_VMEM = 60 * 2**20
 
@@ -147,20 +148,32 @@
     return pl.ds(pl.multiple_of(which * size, size), size)
 
 
-def away_kernel(core_ref, gate_ref, up_ref, down_ref, in_ref, grad_ref, out_ref):
-    units, rows = out_ref.shape[0], in_ref.shape[0]
+def away_kernel(capacity, core_ref, gate_ref, up_ref, down_ref, recv_ref, out_ref, rows_ref):
+    rows = rows_ref.shape[0] // 2
+    size = GROUP * capacity
+    row = lax.broadcasted_iota(jnp.int32, (size, GROUP), 0)
+    start = lax.broadcasted_iota(jnp.int32, (size, GROUP), 1) * capacity
+    inside = (row >= start) & (row < start + capacity)
+    source = jnp.sum(jnp.where(inside, row + start, 0).astype(F32), axis=1, keepdims=True)
+    column = lax.broadcasted_iota(jnp.int32, (size, 2 * size), 1).astype(F32)
+    for k, place in enumerate((source, source + capacity)):
+        pick = jnp.where(column == place, 1.0, 0.0).astype(BF16)
+        for g in range(rows // size):
+            block = recv_ref[2 * g * size : 2 * (g + 1) * size, :]
+            rows_ref[k * rows + g * size : k * rows + (g + 1) * size, :] = dot(pick, block, 1, 0).astype(BF16)
+    units = out_ref.shape[0]
     cut = side(1 - core_ref[0], units)
-    out_ref[:, :rows] = dot(gate_ref[cut, :], in_ref[...], 1, 1).astype(BF16)
-    out_ref[:, rows : 2 * rows] = dot(up_ref[cut, :], in_ref[...], 1, 1).astype(BF16)
-    out_ref[:, 2 * rows :] = dot(down_ref[cut, :], grad_ref[...], 1, 1).astype(BF16)
-
-
-def keep_kernel(core_ref, gate_ref, up_ref, down_ref, in_ref, grad_ref, out_ref):
-    units, rows = out_ref.shape[0], in_ref.shape[0]
+    out_ref[:, :rows] = dot(gate_ref[cut, :], rows_ref[:rows, :], 1, 1).astype(BF16)
+    out_ref[:, rows : 2 * rows] = dot(up_ref[cut, :], rows_ref[:rows, :], 1, 1).astype(BF16)
+    out_ref[:, 2 * rows :] = dot(down_ref[cut, :], rows_ref[rows:, :], 1, 1).astype(BF16)
+
+
+def keep_kernel(core_ref, gate_ref, up_ref, down_ref, rows_ref, out_ref):
+    units, rows = out_ref.shape[0], rows_ref.shape[0] // 2
     cut = side(core_ref[0], units)
-    out_ref[:, :rows] = dot(gate_ref[cut, :], in_ref[...], 1, 1)
-    out_ref[:, rows : 2 * rows] = dot(up_ref[cut, :], in_ref[...], 1, 1)
-    out_ref[:, 2 * rows :] = dot(down_ref[cut, :], grad_ref[...], 1, 1)
+    out_ref[:, :rows] = dot(gate_ref[cut, :], rows_ref[:rows, :], 1, 1)
+    out_ref[:, rows : 2 * rows] = dot(up_ref[cut, :], rows_ref[:rows, :], 1, 1)
+    out_ref[:, 2 * rows :] = dot(down_ref[cut, :], rows_ref[rows:, :], 1, 1)
 
 
 def half_back(units_ref, weight_refs, cut, rows):
@@ -283,32 +296,40 @@
     send = pick_rows(routes, route_weights, tokens, out_grad, experts, capacity)
     recv = lax.all_to_all(send, BITS, 0, 0, tiled=True)
     gate_t, up_t = gate_w.T, up_w.T
-    cut_1, cut_2 = width // 2, width * 3 // 4
+    cut_1, cut_2 = width // 4, width * 5 // 8
+    weight_2 = gate_w[cut_1:cut_2]
     weight_3 = jnp.concatenate([gate_w[cut_2:], up_w], 0)
+    weight_1 = swap(which, gate_w[:cut_1])
+    recv, weight_1, weight_2, weight_3, gate_t, up_t = lax.optimization_barrier(
+        (recv, weight_1, weight_2, weight_3, gate_t, up_t)
+    )
+    recv = recv.reshape(2 * rows, width)
+
+    feeds = (core_arg, gate_t, up_t, down_w)
+    wide = (half, 3 * rows)
+    away, routed = call(
+        functools.partial(away_kernel, capacity), "away_partials", [wide, recv.shape], feeds + (recv,), 1
+    )
+    arrived = pair_permute(away, "core")
+    kept = call(keep_kernel, "keep_partials", [wide], feeds + (routed,), 1, dtype=F32)[0]
+    chip_sum = (kept + arrived.astype(F32)).astype(BF16)
+
+    chip_sum, routed, weight_2 = lax.optimization_barrier((chip_sum, routed, weight_2))
+
+    piece = (half // n_y, 3 * rows)
+    blocks = lax.all_to_all(chip_sum.reshape((n_y,) + piece), "y", 0, 0, tiled=True)
+    mate_routed, weight_2, routes, sign_bits = lax.optimization_barrier(
+        swap(which, (routed, weight_2)) + (routes, sign_bits)
+    )
     padded = -(-capacity // 16) * 16
     picker = jnp.take(slot_picker(routes, experts, capacity), partner, axis=0)
     picker = jnp.pad(picker, ((0, 0), (0, padded - capacity), (0, 0))).reshape(experts * padded, tok_count)
-    weight_1 = swap(which, gate_w[:cut_1])
-    recv, weight_1, weight_3, gate_t, up_t, picker = lax.optimization_barrier(
-        (recv, weight_1, weight_3, gate_t, up_t, picker)
-    )
-    rows_in = recv[:, :capacity].reshape(rows, width)
-    rows_grad = recv[:, capacity:].reshape(rows, width)
-
-    feeds = (core_arg, gate_t, up_t, down_w, rows_in, rows_grad)
-    wide = (half, 3 * rows)
-    away = call(away_kernel, "away_partials", [wide], feeds, 1)[0]
-    arrived = pair_permute(away, "core")
-    kept = call(keep_kernel, "keep_partials", [wide], feeds, 1, dtype=F32)[0]
-    chip_sum = (kept + arrived.astype(F32)).astype(BF16)
-
-    weight_2 = gate_w[cut_1:cut_2]
-    chip_sum, recv, weight_2 = lax.optimization_barrier((chip_sum, recv, weight_2))
-
-    piece = (half // n_y, 3 * rows)
-    blocks = lax.all_to_all(chip_sum.reshape((n_y,) + piece), "y", 0, 0, tiled=True)
-    mate_recv, weight_2 = swap(which, (recv, weight_2))
-    blocks, mate_recv, weight_2 = lax.optimization_barrier((blocks, mate_recv, weight_2))
+    flip_signs = (1 - 2 * lax.dynamic_index_in_dim(sign_bits, mate, 0, keepdims=False)).astype(BF16)
+    rotation = sylvester(HBLOCK) * flip_signs[:, None]
+    mate_rows = jnp.concatenate([mate_routed[:rows].T, mate_routed[rows:].T], 0)
+    blocks, mate_rows, weight_2, picker, rotation = lax.optimization_barrier(
+        (blocks, mate_rows, weight_2, picker, rotation)
+    )
     sums = jnp.sum(blocks.astype(F32), axis=0)
     gate_sum, up_sum, hid_grad = sums[:, :rows], sums[:, rows : 2 * rows], sums[:, 2 * rows :]
     sig = jax.nn.sigmoid(gate_sum)
@@ -319,12 +340,7 @@
     acts, weight_3 = lax.optimization_barrier((swap(which, acts), weight_3))
     mine = lax.all_to_all(copies(acts, n_y), "y", 0, 0, tiled=True).reshape(wide)
     weight_3 = swap(which, weight_3)
-    mate_rows = jnp.concatenate(
-        [mate_recv[:, :capacity].reshape(rows, width).T, mate_recv[:, capacity:].reshape(rows, width).T], 0
-    )
-    flip_signs = (1 - 2 * lax.dynamic_index_in_dim(sign_bits, mate, 0, keepdims=False)).astype(BF16)
-    rotation = sylvester(HBLOCK) * flip_signs[:, None]
-    mine, weight_3, mate_rows, rotation = lax.optimization_barrier((mine, weight_3, mate_rows, rotation))
+    mine, weight_3 = lax.optimization_barrier((mine, weight_3))
     theirs = pair_permute(mine, "core")
 
     weights = (weight_1, weight_2, weight_3)

time: 149 us -> 172 us (1.15)
  waiting for transfers between devices: 62.8 us -> 75.1 us
  starting transfers between devices: 58.2 us -> 68.9 us
    ppermute x2 -> x7, waiting for transfers between devices: 2.09 us -> 31.9 us  [pair_permute(): return lax.ppermute(x, axis, [(0, 1), (1, 0)])]
    ppermute x2 -> x7, starting transfers between devices: 10.1 us -> 19.4 us  [pair_permute(): return lax.ppermute(x, axis, [(0, 1), (1, 0)])]
    all_to_all x1, waiting for transfers between devices: 19.1 us -> 10.9 us  [shards(): lax.all_to_all(copies(acts, n_y), 'y', 0, 0, tiled=True).reshape(wide)]
    all_to_all x1, waiting for transfers between devices: 10.4 us -> 3.16 us  [shards(): recv = lax.all_to_all(send, BITS, 0, 0, tiled=True)]
    all_to_all x1, waiting for transfers between devices: 25.7 us -> 23.5 us  [shards(): lax.all_to_all(chip_sum.reshape((n_y,) + piece), 'y', 0, 0, tiled=True)]
  transfers between devices with their start and end apart: 6 -> 11, of which waited for: 6 -> 9; matrix products, arithmetic and copies ran while one was open for 3% -> 3% of each run, Pallas kernels for 5% -> 5%
where the time goes in v10:
time: 172 us; the launch traced here: 171 us
  waiting for transfers between devices  75.1 us (44%)
  starting transfers between devices  68.9 us (40%)
  Pallas kernels  14.4 us (8%)
  other arithmetic  3.96 us (2%)
  local copies, waits for them, and re-layouts  3.6 us (2%)
  between operations  3.59 us (2%)
    ppermute x7, waiting for transfers between devices, pair_permute(): return lax.ppermute(x, axis, [(0, 1), (1, 0)])  31.9 us
    all_to_all x1, starting transfers between devices, shards(): lax.all_to_all(slot_back.reshape(experts, padded, width), BITS, 0, 0, til...  25.4 us
    all_to_all x1, waiting for transfers between devices, shards(): lax.all_to_all(chip_sum.reshape((n_y,) + piece), 'y', 0, 0, tiled=True)  23.5 us
    ppermute x7, starting transfers between devices, pair_permute(): return lax.ppermute(x, axis, [(0, 1), (1, 0)])  19.4 us
    all_to_all x1, starting transfers between devices, shards(): recv = lax.all_to_all(send, BITS, 0, 0, tiled=True)  13.7 us
    pallas_call x6, Pallas kernels, call(): pl.pallas_call(kernel, out_shape=outs, in_specs=[smem] * scalars + [rest]...  13.4 us
    all_to_all x1, waiting for transfers between devices, shards(): lax.all_to_all(copies(acts, n_y), 'y', 0, 0, tiled=True).reshape(wide)  10.9 us
    all_to_all x1, starting transfers between devices, shards(): lax.all_to_all(chip_sum.reshape((n_y,) + piece), 'y', 0, 0, tiled=True)  6.82 us
  transfers between devices with their start and end apart: 11, of which 9 were waited for; matrix products, arithmetic and copies ran while one was open for 3% of the time, Pallas kernels for 5%

profile of v10, /device:TPU:1, one launch (start us, length us, event | category | flops | bytes accessed | tf_op | source)
XLA Modules:
  0.0 170.6 jit_solution(16734018078769868801)
XLA Ops:
  0.7 2.4 %pick_rows.1 = bf16[768,256]{1,0:T(8,128)(2,1)} custom-call(s32[8,32]{1,0:T(8,128)} %bitcast.53, f32[8,32]{1,0:T(8,128)} %bitcast.57, bf16[32,256]{1,0:T(8,128)(2,1)} %tok_in.1, bf16[32,256]{1,0:T(8,128)(2,1)} %grad_in.1), custom_call_target="tpu_custom_call" | custom-call | flops 452984832 | bytes 427008 | tf_op jit(solution)/shard_map/pick_rows/pallas_call | solution.py:102
  3.1 13.7 %all-to-all-start = ((bf16[32,24,256]{2,1,0:T(8,128)(2,1)}), bf16[32,24,256]{2,1,0:T(8,128)(2,1)S(1)}, u32[]{:S(2)}, u32[]{:S(2)}) async-start(bf16[32,24,256]{2,1,0:T(8,128)(2,1)} %bitcast.52), calls=%async_computation | async-start | bytes 786432 | tf_op jit(solution)/shard_map/all_to_all | solution.py:297
  18.5 7.9 %conditional.4 = (bf16[64,768]{1,0:T(8,128)(2,1)S(1)}) conditional(s32[]{:T(128)} %clamp.2, bf16[64,768]{1,0:T(8,128)(2,1)S(1)} %slice_bitcast_fusion.4, bf16[64,768]{1,0:T(8,128)(2,1)S(1)} %slice_bitcast_fusion.4, bf16[64,768]{1,0:T(8,128)(2,1)S(1)} %slice_bitcast_fusion.4, ...), branch_computations={%region_0.0_spmd, %region_1.0_spmd, %region_2.0_spmd, %region_3.0_... | conditional | bytes 589872 | solution.py:268
  18.5 3.1 %collective-permute-start = (bf16[64,768]{1,0:T(8,128)(2,1)S(1)}, bf16[64,768]{1,0:T(8,128)(2,1)S(1)}, u32[]{:S(2)}, u32[]{:S(2)}) collective-permute-start(bf16[64,768]{1,0:T(8,128)(2,1)S(1)} %param.1), channel_id=1, source_target_pairs={{0,1},{1,0},{2,3},{3,2},{4,5},{5,4},{6,7},{7,6},{8,9},{9,8},{10,11... | collective-permute-start | bytes 294920 | tf_op jit(solution)/shard_map/cond/branch_1_fun/ppermute | solution.py:263
  21.7 4.7 %collective-permute-done = bf16[64,768]{1,0:T(8,128)(2,1)S(1)} collective-permute-done((bf16[64,768]{1,0:T(8,128)(2,1)S(1)}, bf16[64,768]{1,0:T(8,128)(2,1)S(1)}, u32[]{:S(2)}, u32[]{:S(2)}) %collective-permute-start) | collective-permute-done | bytes 98336 | tf_op jit(solution)/shard_map/cond/branch_1_fun/ppermute | solution.py:263
  27.5 3.2 %all-to-all-done = bf16[32,24,256]{2,1,0:T(8,128)(2,1)S(1)} async-done(((bf16[32,24,256]{2,1,0:T(8,128)(2,1)}), bf16[32,24,256]{2,1,0:T(8,128)(2,1)S(1)}, u32[]{:S(2)}, u32[]{:S(2)}) %all-to-all-start) | async-done | bytes 393248 | tf_op jit(solution)/shard_map/all_to_all | solution.py:297
  30.6 0.8 away_partials.1
  31.4 4.4 %collective-permute-start.25 = (bf16[384,1152]{1,0:T(8,128)(2,1)S(1)}, bf16[384,1152]{1,0:T(8,128)(2,1)}, u32[]{:S(2)}, u32[]{:S(2)}) collective-permute-start(bf16[384,1152]{1,0:T(8,128)(2,1)S(1)} %get-tuple-element.110), channel_id=1, source_target_pairs={{0,32},{32,0},{1,33},{33,1},{2,34},{34,2},{3,35},{35,3},{4,36},{36... | collective-permute-start | bytes 2654216 | tf_op jit(solution)/shard_map/ppermute | solution.py:263
  38.3 2.3 %add_convert_fusion = bf16[384,1152]{1,0:T(8,128)(2,1)} fusion(f32[384,1152]{1,0:T(8,128)S(1)} %keep_partials.1, bf16[384,1152]{1,0:T(8,128)(2,1)} %collective-permute-done.25), kind=kLoop, calls=%fused_computation.2 | loop fusion | flops 1327104 | bytes 3538944 | tf_op jit(solution)/shard_map/convert_element_type | solution.py:315
  40.6 15.8 %conditional.5 = ((bf16[768,256]{1,0:T(8,128)(2,1)S(1)}, bf16[96,768]{1,0:T(8,128)(2,1)S(1)})) conditional(s32[]{:T(128)} %clamp.2, (bf16[768,256]{1,0:T(8,128)(2,1)S(1)}, bf16[96,768]{1,0:T(8,128)(2,1)S(1)}) %tuple.132, (bf16[768,256]{1,0:T(8,128)(2,1)S(1)}, bf16[96,768]{1,0:T(8,128)(2,1)S(1)}) %tuple.133, ...), branch_computations={%region_6.0_spmd, %region_7.0_spmd, %region_8.0_spmd, %region_9.0_... | conditional | bytes 3244136 | solution.py:268
  40.6 2.1 %collective-permute-start.5 = (bf16[768,256]{1,0:T(8,128)(2,1)S(1)}, bf16[768,256]{1,0:T(8,128)(2,1)S(1)}, u32[]{:S(2)}, u32[]{:S(2)}) collective-permute-start(bf16[768,256]{1,0:T(8,128)(2,1)S(1)} %get-tuple-element.63), channel_id=1, source_target_pairs={{0,1},{1,0},{2,3},{3,2},{4,5},{5,4},{6,7},{7,6},{8,9},{9,8},{10,11... | collective-permute-start | bytes 1179656 | tf_op jit(solution)/shard_map/cond/branch_1_fun/ppermute | solution.py:263
  42.7 3.2 %collective-permute-start.6 = (bf16[96,768]{1,0:T(8,128)(2,1)S(1)}, bf16[96,768]{1,0:T(8,128)(2,1)S(1)}, u32[]{:S(2)}, u32[]{:S(2)}) collective-permute-start(bf16[96,768]{1,0:T(8,128)(2,1)S(1)} %get-tuple-element.64), channel_id=1, source_target_pairs={{0,1},{1,0},{2,3},{3,2},{4,5},{5,4},{6,7},{7,6},{8,9},{9,8},{10,11... | collective-permute-start | bytes 442376 | tf_op jit(solution)/shard_map/cond/branch_1_fun/ppermute | solution.py:263
  45.9 10.4 %collective-permute-done.6 = bf16[96,768]{1,0:T(8,128)(2,1)S(1)} collective-permute-done((bf16[96,768]{1,0:T(8,128)(2,1)S(1)}, bf16[96,768]{1,0:T(8,128)(2,1)S(1)}, u32[]{:S(2)}, u32[]{:S(2)}) %collective-permute-start.6) | collective-permute-done | bytes 147488 | tf_op jit(solution)/shard_map/cond/branch_1_fun/ppermute | solution.py:263
  57.1 6.8 %all-to-all-start.1 = ((bf16[8,48,1152]{2,1,0:T(8,128)(2,1)}), bf16[8,48,1152]{2,1,0:T(8,128)(2,1)S(1)}, u32[]{:S(2)}, u32[]{:S(2)}) async-start(bf16[8,48,1152]{2,1,0:T(8,128)(2,1)} %bitcast.14), calls=%async_computation.1 | async-start | bytes 1769472 | tf_op jit(solution)/shard_map/all_to_all | solution.py:320
  65.1 0.7 convert_bitcast_fusion
  66.0 23.5 %all-to-all-done.1 = bf16[8,48,1152]{2,1,0:T(8,128)(2,1)S(1)} async-done(((bf16[8,48,1152]{2,1,0:T(8,128)(2,1)}), bf16[8,48,1152]{2,1,0:T(8,128)(2,1)S(1)}, u32[]{:S(2)}, u32[]{:S(2)}) %all-to-all-start.1) | async-done | bytes 884768 | tf_op jit(solution)/shard_map/all_to_all | solution.py:320
  89.8 6.1 %conditional.6 = (bf16[48,1152]{1,0:T(8,128)(2,1)S(1)}) conditional(s32[]{:T(128)} %clamp.2, bf16[48,1152]{1,0:T(8,128)(2,1)S(1)} %pad_maximum_fusion.2, bf16[48,1152]{1,0:T(8,128)(2,1)S(1)} %pad_maximum_fusion.2, bf16[48,1152]{1,0:T(8,128)(2,1)S(1)} %pad_maximum_fusion.2, ...), branch_computations={%region_15.16_spmd, %region_16.17_spmd, %region_17.18_spmd, %regio... | conditional | bytes 663600 | solution.py:268
  89.8 2.1 %collective-permute-start.15 = (bf16[48,1152]{1,0:T(8,128)(2,1)S(1)}, bf16[48,1152]{1,0:T(8,128)(2,1)S(1)}, u32[]{:S(2)}, u32[]{:S(2)}) collective-permute-start(bf16[48,1152]{1,0:T(8,128)(2,1)S(1)} %param.13), channel_id=1, source_target_pairs={{0,1},{1,0},{2,3},{3,2},{4,5},{5,4},{6,7},{7,6},{8,9},{9,8},{10,11... | collective-permute-start | bytes 331784 | tf_op jit(solution)/shard_map/cond/branch_1_fun/ppermute | solution.py:263
  91.9 3.9 %collective-permute-done.15 = bf16[48,1152]{1,0:T(8,128)(2,1)S(1)} collective-permute-done((bf16[48,1152]{1,0:T(8,128)(2,1)S(1)}, bf16[48,1152]{1,0:T(8,128)(2,1)S(1)}, u32[]{:S(2)}, u32[]{:S(2)}) %collective-permute-start.15) | collective-permute-done | bytes 110624 | tf_op jit(solution)/shard_map/cond/branch_1_fun/ppermute | solution.py:263
  95.9 1.0 copies.1
  96.9 3.6 %all-to-all-start.2 = ((bf16[8,48,1152]{2,1,0:T(8,128)(2,1)}), bf16[8,48,1152]{2,1,0:T(8,128)(2,1)S(1)}, u32[]{:S(2)}, u32[]{:S(2)}) async-start(bf16[8,48,1152]{2,1,0:T(8,128)(2,1)} %copies.1), calls=%async_computation.2 | async-start | bytes 1769472 | tf_op jit(solution)/shard_map/all_to_all | solution.py:341
  100.4 14.7 %conditional.7 = (bf16[352,768]{1,0:T(8,128)(2,1)}) conditional(s32[]{:T(128)} %clamp.2, bf16[352,768]{0,1:T(8,128)(2,1)S(1)} %pad_maximum_fusion, bf16[352,768]{0,1:T(8,128)(2,1)S(1)} %pad_maximum_fusion, bf16[352,768]{0,1:T(8,128)(2,1)S(1)} %pad_maximum_fusion, bf16[352,768]{0,1:T(8,128)(2,1)S(1)} %pad_maximum_fusion, ...), branch_computations={%region_21.22_spmd, %region_22.23_spmd, %region_23.24_spmd, %regio... | conditional | bytes 3244080 | solution.py:268
  100.7 2.1 %collective-permute-start.20 = (bf16[352,768]{1,0:T(8,128)(2,1)S(1)}, bf16[352,768]{1,0:T(8,128)(2,1)}, u32[]{:S(2)}, u32[]{:S(2)}) collective-permute-start(bf16[352,768]{1,0:T(8,128)(2,1)S(1)} %copy.36), channel_id=1, source_target_pairs={{0,1},{1,0},{2,3},{3,2},{4,5},{5,4},{6,7},{7,6},{8,9},{9,8},{10,11... | collective-permute-start | bytes 1622024 | tf_op jit(solution)/shard_map/cond/branch_1_fun/ppermute | solution.py:263
  102.8 12.3 %collective-permute-done.20 = bf16[352,768]{1,0:T(8,128)(2,1)} collective-permute-done((bf16[352,768]{1,0:T(8,128)(2,1)S(1)}, bf16[352,768]{1,0:T(8,128)(2,1)}, u32[]{:S(2)}, u32[]{:S(2)}) %collective-permute-start.20) | collective-permute-done | bytes 540704 | tf_op jit(solution)/shard_map/cond/branch_1_fun/ppermute | solution.py:263
  115.1 10.9 %all-to-all-done.2 = bf16[8,48,1152]{2,1,0:T(8,128)(2,1)S(1)} async-done(((bf16[8,48,1152]{2,1,0:T(8,128)(2,1)}), bf16[8,48,1152]{2,1,0:T(8,128)(2,1)S(1)}, u32[]{:S(2)}, u32[]{:S(2)}) %all-to-all-start.2) | async-done | bytes 884768 | tf_op jit(solution)/shard_map/all_to_all | solution.py:341
  126.0 2.4 %collective-permute-start.26 = (bf16[384,1152]{1,0:T(8,128)(2,1)S(1)}, bf16[384,1152]{1,0:T(8,128)(2,1)S(1)}, u32[]{:S(2)}, u32[]{:S(2)}) collective-permute-start(bf16[384,1152]{1,0:T(8,128)(2,1)S(1)} %bitcast.39), channel_id=1, source_target_pairs={{0,32},{32,0},{1,33},{33,1},{2,34},{34,2},{3,35},{35,3},{4,36},{36... | collective-permute-start | bytes 2654216 | tf_op jit(solution)/shard_map/ppermute | solution.py:263
  128.4 1.5 mine_back.1.refs_3_
  130.4 2.5 %slot_back.1 = bf16[512,256]{1,0:T(8,128)(2,1)} custom-call(s32[1]{0:T(128)} %bitcast.core_ref, bf16[384,1152]{1,0:T(8,128)(2,1)S(1)} %collective-permute-done.26.theirs_ref, bf16[64,768]{1,0:T(8,128)(2,1)S(1)} %get-tuple-element.152.refs_0_, bf16[96,768]{1,0:T(8,128)(2,1)S(1)} %copy-done.3, bf16[352,768]{1,0:T(8,128)(2,1)} %get-tuple-element.155.refs_2_, ...), custom_call_target="tpu_custom_call" | custom-call | flops 452984832 | bytes 2129922 | tf_op jit(solution)/shard_map/slot_back/pallas_call | solution.py:102
  133.0 25.4 %all-to-all-start.3 = ((bf16[32,16,256]{2,1,0:T(8,128)(2,1)}), bf16[32,16,256]{2,1,0:T(8,128)(2,1)S(1)}, u32[]{:S(2)}, u32[]{:S(2)}) async-start(bf16[32,16,256]{2,1,0:T(8,128)(2,1)} %bitcast.25), calls=%async_computation.3 | async-start | bytes 524288 | tf_op jit(solution)/shard_map/all_to_all | solution.py:357
  158.4 5.8 %weight_grads.1 = (bf16[256,768]{1,0:T(8,128)(2,1)}, bf16[256,768]{1,0:T(8,128)(2,1)}, bf16[768,256]{1,0:T(8,128)(2,1)}) custom-call(s32[1]{0:T(128)} %bitcast.core_ref, bf16[384,1152]{1,0:T(8,128)(2,1)S(1)} %bitcast.41, bf16[384,1152]{1,0:T(8,128)(2,1)S(1)} %collective-permute-done.26.theirs_ref, bf16[512,384]{1,0:T(8,128)(2,1)S(1)} %pad_maximum_fusion.1.rows_ref, ...), custom_call_target="tpu_custom_call" | custom-call | flops 452984832 | bytes 3375106 | tf_op jit(solution)/shard_map/weight_grads/pallas_call | solution.py:102
  164.2 5.6 %all-to-all-done.3 = bf16[32,16,256]{2,1,0:T(8,128)(2,1)S(1)} async-done(((bf16[32,16,256]{2,1,0:T(8,128)(2,1)}), bf16[32,16,256]{2,1,0:T(8,128)(2,1)S(1)}, u32[]{:S(2)}, u32[]{:S(2)}) %all-to-all-start.3) | async-done | bytes 262176 | tf_op jit(solution)/shard_map/all_to_all | solution.py:357
  169.8 0.8 convolution_convert_fusion
  (53 shorter events, 5.6 us)
Async XLA Ops:
  0.6 16.2 %copy-start.7 = (s32[32]{0:T(128)S(1)}, s32[32]{0:T(128)}, u32[]{:S(2)}) copy-start(s32[32]{0:T(128)} %param.41) | copy-start | bytes 388
  0.6 17.5 %copy-start.5 = (bf16[1,256,768]{2,1,0:T(8,128)(2,1)S(1)}, bf16[1,256,768]{2,1,0:T(8,128)(2,1)}, u32[]{:S(2)}) copy-start(bf16[1,256,768]{2,1,0:T(8,128)(2,1)} %param.38) | copy-start | bytes 1179652
  0.7 17.6 %copy-start.4 = (bf16[1,256,768]{2,1,0:T(8,128)(2,1)S(1)}, bf16[1,256,768]{2,1,0:T(8,128)(2,1)}, u32[]{:S(2)}) copy-start(bf16[1,256,768]{2,1,0:T(8,128)(2,1)} %param.37) | copy-start | bytes 1179652
  3.1 27.5 %all-to-all-start = ((bf16[32,24,256]{2,1,0:T(8,128)(2,1)}), bf16[32,24,256]{2,1,0:T(8,128)(2,1)S(1)}, u32[]{:S(2)}, u32[]{:S(2)}) async-start(bf16[32,24,256]{2,1,0:T(8,128)(2,1)} %bitcast.52), calls=%async_computation | async-start | bytes 786432 | tf_op jit(solution)/shard_map/all_to_all | solution.py:297
  18.3 12.3 %copy-start = (bf16[1,768,256]{2,1,0:T(8,128)(2,1)S(1)}, bf16[1,768,256]{2,1,0:T(8,128)(2,1)}, u32[]{:S(2)}) copy-start(bf16[1,768,256]{2,1,0:T(8,128)(2,1)} %param.39) | copy-start | bytes 1179652
  18.5 7.8 %collective-permute-start = (bf16[64,768]{1,0:T(8,128)(2,1)S(1)}, bf16[64,768]{1,0:T(8,128)(2,1)S(1)}, u32[]{:S(2)}, u32[]{:S(2)}) collective-permute-start(bf16[64,768]{1,0:T(8,128)(2,1)S(1)} %param.1), channel_id=1, source_target_pairs={{0,1},{1,0},{2,3},{3,2},{4,5},{5,4},{6,7},{7,6},{8,9},{9,8},{10,11... | collective-permute-start | bytes 294920 | tf_op jit(solution)/shard_map/cond/branch_1_fun/ppermute | solution.py:263
  31.4 6.9 %collective-permute-start.25 = (bf16[384,1152]{1,0:T(8,128)(2,1)S(1)}, bf16[384,1152]{1,0:T(8,128)(2,1)}, u32[]{:S(2)}, u32[]{:S(2)}) collective-permute-start(bf16[384,1152]{1,0:T(8,128)(2,1)S(1)} %get-tuple-element.110), channel_id=1, source_target_pairs={{0,32},{32,0},{1,33},{33,1},{2,34},{34,2},{3,35},{35,3},{4,36},{36... | collective-permute-start | bytes 2654216 | tf_op jit(solution)/shard_map/ppermute | solution.py:263
  38.3 2.3 %copy-start.1 = (bf16[96,768]{1,0:T(8,128)(2,1)S(1)}, bf16[96,768]{1,0:T(8,128)(2,1)}, u32[]{:S(2)}) copy-start(bf16[96,768]{1,0:T(8,128)(2,1)} %slice_bitcast_fusion.3) | copy-start | bytes 442372
  40.6 15.8 %collective-permute-start.5 = (bf16[768,256]{1,0:T(8,128)(2,1)S(1)}, bf16[768,256]{1,0:T(8,128)(2,1)S(1)}, u32[]{:S(2)}, u32[]{:S(2)}) collective-permute-start(bf16[768,256]{1,0:T(8,128)(2,1)S(1)} %get-tuple-element.63), channel_id=1, source_target_pairs={{0,1},{1,0},{2,3},{3,2},{4,5},{5,4},{6,7},{7,6},{8,9},{9,8},{10,11... | collective-permute-start | bytes 1179656 | tf_op jit(solution)/shard_map/cond/branch_1_fun/ppermute | solution.py:263
  42.7 13.7 %collective-permute-start.6 = (bf16[96,768]{1,0:T(8,128)(2,1)S(1)}, bf16[96,768]{1,0:T(8,128)(2,1)S(1)}, u32[]{:S(2)}, u32[]{:S(2)}) collective-permute-start(bf16[96,768]{1,0:T(8,128)(2,1)S(1)} %get-tuple-element.64), channel_id=1, source_target_pairs={{0,1},{1,0},{2,3},{3,2},{4,5},{5,4},{6,7},{7,6},{8,9},{9,8},{10,11... | collective-permute-start | bytes 442376 | tf_op jit(solution)/shard_map/cond/branch_1_fun/ppermute | solution.py:263
  56.4 0.7 copy-start.2
  56.4 7.5 %copy-start.6 = (s32[32,8]{0,1:T(8,128)S(1)}, s32[32,8]{0,1:T(8,128)}, u32[]{:S(2)}) copy-start(s32[32,8]{0,1:T(8,128)} %param.35) | copy-start | bytes 3076
  57.1 32.5 %all-to-all-start.1 = ((bf16[8,48,1152]{2,1,0:T(8,128)(2,1)}), bf16[8,48,1152]{2,1,0:T(8,128)(2,1)S(1)}, u32[]{:S(2)}, u32[]{:S(2)}) async-start(bf16[8,48,1152]{2,1,0:T(8,128)(2,1)} %bitcast.14), calls=%async_computation.1 | async-start | bytes 1769472 | tf_op jit(solution)/shard_map/all_to_all | solution.py:320
  89.8 6.0 %collective-permute-start.15 = (bf16[48,1152]{1,0:T(8,128)(2,1)S(1)}, bf16[48,1152]{1,0:T(8,128)(2,1)S(1)}, u32[]{:S(2)}, u32[]{:S(2)}) collective-permute-start(bf16[48,1152]{1,0:T(8,128)(2,1)S(1)} %param.13), channel_id=1, source_target_pairs={{0,1},{1,0},{2,3},{3,2},{4,5},{5,4},{6,7},{7,6},{8,9},{9,8},{10,11... | collective-permute-start | bytes 331784 | tf_op jit(solution)/shard_map/cond/branch_1_fun/ppermute | solution.py:263
  96.9 29.2 %all-to-all-start.2 = ((bf16[8,48,1152]{2,1,0:T(8,128)(2,1)}), bf16[8,48,1152]{2,1,0:T(8,128)(2,1)S(1)}, u32[]{:S(2)}, u32[]{:S(2)}) async-start(bf16[8,48,1152]{2,1,0:T(8,128)(2,1)} %copies.1), calls=%async_computation.2 | async-start | bytes 1769472 | tf_op jit(solution)/shard_map/all_to_all | solution.py:341
  100.4 28.0 %copy-start.3 = (bf16[96,768]{1,0:T(8,128)(2,1)S(1)}, bf16[96,768]{1,0:T(8,128)(2,1)}, u32[]{:S(2)}) copy-start(bf16[96,768]{1,0:T(8,128)(2,1)} %copy-done.2) | copy-start | bytes 442372
  100.7 14.4 %collective-permute-start.20 = (bf16[352,768]{1,0:T(8,128)(2,1)S(1)}, bf16[352,768]{1,0:T(8,128)(2,1)}, u32[]{:S(2)}, u32[]{:S(2)}) collective-permute-start(bf16[352,768]{1,0:T(8,128)(2,1)S(1)} %copy.36), channel_id=1, source_target_pairs={{0,1},{1,0},{2,3},{3,2},{4,5},{5,4},{6,7},{7,6},{8,9},{9,8},{10,11... | collective-permute-start | bytes 1622024 | tf_op jit(solution)/shard_map/cond/branch_1_fun/ppermute | solution.py:263
  126.0 4.4 %collective-permute-start.26 = (bf16[384,1152]{1,0:T(8,128)(2,1)S(1)}, bf16[384,1152]{1,0:T(8,128)(2,1)S(1)}, u32[]{:S(2)}, u32[]{:S(2)}) collective-permute-start(bf16[384,1152]{1,0:T(8,128)(2,1)S(1)} %bitcast.39), channel_id=1, source_target_pairs={{0,32},{32,0},{1,33},{33,1},{2,34},{34,2},{3,35},{35,3},{4,36},{36... | collective-permute-start | bytes 2654216 | tf_op jit(solution)/shard_map/ppermute | solution.py:263
  133.0 36.8 %all-to-all-start.3 = ((bf16[32,16,256]{2,1,0:T(8,128)(2,1)}), bf16[32,16,256]{2,1,0:T(8,128)(2,1)S(1)}, u32[]{:S(2)}, u32[]{:S(2)}) async-start(bf16[32,16,256]{2,1,0:T(8,128)(2,1)} %bitcast.25), calls=%async_computation.3 | async-start | bytes 524288 | tf_op jit(solution)/shard_map/all_to_all | solution.py:357

commit v11 on v10

--- a/solution.py
+++ b/solution.py
@@ -171,37 +171,26 @@
 def keep_kernel(core_ref, gate_ref, up_ref, down_ref, rows_ref, out_ref):
     units, rows = out_ref.shape[0], rows_ref.shape[0] // 2
     cut = side(core_ref[0], units)
-    out_ref[:, :rows] = dot(gate_ref[cut, :], rows_ref[:rows, :], 1, 1)
-    out_ref[:, rows : 2 * rows] = dot(up_ref[cut, :], rows_ref[:rows, :], 1, 1)
-    out_ref[:, 2 * rows :] = dot(down_ref[cut, :], rows_ref[rows:, :], 1, 1)
-
-
-def half_back(units_ref, weight_refs, cut, rows):
-    gate, up = units_ref[:, :rows], units_ref[:, rows : 2 * rows]
-    width = sum(ref.shape[0] for ref in weight_refs) // 2
-    parts = []
-    done = 0
-    for ref in weight_refs:
-        for_gate = min(max(width - done, 0), ref.shape[0])
-        if for_gate > 0:
-            parts.append(dot(ref[:for_gate, cut], gate, 1, 0))
-        if for_gate < ref.shape[0]:
-            upper = dot(ref[for_gate:, cut], up, 1, 0)
-        done += ref.shape[0]
-    return jnp.concatenate(parts, 0) + upper
-
-
-def mine_back_kernel(core_ref, mine_ref, *refs):
-    weight_refs, out_ref = refs[:-1], refs[-1]
+    out_ref[:, :rows] = dot(gate_ref[cut, :], rows_ref[:rows, :], 1, 1).astype(BF16)
+    out_ref[:, rows : 2 * rows] = dot(up_ref[cut, :], rows_ref[:rows, :], 1, 1).astype(BF16)
+    out_ref[:, 2 * rows :] = dot(down_ref[cut, :], rows_ref[rows:, :], 1, 1).astype(BF16)
+
+
+def half_back(units_ref, weight_ref, cut, rows):
+    width = weight_ref.shape[0] // 2
+    part = dot(weight_ref[:width, cut], units_ref[:, :rows], 1, 0)
+    return part + dot(weight_ref[width:, cut], units_ref[:, rows : 2 * rows], 1, 0)
+
+
+def mine_back_kernel(core_ref, mine_ref, weight_ref, out_ref):
     units, rows = mine_ref.shape[0], out_ref.shape[1]
-    out_ref[...] = half_back(mine_ref, weight_refs, side(core_ref[0], units), rows)
-
-
-def back_kernel(capacity, core_ref, theirs_ref, *refs):
-    weight_refs, (total_ref, out_ref) = refs[:-2], refs[-2:]
+    out_ref[...] = half_back(mine_ref, weight_ref, side(core_ref[0], units), rows)
+
+
+def back_kernel(capacity, core_ref, theirs_ref, weight_ref, total_ref, out_ref):
     units, rows = theirs_ref.shape[0], total_ref.shape[1]
     out_rows = out_ref.shape[0]
-    total = total_ref[...] + half_back(theirs_ref, weight_refs, side(1 - core_ref[0], units), rows)
+    total = total_ref[...] + half_back(theirs_ref, weight_ref, side(1 - core_ref[0], units), rows)
     groups = rows // capacity
     padded = out_rows // groups
     row = lax.broadcasted_iota(jnp.int32, (out_rows, groups), 0)
@@ -311,24 +300,21 @@
         functools.partial(away_kernel, capacity), "away_partials", [wide, recv.shape], feeds + (recv,), 1
     )
     arrived = pair_permute(away, "core")
-    kept = call(keep_kernel, "keep_partials", [wide], feeds + (routed,), 1, dtype=F32)[0]
-    chip_sum = (kept + arrived.astype(F32)).astype(BF16)
+    kept = call(keep_kernel, "keep_partials", [wide], feeds + (routed,), 1)[0]
+    chip_sum = (kept.astype(F32) + arrived.astype(F32)).astype(BF16)
 
     chip_sum, routed, weight_2 = lax.optimization_barrier((chip_sum, routed, weight_2))
 
     piece = (half // n_y, 3 * rows)
     blocks = lax.all_to_all(chip_sum.reshape((n_y,) + piece), "y", 0, 0, tiled=True)
-    mate_routed, weight_2, routes, sign_bits = lax.optimization_barrier(
-        swap(which, (routed, weight_2)) + (routes, sign_bits)
-    )
+    mate_routed, weight_2 = swap(which, (routed, weight_2))
     padded = -(-capacity // 16) * 16
     picker = jnp.take(slot_picker(routes, experts, capacity), partner, axis=0)
     picker = jnp.pad(picker, ((0, 0), (0, padded - capacity), (0, 0))).reshape(experts * padded, tok_count)
     flip_signs = (1 - 2 * lax.dynamic_index_in_dim(sign_bits, mate, 0, keepdims=False)).astype(BF16)
     rotation = sylvester(HBLOCK) * flip_signs[:, None]
-    mate_rows = jnp.concatenate([mate_routed[:rows].T, mate_routed[rows:].T], 0)
-    blocks, mate_rows, weight_2, picker, rotation = lax.optimization_barrier(
-        (blocks, mate_rows, weight_2, picker, rotation)
+    blocks, mate_routed, weight_2, picker, rotation = lax.optimization_barrier(
+        (blocks, mate_routed, weight_2, picker, rotation)
     )
     sums = jnp.sum(blocks.astype(F32), axis=0)
     gate_sum, up_sum, hid_grad = sums[:, :rows], sums[:, rows : 2 * rows], sums[:, 2 * rows :]
@@ -340,18 +326,19 @@
     acts, weight_3 = lax.optimization_barrier((swap(which, acts), weight_3))
     mine = lax.all_to_all(copies(acts, n_y), "y", 0, 0, tiled=True).reshape(wide)
     weight_3 = swap(which, weight_3)
-    mine, weight_3 = lax.optimization_barrier((mine, weight_3))
+    mate_rows = jnp.concatenate([mate_routed[:rows].T, mate_routed[rows:].T], 0)
+    weights = jnp.concatenate([weight_1, weight_2, weight_3], 0)
+    mine, weights, mate_rows = lax.optimization_barrier((mine, weights, mate_rows))
     theirs = pair_permute(mine, "core")
 
-    weights = (weight_1, weight_2, weight_3)
     mine_back = call(
-        mine_back_kernel, "mine_back", [(width, rows)], (core_arg, mine) + weights, 1, dtype=F32
+        mine_back_kernel, "mine_back", [(width, rows)], (core_arg, mine, weights), 1, dtype=F32
     )[0]
     slot_back = call(
         functools.partial(back_kernel, capacity),
         "slot_back",
         [(experts * padded, width)],
-        (core_arg, theirs) + weights + (mine_back,),
+        (core_arg, theirs, weights, mine_back),
         1,
     )[0]
     returned = lax.all_to_all(slot_back.reshape(experts, padded, width), BITS, 0, 0, tiled=True)

time: 172 us -> 155 us (0.901)
  waiting for transfers between devices: 75.1 us -> 57.5 us
  Pallas kernels: 14.4 us -> 12.2 us
  other arithmetic: 3.96 us -> 5.87 us
  starting transfers between devices: 68.9 us -> 70.8 us
    all_to_all x1, waiting for transfers between devices: 23.5 us -> 8.13 us  [shards(): lax.all_to_all(chip_sum.reshape((n_y,) + piece), 'y', 0, 0, tiled=True)]
    all_to_all x1, waiting for transfers between devices: 3.16 us -> 0.64 us  [shards(): recv = lax.all_to_all(send, BITS, 0, 0, tiled=True)]
    pallas_call x6, Pallas kernels: 13.4 us -> 11.2 us  [call(): pl.pallas_call(kernel, out_shape=outs, in_specs=[smem] * scalars + [rest]...]
  transfers between devices with their start and end apart: 11 -> 11, of which waited for: 9 -> 9; matrix products, arithmetic and copies ran while one was open for 3% -> 4% of each run, Pallas kernels for 5% -> 4%
where the time goes in v11:
time: 155 us; the launch traced here: 153 us
  starting transfers between devices  70.8 us (46%)
  waiting for transfers between devices  57.5 us (37%)
  Pallas kernels  12.2 us (8%)
  other arithmetic  5.87 us (4%)
  between operations  3.59 us (2%)
  local copies, waits for them, and re-layouts  2.47 us (2%)
    ppermute x7, waiting for transfers between devices, pair_permute(): return lax.ppermute(x, axis, [(0, 1), (1, 0)])  33.6 us
    all_to_all x1, starting transfers between devices, shards(): lax.all_to_all(slot_back.reshape(experts, padded, width), BITS, 0, 0, til...  25.9 us
    ppermute x7, starting transfers between devices, pair_permute(): return lax.ppermute(x, axis, [(0, 1), (1, 0)])  20.6 us
    all_to_all x1, starting transfers between devices, shards(): recv = lax.all_to_all(send, BITS, 0, 0, tiled=True)  13.9 us
    pallas_call x6, Pallas kernels, call(): pl.pallas_call(kernel, out_shape=outs, in_specs=[smem] * scalars + [rest]...  11.2 us
    all_to_all x1, waiting for transfers between devices, shards(): lax.all_to_all(copies(acts, n_y), 'y', 0, 0, tiled=True).reshape(wide)  9.5 us
    all_to_all x1, waiting for transfers between devices, shards(): lax.all_to_all(chip_sum.reshape((n_y,) + piece), 'y', 0, 0, tiled=True)  8.13 us
    all_to_all x1, starting transfers between devices, shards(): lax.all_to_all(chip_sum.reshape((n_y,) + piece), 'y', 0, 0, tiled=True)  6.8 us
  transfers between devices with their start and end apart: 11, of which 9 were waited for; matrix products, arithmetic and copies ran while one was open for 4% of the time, Pallas kernels for 4%

profile of v11, /device:TPU:1, one launch (start us, length us, event | category | flops | bytes accessed | tf_op | source)
XLA Modules:
  0.0 153.4 jit_solution(4116530904984131058)
XLA Ops:
  0.7 2.4 %pick_rows.1 = bf16[768,256]{1,0:T(8,128)(2,1)} custom-call(s32[8,32]{1,0:T(8,128)} %bitcast.53, f32[8,32]{1,0:T(8,128)} %bitcast.57, bf16[32,256]{1,0:T(8,128)(2,1)} %tok_in.1, bf16[32,256]{1,0:T(8,128)(2,1)} %grad_in.1), custom_call_target="tpu_custom_call" | custom-call | flops 452984832 | bytes 427008 | tf_op jit(solution)/shard_map/pick_rows/pallas_call | solution.py:102
  3.1 13.9 %all-to-all-start = ((bf16[32,24,256]{2,1,0:T(8,128)(2,1)}), bf16[32,24,256]{2,1,0:T(8,128)(2,1)S(1)}, u32[]{:S(2)}, u32[]{:S(2)}) async-start(bf16[32,24,256]{2,1,0:T(8,128)(2,1)} %bitcast.52), calls=%async_computation | async-start | bytes 786432 | tf_op jit(solution)/shard_map/all_to_all | solution.py:286
  18.6 10.2 %conditional.4 = (bf16[64,768]{1,0:T(8,128)(2,1)S(1)}) conditional(s32[]{:T(128)} %clamp.2, bf16[64,768]{1,0:T(8,128)(2,1)S(1)} %slice_bitcast_fusion.4, bf16[64,768]{1,0:T(8,128)(2,1)S(1)} %slice_bitcast_fusion.4, bf16[64,768]{1,0:T(8,128)(2,1)S(1)} %slice_bitcast_fusion.4, ...), branch_computations={%region_0.0_spmd, %region_1.0_spmd, %region_2.0_spmd, %region_3.0_... | conditional | bytes 589872 | solution.py:257
  18.6 3.1 %collective-permute-start.2 = (bf16[64,768]{1,0:T(8,128)(2,1)S(1)}, bf16[64,768]{1,0:T(8,128)(2,1)S(1)}, u32[]{:S(2)}, u32[]{:S(2)}) collective-permute-start(bf16[64,768]{1,0:T(8,128)(2,1)S(1)} %param.3), channel_id=1, source_target_pairs={{0,4},{4,0},{1,5},{5,1},{2,6},{6,2},{3,7},{7,3},{8,12},{12,8},{9,1... | collective-permute-start | bytes 294920 | tf_op jit(solution)/shard_map/cond/branch_3_fun/ppermute | solution.py:252
  21.8 7.1 %collective-permute-done.2 = bf16[64,768]{1,0:T(8,128)(2,1)S(1)} collective-permute-done((bf16[64,768]{1,0:T(8,128)(2,1)S(1)}, bf16[64,768]{1,0:T(8,128)(2,1)S(1)}, u32[]{:S(2)}, u32[]{:S(2)}) %collective-permute-start.2) | collective-permute-done | bytes 98336 | tf_op jit(solution)/shard_map/cond/branch_3_fun/ppermute | solution.py:252
  29.0 1.1 pad_maximum_fusion.1
  30.7 0.8 away_partials.1
  31.5 4.4 %collective-permute-start.25 = (bf16[384,1152]{1,0:T(8,128)(2,1)S(1)}, bf16[384,1152]{1,0:T(8,128)(2,1)}, u32[]{:S(2)}, u32[]{:S(2)}) collective-permute-start(bf16[384,1152]{1,0:T(8,128)(2,1)S(1)} %get-tuple-element.107), channel_id=1, source_target_pairs={{0,32},{32,0},{1,33},{33,1},{2,34},{34,2},{3,35},{35,3},{4,36},{36... | collective-permute-start | bytes 2654216 | tf_op jit(solution)/shard_map/ppermute | solution.py:252
  38.1 2.3 %add_convert_fusion = bf16[384,1152]{1,0:T(8,128)(2,1)} fusion(bf16[384,1152]{1,0:T(8,128)(2,1)} %collective-permute-done.25, bf16[384,1152]{1,0:T(8,128)(2,1)S(1)} %keep_partials.1), kind=kLoop, calls=%fused_computation.2 | loop fusion | flops 1769472 | bytes 2654208 | tf_op jit(solution)/shard_map/convert_element_type | solution.py:304
  40.4 6.8 %all-to-all-start.1 = ((bf16[8,48,1152]{2,1,0:T(8,128)(2,1)}), bf16[8,48,1152]{2,1,0:T(8,128)(2,1)S(1)}, u32[]{:S(2)}, u32[]{:S(2)}) async-start(bf16[8,48,1152]{2,1,0:T(8,128)(2,1)} %bitcast.14), calls=%async_computation.1 | async-start | bytes 1769472 | tf_op jit(solution)/shard_map/all_to_all | solution.py:309
  49.6 15.1 %conditional.5 = ((bf16[768,256]{1,0:T(8,128)(2,1)S(1)}, bf16[96,768]{1,0:T(8,128)(2,1)S(1)})) conditional(s32[]{:T(128)} %clamp.2, (bf16[768,256]{1,0:T(8,128)(2,1)S(1)}, bf16[96,768]{1,0:T(8,128)(2,1)S(1)}) %tuple.92, (bf16[768,256]{1,0:T(8,128)(2,1)S(1)}, bf16[96,768]{1,0:T(8,128)(2,1)S(1)}) %tuple.92, ...), branch_computations={%region_6.0_spmd, %region_7.0_spmd, %region_8.0_spmd, %region_9.0_... | conditional | bytes 3244136 | solution.py:257
  49.7 2.7 %collective-permute-start.9 = (bf16[768,256]{1,0:T(8,128)(2,1)S(1)}, bf16[768,256]{1,0:T(8,128)(2,1)S(1)}, u32[]{:S(2)}, u32[]{:S(2)}) collective-permute-start(bf16[768,256]{1,0:T(8,128)(2,1)S(1)} %get-tuple-element.67), channel_id=1, source_target_pairs={{0,4},{4,0},{1,5},{5,1},{2,6},{6,2},{3,7},{7,3},{8,12},{12,8},{9,1... | collective-permute-start | bytes 1179656 | tf_op jit(solution)/shard_map/cond/branch_3_fun/ppermute | solution.py:252
  52.3 2.6 %collective-permute-start.10 = (bf16[96,768]{1,0:T(8,128)(2,1)S(1)}, bf16[96,768]{1,0:T(8,128)(2,1)S(1)}, u32[]{:S(2)}, u32[]{:S(2)}) collective-permute-start(bf16[96,768]{1,0:T(8,128)(2,1)S(1)} %get-tuple-element.68), channel_id=1, source_target_pairs={{0,4},{4,0},{1,5},{5,1},{2,6},{6,2},{3,7},{7,3},{8,12},{12,8},{9,1... | collective-permute-start | bytes 442376 | tf_op jit(solution)/shard_map/cond/branch_3_fun/ppermute | solution.py:252
  55.0 9.8 %collective-permute-done.10 = bf16[96,768]{1,0:T(8,128)(2,1)S(1)} collective-permute-done((bf16[96,768]{1,0:T(8,128)(2,1)S(1)}, bf16[96,768]{1,0:T(8,128)(2,1)S(1)}, u32[]{:S(2)}, u32[]{:S(2)}) %collective-permute-start.10) | collective-permute-done | bytes 147488 | tf_op jit(solution)/shard_map/cond/branch_3_fun/ppermute | solution.py:252
  64.8 8.1 %all-to-all-done.1 = bf16[8,48,1152]{2,1,0:T(8,128)(2,1)S(1)} async-done(((bf16[8,48,1152]{2,1,0:T(8,128)(2,1)}), bf16[8,48,1152]{2,1,0:T(8,128)(2,1)S(1)}, u32[]{:S(2)}, u32[]{:S(2)}) %all-to-all-start.1) | async-done | bytes 884768 | tf_op jit(solution)/shard_map/all_to_all | solution.py:309
  73.1 6.1 %conditional.6 = (bf16[48,1152]{1,0:T(8,128)(2,1)S(1)}) conditional(s32[]{:T(128)} %clamp.2, bf16[48,1152]{1,0:T(8,128)(2,1)S(1)} %pad_maximum_fusion.3, bf16[48,1152]{1,0:T(8,128)(2,1)S(1)} %pad_maximum_fusion.3, bf16[48,1152]{1,0:T(8,128)(2,1)S(1)} %pad_maximum_fusion.3, ...), branch_computations={%region_15.16_spmd, %region_16.17_spmd, %region_17.18_spmd, %regio... | conditional | bytes 663600 | solution.py:257
  73.1 2.7 %collective-permute-start.17 = (bf16[48,1152]{1,0:T(8,128)(2,1)S(1)}, bf16[48,1152]{1,0:T(8,128)(2,1)S(1)}, u32[]{:S(2)}, u32[]{:S(2)}) collective-permute-start(bf16[48,1152]{1,0:T(8,128)(2,1)S(1)} %param.15), channel_id=1, source_target_pairs={{0,4},{4,0},{1,5},{5,1},{2,6},{6,2},{3,7},{7,3},{8,12},{12,8},{9,1... | collective-permute-start | bytes 331784 | tf_op jit(solution)/shard_map/cond/branch_3_fun/ppermute | solution.py:252
  75.8 3.4 %collective-permute-done.17 = bf16[48,1152]{1,0:T(8,128)(2,1)S(1)} collective-permute-done((bf16[48,1152]{1,0:T(8,128)(2,1)S(1)}, bf16[48,1152]{1,0:T(8,128)(2,1)S(1)}, u32[]{:S(2)}, u32[]{:S(2)}) %collective-permute-start.17) | collective-permute-done | bytes 110624 | tf_op jit(solution)/shard_map/cond/branch_3_fun/ppermute | solution.py:252
  79.2 1.0 copies.1
  80.2 3.7 %all-to-all-start.2 = ((bf16[8,48,1152]{2,1,0:T(8,128)(2,1)}), bf16[8,48,1152]{2,1,0:T(8,128)(2,1)S(1)}, u32[]{:S(2)}, u32[]{:S(2)}) async-start(bf16[8,48,1152]{2,1,0:T(8,128)(2,1)} %copies.1), calls=%async_computation.2 | async-start | bytes 1769472 | tf_op jit(solution)/shard_map/all_to_all | solution.py:327
  84.1 14.7 %conditional.7 = (bf16[352,768]{1,0:T(8,128)(2,1)}) conditional(s32[]{:T(128)} %clamp.2, bf16[352,768]{0,1:T(8,128)(2,1)S(1)} %copy-done.1, bf16[352,768]{0,1:T(8,128)(2,1)S(1)} %copy-done.1, bf16[352,768]{0,1:T(8,128)(2,1)S(1)} %copy-done.1, bf16[352,768]{0,1:T(8,128)(2,1)S(1)} %copy-done.1, ...), branch_computations={%region_21.22_spmd, %region_22.23_spmd, %region_23.24_spmd, %regio... | conditional | bytes 3244080 | solution.py:257
  84.4 2.7 %collective-permute-start.22 = (bf16[352,768]{1,0:T(8,128)(2,1)S(1)}, bf16[352,768]{1,0:T(8,128)(2,1)}, u32[]{:S(2)}, u32[]{:S(2)}) collective-permute-start(bf16[352,768]{1,0:T(8,128)(2,1)S(1)} %copy.36), channel_id=1, source_target_pairs={{0,4},{4,0},{1,5},{5,1},{2,6},{6,2},{3,7},{7,3},{8,12},{12,8},{9,1... | collective-permute-start | bytes 1622024 | tf_op jit(solution)/shard_map/cond/branch_3_fun/ppermute | solution.py:252
  87.1 11.8 %collective-permute-done.22 = bf16[352,768]{1,0:T(8,128)(2,1)} collective-permute-done((bf16[352,768]{1,0:T(8,128)(2,1)S(1)}, bf16[352,768]{1,0:T(8,128)(2,1)}, u32[]{:S(2)}, u32[]{:S(2)}) %collective-permute-start.22) | collective-permute-done | bytes 540704 | tf_op jit(solution)/shard_map/cond/branch_3_fun/ppermute | solution.py:252
  98.9 1.1 pad_maximum_fusion.weight_ref
  100.0 9.5 %all-to-all-done.2 = bf16[8,48,1152]{2,1,0:T(8,128)(2,1)S(1)} async-done(((bf16[8,48,1152]{2,1,0:T(8,128)(2,1)}), bf16[8,48,1152]{2,1,0:T(8,128)(2,1)S(1)}, u32[]{:S(2)}, u32[]{:S(2)}) %all-to-all-start.2) | async-done | bytes 884768 | tf_op jit(solution)/shard_map/all_to_all | solution.py:327
  109.5 2.4 %collective-permute-start.26 = (bf16[384,1152]{1,0:T(8,128)(2,1)S(1)}, bf16[384,1152]{1,0:T(8,128)(2,1)S(1)}, u32[]{:S(2)}, u32[]{:S(2)}) collective-permute-start(bf16[384,1152]{1,0:T(8,128)(2,1)S(1)} %bitcast.39), channel_id=1, source_target_pairs={{0,32},{32,0},{1,33},{33,1},{2,34},{34,2},{3,35},{35,3},{4,36},{36... | collective-permute-start | bytes 2654216 | tf_op jit(solution)/shard_map/ppermute | solution.py:252
  112.3 1.6 %collective-permute-done.26.theirs_ref = bf16[384,1152]{1,0:T(8,128)(2,1)S(1)} collective-permute-done((bf16[384,1152]{1,0:T(8,128)(2,1)S(1)}, bf16[384,1152]{1,0:T(8,128)(2,1)S(1)}, u32[]{:S(2)}, u32[]{:S(2)}) %collective-permute-start.26) | collective-permute-done | bytes 884768 | tf_op jit(solution)/shard_map/ppermute | solution.py:252
  113.9 1.4 slot_back.1
  115.4 25.9 %all-to-all-start.3 = ((bf16[32,16,256]{2,1,0:T(8,128)(2,1)}), bf16[32,16,256]{2,1,0:T(8,128)(2,1)S(1)}, u32[]{:S(2)}, u32[]{:S(2)}) async-start(bf16[32,16,256]{2,1,0:T(8,128)(2,1)} %bitcast.25), calls=%async_computation.3 | async-start | bytes 524288 | tf_op jit(solution)/shard_map/all_to_all | solution.py:344
  141.3 5.8 %weight_grads.1 = (bf16[256,768]{1,0:T(8,128)(2,1)}, bf16[256,768]{1,0:T(8,128)(2,1)}, bf16[768,256]{1,0:T(8,128)(2,1)}) custom-call(s32[1]{0:T(128)} %bitcast.core_ref, bf16[384,1152]{1,0:T(8,128)(2,1)S(1)} %bitcast.41, bf16[384,1152]{1,0:T(8,128)(2,1)S(1)} %collective-permute-done.26.theirs_ref, bf16[512,384]{1,0:T(8,128)(2,1)S(1)} %pad_maximum_fusion.2.rows_ref, ...), custom_call_target="tpu_custom_call" | custom-call | flops 452984832 | bytes 3375106 | tf_op jit(solution)/shard_map/weight_grads/pallas_call | solution.py:102
  147.0 5.6 %all-to-all-done.3 = bf16[32,16,256]{2,1,0:T(8,128)(2,1)S(1)} async-done(((bf16[32,16,256]{2,1,0:T(8,128)(2,1)}), bf16[32,16,256]{2,1,0:T(8,128)(2,1)S(1)}, u32[]{:S(2)}, u32[]{:S(2)}) %all-to-all-start.3) | async-done | bytes 262176 | tf_op jit(solution)/shard_map/all_to_all | solution.py:344
  152.6 0.8 convolution_convert_fusion
  (50 shorter events, 5.4 us)
Async XLA Ops:
  0.6 16.3 %copy-start.5 = (s32[32]{0:T(128)S(1)}, s32[32]{0:T(128)}, u32[]{:S(2)}) copy-start(s32[32]{0:T(128)} %param.41) | copy-start | bytes 388
  0.6 17.6 %copy-start.2 = (bf16[1,256,768]{2,1,0:T(8,128)(2,1)S(1)}, bf16[1,256,768]{2,1,0:T(8,128)(2,1)}, u32[]{:S(2)}) copy-start(bf16[1,256,768]{2,1,0:T(8,128)(2,1)} %param.37) | copy-start | bytes 1179652
  3.1 15.3 %copy-start.3 = (bf16[1,256,768]{2,1,0:T(8,128)(2,1)S(1)}, bf16[1,256,768]{2,1,0:T(8,128)(2,1)}, u32[]{:S(2)}) copy-start(bf16[1,256,768]{2,1,0:T(8,128)(2,1)} %param.38) | copy-start | bytes 1179652
  3.1 27.7 %all-to-all-start = ((bf16[32,24,256]{2,1,0:T(8,128)(2,1)}), bf16[32,24,256]{2,1,0:T(8,128)(2,1)S(1)}, u32[]{:S(2)}, u32[]{:S(2)}) async-start(bf16[32,24,256]{2,1,0:T(8,128)(2,1)} %bitcast.52), calls=%async_computation | async-start | bytes 786432 | tf_op jit(solution)/shard_map/all_to_all | solution.py:286
  18.6 10.2 %collective-permute-start.2 = (bf16[64,768]{1,0:T(8,128)(2,1)S(1)}, bf16[64,768]{1,0:T(8,128)(2,1)S(1)}, u32[]{:S(2)}, u32[]{:S(2)}) collective-permute-start(bf16[64,768]{1,0:T(8,128)(2,1)S(1)} %param.3), channel_id=1, source_target_pairs={{0,4},{4,0},{1,5},{5,1},{2,6},{6,2},{3,7},{7,3},{8,12},{12,8},{9,1... | collective-permute-start | bytes 294920 | tf_op jit(solution)/shard_map/cond/branch_3_fun/ppermute | solution.py:252
  28.9 1.9 %copy-start = (bf16[1,768,256]{2,1,0:T(8,128)(2,1)S(1)}, bf16[1,768,256]{2,1,0:T(8,128)(2,1)}, u32[]{:S(2)}) copy-start(bf16[1,768,256]{2,1,0:T(8,128)(2,1)} %param.39) | copy-start | bytes 1179652
  30.1 7.2 %copy-start.4 = (s32[32,8]{0,1:T(8,128)S(1)}, s32[32,8]{0,1:T(8,128)}, u32[]{:S(2)}) copy-start(s32[32,8]{0,1:T(8,128)} %param.35) | copy-start | bytes 3076
  31.5 6.6 %collective-permute-start.25 = (bf16[384,1152]{1,0:T(8,128)(2,1)S(1)}, bf16[384,1152]{1,0:T(8,128)(2,1)}, u32[]{:S(2)}, u32[]{:S(2)}) collective-permute-start(bf16[384,1152]{1,0:T(8,128)(2,1)S(1)} %get-tuple-element.107), channel_id=1, source_target_pairs={{0,32},{32,0},{1,33},{33,1},{2,34},{34,2},{3,35},{35,3},{4,36},{36... | collective-permute-start | bytes 2654216 | tf_op jit(solution)/shard_map/ppermute | solution.py:252
  40.4 32.5 %all-to-all-start.1 = ((bf16[8,48,1152]{2,1,0:T(8,128)(2,1)}), bf16[8,48,1152]{2,1,0:T(8,128)(2,1)S(1)}, u32[]{:S(2)}, u32[]{:S(2)}) async-start(bf16[8,48,1152]{2,1,0:T(8,128)(2,1)} %bitcast.14), calls=%async_computation.1 | async-start | bytes 1769472 | tf_op jit(solution)/shard_map/all_to_all | solution.py:309
  49.7 15.1 %collective-permute-start.9 = (bf16[768,256]{1,0:T(8,128)(2,1)S(1)}, bf16[768,256]{1,0:T(8,128)(2,1)S(1)}, u32[]{:S(2)}, u32[]{:S(2)}) collective-permute-start(bf16[768,256]{1,0:T(8,128)(2,1)S(1)} %get-tuple-element.67), channel_id=1, source_target_pairs={{0,4},{4,0},{1,5},{5,1},{2,6},{6,2},{3,7},{7,3},{8,12},{12,8},{9,1... | collective-permute-start | bytes 1179656 | tf_op jit(solution)/shard_map/cond/branch_3_fun/ppermute | solution.py:252
  52.3 12.4 %collective-permute-start.10 = (bf16[96,768]{1,0:T(8,128)(2,1)S(1)}, bf16[96,768]{1,0:T(8,128)(2,1)S(1)}, u32[]{:S(2)}, u32[]{:S(2)}) collective-permute-start(bf16[96,768]{1,0:T(8,128)(2,1)S(1)} %get-tuple-element.68), channel_id=1, source_target_pairs={{0,4},{4,0},{1,5},{5,1},{2,6},{6,2},{3,7},{7,3},{8,12},{12,8},{9,1... | collective-permute-start | bytes 442376 | tf_op jit(solution)/shard_map/cond/branch_3_fun/ppermute | solution.py:252
  73.1 6.0 %collective-permute-start.17 = (bf16[48,1152]{1,0:T(8,128)(2,1)S(1)}, bf16[48,1152]{1,0:T(8,128)(2,1)S(1)}, u32[]{:S(2)}, u32[]{:S(2)}) collective-permute-start(bf16[48,1152]{1,0:T(8,128)(2,1)S(1)} %param.15), channel_id=1, source_target_pairs={{0,4},{4,0},{1,5},{5,1},{2,6},{6,2},{3,7},{7,3},{8,12},{12,8},{9,1... | collective-permute-start | bytes 331784 | tf_op jit(solution)/shard_map/cond/branch_3_fun/ppermute | solution.py:252
  80.2 3.7 %copy-start.1 = (bf16[352,768]{0,1:T(8,128)(2,1)S(1)}, bf16[352,768]{0,1:T(8,128)(2,1)}, u32[]{:S(2)}) copy-start(bf16[352,768]{0,1:T(8,128)(2,1)} %pad_maximum_fusion.1) | copy-start | bytes 1622020
  80.2 29.3 %all-to-all-start.2 = ((bf16[8,48,1152]{2,1,0:T(8,128)(2,1)}), bf16[8,48,1152]{2,1,0:T(8,128)(2,1)S(1)}, u32[]{:S(2)}, u32[]{:S(2)}) async-start(bf16[8,48,1152]{2,1,0:T(8,128)(2,1)} %copies.1), calls=%async_computation.2 | async-start | bytes 1769472 | tf_op jit(solution)/shard_map/all_to_all | solution.py:327
  84.4 14.4 %collective-permute-start.22 = (bf16[352,768]{1,0:T(8,128)(2,1)S(1)}, bf16[352,768]{1,0:T(8,128)(2,1)}, u32[]{:S(2)}, u32[]{:S(2)}) collective-permute-start(bf16[352,768]{1,0:T(8,128)(2,1)S(1)} %copy.36), channel_id=1, source_target_pairs={{0,4},{4,0},{1,5},{5,1},{2,6},{6,2},{3,7},{7,3},{8,12},{12,8},{9,1... | collective-permute-start | bytes 1622024 | tf_op jit(solution)/shard_map/cond/branch_3_fun/ppermute | solution.py:252
  109.5 4.4 %collective-permute-start.26 = (bf16[384,1152]{1,0:T(8,128)(2,1)S(1)}, bf16[384,1152]{1,0:T(8,128)(2,1)S(1)}, u32[]{:S(2)}, u32[]{:S(2)}) collective-permute-start(bf16[384,1152]{1,0:T(8,128)(2,1)S(1)} %bitcast.39), channel_id=1, source_target_pairs={{0,32},{32,0},{1,33},{33,1},{2,34},{34,2},{3,35},{35,3},{4,36},{36... | collective-permute-start | bytes 2654216 | tf_op jit(solution)/shard_map/ppermute | solution.py:252
  115.4 37.2 %all-to-all-start.3 = ((bf16[32,16,256]{2,1,0:T(8,128)(2,1)}), bf16[32,16,256]{2,1,0:T(8,128)(2,1)S(1)}, u32[]{:S(2)}, u32[]{:S(2)}) async-start(bf16[32,16,256]{2,1,0:T(8,128)(2,1)} %bitcast.25), calls=%async_computation.3 | async-start | bytes 524288 | tf_op jit(solution)/shard_map/all_to_all | solution.py:344

commit v12 on v11

--- a/solution.py
+++ b/solution.py
@@ -168,12 +168,17 @@
     out_ref[:, 2 * rows :] = dot(down_ref[cut, :], rows_ref[rows:, :], 1, 1).astype(BF16)
 
 
-def keep_kernel(core_ref, gate_ref, up_ref, down_ref, rows_ref, out_ref):
+def keep_kernel(core_ref, gate_ref, up_ref, down_ref, rows_ref, add_ref, out_ref):
     units, rows = out_ref.shape[0], rows_ref.shape[0] // 2
     cut = side(core_ref[0], units)
-    out_ref[:, :rows] = dot(gate_ref[cut, :], rows_ref[:rows, :], 1, 1).astype(BF16)
-    out_ref[:, rows : 2 * rows] = dot(up_ref[cut, :], rows_ref[:rows, :], 1, 1).astype(BF16)
-    out_ref[:, 2 * rows :] = dot(down_ref[cut, :], rows_ref[rows:, :], 1, 1).astype(BF16)
+
+    def put(k, part):
+        lanes = slice(k * rows, (k + 1) * rows)
+        out_ref[:, lanes] = (part + add_ref[:, lanes].astype(F32)).astype(BF16)
+
+    put(0, dot(gate_ref[cut, :], rows_ref[:rows, :], 1, 1))
+    put(1, dot(up_ref[cut, :], rows_ref[:rows, :], 1, 1))
+    put(2, dot(down_ref[cut, :], rows_ref[rows:, :], 1, 1))
 
 
 def half_back(units_ref, weight_ref, cut, rows):
@@ -300,8 +305,7 @@
         functools.partial(away_kernel, capacity), "away_partials", [wide, recv.shape], feeds + (recv,), 1
     )
     arrived = pair_permute(away, "core")
-    kept = call(keep_kernel, "keep_partials", [wide], feeds + (routed,), 1)[0]
-    chip_sum = (kept.astype(F32) + arrived.astype(F32)).astype(BF16)
+    chip_sum = call(keep_kernel, "keep_partials", [wide], feeds + (routed, arrived), 1)[0]
 
     chip_sum, routed, weight_2 = lax.optimization_barrier((chip_sum, routed, weight_2))
 
@@ -309,13 +313,7 @@
     blocks = lax.all_to_all(chip_sum.reshape((n_y,) + piece), "y", 0, 0, tiled=True)
     mate_routed, weight_2 = swap(which, (routed, weight_2))
     padded = -(-capacity // 16) * 16
-    picker = jnp.take(slot_picker(routes, experts, capacity), partner, axis=0)
-    picker = jnp.pad(picker, ((0, 0), (0, padded - capacity), (0, 0))).reshape(experts * padded, tok_count)
-    flip_signs = (1 - 2 * lax.dynamic_index_in_dim(sign_bits, mate, 0, keepdims=False)).astype(BF16)
-    rotation = sylvester(HBLOCK) * flip_signs[:, None]
-    blocks, mate_routed, weight_2, picker, rotation = lax.optimization_barrier(
-        (blocks, mate_routed, weight_2, picker, rotation)
-    )
+    blocks, mate_routed, weight_2 = lax.optimization_barrier((blocks, mate_routed, weight_2))
     sums = jnp.sum(blocks.astype(F32), axis=0)
     gate_sum, up_sum, hid_grad = sums[:, :rows], sums[:, rows : 2 * rows], sums[:, 2 * rows :]
     sig = jax.nn.sigmoid(gate_sum)
@@ -341,7 +339,12 @@
         (core_arg, theirs, weights, mine_back),
         1,
     )[0]
+    slot_back, routes, sign_bits = lax.optimization_barrier((slot_back, routes, sign_bits))
     returned = lax.all_to_all(slot_back.reshape(experts, padded, width), BITS, 0, 0, tiled=True)
+    picker = jnp.take(slot_picker(routes, experts, capacity), partner, axis=0)
+    picker = jnp.pad(picker, ((0, 0), (0, padded - capacity), (0, 0))).reshape(experts * padded, tok_count)
+    flip_signs = (1 - 2 * lax.dynamic_index_in_dim(sign_bits, mate, 0, keepdims=False)).astype(BF16)
+    rotation = sylvester(HBLOCK) * flip_signs[:, None]
     input_grad = dot(picker, returned.reshape(experts * padded, width), 0, 0).astype(BF16)
 
     gate_new, up_new, down_new = call(

time: 155 us -> 139 us (0.90)
  starting transfers between devices: 70.8 us -> 49.9 us
  waiting for transfers between devices: 57.5 us -> 64.6 us
  other arithmetic: 5.87 us -> 2.65 us
    ppermute x7 -> x2, waiting for transfers between devices: 33.6 us -> 2.03 us  [pair_permute(): return lax.ppermute(x, axis, [(0, 1), (1, 0)])]
    all_to_all x1, waiting for transfers between devices: 8.13 us -> 25.7 us  [shards(): lax.all_to_all(chip_sum.reshape((n_y,) + piece), 'y', 0, 0, tiled=True)]
    ppermute x7 -> x2, starting transfers between devices: 20.6 us -> 8.95 us  [pair_permute(): return lax.ppermute(x, axis, [(0, 1), (1, 0)])]
    all_to_all x1, waiting for transfers between devices: 9.5 us -> 21 us  [shards(): lax.all_to_all(copies(acts, n_y), 'y', 0, 0, tiled=True).reshape(wide)]
    all_to_all x1, waiting for transfers between devices: 0.64 us -> 11.7 us  [shards(): recv = lax.all_to_all(send, BITS, 0, 0, tiled=True)]
    all_to_all x1, starting transfers between devices: 25.9 us -> 16.7 us  [shards(): lax.all_to_all(slot_back.reshape(experts, padded, width), BITS, 0, 0, til...]
    convert_element_type x1 -> x0, other arithmetic: 2.33 us -> none  [shards(): chip_sum = (kept.astype(F32) + arrived.astype(F32)).astype(BF16)]
  transfers between devices with their start and end apart: 11 -> 6, of which waited for: 9 -> 5; matrix products, arithmetic and copies ran while one was open for 4% -> 4% of each run, Pallas kernels for 4% -> 4%
where the time goes in v12:
time: 139 us; the launch traced here: 138 us
  waiting for transfers between devices  64.6 us (46%)
  starting transfers between devices  49.9 us (36%)
  Pallas kernels  13.2 us (9%)
  between operations  3.55 us (3%)
  local copies, waits for them, and re-layouts  3.37 us (2%)
  other arithmetic  2.65 us (2%)
    all_to_all x1, waiting for transfers between devices, shards(): lax.all_to_all(chip_sum.reshape((n_y,) + piece), 'y', 0, 0, tiled=True)  25.7 us
    all_to_all x1, waiting for transfers between devices, shards(): lax.all_to_all(copies(acts, n_y), 'y', 0, 0, tiled=True).reshape(wide)  21 us
    all_to_all x1, starting transfers between devices, shards(): lax.all_to_all(slot_back.reshape(experts, padded, width), BITS, 0, 0, til...  16.7 us
    all_to_all x1, starting transfers between devices, shards(): recv = lax.all_to_all(send, BITS, 0, 0, tiled=True)  13.9 us
    pallas_call x6, Pallas kernels, call(): pl.pallas_call(kernel, out_shape=outs, in_specs=[smem] * scalars + [rest]...  12.2 us
    all_to_all x1, waiting for transfers between devices, shards(): recv = lax.all_to_all(send, BITS, 0, 0, tiled=True)  11.7 us
    ppermute x2, starting transfers between devices, pair_permute(): return lax.ppermute(x, axis, [(0, 1), (1, 0)])  8.95 us
    all_to_all x1, starting transfers between devices, shards(): lax.all_to_all(chip_sum.reshape((n_y,) + piece), 'y', 0, 0, tiled=True)  6.83 us
  transfers between devices with their start and end apart: 6, of which 5 were waited for; matrix products, arithmetic and copies ran while one was open for 4% of the time, Pallas kernels for 4%

profile of v12, /device:TPU:1, one launch (start us, length us, event | category | flops | bytes accessed | tf_op | source)
XLA Modules:
  0.0 138.1 jit_solution(18443617784242674568)
XLA Ops:
  0.7 2.4 %pick_rows.1 = bf16[768,256]{1,0:T(8,128)(2,1)} custom-call(s32[8,32]{1,0:T(8,128)} %bitcast.51, f32[8,32]{1,0:T(8,128)} %bitcast.55, bf16[32,256]{1,0:T(8,128)(2,1)} %tok_in.1, bf16[32,256]{1,0:T(8,128)(2,1)} %grad_in.1), custom_call_target="tpu_custom_call" | custom-call | flops 452984832 | bytes 427008 | tf_op jit(solution)/shard_map/pick_rows/pallas_call | solution.py:102
  3.1 13.9 %all-to-all-start = ((bf16[32,24,256]{2,1,0:T(8,128)(2,1)}), bf16[32,24,256]{2,1,0:T(8,128)(2,1)S(1)}, u32[]{:S(2)}, u32[]{:S(2)}) async-start(bf16[32,24,256]{2,1,0:T(8,128)(2,1)} %bitcast.50), calls=%async_computation | async-start | bytes 786432 | tf_op jit(solution)/shard_map/all_to_all | solution.py:291
  17.0 0.6 dynamic_slice.7
  18.2 0.2 copy.61
  18.4 0.2 copy.60
  18.6 0.1 slice_bitcast_fusion.2
  18.8 0.3 pad_maximum_fusion.1
  19.1 11.7 %all-to-all-done = bf16[32,24,256]{2,1,0:T(8,128)(2,1)S(1)} async-done(((bf16[32,24,256]{2,1,0:T(8,128)(2,1)}), bf16[32,24,256]{2,1,0:T(8,128)(2,1)S(1)}, u32[]{:S(2)}, u32[]{:S(2)}) %all-to-all-start) | async-done | bytes 393248 | tf_op jit(solution)/shard_map/all_to_all | solution.py:291
  30.7 0.8 away_partials.1
  31.5 4.4 %collective-permute-start.25 = (bf16[384,1152]{1,0:T(8,128)(2,1)S(1)}, bf16[384,1152]{1,0:T(8,128)(2,1)S(1)}, u32[]{:S(2)}, u32[]{:S(2)}) collective-permute-start(bf16[384,1152]{1,0:T(8,128)(2,1)S(1)} %get-tuple-element.108), channel_id=1, source_target_pairs={{0,32},{32,0},{1,33},{33,1},{2,34},{34,2},{3,35},{35,3},{4,36},{36... | collective-permute-start | bytes 2654216 | tf_op jit(solution)/shard_map/ppermute | solution.py:257
  35.9 2.0 %collective-permute-done.25.add_ref = bf16[384,1152]{1,0:T(8,128)(2,1)S(1)} collective-permute-done((bf16[384,1152]{1,0:T(8,128)(2,1)S(1)}, bf16[384,1152]{1,0:T(8,128)(2,1)S(1)}, u32[]{:S(2)}, u32[]{:S(2)}) %collective-permute-start.25) | collective-permute-done | bytes 884768 | tf_op jit(solution)/shard_map/ppermute | solution.py:257
  37.9 1.4 %keep_partials.1 = bf16[384,1152]{1,0:T(8,128)(2,1)} custom-call(s32[1]{0:T(128)} %bitcast.core_ref, bf16[768,256]{1,0:T(8,128)(2,1)S(1)} %bitcast.46, bf16[768,256]{1,0:T(8,128)(2,1)S(1)} %bitcast.44, bf16[768,256]{1,0:T(8,128)(2,1)S(1)} %bitcast.49, bf16[768,256]{1,0:T(8,128)(2,1)S(1)} %get-tuple-element.111.rows_ref, ...), custom_call_target="tpu_custom_call" | custom-call | flops 452984832 | bytes 3342338 | tf_op jit(solution)/shard_map/keep_partials/pallas_call | solution.py:102
  39.3 6.8 %all-to-all-start.1 = ((bf16[8,48,1152]{2,1,0:T(8,128)(2,1)}), bf16[8,48,1152]{2,1,0:T(8,128)(2,1)S(1)}, u32[]{:S(2)}, u32[]{:S(2)}) async-start(bf16[8,48,1152]{2,1,0:T(8,128)(2,1)} %bitcast.14), calls=%async_computation.1 | async-start | bytes 1769472 | tf_op jit(solution)/shard_map/all_to_all | solution.py:313
  46.2 25.7 %all-to-all-done.1 = bf16[8,48,1152]{2,1,0:T(8,128)(2,1)S(1)} async-done(((bf16[8,48,1152]{2,1,0:T(8,128)(2,1)}), bf16[8,48,1152]{2,1,0:T(8,128)(2,1)S(1)}, u32[]{:S(2)}, u32[]{:S(2)}) %all-to-all-start.1) | async-done | bytes 884768 | tf_op jit(solution)/shard_map/all_to_all | solution.py:313
  72.1 1.0 copies.1
  73.1 3.6 %all-to-all-start.2 = ((bf16[8,48,1152]{2,1,0:T(8,128)(2,1)}), bf16[8,48,1152]{2,1,0:T(8,128)(2,1)S(1)}, u32[]{:S(2)}, u32[]{:S(2)}) async-start(bf16[8,48,1152]{2,1,0:T(8,128)(2,1)} %copies.1), calls=%async_computation.2 | async-start | bytes 1769472 | tf_op jit(solution)/shard_map/all_to_all | solution.py:325
  76.6 1.1 conditional.7
  76.7 1.1 copy.63
  77.7 0.2 copy.69
  78.0 1.1 pad_maximum_fusion.weight_ref
  79.1 21.0 %all-to-all-done.2 = bf16[8,48,1152]{2,1,0:T(8,128)(2,1)S(1)} async-done(((bf16[8,48,1152]{2,1,0:T(8,128)(2,1)}), bf16[8,48,1152]{2,1,0:T(8,128)(2,1)S(1)}, u32[]{:S(2)}, u32[]{:S(2)}) %all-to-all-start.2) | async-done | bytes 884768 | tf_op jit(solution)/shard_map/all_to_all | solution.py:325
  100.1 4.6 %collective-permute-start.26 = (bf16[384,1152]{1,0:T(8,128)(2,1)S(1)}, bf16[384,1152]{1,0:T(8,128)(2,1)S(1)}, u32[]{:S(2)}, u32[]{:S(2)}) collective-permute-start(bf16[384,1152]{1,0:T(8,128)(2,1)S(1)} %bitcast.39), channel_id=1, source_target_pairs={{0,32},{32,0},{1,33},{33,1},{2,34},{34,2},{3,35},{35,3},{4,36},{36... | collective-permute-start | bytes 2654216 | tf_op jit(solution)/shard_map/ppermute | solution.py:257
  106.6 0.4 mine_back.1.total_ref
  107.0 1.4 %slot_back.1 = bf16[512,256]{1,0:T(8,128)(2,1)} custom-call(s32[1]{0:T(128)} %bitcast.core_ref, bf16[384,1152]{1,0:T(8,128)(2,1)S(1)} %collective-permute-done.26.theirs_ref, bf16[512,768]{1,0:T(8,128)(2,1)S(1)} %pad_maximum_fusion.weight_ref, f32[256,384]{1,0:T(8,128)S(1)} %mine_back.1.total_ref), custom_call_target="tpu_custom_call" | custom-call | flops 452984832 | bytes 2129922 | tf_op jit(solution)/shard_map/slot_back/pallas_call | solution.py:102
  108.6 0.1 convert_reduce_fusion.1
  108.7 16.7 %all-to-all-start.3 = ((bf16[32,16,256]{2,1,0:T(8,128)(2,1)}), bf16[32,16,256]{2,1,0:T(8,128)(2,1)S(1)}, u32[]{:S(2)}, u32[]{:S(2)}) async-start(bf16[32,16,256]{2,1,0:T(8,128)(2,1)} %bitcast.24), calls=%async_computation.3 | async-start | bytes 524288 | tf_op jit(solution)/shard_map/all_to_all | solution.py:343
  125.7 0.6 gather_fusion
  126.3 0.2 copy.74
  126.5 0.7 convert_bitcast_fusion
  127.3 5.8 %weight_grads.1 = (bf16[256,768]{1,0:T(8,128)(2,1)}, bf16[256,768]{1,0:T(8,128)(2,1)}, bf16[768,256]{1,0:T(8,128)(2,1)}) custom-call(s32[1]{0:T(128)} %bitcast.core_ref, bf16[384,1152]{1,0:T(8,128)(2,1)S(1)} %bitcast.41, bf16[384,1152]{1,0:T(8,128)(2,1)S(1)} %collective-permute-done.26.theirs_ref, bf16[512,384]{1,0:T(8,128)(2,1)S(1)} %pad_maximum_fusion.2.rows_ref, ...), custom_call_target="tpu_custom_call" | custom-call | flops 452984832 | bytes 3375106 | tf_op jit(solution)/shard_map/weight_grads/pallas_call | solution.py:102
  133.0 4.2 %all-to-all-done.3 = bf16[32,16,256]{2,1,0:T(8,128)(2,1)S(1)} async-done(((bf16[32,16,256]{2,1,0:T(8,128)(2,1)}), bf16[32,16,256]{2,1,0:T(8,128)(2,1)S(1)}, u32[]{:S(2)}, u32[]{:S(2)}) %all-to-all-start.3) | async-done | bytes 262176 | tf_op jit(solution)/shard_map/all_to_all | solution.py:343
  137.3 0.8 fusion
  (32 shorter events, 0.8 us)
Async XLA Ops:
  0.6 16.3 %copy-start.4 = (s32[32]{0:T(128)S(1)}, s32[32]{0:T(128)}, u32[]{:S(2)}) copy-start(s32[32]{0:T(128)} %param.41) | copy-start | bytes 388
  0.6 17.6 %copy-start.2 = (bf16[1,256,768]{2,1,0:T(8,128)(2,1)S(1)}, bf16[1,256,768]{2,1,0:T(8,128)(2,1)}, u32[]{:S(2)}) copy-start(bf16[1,256,768]{2,1,0:T(8,128)(2,1)} %param.38) | copy-start | bytes 1179652
  3.1 15.4 %copy-start.1 = (bf16[1,256,768]{2,1,0:T(8,128)(2,1)S(1)}, bf16[1,256,768]{2,1,0:T(8,128)(2,1)}, u32[]{:S(2)}) copy-start(bf16[1,256,768]{2,1,0:T(8,128)(2,1)} %param.37) | copy-start | bytes 1179652
  3.1 27.7 %all-to-all-start = ((bf16[32,24,256]{2,1,0:T(8,128)(2,1)}), bf16[32,24,256]{2,1,0:T(8,128)(2,1)S(1)}, u32[]{:S(2)}, u32[]{:S(2)}) async-start(bf16[32,24,256]{2,1,0:T(8,128)(2,1)} %bitcast.50), calls=%async_computation | async-start | bytes 786432 | tf_op jit(solution)/shard_map/all_to_all | solution.py:291
  18.6 12.1 %copy-start = (bf16[1,768,256]{2,1,0:T(8,128)(2,1)S(1)}, bf16[1,768,256]{2,1,0:T(8,128)(2,1)}, u32[]{:S(2)}) copy-start(bf16[1,768,256]{2,1,0:T(8,128)(2,1)} %param.39) | copy-start | bytes 1179652
  31.5 6.4 %collective-permute-start.25 = (bf16[384,1152]{1,0:T(8,128)(2,1)S(1)}, bf16[384,1152]{1,0:T(8,128)(2,1)S(1)}, u32[]{:S(2)}, u32[]{:S(2)}) collective-permute-start(bf16[384,1152]{1,0:T(8,128)(2,1)S(1)} %get-tuple-element.108), channel_id=1, source_target_pairs={{0,32},{32,0},{1,33},{33,1},{2,34},{34,2},{3,35},{35,3},{4,36},{36... | collective-permute-start | bytes 2654216 | tf_op jit(solution)/shard_map/ppermute | solution.py:257
  39.3 32.5 %all-to-all-start.1 = ((bf16[8,48,1152]{2,1,0:T(8,128)(2,1)}), bf16[8,48,1152]{2,1,0:T(8,128)(2,1)S(1)}, u32[]{:S(2)}, u32[]{:S(2)}) async-start(bf16[8,48,1152]{2,1,0:T(8,128)(2,1)} %bitcast.14), calls=%async_computation.1 | async-start | bytes 1769472 | tf_op jit(solution)/shard_map/all_to_all | solution.py:313
  73.1 27.0 %all-to-all-start.2 = ((bf16[8,48,1152]{2,1,0:T(8,128)(2,1)}), bf16[8,48,1152]{2,1,0:T(8,128)(2,1)S(1)}, u32[]{:S(2)}, u32[]{:S(2)}) async-start(bf16[8,48,1152]{2,1,0:T(8,128)(2,1)} %copies.1), calls=%async_computation.2 | async-start | bytes 1769472 | tf_op jit(solution)/shard_map/all_to_all | solution.py:325
  100.1 7.0 %collective-permute-start.26 = (bf16[384,1152]{1,0:T(8,128)(2,1)S(1)}, bf16[384,1152]{1,0:T(8,128)(2,1)S(1)}, u32[]{:S(2)}, u32[]{:S(2)}) collective-permute-start(bf16[384,1152]{1,0:T(8,128)(2,1)S(1)} %bitcast.39), channel_id=1, source_target_pairs={{0,32},{32,0},{1,33},{33,1},{2,34},{34,2},{3,35},{35,3},{4,36},{36... | collective-permute-start | bytes 2654216 | tf_op jit(solution)/shard_map/ppermute | solution.py:257
  107.0 1.5 %copy-start.3 = (s32[32,8]{0,1:T(8,128)S(1)}, s32[32,8]{0,1:T(8,128)}, u32[]{:S(2)}) copy-start(s32[32,8]{0,1:T(8,128)} %param.35) | copy-start | bytes 3076
  108.7 28.5 %all-to-all-start.3 = ((bf16[32,16,256]{2,1,0:T(8,128)(2,1)}), bf16[32,16,256]{2,1,0:T(8,128)(2,1)S(1)}, u32[]{:S(2)}, u32[]{:S(2)}) async-start(bf16[32,16,256]{2,1,0:T(8,128)(2,1)} %bitcast.24), calls=%async_computation.3 | async-start | bytes 524288 | tf_op jit(solution)/shard_map/all_to_all | solution.py:343

commit v13 on v12

--- a/solution.py
+++ b/solution.py
@@ -43,17 +43,23 @@
 
 
 def pick_kernel(
-    capacity, routes_in, weights_in, tok_in, grad_in, out_ref, routes_ref, weights_ref, tok_ref, grad_ref, sems
+    capacity, routes_in, weights_in, tok_in, grad_in, out_ref, routes_ref, weights_ref, both_ref, sems
 ):
+    choices, tok_count = routes_ref.shape
     loads = [
         pltpu.make_async_copy(src, dst, sems.at[k])
         for k, (src, dst) in enumerate(
-            ((routes_in, routes_ref), (weights_in, weights_ref), (tok_in, tok_ref), (grad_in, grad_ref))
+            (
+                (routes_in, routes_ref),
+                (weights_in, weights_ref),
+                (tok_in, both_ref.at[:tok_count]),
+                (grad_in, both_ref.at[tok_count : 2 * tok_count]),
+                (grad_in, both_ref.at[2 * tok_count :]),
+            )
         )
     ]
     for load in loads:
         load.start()
-    choices, tok_count = routes_ref.shape
     block = 2 * capacity
     out_rows = out_ref.shape[0]
     experts = out_rows // block
@@ -66,6 +72,8 @@
     is_tok = place < capacity
     tok_place = jnp.where(is_tok, place, -2.0)
     grad_place = jnp.where(is_tok, -2.0, place - capacity)
+    lane = lax.broadcasted_iota(jnp.int32, (out_rows, 3 * tok_count), 1)
+    place = jnp.where(lane < tok_count, tok_place, grad_place)
     square = (tok_count, tok_count)
     earlier = lax.broadcasted_iota(jnp.int32, square, 0) < lax.broadcasted_iota(jnp.int32, square, 1)
     earlier = jnp.where(earlier, 1.0, 0.0).astype(BF16)
@@ -80,17 +88,13 @@
         member = member + jnp.where(hit, 1.0, 0.0)
         weight = weight + jnp.where(hit, weights_ref[k : k + 1, :], 0.0)
     rank = dot(member.astype(BF16), earlier, 1, 0)
-    rank = jnp.where(member > 0.0, rank, -1.0).astype(BF16)
-    weight_hi = weight.astype(BF16)
-    weight_lo = (weight - weight_hi.astype(F32)).astype(BF16)
-    rank_of = dot(spread, rank, 1, 0)
-    tok_pick = jnp.where(rank_of == tok_place, 1.0, 0.0).astype(BF16)
-    grad_here = rank_of == grad_place
-    hi = jnp.where(grad_here, dot(spread, weight_hi, 1, 0), 0.0).astype(BF16)
-    lo = jnp.where(grad_here, dot(spread, weight_lo, 1, 0), 0.0).astype(BF16)
-    out = dot(tok_pick, tok_ref[...], 1, 0)
-    out = out + dot(hi, grad_ref[...], 1, 0) + dot(lo, grad_ref[...], 1, 0)
-    out_ref[...] = out.astype(BF16)
+    rank = jnp.where(member > 0.0, rank, -1.0)
+    weight_hi = weight.astype(BF16).astype(F32)
+    rank = jnp.concatenate([rank, rank, rank], 1).astype(BF16)
+    value = jnp.concatenate([jnp.ones_like(weight), weight_hi, weight - weight_hi], 1).astype(BF16)
+    here = dot(spread, rank, 1, 0) == place
+    pick = jnp.where(here, dot(spread, value, 1, 0), 0.0).astype(BF16)
+    out_ref[...] = dot(pick, both_ref[...], 1, 0).astype(BF16)
 
 
 def call(kernel, name, out_shapes, operands, scalars=0, in_hbm=False, scratch=(), dtype=BF16):
@@ -119,7 +123,12 @@
         [(2 * capacity * experts, tokens.shape[1])],
         operands,
         in_hbm=True,
-        scratch=[pltpu.VMEM(v.shape, v.dtype) for v in operands] + [pltpu.SemaphoreType.DMA((4,))],
+        scratch=[
+            pltpu.VMEM(routes.T.shape, routes.dtype),
+            pltpu.VMEM(weights.T.shape, weights.dtype),
+            pltpu.VMEM((3 * tokens.shape[0], tokens.shape[1]), BF16),
+            pltpu.SemaphoreType.DMA((5,)),
+        ],
     )[0]
     return out.reshape(experts, 2 * capacity, tokens.shape[1])
 
@@ -187,15 +196,10 @@
     return part + dot(weight_ref[width:, cut], units_ref[:, rows : 2 * rows], 1, 0)
 
 
-def mine_back_kernel(core_ref, mine_ref, weight_ref, out_ref):
+def mine_back_kernel(capacity, core_ref, mine_ref, weight_ref, out_ref, place_ref):
     units, rows = mine_ref.shape[0], out_ref.shape[1]
     out_ref[...] = half_back(mine_ref, weight_ref, side(core_ref[0], units), rows)
-
-
-def back_kernel(capacity, core_ref, theirs_ref, weight_ref, total_ref, out_ref):
-    units, rows = theirs_ref.shape[0], total_ref.shape[1]
-    out_rows = out_ref.shape[0]
-    total = total_ref[...] + half_back(theirs_ref, weight_ref, side(1 - core_ref[0], units), rows)
+    out_rows = place_ref.shape[0]
     groups = rows // capacity
     padded = out_rows // groups
     row = lax.broadcasted_iota(jnp.int32, (out_rows, groups), 0)
@@ -204,8 +208,13 @@
     source = jnp.where(inside, row - group * (padded - capacity) + 1, 0).astype(F32)
     source = jnp.sum(source, axis=1, keepdims=True) - 1.0
     column = lax.broadcasted_iota(jnp.int32, (out_rows, rows), 1).astype(F32)
-    place = jnp.where(column == source, 1.0, 0.0).astype(BF16)
-    out_ref[...] = dot(place, total.astype(BF16), 1, 1).astype(BF16)
+    place_ref[...] = jnp.where(column == source, 1.0, 0.0)
+
+
+def back_kernel(core_ref, theirs_ref, weight_ref, total_ref, place_ref, out_ref):
+    units, rows = theirs_ref.shape[0], total_ref.shape[1]
+    total = total_ref[...] + half_back(theirs_ref, weight_ref, side(1 - core_ref[0], units), rows)
+    out_ref[...] = dot(place_ref[...].astype(BF16), total.astype(BF16), 1, 1).astype(BF16)
 
 
 def soft_rotate(block, rotation):
@@ -329,14 +338,19 @@
     mine, weights, mate_rows = lax.optimization_barrier((mine, weights, mate_rows))
     theirs = pair_permute(mine, "core")
 
-    mine_back = call(
-        mine_back_kernel, "mine_back", [(width, rows)], (core_arg, mine, weights), 1, dtype=F32
-    )[0]
+    mine_back, place = call(
+        functools.partial(mine_back_kernel, capacity),
+        "mine_back",
+        [(width, rows), (experts * padded, rows)],
+        (core_arg, mine, weights),
+        1,
+        dtype=F32,
+    )
     slot_back = call(
-        functools.partial(back_kernel, capacity),
+        back_kernel,
         "slot_back",
         [(experts * padded, width)],
-        (core_arg, theirs, weights, mine_back),
+        (core_arg, theirs, weights, mine_back, place),
         1,
     )[0]
     slot_back, routes, sign_bits = lax.optimization_barrier((slot_back, routes, sign_bits))

time: 139 us -> 141 us (1.014)
  starting transfers between devices: 49.9 us -> 51.5 us
    all_to_all x1, starting transfers between devices: 16.7 us -> 18.3 us  [shards(): lax.all_to_all(slot_back.reshape(experts, padded, width), BITS, 0, 0, til...]
where the time goes in v13:
time: 141 us; the launch traced here: 140 us
  waiting for transfers between devices  64.6 us (46%)
  starting transfers between devices  51.5 us (37%)
  Pallas kernels  13 us (9%)
  between operations  3.55 us (3%)
  local copies, waits for them, and re-layouts  3.36 us (2%)
  other arithmetic  2.65 us (2%)
    all_to_all x1, waiting for transfers between devices, shards(): lax.all_to_all(chip_sum.reshape((n_y,) + piece), 'y', 0, 0, tiled=True)  25.7 us
    all_to_all x1, waiting for transfers between devices, shards(): lax.all_to_all(copies(acts, n_y), 'y', 0, 0, tiled=True).reshape(wide)  21 us
    all_to_all x1, starting transfers between devices, shards(): lax.all_to_all(slot_back.reshape(experts, padded, width), BITS, 0, 0, til...  18.3 us
    all_to_all x1, starting transfers between devices, shards(): recv = lax.all_to_all(send, BITS, 0, 0, tiled=True)  13.9 us
    pallas_call x6, Pallas kernels, call(): pl.pallas_call(kernel, out_shape=outs, in_specs=[smem] * scalars + [rest]...  12 us
    all_to_all x1, waiting for transfers between devices, shards(): recv = lax.all_to_all(send, BITS, 0, 0, tiled=True)  11.7 us
    ppermute x2, starting transfers between devices, pair_permute(): return lax.ppermute(x, axis, [(0, 1), (1, 0)])  8.97 us
    all_to_all x1, starting transfers between devices, shards(): lax.all_to_all(chip_sum.reshape((n_y,) + piece), 'y', 0, 0, tiled=True)  6.82 us
  transfers between devices with their start and end apart: 6, of which 5 were waited for; matrix products, arithmetic and copies ran while one was open for 4% of the time, Pallas kernels for 4%

profile of v13, /device:TPU:1, one launch (start us, length us, event | category | flops | bytes accessed | tf_op | source)
XLA Modules:
  0.0 139.6 jit_solution(11805823912892156755)
XLA Ops:
  0.7 2.2 %pick_rows.1 = bf16[768,256]{1,0:T(8,128)(2,1)} custom-call(s32[8,32]{1,0:T(8,128)} %bitcast.51, f32[8,32]{1,0:T(8,128)} %bitcast.55, bf16[32,256]{1,0:T(8,128)(2,1)} %tok_in.1, bf16[32,256]{1,0:T(8,128)(2,1)} %grad_in.1), custom_call_target="tpu_custom_call" | custom-call | flops 452984832 | bytes 427008 | tf_op jit(solution)/shard_map/pick_rows/pallas_call | solution.py:106
  2.9 13.9 %all-to-all-start = ((bf16[32,24,256]{2,1,0:T(8,128)(2,1)}), bf16[32,24,256]{2,1,0:T(8,128)(2,1)S(1)}, u32[]{:S(2)}, u32[]{:S(2)}) async-start(bf16[32,24,256]{2,1,0:T(8,128)(2,1)} %bitcast.50), calls=%async_computation | async-start | bytes 786432 | tf_op jit(solution)/shard_map/all_to_all | solution.py:300
  16.8 0.6 dynamic_slice.7
  18.1 0.2 copy.61
  18.3 0.2 copy.60
  18.5 0.1 slice_bitcast_fusion.2
  18.6 0.3 pad_maximum_fusion.1
  18.9 11.7 %all-to-all-done = bf16[32,24,256]{2,1,0:T(8,128)(2,1)S(1)} async-done(((bf16[32,24,256]{2,1,0:T(8,128)(2,1)}), bf16[32,24,256]{2,1,0:T(8,128)(2,1)S(1)}, u32[]{:S(2)}, u32[]{:S(2)}) %all-to-all-start) | async-done | bytes 393248 | tf_op jit(solution)/shard_map/all_to_all | solution.py:300
  30.6 0.8 away_partials.1
  31.4 4.4 %collective-permute-start.25 = (bf16[384,1152]{1,0:T(8,128)(2,1)S(1)}, bf16[384,1152]{1,0:T(8,128)(2,1)S(1)}, u32[]{:S(2)}, u32[]{:S(2)}) collective-permute-start(bf16[384,1152]{1,0:T(8,128)(2,1)S(1)} %get-tuple-element.110), channel_id=1, source_target_pairs={{0,32},{32,0},{1,33},{33,1},{2,34},{34,2},{3,35},{35,3},{4,36},{36... | collective-permute-start | bytes 2654216 | tf_op jit(solution)/shard_map/ppermute | solution.py:266
  35.8 2.0 %collective-permute-done.25.add_ref = bf16[384,1152]{1,0:T(8,128)(2,1)S(1)} collective-permute-done((bf16[384,1152]{1,0:T(8,128)(2,1)S(1)}, bf16[384,1152]{1,0:T(8,128)(2,1)S(1)}, u32[]{:S(2)}, u32[]{:S(2)}) %collective-permute-start.25) | collective-permute-done | bytes 884768 | tf_op jit(solution)/shard_map/ppermute | solution.py:266
  37.8 1.4 %keep_partials.1 = bf16[384,1152]{1,0:T(8,128)(2,1)} custom-call(s32[1]{0:T(128)} %bitcast.core_ref, bf16[768,256]{1,0:T(8,128)(2,1)S(1)} %bitcast.46, bf16[768,256]{1,0:T(8,128)(2,1)S(1)} %bitcast.44, bf16[768,256]{1,0:T(8,128)(2,1)S(1)} %bitcast.49, bf16[768,256]{1,0:T(8,128)(2,1)S(1)} %get-tuple-element.113.rows_ref, ...), custom_call_target="tpu_custom_call" | custom-call | flops 452984832 | bytes 3342338 | tf_op jit(solution)/shard_map/keep_partials/pallas_call | solution.py:106
  39.2 6.8 %all-to-all-start.1 = ((bf16[8,48,1152]{2,1,0:T(8,128)(2,1)}), bf16[8,48,1152]{2,1,0:T(8,128)(2,1)S(1)}, u32[]{:S(2)}, u32[]{:S(2)}) async-start(bf16[8,48,1152]{2,1,0:T(8,128)(2,1)} %bitcast.14), calls=%async_computation.1 | async-start | bytes 1769472 | tf_op jit(solution)/shard_map/all_to_all | solution.py:322
  46.0 25.7 %all-to-all-done.1 = bf16[8,48,1152]{2,1,0:T(8,128)(2,1)S(1)} async-done(((bf16[8,48,1152]{2,1,0:T(8,128)(2,1)}), bf16[8,48,1152]{2,1,0:T(8,128)(2,1)S(1)}, u32[]{:S(2)}, u32[]{:S(2)}) %all-to-all-start.1) | async-done | bytes 884768 | tf_op jit(solution)/shard_map/all_to_all | solution.py:322
  71.9 1.0 copies.1
  73.0 3.6 %all-to-all-start.2 = ((bf16[8,48,1152]{2,1,0:T(8,128)(2,1)}), bf16[8,48,1152]{2,1,0:T(8,128)(2,1)S(1)}, u32[]{:S(2)}, u32[]{:S(2)}) async-start(bf16[8,48,1152]{2,1,0:T(8,128)(2,1)} %copies.1), calls=%async_computation.2 | async-start | bytes 1769472 | tf_op jit(solution)/shard_map/all_to_all | solution.py:334
  76.5 1.1 conditional.7
  76.6 1.1 copy.63
  77.6 0.2 copy.69
  77.9 1.1 pad_maximum_fusion.weight_ref
  79.0 21.0 %all-to-all-done.2 = bf16[8,48,1152]{2,1,0:T(8,128)(2,1)S(1)} async-done(((bf16[8,48,1152]{2,1,0:T(8,128)(2,1)}), bf16[8,48,1152]{2,1,0:T(8,128)(2,1)S(1)}, u32[]{:S(2)}, u32[]{:S(2)}) %all-to-all-start.2) | async-done | bytes 884768 | tf_op jit(solution)/shard_map/all_to_all | solution.py:334
  100.0 4.6 %collective-permute-start.26 = (bf16[384,1152]{1,0:T(8,128)(2,1)S(1)}, bf16[384,1152]{1,0:T(8,128)(2,1)S(1)}, u32[]{:S(2)}, u32[]{:S(2)}) collective-permute-start(bf16[384,1152]{1,0:T(8,128)(2,1)S(1)} %bitcast.39), channel_id=1, source_target_pairs={{0,32},{32,0},{1,33},{33,1},{2,34},{34,2},{3,35},{35,3},{4,36},{36... | collective-permute-start | bytes 2654216 | tf_op jit(solution)/shard_map/ppermute | solution.py:266
  106.5 0.4 mine_back.1
  106.9 1.4 %slot_back.1 = bf16[512,256]{1,0:T(8,128)(2,1)} custom-call(s32[1]{0:T(128)} %bitcast.core_ref, bf16[384,1152]{1,0:T(8,128)(2,1)S(1)} %collective-permute-done.26.theirs_ref, bf16[512,768]{1,0:T(8,128)(2,1)S(1)} %pad_maximum_fusion.weight_ref, f32[256,384]{1,0:T(8,128)S(1)} %get-tuple-element.127.total_ref, f32[512,384]{1,0:T(8,128)S(1)} %get-tuple-element.128.place_ref), custom_call_target="tpu_custom_call" | custom-call | flops 452984832 | bytes 2523138 | tf_op jit(solution)/shard_map/slot_back/pallas_call | solution.py:106
  108.4 0.1 convert_reduce_fusion.1
  108.6 18.3 %all-to-all-start.3 = ((bf16[32,16,256]{2,1,0:T(8,128)(2,1)}), bf16[32,16,256]{2,1,0:T(8,128)(2,1)S(1)}, u32[]{:S(2)}, u32[]{:S(2)}) async-start(bf16[32,16,256]{2,1,0:T(8,128)(2,1)} %bitcast.24), calls=%async_computation.3 | async-start | bytes 524288 | tf_op jit(solution)/shard_map/all_to_all | solution.py:357
  127.2 0.6 gather_fusion
  127.8 0.2 copy.74
  127.9 0.7 convert_bitcast_fusion
  128.7 5.8 %weight_grads.1 = (bf16[256,768]{1,0:T(8,128)(2,1)}, bf16[256,768]{1,0:T(8,128)(2,1)}, bf16[768,256]{1,0:T(8,128)(2,1)}) custom-call(s32[1]{0:T(128)} %bitcast.core_ref, bf16[384,1152]{1,0:T(8,128)(2,1)S(1)} %bitcast.41, bf16[384,1152]{1,0:T(8,128)(2,1)S(1)} %collective-permute-done.26.theirs_ref, bf16[512,384]{1,0:T(8,128)(2,1)S(1)} %pad_maximum_fusion.2.rows_ref, ...), custom_call_target="tpu_custom_call" | custom-call | flops 452984832 | bytes 3375106 | tf_op jit(solution)/shard_map/weight_grads/pallas_call | solution.py:106
  134.5 4.2 %all-to-all-done.3 = bf16[32,16,256]{2,1,0:T(8,128)(2,1)S(1)} async-done(((bf16[32,16,256]{2,1,0:T(8,128)(2,1)}), bf16[32,16,256]{2,1,0:T(8,128)(2,1)S(1)}, u32[]{:S(2)}, u32[]{:S(2)}) %all-to-all-start.3) | async-done | bytes 262176 | tf_op jit(solution)/shard_map/all_to_all | solution.py:357
  138.7 0.8 fusion
  (32 shorter events, 0.8 us)
Async XLA Ops:
  0.6 16.2 %copy-start.4 = (s32[32]{0:T(128)S(1)}, s32[32]{0:T(128)}, u32[]{:S(2)}) copy-start(s32[32]{0:T(128)} %param.41) | copy-start | bytes 388
  0.6 17.4 %copy-start.2 = (bf16[1,256,768]{2,1,0:T(8,128)(2,1)S(1)}, bf16[1,256,768]{2,1,0:T(8,128)(2,1)}, u32[]{:S(2)}) copy-start(bf16[1,256,768]{2,1,0:T(8,128)(2,1)} %param.38) | copy-start | bytes 1179652
  2.9 15.4 %copy-start.1 = (bf16[1,256,768]{2,1,0:T(8,128)(2,1)S(1)}, bf16[1,256,768]{2,1,0:T(8,128)(2,1)}, u32[]{:S(2)}) copy-start(bf16[1,256,768]{2,1,0:T(8,128)(2,1)} %param.37) | copy-start | bytes 1179652
  2.9 27.7 %all-to-all-start = ((bf16[32,24,256]{2,1,0:T(8,128)(2,1)}), bf16[32,24,256]{2,1,0:T(8,128)(2,1)S(1)}, u32[]{:S(2)}, u32[]{:S(2)}) async-start(bf16[32,24,256]{2,1,0:T(8,128)(2,1)} %bitcast.50), calls=%async_computation | async-start | bytes 786432 | tf_op jit(solution)/shard_map/all_to_all | solution.py:300
  18.5 12.1 %copy-start = (bf16[1,768,256]{2,1,0:T(8,128)(2,1)S(1)}, bf16[1,768,256]{2,1,0:T(8,128)(2,1)}, u32[]{:S(2)}) copy-start(bf16[1,768,256]{2,1,0:T(8,128)(2,1)} %param.39) | copy-start | bytes 1179652
  31.4 6.4 %collective-permute-start.25 = (bf16[384,1152]{1,0:T(8,128)(2,1)S(1)}, bf16[384,1152]{1,0:T(8,128)(2,1)S(1)}, u32[]{:S(2)}, u32[]{:S(2)}) collective-permute-start(bf16[384,1152]{1,0:T(8,128)(2,1)S(1)} %get-tuple-element.110), channel_id=1, source_target_pairs={{0,32},{32,0},{1,33},{33,1},{2,34},{34,2},{3,35},{35,3},{4,36},{36... | collective-permute-start | bytes 2654216 | tf_op jit(solution)/shard_map/ppermute | solution.py:266
  39.2 32.5 %all-to-all-start.1 = ((bf16[8,48,1152]{2,1,0:T(8,128)(2,1)}), bf16[8,48,1152]{2,1,0:T(8,128)(2,1)S(1)}, u32[]{:S(2)}, u32[]{:S(2)}) async-start(bf16[8,48,1152]{2,1,0:T(8,128)(2,1)} %bitcast.14), calls=%async_computation.1 | async-start | bytes 1769472 | tf_op jit(solution)/shard_map/all_to_all | solution.py:322
  73.0 27.0 %all-to-all-start.2 = ((bf16[8,48,1152]{2,1,0:T(8,128)(2,1)}), bf16[8,48,1152]{2,1,0:T(8,128)(2,1)S(1)}, u32[]{:S(2)}, u32[]{:S(2)}) async-start(bf16[8,48,1152]{2,1,0:T(8,128)(2,1)} %copies.1), calls=%async_computation.2 | async-start | bytes 1769472 | tf_op jit(solution)/shard_map/all_to_all | solution.py:334
  100.0 6.9 %collective-permute-start.26 = (bf16[384,1152]{1,0:T(8,128)(2,1)S(1)}, bf16[384,1152]{1,0:T(8,128)(2,1)S(1)}, u32[]{:S(2)}, u32[]{:S(2)}) collective-permute-start(bf16[384,1152]{1,0:T(8,128)(2,1)S(1)} %bitcast.39), channel_id=1, source_target_pairs={{0,32},{32,0},{1,33},{33,1},{2,34},{34,2},{3,35},{35,3},{4,36},{36... | collective-permute-start | bytes 2654216 | tf_op jit(solution)/shard_map/ppermute | solution.py:266
  106.9 1.4 %copy-start.3 = (s32[32,8]{0,1:T(8,128)S(1)}, s32[32,8]{0,1:T(8,128)}, u32[]{:S(2)}) copy-start(s32[32,8]{0,1:T(8,128)} %param.35) | copy-start | bytes 3076
  108.6 30.1 %all-to-all-start.3 = ((bf16[32,16,256]{2,1,0:T(8,128)(2,1)}), bf16[32,16,256]{2,1,0:T(8,128)(2,1)S(1)}, u32[]{:S(2)}, u32[]{:S(2)}) async-start(bf16[32,16,256]{2,1,0:T(8,128)(2,1)} %bitcast.24), calls=%async_computation.3 | async-start | bytes 524288 | tf_op jit(solution)/shard_map/all_to_all | solution.py:357
